TPU v7x, 768 devices: a whole 4x8x12 slice. The times are simulated.
768 devices in a mesh: dp: 24 (over z_lo, x, core), fsdp: 32 (over z_hi, y).
Axes of the slice: x: 4, y: 8, z: 12 (z_hi: 4, z_lo: 3; z = z_hi * 3 + z_lo), core: 2. Of those that a mesh axis runs over, the one named last changes fastest.
Arguments:
- patches: bfloat16 [9216, 32, 1280], P(('dp', 'fsdp')), may hold values from -16 to 16
- values: bfloat16 [9216, 32, 640], P(('dp', 'fsdp')), may hold values from -6 to 6
- upstream: bfloat16 [9216, 32, 640], P(('dp', 'fsdp')), may hold values from -6 to 6
- coords: int32 [9216, 2, 32], P(('dp', 'fsdp')), may hold values from 0 to 31, as said below
- counts: int32 [9216], P(('dp', 'fsdp')), may hold values from 1 to 32
- dest: int32 [9216, 1], P(('dp', 'fsdp')), may hold values from 0 to 23; in each aligned block of 12 rows (0 to 11, 12 to 23, ...) no two rows name the same one
- weight: bfloat16 [1280, 1280], P('fsdp'), may hold values from -0.15625 to 0.15625
Outputs:
- context: bfloat16 [18432, 32, 640], P(('dp', 'fsdp'))
- grad_weight: float32 [1280, 1280], P('fsdp')
Inputs may be any that keep to these rules, and one draw needn't show every extreme that they name: `dest`: the 12 windows of one device are assigned to different dp indices. `coords`: A patch's row and column in a grid of some width, in row-major order.
All inputs are finite; a program needn't handle non-finite values.
Results may differ from a plain program's by a relative error of at most 0.033.
The roundings to bfloat16 on the way count: a program that leaves them out, or rounds other values in their place, can miss the bound.
Values may be sent and summed in bfloat16 or wider, within the bound.
No kernel may reach another device: no remote copies, remote signals or barrier semaphores. Data moves between devices by JAX's collectives and lax.ppermute only.
A program may use at most 32 MiB of HBM per device.

v0:
```python
import math

import jax
import jax.numpy as jnp
from jax import lax
from jax.sharding import PartitionSpec as P

HD = 80


def rotary(tensor_in, row_pos, col_pos, turn_sign):
    quarter = tensor_in.shape[-1] // 4
    frequency = 10000.0 ** (-jnp.arange(quarter, dtype=jnp.float32) / quarter)
    pieces = []
    for position, section in (
        (row_pos, tensor_in[..., : 2 * quarter]),
        (col_pos, tensor_in[..., 2 * quarter :]),
    ):
        angles = position[:, None] * frequency[None, :]
        cosine = jnp.cos(angles)[:, None, :]
        sine_part = turn_sign * jnp.sin(angles)[:, None, :]
        front_half = section[..., :quarter]
        back_half = section[..., quarter:]
        pieces.append(front_half * cosine - back_half * sine_part)
        pieces.append(back_half * cosine + front_half * sine_part)
    return jnp.concatenate(pieces, axis=-1)


def per_device(patches, values, upstream, coords, counts, dest, weight):
    peer_count = lax.axis_size("dp")
    window_count, patch_len, model_width = patches.shape
    value_width = values.shape[-1]
    head_count = value_width // HD
    score_scale = 1.0 / math.sqrt(HD)
    row_total = window_count * patch_len
    flat_patches = patches.reshape(row_total, model_width)
    full_weight = lax.all_gather(weight, "fsdp", axis=0, tiled=True)
    projected = jnp.dot(flat_patches, full_weight, preferred_element_type=jnp.float32)
    row_pos = coords[:, 0, :].reshape(row_total).astype(jnp.float32)
    col_pos = coords[:, 1, :].reshape(row_total).astype(jnp.float32)
    valid = (jnp.arange(patch_len, dtype=jnp.int32)[None, :] < counts[:, None]).reshape(row_total)
    group_size = math.gcd(window_count, max(1, 128 // patch_len))
    block_count = window_count // group_size
    block_rows = group_size * patch_len
    head_shape = (block_count, block_rows, head_count, HD)
    queries = rotary(
        projected[:, :value_width].reshape(row_total, head_count, HD), row_pos, col_pos, 1.0
    )
    keys_rot = rotary(
        projected[:, value_width:].reshape(row_total, head_count, HD), row_pos, col_pos, 1.0
    )
    queries = queries.astype(jnp.bfloat16).reshape(head_shape)
    keys_rot = keys_rot.astype(jnp.bfloat16).reshape(head_shape)
    value_heads = values.reshape(head_shape)
    upstream_heads = upstream.reshape(head_shape)
    window_of = jnp.arange(block_rows, dtype=jnp.int32) // patch_len
    same_window = window_of[:, None] == window_of[None, :]
    valid_blocks = valid.reshape(block_count, block_rows)
    key_ok = same_window[None, :, :] & valid_blocks[:, None, :]
    scores = (
        jnp.einsum("bqhd,bkhd->bhqk", queries, keys_rot, preferred_element_type=jnp.float32)
        * score_scale
    )
    scores = jnp.where(key_ok[:, None, :, :], scores, -1e30)
    row_max = jnp.max(scores, axis=-1, keepdims=True)
    exps = jnp.exp(scores - row_max)
    probs = (
        exps
        / jnp.sum(exps, axis=-1, keepdims=True)
        * valid_blocks.astype(jnp.float32)[:, None, :, None]
    )
    probs_low = probs.astype(jnp.bfloat16)
    context = jnp.einsum(
        "bhqk,bkhd->bqhd", probs_low, value_heads, preferred_element_type=jnp.float32
    )
    context = context.astype(jnp.bfloat16).reshape(window_count, patch_len * value_width)
    onehot = (dest[:, 0][:, None] == jnp.arange(peer_count, dtype=jnp.int32)[None, :]).astype(
        jnp.bfloat16
    )
    routed = jnp.einsum("sp,sc->pc", onehot, context, preferred_element_type=jnp.float32)
    routed = routed.astype(jnp.bfloat16).reshape(peer_count, patch_len, value_width)
    placed = lax.all_to_all(routed, "dp", split_axis=0, concat_axis=0, tiled=True)
    dprobs = jnp.einsum(
        "bqhd,bkhd->bhqk", upstream_heads, value_heads, preferred_element_type=jnp.float32
    )
    row_delta = jnp.sum(probs * dprobs, axis=-1, keepdims=True)
    dscores = (probs * (dprobs - row_delta) * score_scale).astype(jnp.bfloat16)
    dquery = jnp.einsum("bhqk,bkhd->bqhd", dscores, keys_rot, preferred_element_type=jnp.float32)
    dkey = jnp.einsum("bhqk,bqhd->bkhd", dscores, queries, preferred_element_type=jnp.float32)
    dquery = rotary(dquery.reshape(row_total, head_count, HD), row_pos, col_pos, -1.0)
    dkey = rotary(dkey.reshape(row_total, head_count, HD), row_pos, col_pos, -1.0)
    grads_proj = jnp.concatenate(
        [dquery.reshape(row_total, value_width), dkey.reshape(row_total, value_width)], axis=-1
    ).astype(jnp.bfloat16)
    partial_value = jnp.einsum(
        "rd,rc->dc", flat_patches, grads_proj, preferred_element_type=jnp.float32
    )
    owned = lax.psum_scatter(
        partial_value.astype(jnp.bfloat16), "fsdp", scatter_dimension=0, tiled=True
    )
    grad_weight = lax.psum(owned, "dp").astype(jnp.float32)
    return (placed, grad_weight)


def solution(mesh):
    return jax.shard_map(
        per_device,
        mesh=mesh,
        in_specs=(
            P(("dp", "fsdp"), None, None),
            P(("dp", "fsdp"), None, None),
            P(("dp", "fsdp"), None, None),
            P(("dp", "fsdp"), None, None),
            P(("dp", "fsdp")),
            P(("dp", "fsdp"), None),
            P("fsdp", None),
        ),
        out_specs=(P(("dp", "fsdp"), None, None), P("fsdp", None)),
        check_vma=False,
    )
```

profile of v0, /device:TPU:1, one launch (start us, length us, event | category | flops | bytes accessed | tf_op | source)
XLA Modules:
  0.0 625.9 jit_solution(9880350370550685695)
XLA Ops:
  7.2 0.7 all-gather.2.cloned.1.call-update
  8.0 0.7 lt.33
  8.9 0.1 lt.35
  9.0 0.8 convert_reduce_fusion.1
  9.9 1.9 reshape.317
  11.9 0.5 copy.63
  12.4 0.8 reshape.320
  13.3 0.7 broadcast_and_fusion
  14.1 1.0 broadcast_multiply_fusion.1
  15.0 1.9 fusion.24
  16.9 116.1 %all-gather.2.cloned.1.call-done = bf16[1280,1280]{1,0:T(8,128)(2,1)} async-done(((bf16[40,1280]{1,0:T(8,128)(2,1)}), bf16[1280,1280]{1,0:T(8,128)(2,1)}) %all-gather.2.cloned.1.call-update) | async-done | bytes 3276816 | tf_op jit(solution)/shard_map/all_gather | solution.py:37
  133.0 3.4 fusion.41
  136.3 1.1 fusion.39
  137.4 1.5 copy.44
  138.9 1.8 subtract_convert_fusion.7
  140.7 1.0 reshape.325
  141.7 0.7 copy.49
  142.4 1.0 reshape.326
  143.4 0.7 copy.50
  144.1 1.0 reshape.328
  145.0 0.7 copy.52
  145.8 0.7 copy.51
  146.5 0.3 copy.53
  146.8 1.0 subtract_convert_fusion.5
  148.2 0.5 copy-done.4
  148.9 2.7 fusion.40
  151.6 0.6 copy-done.10
  152.2 3.6 fusion.14
  155.9 4.0 fusion.17
  160.0 0.6 copy-done.3
  160.6 0.2 subtract_convert_fusion.1
  160.8 0.2 subtract_convert_fusion.3
  161.0 0.1 pad_maximum_fusion.3
  161.2 0.1 pad_maximum_fusion.2
  161.3 3.6 fusion.2
  164.9 5.7 copy.91
  170.6 1.4 copy-done.9
  172.0 0.4 fusion.20
  172.4 0.4 copy.64
  172.8 1.4 reshape.318
  174.2 0.5 convolution_convert_fusion
  174.8 1.1 copy.95
  175.9 8.4 %all-to-all-start = ((bf16[24,32,640]{2,1,0:T(8,128)(2,1)}), bf16[24,32,640]{2,1,0:T(8,128)(2,1)S(1)}, u32[]{:S(2)}, u32[]{:S(2)}) async-start(bf16[24,32,640]{2,1,0:T(8,128)(2,1)} %bitcast.25), calls=%async_computation | async-start | bytes 1966080 | tf_op jit(solution)/shard_map/all_to_all | solution.py:82
  184.4 215.8 %reduce-scatter.4.cloned.1.call-done = bf16[40,1280]{1,0:T(8,128)(2,1)} async-done(((bf16[1280,1280]{1,0:T(8,128)(2,1)}), bf16[40,1280]{1,0:T(8,128)(2,1)}) %reduce-scatter.4.cloned.1.call-update) | async-done | bytes 102416
  400.2 1.8 copy.92
  402.0 214.6 %all-reduce.2.cloned.1.call-done = bf16[40,1280]{0,1:T(8,128)(2,1)} async-done(((bf16[40,1280]{0,1:T(8,128)(2,1)}), bf16[40,1280]{0,1:T(8,128)(2,1)}) %all-reduce.2.cloned.1.call-update) | async-done | bytes 102416 | tf_op jit(solution)/shard_map/psum | solution.py:101
  616.6 1.8 copy.71
  618.4 0.9 copy.104
  (46 shorter events, 1.3 us)
Async XLA Ops:
  7.2 125.8 %copy-start = (bf16[12,32,1280]{2,1,0:T(8,128)(2,1)S(1)}, bf16[12,32,1280]{2,1,0:T(8,128)(2,1)}, u32[]{:S(2)}) copy-start(bf16[12,32,1280]{2,1,0:T(8,128)(2,1)} %param.7) | copy-start | bytes 2949124
  7.2 5.2 copy-start.2
  7.2 125.8 %all-gather.2.cloned.1.call-start = ((), (), s32[]{:S(2)}) async-start(), calls=%async_computation.2 | async-start | bytes 3379200 | tf_op jit(solution)/shard_map/all_gather | solution.py:37
  7.9 392.2 %reduce-scatter.4.cloned.1.call-start = ((), (), s32[]{:S(2)}) async-start(), calls=%async_computation.4 | async-start | bytes 3379200
  140.7 5.0 copy-start.1
  147.8 0.9 copy-start.4
  147.8 1.0 copy-start.5
  147.8 1.0 copy-start.6
  147.8 1.1 copy-start.7
  151.6 0.6 copy-start.10
  159.8 0.8 copy-start.3
  170.6 1.4 copy-start.9
  170.6 1.4 copy-start.11
  172.4 1.8 copy-start.8
  175.9 226.1 %all-to-all-start = ((bf16[24,32,640]{2,1,0:T(8,128)(2,1)}), bf16[24,32,640]{2,1,0:T(8,128)(2,1)S(1)}, u32[]{:S(2)}, u32[]{:S(2)}) async-start(bf16[24,32,640]{2,1,0:T(8,128)(2,1)} %bitcast.25), calls=%async_computation | async-start | bytes 1966080 | tf_op jit(solution)/shard_map/all_to_all | solution.py:82
  184.3 432.3 %all-reduce.2.cloned.1.call-start = ((), (), s32[]{:S(2)}) async-start(), calls=%async_computation.3 | async-start | bytes 655360 | tf_op jit(solution)/shard_map/psum | solution.py:101
Sparse Core Ops, SparseCore 0:
  11.7 121.1 all-gather.1
  170.7 229.4 reduce-scatter.3
  403.7 212.8 all-reduce.1
where the time goes:
time: 637 us; the launch traced here: 626 us
  waiting for transfers between devices  547 us (86%)
  local copies, waits for them, and re-layouts  29.9 us (5%)
  matrix products  20 us (3%)
  between operations  14 us (2%)
  starting transfers between devices  8.56 us (1%)
    unnamed x4, waiting for transfers between devices  217 us
    psum x1, waiting for transfers between devices, per_device(): grad_weight = lax.psum(owned, 'dp').astype(jnp.float32)  215 us
    all_gather x1, waiting for transfers between devices, per_device(): full_weight = lax.all_gather(weight, 'fsdp', axis=0, tiled=True)  116 us
    unnamed x29, local copies, waits for them, and re-layouts  14.6 us
  transfers between devices with their start and end apart: 4, of which 3 were waited for; matrix products, arithmetic and copies ran while one was open for 2% of the time, Pallas kernels for 0%

commit v1 on v0

--- a/solution.py
+++ b/solution.py
@@ -3,9 +3,12 @@
 import jax
 import jax.numpy as jnp
 from jax import lax
+from jax.sharding import Mesh
 from jax.sharding import PartitionSpec as P
 
 HD = 80
+SPLIT = (3, 4, 2, 4, 8)
+AXES = ("zl", "x", "c", "zh", "y")
 
 
 def rotary(tensor_in, row_pos, col_pos, turn_sign):
@@ -26,16 +29,64 @@
     return jnp.concatenate(pieces, axis=-1)
 
 
+def core_swap(array):
+    return lax.ppermute(array, "c", [(0, 1), (1, 0)])
+
+
+def swap_x_zh(array):
+    nx, nz = lax.axis_size("x"), lax.axis_size("zh")
+    pairs = [(i * nz + j, j * nz + i) for i in range(nx) for j in range(nz)]
+    return lax.ppermute(array, ("x", "zh"), pairs)
+
+
+def spread(array, axes):
+    count = lax.axis_size(axes)
+    copies = jnp.broadcast_to(array[None], (count,) + array.shape)
+    return lax.all_to_all(copies, axes, split_axis=0, concat_axis=0, tiled=True)
+
+
+def gather_weight(weight, core):
+    width = weight.shape[1] // 2
+    own = lax.dynamic_slice_in_dim(weight, core * width, width, axis=1)
+    own = swap_x_zh(own)
+    own = spread(own, "y").reshape(-1, width)
+    own = spread(own, "x").reshape(-1, width)
+    return own, core_swap(own)
+
+
+def reduce_gradient(part, core):
+    ny, nx = lax.axis_size("y"), lax.axis_size("x")
+    rows, width = part.shape
+    part = part.astype(jnp.bfloat16).reshape(nx, rows // nx, width)
+    part = lax.all_to_all(part, "x", split_axis=0, concat_axis=0, tiled=True)
+    part = jnp.sum(part.astype(jnp.float32), axis=0).astype(jnp.bfloat16)
+    part = part.reshape(ny, rows // (nx * ny), width)
+    part = lax.all_to_all(part, "y", split_axis=0, concat_axis=0, tiled=True)
+    part = jnp.sum(part.astype(jnp.float32), axis=0).astype(jnp.bfloat16)
+    part = swap_x_zh(part)
+    part = spread(part, ("zl", "x"))
+    part = jnp.sum(part.astype(jnp.float32), axis=0).astype(jnp.bfloat16)
+    other = core_swap(part)
+    first = jnp.where(core == 0, part, other)
+    second = jnp.where(core == 0, other, part)
+    return jnp.concatenate([first, second], axis=1).astype(jnp.float32)
+
+
 def per_device(patches, values, upstream, coords, counts, dest, weight):
-    peer_count = lax.axis_size("dp")
+    core = lax.axis_index("c")
+    peer_count = lax.axis_size(("zl", "x", "c"))
     window_count, patch_len, model_width = patches.shape
     value_width = values.shape[-1]
     head_count = value_width // HD
     score_scale = 1.0 / math.sqrt(HD)
     row_total = window_count * patch_len
     flat_patches = patches.reshape(row_total, model_width)
-    full_weight = lax.all_gather(weight, "fsdp", axis=0, tiled=True)
-    projected = jnp.dot(flat_patches, full_weight, preferred_element_type=jnp.float32)
+    other_patches = core_swap(flat_patches)
+    own_w, other_w = gather_weight(weight, core)
+    own_proj = jnp.dot(flat_patches, own_w, preferred_element_type=jnp.float32)
+    other_proj = jnp.dot(flat_patches, other_w, preferred_element_type=jnp.float32)
+    q_proj = jnp.where(core == 0, own_proj, other_proj)
+    k_proj = jnp.where(core == 0, other_proj, own_proj)
     row_pos = coords[:, 0, :].reshape(row_total).astype(jnp.float32)
     col_pos = coords[:, 1, :].reshape(row_total).astype(jnp.float32)
     valid = (jnp.arange(patch_len, dtype=jnp.int32)[None, :] < counts[:, None]).reshape(row_total)
@@ -43,12 +94,8 @@
     block_count = window_count // group_size
     block_rows = group_size * patch_len
     head_shape = (block_count, block_rows, head_count, HD)
-    queries = rotary(
-        projected[:, :value_width].reshape(row_total, head_count, HD), row_pos, col_pos, 1.0
-    )
-    keys_rot = rotary(
-        projected[:, value_width:].reshape(row_total, head_count, HD), row_pos, col_pos, 1.0
-    )
+    queries = rotary(q_proj.reshape(row_total, head_count, HD), row_pos, col_pos, 1.0)
+    keys_rot = rotary(k_proj.reshape(row_total, head_count, HD), row_pos, col_pos, 1.0)
     queries = queries.astype(jnp.bfloat16).reshape(head_shape)
     keys_rot = keys_rot.astype(jnp.bfloat16).reshape(head_shape)
     value_heads = values.reshape(head_shape)
@@ -79,7 +126,7 @@
     )
     routed = jnp.einsum("sp,sc->pc", onehot, context, preferred_element_type=jnp.float32)
     routed = routed.astype(jnp.bfloat16).reshape(peer_count, patch_len, value_width)
-    placed = lax.all_to_all(routed, "dp", split_axis=0, concat_axis=0, tiled=True)
+    placed = lax.all_to_all(routed, ("zl", "x", "c"), split_axis=0, concat_axis=0, tiled=True)
     dprobs = jnp.einsum(
         "bqhd,bkhd->bhqk", upstream_heads, value_heads, preferred_element_type=jnp.float32
     )
@@ -89,32 +136,31 @@
     dkey = jnp.einsum("bhqk,bqhd->bkhd", dscores, queries, preferred_element_type=jnp.float32)
     dquery = rotary(dquery.reshape(row_total, head_count, HD), row_pos, col_pos, -1.0)
     dkey = rotary(dkey.reshape(row_total, head_count, HD), row_pos, col_pos, -1.0)
-    grads_proj = jnp.concatenate(
-        [dquery.reshape(row_total, value_width), dkey.reshape(row_total, value_width)], axis=-1
-    ).astype(jnp.bfloat16)
-    partial_value = jnp.einsum(
-        "rd,rc->dc", flat_patches, grads_proj, preferred_element_type=jnp.float32
-    )
-    owned = lax.psum_scatter(
-        partial_value.astype(jnp.bfloat16), "fsdp", scatter_dimension=0, tiled=True
-    )
-    grad_weight = lax.psum(owned, "dp").astype(jnp.float32)
-    return (placed, grad_weight)
+    dquery = dquery.reshape(row_total, value_width).astype(jnp.bfloat16)
+    dkey = dkey.reshape(row_total, value_width).astype(jnp.bfloat16)
+    kept = jnp.where(core == 0, dquery, dkey)
+    sent = jnp.where(core == 0, dkey, dquery)
+    received = core_swap(sent)
+    both_patches = jnp.concatenate([flat_patches, other_patches], axis=0)
+    both_grads = jnp.concatenate([kept, received], axis=0)
+    part = jnp.einsum("rd,rc->dc", both_patches, both_grads, preferred_element_type=jnp.float32)
+    return (placed, reduce_gradient(part, core))
 
 
 def solution(mesh):
+    fine = Mesh(mesh.devices.reshape(SPLIT), AXES)
     return jax.shard_map(
         per_device,
-        mesh=mesh,
+        mesh=fine,
         in_specs=(
-            P(("dp", "fsdp"), None, None),
-            P(("dp", "fsdp"), None, None),
-            P(("dp", "fsdp"), None, None),
-            P(("dp", "fsdp"), None, None),
-            P(("dp", "fsdp")),
-            P(("dp", "fsdp"), None),
-            P("fsdp", None),
+            P(AXES, None, None),
+            P(AXES, None, None),
+            P(AXES, None, None),
+            P(AXES, None, None),
+            P(AXES),
+            P(AXES, None),
+            P(("zh", "y"), None),
         ),
-        out_specs=(P(("dp", "fsdp"), None, None), P("fsdp", None)),
+        out_specs=(P(AXES, None, None), P(("zh", "y"), None)),
         check_vma=False,
     )

time: 637 us -> 202 us (0.32); the launches traced: 626 us -> 201 us
  waiting for transfers between devices: 547 us -> 34.6 us
  starting transfers between devices: 8.56 us -> 68.1 us
  blocking collectives: 0 us -> 58.8 us
  local copies, waits for them, and re-layouts: 29.9 us -> 13 us
  between operations: 14 us -> 1.05 us
    unnamed x4 -> x0, waiting for transfers between devices: 217 us -> none
    psum x1 -> x0, waiting for transfers between devices: 215 us -> none  [per_device(): grad_weight = lax.psum(owned, 'dp').astype(jnp.float32)]
    all_gather x1 -> x0, waiting for transfers between devices: 116 us -> none  [per_device(): full_weight = lax.all_gather(weight, 'fsdp', axis=0, tiled=True)]
    all_to_all x0 -> x3, blocking collectives: none -> 58.8 us  [the longest x1 23.9 us: reduce_gradient(): part = lax.all_to_all(part, 'x', split_axis=0, concat_axis=0, tiled=True)]
    all_to_all x1 -> x3, starting transfers between devices: 8.44 us -> 52.6 us  [the longest x2 43 us: spread(): return lax.all_to_all(copies, axes, split_axis=0, concat_axis=0, tiled=True)]
    all_to_all x1 -> x3, waiting for transfers between devices: 0.01 us -> 32.8 us  [the longest x2 17.2 us: spread(): return lax.all_to_all(copies, axes, split_axis=0, concat_axis=0, tiled=True)]
    ppermute x0 -> x6, starting transfers between devices: none -> 15.5 us  [the longest x4 14.2 us: core_swap(): return lax.ppermute(array, 'c', [(0, 1), (1, 0)])]
    unnamed x29 -> x24, local copies, waits for them, and re-layouts: 14.6 us -> 3.58 us
  transfers between devices with their start and end apart: 4 -> 9, of which waited for: 3 -> 4; matrix products, arithmetic and copies ran while one was open for 2% -> 15% of each run, Pallas kernels for 0% -> 0%
where the time goes in v1:
time: 202 us; the launch traced here: 201 us
  starting transfers between devices  68.1 us (34%)
  blocking collectives  58.8 us (29%)
  waiting for transfers between devices  34.6 us (17%)
  matrix products  21.7 us (11%)
  local copies, waits for them, and re-layouts  13 us (6%)
  other arithmetic  3.79 us (2%)
    all_to_all x2, starting transfers between devices, spread(): return lax.all_to_all(copies, axes, split_axis=0, concat_axis=0, tiled=True)  43 us
    all_to_all x1, blocking collectives, reduce_gradient(): part = lax.all_to_all(part, 'x', split_axis=0, concat_axis=0, tiled=True)  23.9 us
    all_to_all x1, blocking collectives, spread(): return lax.all_to_all(copies, axes, split_axis=0, concat_axis=0, tiled=True)  18.6 us
    all_to_all x2, waiting for transfers between devices, spread(): return lax.all_to_all(copies, axes, split_axis=0, concat_axis=0, tiled=True)  17.2 us
    all_to_all x1, blocking collectives, reduce_gradient(): part = lax.all_to_all(part, 'y', split_axis=0, concat_axis=0, tiled=True)  16.4 us
    all_to_all x1, waiting for transfers between devices, per_device(): lax.all_to_all(routed, ('zl', 'x', 'c'), split_axis=0, concat_axis=0, til...  15.6 us
    ppermute x4, starting transfers between devices, core_swap(): return lax.ppermute(array, 'c', [(0, 1), (1, 0)])  14.2 us
    all_to_all x1, starting transfers between devices, per_device(): lax.all_to_all(routed, ('zl', 'x', 'c'), split_axis=0, concat_axis=0, til...  9.58 us
  transfers between devices with their start and end apart: 9, of which 4 were waited for; matrix products, arithmetic and copies ran while one was open for 15% of the time, Pallas kernels for 0%

profile of v1, /device:TPU:1, one launch (start us, length us, event | category | flops | bytes accessed | tf_op | source)
XLA Modules:
  0.0 201.0 jit_solution(10315386183728421458)
XLA Ops:
  0.7 0.9 copy-done
  1.5 0.7 collective-permute-start
  2.2 18.6 %all_to_all.30 = bf16[8,40,640]{2,1,0:T(8,128)(2,1)S(1)} all-to-all(bf16[8,40,640]{2,1,0:T(8,128)(2,1)S(1)} %broadcast_in_dim.17), channel_id=1, replica_groups=mesh['zl'=3,'x'=4,'c'=2,'zh'=4,'y'=8] {'y'}, dimensions={0} | all-to-all | bytes 819200 | tf_op jit(solution)/shard_map/all_to_all | solution.py:45
  20.8 1.3 broadcast_in_dim.19
  22.1 24.5 %all-to-all-start.1 = ((bf16[4,320,640]{2,1,0:T(8,128)(2,1)}), bf16[4,320,640]{2,1,0:T(8,128)(2,1)}, u32[]{:S(2)}, u32[]{:S(2)}) async-start(bf16[4,320,640]{2,1,0:T(8,128)(2,1)} %broadcast_in_dim.19), calls=%async_computation.1 | async-start | bytes 3276800 | tf_op jit(solution)/shard_map/all_to_all | solution.py:45
  46.6 4.7 %collective-permute-start.2 = (bf16[384,1280]{1,0:T(8,128)(2,1)S(1)}, bf16[384,1280]{1,0:T(8,128)(2,1)}, u32[]{:S(2)}, u32[]{:S(2)}) collective-permute-start(bf16[384,1280]{1,0:T(8,128)(2,1)S(1)} %bitcast.63), channel_id=1, source_target_pairs={{0,32},{32,0},{1,33},{33,1},{2,34},{34,2},{3,35},{35,3},{4,36},{36... | collective-permute-start | bytes 2949128 | tf_op jit(solution)/shard_map/ppermute | solution.py:33
  51.3 14.2 %all-to-all-done.1 = bf16[4,320,640]{2,1,0:T(8,128)(2,1)} async-done(((bf16[4,320,640]{2,1,0:T(8,128)(2,1)}), bf16[4,320,640]{2,1,0:T(8,128)(2,1)}, u32[]{:S(2)}, u32[]{:S(2)}) %all-to-all-start.1) | async-done | bytes 1638432 | tf_op jit(solution)/shard_map/all_to_all | solution.py:45
  65.5 5.5 %collective-permute-start.1 = (bf16[1280,640]{1,0:T(8,128)(2,1)}, bf16[1280,640]{1,0:T(8,128)(2,1)}, u32[]{:S(2)}, u32[]{:S(2)}) collective-permute-start(bf16[1280,640]{1,0:T(8,128)(2,1)} %bitcast.2), channel_id=1, source_target_pairs={{0,32},{32,0},{1,33},{33,1},{2,34},{34,2},{3,35},{35,3},{4,36},{36... | collective-permute-start | bytes 4915208 | tf_op jit(solution)/shard_map/ppermute | solution.py:33
  71.6 0.8 reshape.330
  72.4 0.5 copy.57
  72.9 0.8 reshape.333
  73.8 0.7 broadcast_and_fusion
  74.5 0.3 broadcast_multiply_fusion.1
  74.9 1.9 fusion.26
  76.7 2.5 %fusion.42 = f32[640,384]{1,0:T(8,128)S(1)} fusion(bf16[1280,640]{1,0:T(8,128)(2,1)} %bitcast.2, bf16[384,1280]{1,0:T(8,128)(2,1)S(1)} %bitcast.64), kind=kOutput, calls=%fused_computation.86 | convolution fusion | flops 629145600 | bytes 3604480 | tf_op jit(solution)/shard_map/dot_general | solution.py:86
  79.2 2.5 %broadcast_select_fusion.3 = (f32[640,384]{1,0:T(8,128)S(1)}, f32[640,384]{1,0:T(8,128)S(1)}) fusion(f32[640,384]{1,0:T(8,128)S(1)} %fusion.42, pred[]{:T(512)S(6)} %eq.47, bf16[1280,640]{1,0:T(8,128)(2,1)} %collective-permute-done.1, bf16[384,1280]{1,0:T(8,128)(2,1)S(1)} %bitcast.65), kind=kOutput, calls=%fused_computation.37 | convolution fusion | flops 629637120 | bytes 5570561 | tf_op jit(solution)/shard_map/dot_general | solution.py:87
  81.7 0.2 subtract_convert_fusion.7
  82.1 0.7 copy.45
  82.9 0.7 copy.46
  83.6 0.7 copy.47
  84.3 0.2 subtract_convert_fusion.5
  84.9 0.5 copy-done.4
  85.6 1.9 fusion.41
  87.5 3.7 %fusion.16 = f32[3,8,10,8,128]{4,3,2,1,0:T(8,128)S(1)} fusion(f32[3,8,128,128]{2,3,1,0:T(8,128)} %fusion.26, bf16[3,128,8,20]{1,3,2,0:T(8,128)(2,1)S(1)} %copy.55, bf16[3,128,8,20]{1,3,2,0:T(8,128)(2,1)S(1)} %copy.54, bf16[3,128,8,20]{1,3,2,0:T(8,128)(2,1)S(1)} %copy.53, bf16[3,128,8,20]{1,3,2,0:T(8,128)(2,1)S(1)} %copy.52, ...), kind=kOutput, calls=%fused_computation.16 | convolution fusion | flops 68422784 | bytes 4634112 | tf_op jit(solution)/shard_map/bhqk,bkhd->bqhd/dot_general | solution.py:135
  91.3 0.2 subtract_convert_fusion.3
  91.5 3.9 %fusion.19 = f32[3,8,10,8,128]{4,3,2,1,0:T(8,128)S(1)} fusion(f32[3,8,128,128]{2,3,1,0:T(8,128)} %fusion.26, bf16[3,128,8,20]{1,3,2,0:T(8,128)(2,1)} %copy.47, bf16[3,128,8,20]{1,3,2,0:T(8,128)(2,1)} %copy.46, bf16[3,128,8,20]{1,3,2,0:T(8,128)(2,1)} %copy.45, bf16[3,128,8,20]{1,3,2,0:T(8,128)(2,1)S(1)} %copy.44, f32[3,8,128,128]{2,3,1,0:T(8,128)} %get-tuple-element.46, ...), kind=kOutput, calls=%fused_computation.17 | convolution fusion | flops 68422784 | bytes 4634112 | tf_op jit(solution)/shard_map/bhqk,bqhd->bkhd/dot_general | solution.py:136
  95.5 0.2 subtract_convert_fusion.1
  95.7 0.4 broadcast_select_fusion.1
  96.1 1.9 collective-permute-start.3
  98.0 1.8 collective-permute-done.3
  99.8 3.0 %convolution_convert_fusion.1 = bf16[1280,640]{1,0:T(8,128)(2,1)S(1)} fusion(bf16[384,1280]{1,0:T(8,128)(2,1)} %collective-permute-done.2, bf16[384,1280]{1,0:T(8,128)(2,1)S(1)} %bitcast.66, bf16[384,640]{0,1:T(8,128)(2,1)S(1)} %collective-permute-done.3, bf16[384,640]{0,1:T(8,128)(2,1)S(1)} %bitcast.67), kind=kOutput, calls=%fused_computation.3 | convolution fusion | flops 1265008640 | bytes 4587520 | tf_op jit(solution)/shard_map/rd,rc->dc/dot_general | solution.py:146
  102.8 23.9 %all_to_all.31 = bf16[4,320,640]{2,1,0:T(8,128)(2,1)S(1)} all-to-all(bf16[4,320,640]{2,1,0:T(8,128)(2,1)S(1)} %bitcast.60), channel_id=1, replica_groups=mesh['zl'=3,'x'=4,'c'=2,'zh'=4,'y'=8] {'x'}, dimensions={0} | all-to-all | bytes 3276800 | tf_op jit(solution)/shard_map/all_to_all | solution.py:61
  126.7 0.4 reduce_sum.56
  127.1 16.4 %all_to_all.32 = bf16[8,40,640]{2,1,0:T(8,128)(2,1)S(1)} all-to-all(bf16[8,40,640]{2,1,0:T(8,128)(2,1)S(1)} %bitcast.62), channel_id=1, replica_groups=mesh['zl'=3,'x'=4,'c'=2,'zh'=4,'y'=8] {'y'}, dimensions={0} | all-to-all | bytes 819200 | tf_op jit(solution)/shard_map/all_to_all | solution.py:64
  143.5 0.7 collective-permute-start.4
  144.2 0.9 broadcast_in_dim.21
  145.1 18.5 %all-to-all-start.5 = ((bf16[12,40,640]{2,1,0:T(8,128)(2,1)}), bf16[12,40,640]{2,1,0:T(8,128)(2,1)S(1)}, u32[]{:S(2)}, u32[]{:S(2)}) async-start(bf16[12,40,640]{2,1,0:T(8,128)(2,1)} %broadcast_in_dim.21), calls=%async_computation.5 | async-start | bytes 1228800 | tf_op jit(solution)/shard_map/all_to_all | solution.py:45
  163.6 1.8 fusion.22
  165.5 0.4 copy.58
  165.9 1.4 reshape.331
  167.4 0.5 convolution_convert_fusion
  167.9 1.1 copy.86
  169.0 3.0 %all-to-all-done.5 = bf16[12,40,640]{2,1,0:T(8,128)(2,1)S(1)} async-done(((bf16[12,40,640]{2,1,0:T(8,128)(2,1)}), bf16[12,40,640]{2,1,0:T(8,128)(2,1)S(1)}, u32[]{:S(2)}, u32[]{:S(2)}) %all-to-all-start.5) | async-done | bytes 614432 | tf_op jit(solution)/shard_map/all_to_all | solution.py:45
  171.9 9.6 %all-to-all-start.2 = ((bf16[24,32,640]{2,1,0:T(8,128)(2,1)}), bf16[24,32,640]{2,1,0:T(8,128)(2,1)S(1)}, u32[]{:S(2)}, u32[]{:S(2)}) async-start(bf16[24,32,640]{2,1,0:T(8,128)(2,1)} %bitcast.31), calls=%async_computation.2 | async-start | bytes 1966080 | tf_op jit(solution)/shard_map/all_to_all | solution.py:129
  181.6 2.1 %collective-permute-start.5 = (bf16[40,640]{1,0:T(8,128)(2,1)S(1)}, bf16[40,640]{1,0:T(8,128)(2,1)S(1)}, u32[]{:S(2)}, u32[]{:S(2)}) collective-permute-start(bf16[40,640]{1,0:T(8,128)(2,1)S(1)} %reduce_sum.58), channel_id=1, source_target_pairs={{0,32},{32,0},{1,33},{33,1},{2,34},{34,2},{3,35},{35,3},{4,36},{36... | collective-permute-start | bytes 153608 | tf_op jit(solution)/shard_map/ppermute | solution.py:33
  183.7 15.6 %all-to-all-done.2 = bf16[24,32,640]{2,1,0:T(8,128)(2,1)S(1)} async-done(((bf16[24,32,640]{2,1,0:T(8,128)(2,1)}), bf16[24,32,640]{2,1,0:T(8,128)(2,1)S(1)}, u32[]{:S(2)}, u32[]{:S(2)}) %all-to-all-start.2) | async-done | bytes 983072 | tf_op jit(solution)/shard_map/all_to_all | solution.py:129
  199.3 0.7 maximum_convert_fusion
  200.0 0.9 copy.94
  (57 shorter events, 1.7 us)
Async XLA Ops:
  0.6 0.9 copy-start
  1.5 0.7 collective-permute-start
  22.1 24.5 %copy-start.1 = (bf16[12,32,1280]{2,1,0:T(8,128)(2,1)S(1)}, bf16[12,32,1280]{2,1,0:T(8,128)(2,1)}, u32[]{:S(2)}) copy-start(bf16[12,32,1280]{2,1,0:T(8,128)(2,1)} %param.7) | copy-start | bytes 2949124
  22.1 29.1 %copy-start.8 = (s32[12,2,32]{2,1,0:T(2,128)S(1)}, s32[12,2,32]{2,1,0:T(2,128)}, u32[]{:S(2)}) copy-start(s32[12,2,32]{2,1,0:T(2,128)} %param.10) | copy-start | bytes 9220
  22.1 49.1 %copy-start.10 = (s32[12]{0:T(128)S(1)}, s32[12]{0:T(128)}, u32[]{:S(2)}) copy-start(s32[12]{0:T(128)} %param.11) | copy-start | bytes 148
  22.1 49.5 %copy-start.2 = (bf16[12,32,640]{2,1,0:T(8,128)(2,1)S(1)}, bf16[12,32,640]{2,1,0:T(8,128)(2,1)}, u32[]{:S(2)}) copy-start(bf16[12,32,640]{2,1,0:T(8,128)(2,1)} %param.8) | copy-start | bytes 1474564
  22.1 43.4 %all-to-all-start.1 = ((bf16[4,320,640]{2,1,0:T(8,128)(2,1)}), bf16[4,320,640]{2,1,0:T(8,128)(2,1)}, u32[]{:S(2)}, u32[]{:S(2)}) async-start(bf16[4,320,640]{2,1,0:T(8,128)(2,1)} %broadcast_in_dim.19), calls=%async_computation.1 | async-start | bytes 3276800 | tf_op jit(solution)/shard_map/all_to_all | solution.py:45
  46.6 26.3 %copy-start.3 = (bf16[12,32,640]{2,1,0:T(8,128)(2,1)S(1)}, bf16[12,32,640]{2,1,0:T(8,128)(2,1)}, u32[]{:S(2)}) copy-start(bf16[12,32,640]{2,1,0:T(8,128)(2,1)} %param.9) | copy-start | bytes 1474564
  46.6 51.4 %collective-permute-start.2 = (bf16[384,1280]{1,0:T(8,128)(2,1)S(1)}, bf16[384,1280]{1,0:T(8,128)(2,1)}, u32[]{:S(2)}, u32[]{:S(2)}) collective-permute-start(bf16[384,1280]{1,0:T(8,128)(2,1)S(1)} %bitcast.63), channel_id=1, source_target_pairs={{0,32},{32,0},{1,33},{33,1},{2,34},{34,2},{3,35},{35,3},{4,36},{36... | collective-permute-start | bytes 2949128 | tf_op jit(solution)/shard_map/ppermute | solution.py:33
  65.5 13.7 %collective-permute-start.1 = (bf16[1280,640]{1,0:T(8,128)(2,1)}, bf16[1280,640]{1,0:T(8,128)(2,1)}, u32[]{:S(2)}, u32[]{:S(2)}) collective-permute-start(bf16[1280,640]{1,0:T(8,128)(2,1)} %bitcast.2), channel_id=1, source_target_pairs={{0,32},{32,0},{1,33},{33,1},{2,34},{34,2},{3,35},{35,3},{4,36},{36... | collective-permute-start | bytes 4915208 | tf_op jit(solution)/shard_map/ppermute | solution.py:33
  84.5 0.9 copy-start.4
  84.5 1.0 copy-start.5
  84.5 1.0 copy-start.6
  84.6 1.0 copy-start.7
  96.1 3.8 %collective-permute-start.3 = (bf16[384,640]{0,1:T(8,128)(2,1)S(1)}, bf16[384,640]{0,1:T(8,128)(2,1)S(1)}, u32[]{:S(2)}, u32[]{:S(2)}) collective-permute-start(bf16[384,640]{0,1:T(8,128)(2,1)S(1)} %bitcast.68), channel_id=1, source_target_pairs={{0,32},{32,0},{1,33},{33,1},{2,34},{34,2},{3,35},{35,3},{4,36},{36... | collective-permute-start | bytes 1474568 | tf_op jit(solution)/shard_map/ppermute | solution.py:33
  143.5 0.7 collective-permute-start.4
  145.1 26.8 %all-to-all-start.5 = ((bf16[12,40,640]{2,1,0:T(8,128)(2,1)}), bf16[12,40,640]{2,1,0:T(8,128)(2,1)S(1)}, u32[]{:S(2)}, u32[]{:S(2)}) async-start(bf16[12,40,640]{2,1,0:T(8,128)(2,1)} %broadcast_in_dim.21), calls=%async_computation.5 | async-start | bytes 1228800 | tf_op jit(solution)/shard_map/all_to_all | solution.py:45
  165.5 1.9 copy-start.9
  171.9 27.4 %all-to-all-start.2 = ((bf16[24,32,640]{2,1,0:T(8,128)(2,1)}), bf16[24,32,640]{2,1,0:T(8,128)(2,1)S(1)}, u32[]{:S(2)}, u32[]{:S(2)}) async-start(bf16[24,32,640]{2,1,0:T(8,128)(2,1)} %bitcast.31), calls=%async_computation.2 | async-start | bytes 1966080 | tf_op jit(solution)/shard_map/all_to_all | solution.py:129
  181.6 17.7 %collective-permute-start.5 = (bf16[40,640]{1,0:T(8,128)(2,1)S(1)}, bf16[40,640]{1,0:T(8,128)(2,1)S(1)}, u32[]{:S(2)}, u32[]{:S(2)}) collective-permute-start(bf16[40,640]{1,0:T(8,128)(2,1)S(1)} %reduce_sum.58), channel_id=1, source_target_pairs={{0,32},{32,0},{1,33},{33,1},{2,34},{34,2},{3,35},{35,3},{4,36},{36... | collective-permute-start | bytes 153608 | tf_op jit(solution)/shard_map/ppermute | solution.py:33

commit v2 on v1

v2 whole, which is shorter than its diff:
```python
import functools
import math

import jax
import jax.numpy as jnp
from jax import lax
from jax.experimental import pallas as pl
from jax.experimental.pallas import tpu as pltpu
from jax.sharding import Mesh
from jax.sharding import PartitionSpec as P

HD = 80
SPLIT = (3, 4, 2, 4, 8)
AXES = ("zl", "x", "c", "zh", "y")


def core_swap(array):
    return lax.ppermute(array, "c", [(0, 1), (1, 0)])


def swap_x_zh(array):
    nx, nz = lax.axis_size("x"), lax.axis_size("zh")
    pairs = [(i * nz + j, j * nz + i) for i in range(nx) for j in range(nz)]
    return lax.ppermute(array, ("x", "zh"), pairs)


def spread(array, axes):
    count = lax.axis_size(axes)
    copies = jnp.broadcast_to(array[None], (count,) + array.shape)
    return lax.all_to_all(copies, axes, split_axis=0, concat_axis=0, tiled=True)


def gather_weight(weight, core):
    width = weight.shape[1] // 2
    own = lax.dynamic_slice_in_dim(weight, core * width, width, axis=1)
    own = swap_x_zh(own)
    own = spread(own, "y").reshape(-1, width)
    own = spread(own, "x").reshape(-1, width)
    return own, core_swap(own)


def reduce_gradient(part, core):
    ny, nx = lax.axis_size("y"), lax.axis_size("x")
    rows, width = part.shape
    part = part.astype(jnp.bfloat16).reshape(nx, rows // nx, width)
    part = lax.all_to_all(part, "x", split_axis=0, concat_axis=0, tiled=True)
    part = jnp.sum(part.astype(jnp.float32), axis=0).astype(jnp.bfloat16)
    part = part.reshape(ny, rows // (nx * ny), width)
    part = lax.all_to_all(part, "y", split_axis=0, concat_axis=0, tiled=True)
    part = jnp.sum(part.astype(jnp.float32), axis=0).astype(jnp.bfloat16)
    part = swap_x_zh(part)
    part = spread(part, ("zl", "x"))
    part = jnp.sum(part.astype(jnp.float32), axis=0).astype(jnp.bfloat16)
    other = core_swap(part)
    first = jnp.where(core == 0, part, other)
    second = jnp.where(core == 0, other, part)
    return jnp.concatenate([first, second], axis=1).astype(jnp.float32)


def partner(array):
    width = array.shape[1]
    quarter = HD // 4
    lane = lax.broadcasted_iota(jnp.int32, array.shape, 1)
    front = lax.rem(lane, 2 * quarter) < quarter
    ahead = pltpu.roll(array, width - quarter, 1)
    behind = pltpu.roll(array, quarter, 1)
    return jnp.where(front, -ahead, behind)


def dot(a, b, dims):
    return lax.dot_general(a, b, (dims, ((), ())), preferred_element_type=jnp.float32)


def attention_kernel(
    patch_len,
    group,
    scalars,
    patches_ref,
    weight_ref,
    own_ref,
    cos_ref,
    sin_ref,
    values_ref,
    upstream_ref,
    routed_ref,
    kept_ref,
    sent_ref,
    proj_ref,
    query_ref,
    key_ref,
    dquery_ref,
    dkey_ref,
    context_ref,
):
    rows, width = own_ref.shape
    windows = rows // patch_len
    heads = width // HD
    scale = 1.0 / math.sqrt(HD)
    is_first = scalars[0] == 0
    proj_ref[...] = dot(patches_ref[...], weight_ref[...], ((1,), (0,)))
    routed_ref[...] = jnp.zeros_like(routed_ref)
    block = group * patch_len
    step = 32
    for start in range(0, rows, step):
        span = pl.ds(start, step)
        own, other = own_ref[span, :], proj_ref[span, :]
        cosine, sine = cos_ref[span, :], sin_ref[span, :]
        query = jnp.where(is_first, own, other)
        key = jnp.where(is_first, other, own)
        query_ref[span, :] = (query * cosine + partner(query) * sine).astype(jnp.bfloat16)
        key_ref[span, :] = (key * cosine + partner(key) * sine).astype(jnp.bfloat16)
    row_at = lax.broadcasted_iota(jnp.int32, (block, block), 0)
    key_at = lax.broadcasted_iota(jnp.int32, (block, block), 1)
    row_win, key_win = row_at // patch_len, key_at // patch_len
    row_one = lax.broadcasted_iota(jnp.int32, (block, 1), 0)
    same = row_win == key_win
    for first in range(0, windows, group):
        key_count = jnp.full((block, block), scalars[1 + first], jnp.int32)
        row_count = jnp.full((block, 1), scalars[1 + first], jnp.int32)
        for later in range(1, group):
            count = scalars[1 + first + later]
            key_count = jnp.where(key_win == later, count, key_count)
            row_count = jnp.where(row_one // patch_len == later, count, row_count)
        key_ok = same & (key_at - key_win * patch_len < key_count)
        row_live = (row_one - row_one // patch_len * patch_len < row_count).astype(jnp.float32)
        span = pl.ds(first * patch_len, block)
        for head in range(heads):
            lanes = pl.ds(head * HD, HD)
            q, k = query_ref[span, lanes], key_ref[span, lanes]
            v, u = values_ref[span, lanes], upstream_ref[span, lanes]
            scores = jnp.where(key_ok, dot(q, k, ((1,), (1,))) * scale, -1e30)
            exps = jnp.exp(scores - jnp.max(scores, axis=1, keepdims=True))
            factor = row_live / jnp.sum(exps, axis=1, keepdims=True)
            probs = exps * factor
            low = probs.astype(jnp.bfloat16)
            context_ref[span, lanes] = dot(low, v, ((1,), (0,))).astype(jnp.bfloat16)
            dprobs = dot(u, v, ((1,), (1,)))
            delta = jnp.sum(probs * dprobs, axis=1, keepdims=True)
            dscores = (probs * (dprobs - delta) * scale).astype(jnp.bfloat16)
            dquery_ref[span, lanes] = dot(dscores, k, ((1,), (0,)))
            dkey_ref[span, lanes] = dot(dscores, q, ((0,), (0,)))
        for window in range(first, first + group):
            here = pl.ds(window * patch_len, patch_len)
            routed_ref[scalars[1 + windows + window]] = context_ref[here, :]
    for start in range(0, rows, step):
        span = pl.ds(start, step)
        cosine, sine = cos_ref[span, :], sin_ref[span, :]
        dquery, dkey = dquery_ref[span, :], dkey_ref[span, :]
        dquery = (dquery * cosine - partner(dquery) * sine).astype(jnp.bfloat16)
        dkey = (dkey * cosine - partner(dkey) * sine).astype(jnp.bfloat16)
        kept_ref[span, :] = jnp.where(is_first, dquery, dkey)
        sent_ref[span, :] = jnp.where(is_first, dkey, dquery)


def attention(scalars, patches, weight, own, cosine, sine, values, upstream, patch_len, slots):
    rows, width = own.shape
    windows = rows // patch_len
    group = math.gcd(windows, max(1, 128 // patch_len))
    vmem = pl.BlockSpec(memory_space=pltpu.VMEM)
    return pl.pallas_call(
        functools.partial(attention_kernel, patch_len, group),
        in_specs=[pl.BlockSpec(memory_space=pltpu.SMEM)] + [vmem] * 7,
        out_specs=[vmem] * 3,
        out_shape=[
            jax.ShapeDtypeStruct((slots, patch_len, width), jnp.bfloat16),
            jax.ShapeDtypeStruct((rows, width), jnp.bfloat16),
            jax.ShapeDtypeStruct((rows, width), jnp.bfloat16),
        ],
        scratch_shapes=[
            pltpu.VMEM((rows, width), jnp.float32),
            pltpu.VMEM((rows, width), jnp.bfloat16),
            pltpu.VMEM((rows, width), jnp.bfloat16),
            pltpu.VMEM((rows, width), jnp.float32),
            pltpu.VMEM((rows, width), jnp.float32),
            pltpu.VMEM((rows, width), jnp.bfloat16),
        ],
        compiler_params=pltpu.CompilerParams(vmem_limit_bytes=40 * 1024 * 1024),
        cost_estimate=pl.CostEstimate(
            flops=2 * rows * width * 1280 + 10 * rows * 128 * width,
            bytes_accessed=12_000_000,
            transcendentals=rows * 128 * 8,
        ),
        name="window_attention",
    )(scalars, patches, weight, own, cosine, sine, values, upstream)


def rotary_tables(coords, heads):
    quarter = HD // 4
    frequency = 10000.0 ** (-jnp.arange(quarter, dtype=jnp.float32) / quarter)
    position = coords.astype(jnp.float32)
    angles = position[:, :, :, None] * frequency
    angles = jnp.concatenate([angles[:, 0], angles[:, 0], angles[:, 1], angles[:, 1]], axis=-1)
    angles = angles.reshape(-1, HD)
    return jnp.tile(jnp.cos(angles), (1, heads)), jnp.tile(jnp.sin(angles), (1, heads))


def per_device(patches, values, upstream, coords, counts, dest, weight):
    core = lax.axis_index("c")
    slots = lax.axis_size(("zl", "x", "c"))
    window_count, patch_len, model_width = patches.shape
    value_width = values.shape[-1]
    row_total = window_count * patch_len
    flat_patches = patches.reshape(row_total, model_width)
    other_patches = core_swap(flat_patches)
    cosine, sine = rotary_tables(coords, value_width // HD)
    own_w, other_w = gather_weight(weight, core)
    own_proj = jnp.dot(flat_patches, own_w, preferred_element_type=jnp.float32)
    scalars = jnp.concatenate([core.astype(jnp.int32)[None], counts, dest[:, 0]])
    routed, kept, sent = attention(
        scalars,
        flat_patches,
        other_w,
        own_proj,
        cosine,
        sine,
        values.reshape(row_total, value_width),
        upstream.reshape(row_total, value_width),
        patch_len,
        slots,
    )
    received = core_swap(sent)
    both_patches = jnp.concatenate([flat_patches, other_patches], axis=0)
    both_grads = jnp.concatenate([kept, received], axis=0)
    part = jnp.einsum("rd,rc->dc", both_patches, both_grads, preferred_element_type=jnp.float32)
    placed = lax.all_to_all(routed, ("zl", "x", "c"), split_axis=0, concat_axis=0, tiled=True)
    return (placed, reduce_gradient(part, core))


def solution(mesh):
    fine = Mesh(mesh.devices.reshape(SPLIT), AXES)
    return jax.shard_map(
        per_device,
        mesh=fine,
        in_specs=(
            P(AXES, None, None),
            P(AXES, None, None),
            P(AXES, None, None),
            P(AXES, None, None),
            P(AXES),
            P(AXES, None),
            P(("zh", "y"), None),
        ),
        out_specs=(P(AXES, None, None), P(("zh", "y"), None)),
        check_vma=False,
    )
```

time: 202 us -> 199 us (0.985)
  blocking collectives: 58.8 us -> 129 us
  starting transfers between devices: 68.1 us -> 22.3 us
  waiting for transfers between devices: 34.6 us -> 16.9 us
  matrix products: 21.7 us -> 5.39 us
  Pallas kernels: 0 us -> 16.1 us
  local copies, waits for them, and re-layouts: 13 us -> 5.24 us
    all_to_all x1 -> x3, blocking collectives: 18.6 us -> 90.6 us  [spread(): return lax.all_to_all(copies, axes, split_axis=0, concat_axis=0, tiled=True)]
    all_to_all x2 -> x0, starting transfers between devices: 43 us -> none  [spread(): return lax.all_to_all(copies, axes, split_axis=0, concat_axis=0, tiled=True)]
    all_to_all x2 -> x0, waiting for transfers between devices: 17.2 us -> none  [spread(): return lax.all_to_all(copies, axes, split_axis=0, concat_axis=0, tiled=True)]
    pallas_call x0 -> x1, Pallas kernels: none -> 16.1 us  [attention(): pl.pallas_call(functools.partial(attention_kernel, patch_len, group), in_...]
    dot_general x6 -> x0, matrix products: 14.3 us -> none  [the longest x1 3.93 us: per_device(): jnp.einsum('bhqk,bqhd->bkhd', dscores, queries, preferred_element_type=jn...]
    reshape x6 -> x0, local copies, waits for them, and re-layouts: 3.64 us -> none  [the longest x1 1.42 us: per_device(): context.astype(jnp.bfloat16).reshape(window_count, patch_len * value_width)]
    another operation x0 -> x4, local copies, waits for them, and re-layouts: none -> 2.93 us  [the longest x2 2.54 us: rotary_tables(): jnp.tile(jnp.sin(angles), (1, heads))]
    concatenate x16 -> x2, local copies, waits for them, and re-layouts: 2.63 us -> 0.2 us  [rotary_tables(): jnp.concatenate([angles[:, 0], angles[:, 0], angles[:, 1], angles[:, 1]],...]
  transfers between devices with their start and end apart: 9 -> 7, of which waited for: 4 -> 2; matrix products, arithmetic and copies ran while one was open for 15% -> 3% of each run, Pallas kernels for 0% -> 8%
where the time goes in v2:
time: 199 us; the launch traced here: 198 us
  blocking collectives  129 us (65%)
  starting transfers between devices  22.3 us (11%)
  waiting for transfers between devices  16.9 us (8%)
  Pallas kernels  16.1 us (8%)
  matrix products  5.39 us (3%)
  local copies, waits for them, and re-layouts  5.24 us (3%)
    all_to_all x3, blocking collectives, spread(): return lax.all_to_all(copies, axes, split_axis=0, concat_axis=0, tiled=True)  90.6 us
    all_to_all x1, blocking collectives, reduce_gradient(): part = lax.all_to_all(part, 'x', split_axis=0, concat_axis=0, tiled=True)  23.3 us
    pallas_call x1, Pallas kernels, attention(): pl.pallas_call(functools.partial(attention_kernel, patch_len, group), in_...  16.1 us
    all_to_all x1, waiting for transfers between devices, per_device(): lax.all_to_all(routed, ('zl', 'x', 'c'), split_axis=0, concat_axis=0, til...  15.6 us
    all_to_all x1, blocking collectives, reduce_gradient(): part = lax.all_to_all(part, 'y', split_axis=0, concat_axis=0, tiled=True)  15.4 us
    ppermute x4, starting transfers between devices, core_swap(): return lax.ppermute(array, 'c', [(0, 1), (1, 0)])  12.2 us
    all_to_all x1, starting transfers between devices, per_device(): lax.all_to_all(routed, ('zl', 'x', 'c'), split_axis=0, concat_axis=0, til...  8.83 us
  transfers between devices with their start and end apart: 7, of which 2 were waited for; matrix products, arithmetic and copies ran while one was open for 3% of the time, Pallas kernels for 8%

profile of v2, /device:TPU:1, one launch (start us, length us, event | category | flops | bytes accessed | tf_op | source)
XLA Modules:
  0.0 198.2 jit_solution(14147051725683067448)
XLA Ops:
  0.6 0.0 copy-start
  0.6 0.9 copy-done
  1.5 0.7 collective-permute-start
  2.2 0.0 collective-permute-done
  2.2 18.6 %all_to_all.30 = bf16[8,40,640]{2,1,0:T(8,128)(2,1)S(1)} all-to-all(bf16[8,40,640]{2,1,0:T(8,128)(2,1)S(1)} %broadcast_in_dim.11), channel_id=1, replica_groups=mesh['zl'=3,'x'=4,'c'=2,'zh'=4,'y'=8] {'y'}, dimensions={0} | all-to-all | bytes 819200 | tf_op jit(solution)/shard_map/all_to_all | solution.py:30
  20.8 0.1 broadcast_in_dim.13
  20.9 0.0 copy-start.1
  21.0 0.0 copy-start.4
  21.0 43.2 %all_to_all.31 = bf16[4,320,640]{2,1,0:T(8,128)(2,1)} all-to-all(bf16[4,320,640]{2,1,0:T(8,128)(2,1)S(1)} %broadcast_in_dim.13), channel_id=1, replica_groups=mesh['zl'=3,'x'=4,'c'=2,'zh'=4,'y'=8] {'x'}, dimensions={0} | all-to-all | bytes 3276800 | tf_op jit(solution)/shard_map/all_to_all | solution.py:30
  64.1 5.5 %collective-permute-start.1 = (bf16[1280,640]{1,0:T(8,128)(2,1)}, bf16[1280,640]{1,0:T(8,128)(2,1)}, u32[]{:S(2)}, u32[]{:S(2)}) collective-permute-start(bf16[1280,640]{1,0:T(8,128)(2,1)} %bitcast.4), channel_id=1, source_target_pairs={{0,32},{32,0},{1,33},{33,1},{2,34},{34,2},{3,35},{35,3},{4,36},{36... | collective-permute-start | bytes 4915208 | tf_op jit(solution)/shard_map/ppermute | solution.py:18
  69.6 0.0 copy-done.1
  69.6 1.9 collective-permute-start.2
  71.5 0.0 copy-done.4
  71.6 0.1 broadcast_multiply_fusion
  71.7 0.1 concatenate.29
  71.8 0.1 concatenate.30
  71.9 0.4 fusion.6
  72.4 0.1 tile.8
  72.4 0.3 copy.21.cos_ref
  72.8 0.0 copy-start.5
  72.8 0.0 copy-start.6
  72.8 1.0 tile.20
  73.8 1.5 copy.22.sin_ref
  75.3 0.0 copy-done.5
  75.4 0.1 pad_add_fusion.scalars
  75.4 2.4 %convolution_bitcast_fusion.own_ref = f32[384,640]{1,0:T(8,128)S(1)} fusion(bf16[384,1280]{1,0:T(8,128)(2,1)S(1)} %bitcast.20, bf16[1280,640]{1,0:T(8,128)(2,1)} %bitcast.4), kind=kOutput, calls=%fused_computation.4 | convolution fusion | flops 629145600 | bytes 3604480 | tf_op jit(solution)/shard_map/dot_general | solution.py:207
  77.9 0.0 collective-permute-done.1.weight_ref
  77.9 0.0 copy-done.2
  77.9 0.0 copy-done.3
  77.9 16.1 %window_attention.1 = (bf16[24,32,640]{2,1,0:T(8,128)(2,1)}, bf16[384,640]{1,0:T(8,128)(2,1)S(1)}, bf16[384,640]{1,0:T(8,128)(2,1)S(1)}) custom-call(s32[25]{0:T(128)S(1)} %pad_add_fusion.scalars, bf16[384,1280]{1,0:T(8,128)(2,1)S(1)} %bitcast.21, bf16[1280,640]{1,0:T(8,128)(2,1)} %collective-permute-done.1.weight_ref, ...), custom_call_target="tpu_custom_call" | custom-call | flops 943718400 | bytes 12000000 | tf_op jit(solution)/shard_map/window_attention/pallas_call | solution.py:160
  94.1 2.6 %collective-permute-start.3 = (bf16[384,640]{1,0:T(8,128)(2,1)S(1)}, bf16[384,640]{1,0:T(8,128)(2,1)S(1)}, u32[]{:S(2)}, u32[]{:S(2)}) collective-permute-start(bf16[384,640]{1,0:T(8,128)(2,1)S(1)} %get-tuple-element.7), channel_id=1, source_target_pairs={{0,32},{32,0},{1,33},{33,1},{2,34},{34,2},{3,35},{35,3},{4,36},{36... | collective-permute-start | bytes 1474568 | tf_op jit(solution)/shard_map/ppermute | solution.py:18
  96.6 0.0 collective-permute-done.2
  96.7 1.3 collective-permute-done.3
  97.9 2.9 %convolution_convert_fusion = bf16[1280,640]{1,0:T(8,128)(2,1)S(1)} fusion(bf16[384,1280]{1,0:T(8,128)(2,1)} %collective-permute-done.2, bf16[384,1280]{1,0:T(8,128)(2,1)S(1)} %bitcast.22, bf16[384,640]{1,0:T(8,128)(2,1)S(1)} %collective-permute-done.3, bf16[384,640]{1,0:T(8,128)(2,1)S(1)} %get-tuple-element.6), kind=kOutput, calls=%fused_computation | convolution fusion | flops 1265008640 | bytes 4587520 | tf_op jit(solution)/shard_map/rd,rc->dc/dot_general | solution.py:224
  100.9 23.3 %all_to_all.32 = bf16[4,320,640]{2,1,0:T(8,128)(2,1)S(1)} all-to-all(bf16[4,320,640]{2,1,0:T(8,128)(2,1)S(1)} %bitcast.27), channel_id=1, replica_groups=mesh['zl'=3,'x'=4,'c'=2,'zh'=4,'y'=8] {'x'}, dimensions={0} | all-to-all | bytes 3276800 | tf_op jit(solution)/shard_map/all_to_all | solution.py:46
  124.2 0.4 reduce_sum.36
  124.6 15.4 %all_to_all.33 = bf16[8,40,640]{2,1,0:T(8,128)(2,1)S(1)} all-to-all(bf16[8,40,640]{2,1,0:T(8,128)(2,1)S(1)} %bitcast.29), channel_id=1, replica_groups=mesh['zl'=3,'x'=4,'c'=2,'zh'=4,'y'=8] {'y'}, dimensions={0} | all-to-all | bytes 819200 | tf_op jit(solution)/shard_map/all_to_all | solution.py:49
  140.1 0.1 reduce_sum.37
  140.1 0.7 collective-permute-start.4
  140.8 0.0 collective-permute-done.4
  140.9 28.9 %all_to_all.34 = bf16[12,40,640]{2,1,0:T(8,128)(2,1)S(1)} all-to-all(bf16[12,40,640]{2,1,0:T(8,128)(2,1)S(1)} %broadcast_in_dim.28), channel_id=1, replica_groups=mesh['zl'=3,'x'=4,'c'=2,'zh'=4,'y'=8] {'zl','x'}, dimensions={0} | all-to-all | bytes 1228800 | tf_op jit(solution)/shard_map/all_to_all | solution.py:30
  169.8 8.8 %all-to-all-start.2 = ((bf16[24,32,640]{2,1,0:T(8,128)(2,1)}), bf16[24,32,640]{2,1,0:T(8,128)(2,1)S(1)}, u32[]{:S(2)}, u32[]{:S(2)}) async-start(bf16[24,32,640]{2,1,0:T(8,128)(2,1)} %get-tuple-element.5), calls=%async_computation.2 | async-start | bytes 1966080 | tf_op jit(solution)/shard_map/all_to_all | solution.py:225
  178.6 0.1 reduce_sum.38
  178.7 2.2 %collective-permute-start.5 = (bf16[40,640]{1,0:T(8,128)(2,1)S(1)}, bf16[40,640]{1,0:T(8,128)(2,1)S(1)}, u32[]{:S(2)}, u32[]{:S(2)}) collective-permute-start(bf16[40,640]{1,0:T(8,128)(2,1)S(1)} %reduce_sum.38), channel_id=1, source_target_pairs={{0,32},{32,0},{1,33},{33,1},{2,34},{34,2},{3,35},{35,3},{4,36},{36... | collective-permute-start | bytes 153608 | tf_op jit(solution)/shard_map/ppermute | solution.py:18
  180.9 15.6 %all-to-all-done.2 = bf16[24,32,640]{2,1,0:T(8,128)(2,1)S(1)} async-done(((bf16[24,32,640]{2,1,0:T(8,128)(2,1)}), bf16[24,32,640]{2,1,0:T(8,128)(2,1)S(1)}, u32[]{:S(2)}, u32[]{:S(2)}) %all-to-all-start.2) | async-done | bytes 983072 | tf_op jit(solution)/shard_map/all_to_all | solution.py:225
  196.5 0.0 collective-permute-done.5
  196.6 0.7 maximum_convert_fusion
  197.3 0.9 copy.25
  (11 shorter events, 0.2 us)
Async XLA Ops:
  0.6 0.9 copy-start
  1.5 0.7 collective-permute-start
  20.9 48.6 %copy-start.1 = (bf16[12,32,1280]{2,1,0:T(8,128)(2,1)S(1)}, bf16[12,32,1280]{2,1,0:T(8,128)(2,1)}, u32[]{:S(2)}) copy-start(bf16[12,32,1280]{2,1,0:T(8,128)(2,1)} %param.7) | copy-start | bytes 2949124
  21.0 50.6 %copy-start.4 = (s32[12,2,32]{2,1,0:T(2,128)S(1)}, s32[12,2,32]{2,1,0:T(2,128)}, u32[]{:S(2)}) copy-start(s32[12,2,32]{2,1,0:T(2,128)} %param.10) | copy-start | bytes 9220
  64.1 13.8 %collective-permute-start.1 = (bf16[1280,640]{1,0:T(8,128)(2,1)}, bf16[1280,640]{1,0:T(8,128)(2,1)}, u32[]{:S(2)}, u32[]{:S(2)}) collective-permute-start(bf16[1280,640]{1,0:T(8,128)(2,1)} %bitcast.4), channel_id=1, source_target_pairs={{0,32},{32,0},{1,33},{33,1},{2,34},{34,2},{3,35},{35,3},{4,36},{36... | collective-permute-start | bytes 4915208 | tf_op jit(solution)/shard_map/ppermute | solution.py:18
  69.6 27.0 %collective-permute-start.2 = (bf16[384,1280]{1,0:T(8,128)(2,1)S(1)}, bf16[384,1280]{1,0:T(8,128)(2,1)}, u32[]{:S(2)}, u32[]{:S(2)}) collective-permute-start(bf16[384,1280]{1,0:T(8,128)(2,1)S(1)} %bitcast.19), channel_id=1, source_target_pairs={{0,32},{32,0},{1,33},{33,1},{2,34},{34,2},{3,35},{35,3},{4,36},{36... | collective-permute-start | bytes 2949128 | tf_op jit(solution)/shard_map/ppermute | solution.py:18
  72.8 2.6 %copy-start.5 = (s32[12,1]{0,1:T(1,128)S(1)}, s32[12,1]{0,1:T(1,128)}, u32[]{:S(2)}) copy-start(s32[12,1]{0,1:T(1,128)} %param.12) | copy-start | bytes 148
  72.8 2.6 %copy-start.6 = (s32[12]{0:T(128)S(1)}, s32[12]{0:T(128)}, u32[]{:S(2)}) copy-start(s32[12]{0:T(128)} %param.11) | copy-start | bytes 148
  75.4 2.5 %copy-start.2 = (bf16[12,32,640]{2,1,0:T(8,128)(2,1)S(1)}, bf16[12,32,640]{2,1,0:T(8,128)(2,1)}, u32[]{:S(2)}) copy-start(bf16[12,32,640]{2,1,0:T(8,128)(2,1)} %param.8) | copy-start | bytes 1474564
  75.4 2.5 %copy-start.3 = (bf16[12,32,640]{2,1,0:T(8,128)(2,1)S(1)}, bf16[12,32,640]{2,1,0:T(8,128)(2,1)}, u32[]{:S(2)}) copy-start(bf16[12,32,640]{2,1,0:T(8,128)(2,1)} %param.9) | copy-start | bytes 1474564
  94.1 3.9 %collective-permute-start.3 = (bf16[384,640]{1,0:T(8,128)(2,1)S(1)}, bf16[384,640]{1,0:T(8,128)(2,1)S(1)}, u32[]{:S(2)}, u32[]{:S(2)}) collective-permute-start(bf16[384,640]{1,0:T(8,128)(2,1)S(1)} %get-tuple-element.7), channel_id=1, source_target_pairs={{0,32},{32,0},{1,33},{33,1},{2,34},{34,2},{3,35},{35,3},{4,36},{36... | collective-permute-start | bytes 1474568 | tf_op jit(solution)/shard_map/ppermute | solution.py:18
  140.1 0.7 collective-permute-start.4
  169.8 26.7 %all-to-all-start.2 = ((bf16[24,32,640]{2,1,0:T(8,128)(2,1)}), bf16[24,32,640]{2,1,0:T(8,128)(2,1)S(1)}, u32[]{:S(2)}, u32[]{:S(2)}) async-start(bf16[24,32,640]{2,1,0:T(8,128)(2,1)} %get-tuple-element.5), calls=%async_computation.2 | async-start | bytes 1966080 | tf_op jit(solution)/shard_map/all_to_all | solution.py:225
  178.7 17.8 %collective-permute-start.5 = (bf16[40,640]{1,0:T(8,128)(2,1)S(1)}, bf16[40,640]{1,0:T(8,128)(2,1)S(1)}, u32[]{:S(2)}, u32[]{:S(2)}) collective-permute-start(bf16[40,640]{1,0:T(8,128)(2,1)S(1)} %reduce_sum.38), channel_id=1, source_target_pairs={{0,32},{32,0},{1,33},{33,1},{2,34},{34,2},{3,35},{35,3},{4,36},{36... | collective-permute-start | bytes 153608 | tf_op jit(solution)/shard_map/ppermute | solution.py:18

commit v3 on v2

v3 whole, which is shorter than its diff:
```python
import functools
import math

import jax
import jax.numpy as jnp
from jax import lax
from jax.experimental import pallas as pl
from jax.experimental.pallas import tpu as pltpu
from jax.sharding import Mesh
from jax.sharding import PartitionSpec as P

HD = 80
LANES = 128
SPLIT = (3, 4, 2, 4, 8)
AXES = ("zl", "x", "c", "zh", "y")
BF16 = jnp.bfloat16
F32 = jnp.float32


def core_swap(array):
    return lax.ppermute(array, "c", [(0, 1), (1, 0)])


def ring_x(array, step):
    count = lax.axis_size("x")
    return lax.ppermute(array, "x", [(i, (i + step) % count) for i in range(count)])


def exchange(array, axes):
    return lax.all_to_all(array, axes, split_axis=0, concat_axis=0, tiled=True)


def spread(array, axes):
    count = lax.axis_size(axes)
    return exchange(jnp.broadcast_to(array[None], (count,) + array.shape), axes)


def dot(a, b, dims):
    return lax.dot_general(a, b, (dims, ((), ())), preferred_element_type=F32)


def partner(array):
    quarter = HD // 4
    lane = lax.broadcasted_iota(jnp.int32, array.shape, 1)
    front = lax.rem(lane, 2 * quarter) < quarter
    ahead = pltpu.roll(array, LANES - quarter, 1)
    behind = pltpu.roll(array, quarter, 1)
    return jnp.where(front, -ahead, behind)


def head_kernel(
    patch_len,
    group,
    counts,
    weight_ref,
    patches_ref,
    turned_ref,
    cos_ref,
    sin_ref,
    values_ref,
    upstream_ref,
    context_ref,
    grad_ref,
    full_ref,
    proj_ref,
    dproj_ref,
):
    rows = patches_ref.shape[0]
    windows = rows // patch_len
    strip, strips = weight_ref.shape[0], weight_ref.shape[1] // (2 * HD)
    scale = 1.0 / math.sqrt(HD)
    full_ref[...] = jnp.zeros_like(full_ref)
    for z in range(strips):
        span, at = pl.ds(z * strip, strip), z * 2 * HD
        full_ref[span, pl.ds(0, HD)] = weight_ref[:, pl.ds(at, HD)]
        full_ref[span, pl.ds(LANES, HD)] = weight_ref[:, pl.ds(at + HD, HD)]
    proj_ref[...] = dot(patches_ref[...], full_ref[...], ((1,), (0,)))
    block = group * patch_len
    row_at = lax.broadcasted_iota(jnp.int32, (block, block), 0)
    key_at = lax.broadcasted_iota(jnp.int32, (block, block), 1)
    row_win, key_win = row_at // patch_len, key_at // patch_len
    row_one = lax.broadcasted_iota(jnp.int32, (block, 1), 0)
    same = row_win == key_win
    for first in range(0, windows, group):
        key_count = jnp.full((block, block), counts[first], jnp.int32)
        row_count = jnp.full((block, 1), counts[first], jnp.int32)
        for later in range(1, group):
            count = counts[first + later]
            key_count = jnp.where(key_win == later, count, key_count)
            row_count = jnp.where(row_one // patch_len == later, count, row_count)
        key_ok = same & (key_at - key_win * patch_len < key_count)
        row_live = (row_one - row_one // patch_len * patch_len < row_count).astype(F32)
        span = pl.ds(first * patch_len, block)
        cosine, sine = cos_ref[span, :], sin_ref[span, :]
        query, key = proj_ref[span, pl.ds(0, LANES)], proj_ref[span, pl.ds(LANES, LANES)]
        q = (query * cosine + partner(query) * sine).astype(BF16)
        k = (key * cosine + partner(key) * sine).astype(BF16)
        v, u = values_ref[span, :], upstream_ref[span, :]
        scores = jnp.where(key_ok, dot(q, k, ((1,), (1,))) * scale, -1e30)
        exps = jnp.exp(scores - jnp.max(scores, axis=1, keepdims=True))
        probs = exps * (row_live / jnp.sum(exps, axis=1, keepdims=True))
        context_ref[span, :] = dot(probs.astype(BF16), v, ((1,), (0,))).astype(BF16)
        dprobs = dot(u, v, ((1,), (1,)))
        delta = jnp.sum(probs * dprobs, axis=1, keepdims=True)
        dscores = (probs * (dprobs - delta) * scale).astype(BF16)
        dquery = dot(dscores, k, ((1,), (0,)))
        dkey = dot(dscores, q, ((0,), (0,)))
        dquery = dquery * cosine - partner(dquery) * sine
        dkey = dkey * cosine - partner(dkey) * sine
        dproj_ref[span, pl.ds(0, LANES)] = dquery.astype(BF16)
        dproj_ref[span, pl.ds(LANES, LANES)] = dkey.astype(BF16)
    for z in range(strips):
        at = z * 2 * HD
        part = dot(turned_ref[pl.ds(z * strip, strip), :], dproj_ref[...], ((1,), (0,)))
        part = part.astype(BF16)
        grad_ref[:, pl.ds(at, HD)] = part[:, :HD]
        grad_ref[:, pl.ds(at + HD, HD)] = part[:, LANES : LANES + HD]


def one_head(counts, weight, patches, turned, cosine, sine, values, upstream, patch_len):
    rows, model_width = patches.shape
    windows = rows // patch_len
    group = math.gcd(windows, max(1, 128 // patch_len))
    vmem = pl.BlockSpec(memory_space=pltpu.VMEM)
    return pl.pallas_call(
        functools.partial(head_kernel, patch_len, group),
        in_specs=[pl.BlockSpec(memory_space=pltpu.SMEM)] + [vmem] * 7,
        out_specs=[vmem] * 2,
        out_shape=[
            jax.ShapeDtypeStruct((rows, LANES), BF16),
            jax.ShapeDtypeStruct(weight.shape, BF16),
        ],
        scratch_shapes=[
            pltpu.VMEM((model_width, 2 * LANES), BF16),
            pltpu.VMEM((rows, 2 * LANES), F32),
            pltpu.VMEM((rows, 2 * LANES), BF16),
        ],
        compiler_params=pltpu.CompilerParams(vmem_limit_bytes=24 * 1024 * 1024),
        cost_estimate=pl.CostEstimate(
            flops=4_000_000_000, bytes_accessed=8_000_000, transcendentals=rows * 128
        ),
        name="one_head",
    )(counts, weight, patches, turned, cosine, sine, values, upstream)


def route_kernel(patch_len, dest, order, stack_ref, routed_ref):
    heads = stack_ref.shape[0]
    windows = stack_ref.shape[1] // patch_len // 2
    routed_ref[...] = jnp.zeros_like(routed_ref)
    for source in range(2):
        first = order[heads + source] * windows
        for window in range(windows):
            here = first + window
            rows = pl.ds(pl.multiple_of(here * patch_len, patch_len), patch_len)
            slot = dest[here]
            for head in range(heads):
                lanes = pl.ds((source * heads + head) * HD, HD)
                routed_ref[slot, :, lanes] = stack_ref[order[head], rows, :][:, :HD]


def route(dest, order, stack, slots, patch_len):
    heads = stack.shape[0]
    vmem = pl.BlockSpec(memory_space=pltpu.VMEM)
    smem = pl.BlockSpec(memory_space=pltpu.SMEM)
    return pl.pallas_call(
        functools.partial(route_kernel, patch_len),
        in_specs=[smem, smem, vmem],
        out_specs=vmem,
        out_shape=jax.ShapeDtypeStruct((slots, patch_len, 2 * heads * HD), BF16),
        compiler_params=pltpu.CompilerParams(vmem_limit_bytes=16 * 1024 * 1024),
        name="route",
    )(dest, order, stack)


def settle_kernel(arrived_ref, placed_ref):
    half = arrived_ref.shape[2] // 2
    for pair in range(0, arrived_ref.shape[0], 2):
        for source in range(2):
            lanes = pl.ds(source * half, half)
            for core in range(2):
                out = pl.ds(core * half, half)
                placed_ref[pair + source, :, out] = arrived_ref[pair + core, :, lanes]


def settle(arrived):
    vmem = pl.BlockSpec(memory_space=pltpu.VMEM)
    return pl.pallas_call(
        settle_kernel,
        in_specs=[vmem],
        out_specs=vmem,
        out_shape=jax.ShapeDtypeStruct(arrived.shape, BF16),
        compiler_params=pltpu.CompilerParams(vmem_limit_bytes=16 * 1024 * 1024),
        name="settle",
    )(arrived)


def rotary_tables(coords):
    quarter = HD // 4
    frequency = 10000.0 ** (-jnp.arange(quarter, dtype=F32) / quarter)
    angles = coords.astype(F32)[:, :, :, None] * frequency
    angles = jnp.concatenate([angles[:, 0], angles[:, 0], angles[:, 1], angles[:, 1]], axis=-1)
    angles = angles.reshape(-1, HD)
    pad = ((0, 0), (0, LANES - HD))
    return jnp.pad(jnp.cos(angles), pad), jnp.pad(jnp.sin(angles), pad)


def head_major(own, core, heads, order):
    rows = own.shape[0]
    width = heads * HD
    kept = lax.dynamic_slice_in_dim(own, core * width, width, axis=1)
    sent = lax.dynamic_slice_in_dim(own, (1 - core) * width, width, axis=1)
    both = jnp.concatenate([kept, core_swap(sent)], axis=0)
    both = jnp.pad(both.reshape(2 * rows, heads, HD), ((0, 0), (0, 0), (0, LANES - HD)))
    return [lax.dynamic_index_in_dim(both, at, axis=1, keepdims=False) for at in order]


def per_device(patches, values, upstream, coords, counts, dest, weight):
    core, here = lax.axis_index("c"), lax.axis_index("x")
    nx, ny, nz = lax.axis_size("x"), lax.axis_size("y"), lax.axis_size("zh")
    slots = lax.axis_size(("zl", "x", "c"))
    window_count, patch_len, model_width = patches.shape
    value_width = values.shape[-1]
    row_total = window_count * patch_len
    depth = weight.shape[0]
    steps = [0, 1, nx - 1] + list(range(2, nx - 1))
    order = [lax.rem(here + step, nx) for step in steps]

    head = core * nx + here
    slice_q = lax.dynamic_slice_in_dim(weight, head * HD, HD, axis=1)
    slice_k = lax.dynamic_slice_in_dim(weight, value_width + head * HD, HD, axis=1)
    own_w = spread(jnp.concatenate([slice_q, slice_k], axis=1), "zh")
    own_w = jnp.transpose(own_w, (1, 0, 2)).reshape(depth, nz * 2 * HD)
    own_w = spread(own_w, "y").reshape(ny * depth, nz * 2 * HD)
    weights = [own_w] + [ring_x(own_w, -step) for step in steps[1:]]

    flat = patches.reshape(row_total, model_width)
    both = jnp.concatenate([flat, core_swap(flat)], axis=0)
    turned = jnp.transpose(both)
    small = jnp.concatenate([coords.reshape(window_count, -1), counts[:, None], dest], axis=1)
    small = jnp.concatenate([small, core_swap(small)], axis=0)
    both_coords = small[:, : 2 * patch_len].reshape(2 * window_count, 2, patch_len)
    both_counts, both_dest = small[:, 2 * patch_len], small[:, 2 * patch_len + 1]
    cosine, sine = rotary_tables(both_coords)
    value_heads = head_major(values.reshape(row_total, value_width), core, nx, order)
    upstream_heads = head_major(upstream.reshape(row_total, value_width), core, nx, order)

    contexts, total = [], None
    for at, step in enumerate(steps):
        context, grad = one_head(
            both_counts,
            weights[at],
            both,
            turned,
            cosine,
            sine,
            value_heads[at],
            upstream_heads[at],
            patch_len,
        )
        contexts.append(context)
        if step:
            grad = ring_x(grad, step)
        total = grad.astype(F32) if total is None else total + grad.astype(F32)

    place = [jnp.int32(0)] * nx
    for at, head_at in enumerate(order):
        place = [jnp.where(head_at == h, at, place[h]) for h in range(nx)]
    place = jnp.stack(place + [core, 1 - core]).astype(jnp.int32)
    routed = route(both_dest, place, jnp.stack(contexts), slots, patch_len)
    placed = settle(exchange(routed, ("zl", "x", "c")))

    total = exchange(total.astype(BF16).reshape(ny, depth, nz * 2 * HD), "y")
    total = jnp.sum(total.astype(F32), axis=0).astype(BF16)
    total = jnp.transpose(total.reshape(depth, nz, 2 * HD), (1, 0, 2))
    copies = lax.axis_size("zl")
    total = jnp.broadcast_to(total[None], (copies,) + total.shape)
    total = exchange(total.reshape(copies * nz, depth, 2 * HD), ("zl", "zh"))
    total = jnp.sum(total.astype(F32), axis=0).astype(BF16)
    total = spread(total, ("x", "c")).reshape(nx, 2, depth, 2, HD)
    grad_weight = jnp.transpose(total, (2, 3, 1, 0, 4)).reshape(depth, 2 * value_width)
    return (placed, grad_weight.astype(F32))


def solution(mesh):
    fine = Mesh(mesh.devices.reshape(SPLIT), AXES)
    return jax.shard_map(
        per_device,
        mesh=fine,
        in_specs=(
            P(AXES, None, None),
            P(AXES, None, None),
            P(AXES, None, None),
            P(AXES, None, None),
            P(AXES),
            P(AXES, None),
            P(("zh", "y"), None),
        ),
        out_specs=(P(AXES, None, None), P(("zh", "y"), None)),
        check_vma=False,
    )
```

time: 199 us -> 211 us (1.060)
  blocking collectives: 129 us -> 13.3 us
  starting transfers between devices: 22.3 us -> 77.1 us
  local copies, waits for them, and re-layouts: 5.24 us -> 36.3 us
  waiting for transfers between devices: 16.9 us -> 38.4 us
  Pallas kernels: 16.1 us -> 33.6 us
  other arithmetic: 1.93 us -> 9.03 us
  matrix products: 5.39 us -> 0 us
    all_to_all x5 -> x1, blocking collectives: 129 us -> 13.3 us  [exchange(): return lax.all_to_all(array, axes, split_axis=0, concat_axis=0, tiled=True)]
    all_to_all x1 -> x5, starting transfers between devices: 8.83 us -> 39.7 us  [exchange(): return lax.all_to_all(array, axes, split_axis=0, concat_axis=0, tiled=True)]
    all_to_all x1 -> x5, waiting for transfers between devices: 15.6 us -> 38.4 us  [exchange(): return lax.all_to_all(array, axes, split_axis=0, concat_axis=0, tiled=True)]
    pallas_call x1 -> x6, Pallas kernels: 16.1 us -> 33.6 us  [the longest x4 30.5 us: one_head(): pl.pallas_call(functools.partial(head_kernel, patch_len, group), in_specs...]
    ppermute x2 -> x6, starting transfers between devices: 1.32 us -> 18.5 us  [ring_x(): lax.ppermute(array, 'x', [(i, (i + step) % count) for i in range(count)])]
    dynamic_slice x1 -> x12, local copies, waits for them, and re-layouts: 0.01 us -> 12.8 us  [the longest x9 9.88 us: head_major(): lax.dynamic_index_in_dim(both, at, axis=1, keepdims=False)]
    unnamed x15 -> x41, local copies, waits for them, and re-layouts: 1.86 us -> 8.79 us
    ppermute x4, starting transfers between devices: 12.2 us -> 18.9 us  [core_swap(): return lax.ppermute(array, 'c', [(0, 1), (1, 0)])]
  transfers between devices with their start and end apart: 7 -> 15, of which waited for: 2 -> 4; matrix products, arithmetic and copies ran while one was open for 3% -> 15% of each run, Pallas kernels for 8% -> 15%
where the time goes in v3:
time: 211 us; the launch traced here: 209 us
  starting transfers between devices  77.1 us (37%)
  waiting for transfers between devices  38.4 us (18%)
  local copies, waits for them, and re-layouts  36.3 us (17%)
  Pallas kernels  33.6 us (16%)
  blocking collectives  13.3 us (6%)
  other arithmetic  9.03 us (4%)
    all_to_all x5, starting transfers between devices, exchange(): return lax.all_to_all(array, axes, split_axis=0, concat_axis=0, tiled=True)  39.7 us
    all_to_all x5, waiting for transfers between devices, exchange(): return lax.all_to_all(array, axes, split_axis=0, concat_axis=0, tiled=True)  38.4 us
    pallas_call x4, Pallas kernels, one_head(): pl.pallas_call(functools.partial(head_kernel, patch_len, group), in_specs...  30.5 us
    ppermute x4, starting transfers between devices, core_swap(): return lax.ppermute(array, 'c', [(0, 1), (1, 0)])  18.9 us
    ppermute x6, starting transfers between devices, ring_x(): lax.ppermute(array, 'x', [(i, (i + step) % count) for i in range(count)])  18.5 us
    all_to_all x1, blocking collectives, exchange(): return lax.all_to_all(array, axes, split_axis=0, concat_axis=0, tiled=True)  13.3 us
    dynamic_slice x9, local copies, waits for them, and re-layouts, head_major(): lax.dynamic_index_in_dim(both, at, axis=1, keepdims=False)  9.88 us
    unnamed x41, local copies, waits for them, and re-layouts  8.79 us
  transfers between devices with their start and end apart: 15, of which 4 were waited for; matrix products, arithmetic and copies ran while one was open for 15% of the time, Pallas kernels for 15%

profile of v3, /device:TPU:1, one launch (start us, length us, event | category | flops | bytes accessed | tf_op | source)
XLA Modules:
  0.0 209.0 jit_solution(13372886023977188338)
XLA Ops:
  3.1 12.4 %collective-permute-start = (s32[12,66]{1,0:T(8,128)S(1)}, s32[12,66]{1,0:T(8,128)S(1)}, u32[]{:S(2)}, u32[]{:S(2)}) collective-permute-start(s32[12,66]{1,0:T(8,128)S(1)} %pad_add_fusion.1), channel_id=1, source_target_pairs={{0,32},{32,0},{1,33},{33,1},{2,34},{34,2},{3,35},{35,3},{4,36},{36... | collective-permute-start | bytes 9512 | tf_op jit(solution)/shard_map/ppermute | solution.py:21
  15.5 0.8 constant_dynamic-slice_fusion.5
  17.1 5.2 %all-to-all-start = ((bf16[4,40,160]{2,1,0:T(8,128)(2,1)}), bf16[4,40,160]{2,1,0:T(8,128)(2,1)S(1)}, u32[]{:S(2)}, u32[]{:S(2)}) async-start(bf16[4,40,160]{2,1,0:T(8,128)(2,1)} %broadcast_in_dim.13), calls=%async_computation | async-start | bytes 163840 | tf_op jit(solution)/shard_map/all_to_all | solution.py:30
  22.3 1.6 copy.124
  23.9 2.2 %collective-permute-start.1 = (bf16[384,1280]{0,1:T(8,128)(2,1)S(1)}, bf16[384,1280]{0,1:T(8,128)(2,1)}, u32[]{:S(2)}, u32[]{:S(2)}) collective-permute-start(bf16[384,1280]{0,1:T(8,128)(2,1)S(1)} %copy.124), channel_id=1, source_target_pairs={{0,32},{32,0},{1,33},{33,1},{2,34},{34,2},{3,35},{35,3},{4,36},{36... | collective-permute-start | bytes 2949128 | tf_op jit(solution)/shard_map/ppermute | solution.py:21
  26.1 1.1 constant_dynamic-slice_fusion.1
  27.2 2.1 %collective-permute-start.3 = (bf16[384,320]{1,0:T(8,128)(2,1)}, bf16[384,320]{1,0:T(8,128)(2,1)}, u32[]{:S(2)}, u32[]{:S(2)}) collective-permute-start(bf16[384,320]{1,0:T(8,128)(2,1)} %get-tuple-element.35), channel_id=1, source_target_pairs={{0,32},{32,0},{1,33},{33,1},{2,34},{34,2},{3,35},{35,3},{4,36},{36... | collective-permute-start | bytes 737288 | tf_op jit(solution)/shard_map/ppermute | solution.py:21
  29.4 1.0 constant_dynamic-slice_fusion.3
  30.4 2.2 %collective-permute-start.2 = (bf16[384,320]{1,0:T(8,128)(2,1)}, bf16[384,320]{1,0:T(8,128)(2,1)}, u32[]{:S(2)}, u32[]{:S(2)}) collective-permute-start(bf16[384,320]{1,0:T(8,128)(2,1)} %get-tuple-element.37), channel_id=1, source_target_pairs={{0,32},{32,0},{1,33},{33,1},{2,34},{34,2},{3,35},{35,3},{4,36},{36... | collective-permute-start | bytes 737288 | tf_op jit(solution)/shard_map/ppermute | solution.py:21
  34.0 6.8 %all-to-all-start.1 = ((bf16[8,40,640]{2,1,0:T(8,128)(2,1)}), bf16[8,40,640]{2,1,0:T(8,128)(2,1)S(1)}, u32[]{:S(2)}, u32[]{:S(2)}) async-start(bf16[8,40,640]{2,1,0:T(8,128)(2,1)} %broadcast_in_dim.15), calls=%async_computation.1 | async-start | bytes 819200 | tf_op jit(solution)/shard_map/all_to_all | solution.py:30
  40.9 1.7 fusion
  43.5 1.0 pad_maximum_fusion.3
  44.6 1.0 copy.128
  45.6 1.0 pad_maximum_fusion.2
  46.6 1.0 copy.126
  47.6 6.8 %all-to-all-done.1 = bf16[8,40,640]{2,1,0:T(8,128)(2,1)S(1)} async-done(((bf16[8,40,640]{2,1,0:T(8,128)(2,1)}), bf16[8,40,640]{2,1,0:T(8,128)(2,1)S(1)}, u32[]{:S(2)}, u32[]{:S(2)}) %all-to-all-start.1) | async-done | bytes 409632 | tf_op jit(solution)/shard_map/all_to_all | solution.py:30
  54.5 4.6 %collective-permute-start.6 = (bf16[320,640]{1,0:T(8,128)(2,1)S(1)}, bf16[320,640]{1,0:T(8,128)(2,1)}, u32[]{:S(2)}, u32[]{:S(2)}) collective-permute-start(bf16[320,640]{1,0:T(8,128)(2,1)S(1)} %bitcast.34), channel_id=1, source_target_pairs={{0,128},{64,192},{128,0},{192,64},{1,129},{65,193},{129,1},{193,65... | collective-permute-start | bytes 1228808 | tf_op jit(solution)/shard_map/ppermute | solution.py:26
  59.1 2.2 %pad_dynamic-slice_fusion.3 = (bf16[768,1,128]{0,2,1:T(8,128)(2,1)}, bf16[768,1,128]{0,2,1:T(8,128)(2,1)S(1)}, bf16[768,1,128]{0,2,1:T(8,128)(2,1)S(1)}, bf16[76...) fusion(s32[]{:T(128)S(6)} %select_n.88, ...), kind=kLoop, calls=%fused_computation.4 | loop fusion | bytes 2555920 | tf_op jit(solution)/shard_map/jit(dynamic_index_in_dim)/dynamic_slice | solution.py:214
  63.9 0.8 copy.131
  65.5 2.2 %collective-permute-start.5 = (bf16[320,640]{1,0:T(8,128)(2,1)S(1)}, bf16[320,640]{1,0:T(8,128)(2,1)}, u32[]{:S(2)}, u32[]{:S(2)}) collective-permute-start(bf16[320,640]{1,0:T(8,128)(2,1)S(1)} %bitcast.35), channel_id=1, source_target_pairs={{0,64},{64,128},{128,192},{192,0},{1,65},{65,129},{129,193},{193,1... | collective-permute-start | bytes 1228808 | tf_op jit(solution)/shard_map/ppermute | solution.py:26
  67.7 4.3 %collective-permute-start.4 = (bf16[320,640]{1,0:T(8,128)(2,1)S(1)}, bf16[320,640]{1,0:T(8,128)(2,1)}, u32[]{:S(2)}, u32[]{:S(2)}) collective-permute-start(bf16[320,640]{1,0:T(8,128)(2,1)S(1)} %bitcast.36), channel_id=1, source_target_pairs={{0,192},{64,0},{128,64},{192,128},{1,193},{65,1},{129,65},{193,129... | collective-permute-start | bytes 1228808 | tf_op jit(solution)/shard_map/ppermute | solution.py:26
  72.0 3.0 %fusion.2 = (bf16[1280,768]{1,0:T(8,128)(2,1)S(1)}, bf16[768,1280]{0,1:T(8,128)(2,1)}) fusion(bf16[384,1280]{0,1:T(8,128)(2,1)} %collective-permute-done.1, bf16[384,1280]{0,1:T(8,128)(2,1)} %copy-done.16), kind=kLoop, calls=%fused_computation.30 | loop fusion | flops 3932160 | bytes 5898240 | tf_op jit(solution)/shard_map/transpose | solution.py:238
  75.1 4.0 %copy.130.patches_ref = bf16[768,1280]{1,0:T(8,128)(2,1)} copy(bf16[768,1280]{0,1:T(8,128)(2,1)} %get-tuple-element.21) | data formatting | bytes 3932160 | tf_op jit(solution)/shard_map/concatenate | solution.py:237
  79.0 1.5 copy-done
  80.6 0.9 copy-done.10
  82.2 7.9 %one_head.7 = (bf16[768,128]{1,0:T(8,128)(2,1)S(1)}, bf16[320,640]{1,0:T(8,128)(2,1)}) custom-call(s32[24]{0:T(128)S(1)} %copy-done.14, bf16[320,640]{1,0:T(8,128)(2,1)} %collective-permute-done.6.weight_ref, bf16[768,1280]{1,0:T(8,128)(2,1)S(1)} %copy-done, bf16[1280,768]{1,0:T(8,128)(2,1)S(1)} %get-tuple-element.20.turned_ref, ...), custom_call_target="tpu_custom_call" | custom-call | flops 4000000000 | bytes 8000000 | tf_op jit(solution)/shard_map/one_head/pallas_call | solution.py:125
  90.1 2.1 %collective-permute-start.9 = (bf16[320,640]{1,0:T(8,128)(2,1)}, bf16[320,640]{1,0:T(8,128)(2,1)}, u32[]{:S(2)}, u32[]{:S(2)}) collective-permute-start(bf16[320,640]{1,0:T(8,128)(2,1)} %get-tuple-element.17), channel_id=1, source_target_pairs={{0,128},{64,192},{128,0},{192,64},{1,129},{65,193},{129,1},{193,65... | collective-permute-start | bytes 1228808 | tf_op jit(solution)/shard_map/ppermute | solution.py:26
  92.3 8.0 %one_head.6 = (bf16[768,128]{1,0:T(8,128)(2,1)S(1)}, bf16[320,640]{1,0:T(8,128)(2,1)}) custom-call(s32[24]{0:T(128)S(1)} %copy-done.14, bf16[320,640]{1,0:T(8,128)(2,1)} %collective-permute-done.5.weight_ref, bf16[768,1280]{1,0:T(8,128)(2,1)S(1)} %copy-done, bf16[1280,768]{1,0:T(8,128)(2,1)S(1)} %get-tuple-element.20.turned_ref, ...), custom_call_target="tpu_custom_call" | custom-call | flops 4000000000 | bytes 8000000 | tf_op jit(solution)/shard_map/one_head/pallas_call | solution.py:125
  100.2 3.4 %collective-permute-start.8 = (bf16[320,640]{1,0:T(8,128)(2,1)}, bf16[320,640]{1,0:T(8,128)(2,1)}, u32[]{:S(2)}, u32[]{:S(2)}) collective-permute-start(bf16[320,640]{1,0:T(8,128)(2,1)} %get-tuple-element.16), channel_id=1, source_target_pairs={{0,192},{64,0},{128,64},{192,128},{1,193},{65,1},{129,65},{193,129... | collective-permute-start | bytes 1228808 | tf_op jit(solution)/shard_map/ppermute | solution.py:26
  103.6 7.9 %one_head.5 = (bf16[768,128]{1,0:T(8,128)(2,1)S(1)}, bf16[320,640]{1,0:T(8,128)(2,1)}) custom-call(s32[24]{0:T(128)S(1)} %copy-done.14, bf16[320,640]{1,0:T(8,128)(2,1)} %collective-permute-done.4.weight_ref, bf16[768,1280]{1,0:T(8,128)(2,1)S(1)} %copy-done, bf16[1280,768]{1,0:T(8,128)(2,1)S(1)} %get-tuple-element.20.turned_ref, ...), custom_call_target="tpu_custom_call" | custom-call | flops 4000000000 | bytes 8000000 | tf_op jit(solution)/shard_map/one_head/pallas_call | solution.py:125
  112.2 1.9 collective-permute-start.7
  114.1 1.8 copy.127
  115.9 1.7 copy.129
  117.6 1.5 copy-done.1
  119.2 0.9 copy-done.11
  120.1 0.9 copy-done.12
  121.7 6.7 %one_head.4 = (bf16[768,128]{1,0:T(8,128)(2,1)S(1)}, bf16[320,640]{1,0:T(8,128)(2,1)S(1)}) custom-call(s32[24]{0:T(128)S(1)} %copy-done.15, bf16[320,640]{1,0:T(8,128)(2,1)S(1)} %bitcast.37, bf16[768,1280]{1,0:T(8,128)(2,1)S(1)} %copy-done.1, bf16[1280,768]{1,0:T(8,128)(2,1)S(1)} %get-tuple-element.20.turned_ref, f32[768,128]{1,0:T(8,128)S(1)} %pad.14.cos_ref, ...), custom_call_target="tpu_custom_call" | custom-call | flops 4000000000 | bytes 8000000 | tf_op jit(solution)/shard_map/one_head/pallas_call | solution.py:125
  128.4 1.5 add_convert_fusion
  130.0 13.3 %all_to_all.30 = bf16[8,40,640]{2,1,0:T(8,128)(2,1)S(1)} all-to-all(bf16[8,40,640]{2,1,0:T(8,128)(2,1)S(1)} %bitcast.52), channel_id=1, replica_groups=mesh['zl'=3,'x'=4,'c'=2,'zh'=4,'y'=8] {'y'}, dimensions={0} | all-to-all | bytes 819200 | tf_op jit(solution)/shard_map/all_to_all | solution.py:30
  144.2 13.8 %all-to-all-start.4 = ((bf16[12,40,160]{2,1,0:T(8,128)(2,1)}), bf16[12,40,160]{2,1,0:T(8,128)(2,1)S(1)}, u32[]{:S(2)}, u32[]{:S(2)}) async-start(bf16[12,40,160]{2,1,0:T(8,128)(2,1)} %bitcast.31), calls=%async_computation.4 | async-start | bytes 491520 | tf_op jit(solution)/shard_map/all_to_all | solution.py:30
  158.1 11.6 %all-to-all-done.4 = bf16[12,40,160]{2,1,0:T(8,128)(2,1)S(1)} async-done(((bf16[12,40,160]{2,1,0:T(8,128)(2,1)}), bf16[12,40,160]{2,1,0:T(8,128)(2,1)S(1)}, u32[]{:S(2)}, u32[]{:S(2)}) %all-to-all-start.4) | async-done | bytes 153632 | tf_op jit(solution)/shard_map/all_to_all | solution.py:30
  170.3 9.4 %all-to-all-start.5 = ((bf16[8,40,160]{2,1,0:T(8,128)(2,1)}), bf16[8,40,160]{2,1,0:T(8,128)(2,1)S(1)}, u32[]{:S(2)}, u32[]{:S(2)}) async-start(bf16[8,40,160]{2,1,0:T(8,128)(2,1)} %broadcast_in_dim.17), calls=%async_computation.5 | async-start | bytes 327680 | tf_op jit(solution)/shard_map/all_to_all | solution.py:30
  179.9 1.9 route.1
  181.8 3.5 %all-to-all-done.5 = bf16[8,40,160]{2,1,0:T(8,128)(2,1)S(1)} async-done(((bf16[8,40,160]{2,1,0:T(8,128)(2,1)}), bf16[8,40,160]{2,1,0:T(8,128)(2,1)S(1)}, u32[]{:S(2)}, u32[]{:S(2)}) %all-to-all-start.5) | async-done | bytes 102432 | tf_op jit(solution)/shard_map/all_to_all | solution.py:30
  185.3 4.5 %all-to-all-start.2 = ((bf16[24,32,640]{2,1,0:T(8,128)(2,1)}), bf16[24,32,640]{2,1,0:T(8,128)(2,1)S(1)}, u32[]{:S(2)}, u32[]{:S(2)}) async-start(bf16[24,32,640]{2,1,0:T(8,128)(2,1)} %route.1), calls=%async_computation.2 | async-start | bytes 1966080 | tf_op jit(solution)/shard_map/all_to_all | solution.py:30
  190.3 1.0 reshape.76
  191.3 16.5 %all-to-all-done.2.arrived_ref = bf16[24,32,640]{2,1,0:T(8,128)(2,1)S(1)} async-done(((bf16[24,32,640]{2,1,0:T(8,128)(2,1)}), bf16[24,32,640]{2,1,0:T(8,128)(2,1)S(1)}, u32[]{:S(2)}, u32[]{:S(2)}) %all-to-all-start.2) | async-done | bytes 983072 | tf_op jit(solution)/shard_map/all_to_all | solution.py:30
  207.8 1.2 settle.1
  (80 shorter events, 13.2 us)
Async XLA Ops:
  0.6 25.5 %copy-start.18 = (bf16[12,32,640]{2,1,0:T(8,128)(2,1)S(1)}, bf16[12,32,640]{2,1,0:T(8,128)(2,1)}, u32[]{:S(2)}) copy-start(bf16[12,32,640]{2,1,0:T(8,128)(2,1)} %param.9) | copy-start | bytes 1474564
  0.6 28.7 %copy-start.19 = (bf16[12,32,640]{2,1,0:T(8,128)(2,1)S(1)}, bf16[12,32,640]{2,1,0:T(8,128)(2,1)}, u32[]{:S(2)}) copy-start(bf16[12,32,640]{2,1,0:T(8,128)(2,1)} %param.8) | copy-start | bytes 1474564
  3.1 29.5 %collective-permute-start = (s32[12,66]{1,0:T(8,128)S(1)}, s32[12,66]{1,0:T(8,128)S(1)}, u32[]{:S(2)}, u32[]{:S(2)}) collective-permute-start(s32[12,66]{1,0:T(8,128)S(1)} %pad_add_fusion.1), channel_id=1, source_target_pairs={{0,32},{32,0},{1,33},{33,1},{2,34},{34,2},{3,35},{35,3},{4,36},{36... | collective-permute-start | bytes 9512 | tf_op jit(solution)/shard_map/ppermute | solution.py:21
  17.1 16.0 %all-to-all-start = ((bf16[4,40,160]{2,1,0:T(8,128)(2,1)}), bf16[4,40,160]{2,1,0:T(8,128)(2,1)S(1)}, u32[]{:S(2)}, u32[]{:S(2)}) async-start(bf16[4,40,160]{2,1,0:T(8,128)(2,1)} %broadcast_in_dim.13), calls=%async_computation | async-start | bytes 163840 | tf_op jit(solution)/shard_map/all_to_all | solution.py:30
  23.9 10.2 %copy-start.16 = (bf16[384,1280]{0,1:T(8,128)(2,1)}, bf16[384,1280]{0,1:T(8,128)(2,1)S(1)}, u32[]{:S(2)}) copy-start(bf16[384,1280]{0,1:T(8,128)(2,1)S(1)} %copy.124) | copy-start | bytes 2949124
  23.9 48.1 %collective-permute-start.1 = (bf16[384,1280]{0,1:T(8,128)(2,1)S(1)}, bf16[384,1280]{0,1:T(8,128)(2,1)}, u32[]{:S(2)}, u32[]{:S(2)}) collective-permute-start(bf16[384,1280]{0,1:T(8,128)(2,1)S(1)} %copy.124), channel_id=1, source_target_pairs={{0,32},{32,0},{1,33},{33,1},{2,34},{34,2},{3,35},{35,3},{4,36},{36... | collective-permute-start | bytes 2949128 | tf_op jit(solution)/shard_map/ppermute | solution.py:21
  27.2 16.3 %collective-permute-start.3 = (bf16[384,320]{1,0:T(8,128)(2,1)}, bf16[384,320]{1,0:T(8,128)(2,1)}, u32[]{:S(2)}, u32[]{:S(2)}) collective-permute-start(bf16[384,320]{1,0:T(8,128)(2,1)} %get-tuple-element.35), channel_id=1, source_target_pairs={{0,32},{32,0},{1,33},{33,1},{2,34},{34,2},{3,35},{35,3},{4,36},{36... | collective-permute-start | bytes 737288 | tf_op jit(solution)/shard_map/ppermute | solution.py:21
  30.4 15.2 %collective-permute-start.2 = (bf16[384,320]{1,0:T(8,128)(2,1)}, bf16[384,320]{1,0:T(8,128)(2,1)}, u32[]{:S(2)}, u32[]{:S(2)}) collective-permute-start(bf16[384,320]{1,0:T(8,128)(2,1)} %get-tuple-element.37), channel_id=1, source_target_pairs={{0,32},{32,0},{1,33},{33,1},{2,34},{34,2},{3,35},{35,3},{4,36},{36... | collective-permute-start | bytes 737288 | tf_op jit(solution)/shard_map/ppermute | solution.py:21
  34.0 20.4 %all-to-all-start.1 = ((bf16[8,40,640]{2,1,0:T(8,128)(2,1)}), bf16[8,40,640]{2,1,0:T(8,128)(2,1)S(1)}, u32[]{:S(2)}, u32[]{:S(2)}) async-start(bf16[8,40,640]{2,1,0:T(8,128)(2,1)} %broadcast_in_dim.15), calls=%async_computation.1 | async-start | bytes 819200 | tf_op jit(solution)/shard_map/all_to_all | solution.py:30
  40.9 2.6 %copy-start.17 = (bf16[384,320]{1,0:T(8,128)(2,1)S(1)}, bf16[384,320]{1,0:T(8,128)(2,1)}, u32[]{:S(2)}) copy-start(bf16[384,320]{1,0:T(8,128)(2,1)} %get-tuple-element.34) | copy-start | bytes 737284
  54.5 24.6 %collective-permute-start.6 = (bf16[320,640]{1,0:T(8,128)(2,1)S(1)}, bf16[320,640]{1,0:T(8,128)(2,1)}, u32[]{:S(2)}, u32[]{:S(2)}) collective-permute-start(bf16[320,640]{1,0:T(8,128)(2,1)S(1)} %bitcast.34), channel_id=1, source_target_pairs={{0,128},{64,192},{128,0},{192,64},{1,129},{65,193},{129,1},{193,65... | collective-permute-start | bytes 1228808 | tf_op jit(solution)/shard_map/ppermute | solution.py:26
  65.5 26.7 %collective-permute-start.5 = (bf16[320,640]{1,0:T(8,128)(2,1)S(1)}, bf16[320,640]{1,0:T(8,128)(2,1)}, u32[]{:S(2)}, u32[]{:S(2)}) collective-permute-start(bf16[320,640]{1,0:T(8,128)(2,1)S(1)} %bitcast.35), channel_id=1, source_target_pairs={{0,64},{64,128},{128,192},{192,0},{1,65},{65,129},{129,193},{193,1... | collective-permute-start | bytes 1228808 | tf_op jit(solution)/shard_map/ppermute | solution.py:26
  67.7 35.9 %collective-permute-start.4 = (bf16[320,640]{1,0:T(8,128)(2,1)S(1)}, bf16[320,640]{1,0:T(8,128)(2,1)}, u32[]{:S(2)}, u32[]{:S(2)}) collective-permute-start(bf16[320,640]{1,0:T(8,128)(2,1)S(1)} %bitcast.36), channel_id=1, source_target_pairs={{0,192},{64,0},{128,64},{192,128},{1,193},{65,1},{129,65},{193,129... | collective-permute-start | bytes 1228808 | tf_op jit(solution)/shard_map/ppermute | solution.py:26
  79.0 1.5 copy-start
  80.6 0.9 copy-start.10
  81.5 0.7 copy-start.14
  82.2 10.0 %copy-start.8 = (bf16[768,1,128]{2,0,1:T(8,128)(2,1)S(1)}, bf16[768,1,128]{2,0,1:T(8,128)(2,1)}, u32[]{:S(2)}) copy-start(bf16[768,1,128]{2,0,1:T(8,128)(2,1)} %copy.134) | copy-start | bytes 589828
  82.2 10.1 %copy-start.9 = (bf16[768,1,128]{2,0,1:T(8,128)(2,1)S(1)}, bf16[768,1,128]{2,0,1:T(8,128)(2,1)}, u32[]{:S(2)}) copy-start(bf16[768,1,128]{2,0,1:T(8,128)(2,1)} %copy.135) | copy-start | bytes 589828
  90.1 38.3 %collective-permute-start.9 = (bf16[320,640]{1,0:T(8,128)(2,1)}, bf16[320,640]{1,0:T(8,128)(2,1)}, u32[]{:S(2)}, u32[]{:S(2)}) collective-permute-start(bf16[320,640]{1,0:T(8,128)(2,1)} %get-tuple-element.17), channel_id=1, source_target_pairs={{0,128},{64,192},{128,0},{192,64},{1,129},{65,193},{129,1},{193,65... | collective-permute-start | bytes 1228808 | tf_op jit(solution)/shard_map/ppermute | solution.py:26
  92.2 11.4 %copy-start.6 = (bf16[768,1,128]{2,0,1:T(8,128)(2,1)S(1)}, bf16[768,1,128]{2,0,1:T(8,128)(2,1)}, u32[]{:S(2)}) copy-start(bf16[768,1,128]{2,0,1:T(8,128)(2,1)} %copy.131) | copy-start | bytes 589828
  92.3 11.4 %copy-start.7 = (bf16[768,1,128]{2,0,1:T(8,128)(2,1)S(1)}, bf16[768,1,128]{2,0,1:T(8,128)(2,1)}, u32[]{:S(2)}) copy-start(bf16[768,1,128]{2,0,1:T(8,128)(2,1)} %copy.132) | copy-start | bytes 589828
  100.2 28.2 %collective-permute-start.8 = (bf16[320,640]{1,0:T(8,128)(2,1)}, bf16[320,640]{1,0:T(8,128)(2,1)}, u32[]{:S(2)}, u32[]{:S(2)}) collective-permute-start(bf16[320,640]{1,0:T(8,128)(2,1)} %get-tuple-element.16), channel_id=1, source_target_pairs={{0,192},{64,0},{128,64},{192,128},{1,193},{65,1},{129,65},{193,129... | collective-permute-start | bytes 1228808 | tf_op jit(solution)/shard_map/ppermute | solution.py:26
  111.5 0.7 copy-start.2
  112.2 16.2 %collective-permute-start.7 = (bf16[320,640]{1,0:T(8,128)(2,1)}, bf16[320,640]{1,0:T(8,128)(2,1)}, u32[]{:S(2)}, u32[]{:S(2)}) collective-permute-start(bf16[320,640]{1,0:T(8,128)(2,1)} %get-tuple-element.15), channel_id=1, source_target_pairs={{0,64},{64,128},{128,192},{192,0},{1,65},{65,129},{129,193},{193,1... | collective-permute-start | bytes 1228808 | tf_op jit(solution)/shard_map/ppermute | solution.py:26
  117.6 1.5 copy-start.1
  119.2 0.9 copy-start.11
  120.1 0.9 copy-start.12
  121.0 0.7 copy-start.15
  128.4 1.5 copy-start.4
  129.9 49.8 %copy-start.3 = (bf16[768,128]{1,0:T(8,128)(2,1)S(1)}, bf16[768,128]{1,0:T(8,128)(2,1)}, u32[]{:S(2)}) copy-start(bf16[768,128]{1,0:T(8,128)(2,1)} %copy-done.2) | copy-start | bytes 589828
  129.9 49.8 %copy-start.5 = (bf16[768,128]{1,0:T(8,128)(2,1)S(1)}, bf16[768,128]{1,0:T(8,128)(2,1)}, u32[]{:S(2)}) copy-start(bf16[768,128]{1,0:T(8,128)(2,1)} %copy-done.4) | copy-start | bytes 589828
  143.2 36.6 %copy-start.13 = (s32[24]{0:T(128)S(1)}, s32[24]{0:T(128)}, u32[]{:S(2)}) copy-start(s32[24]{0:T(128)} %get-tuple-element.19.dest) | copy-start | bytes 292
  144.2 25.5 %all-to-all-start.4 = ((bf16[12,40,160]{2,1,0:T(8,128)(2,1)}), bf16[12,40,160]{2,1,0:T(8,128)(2,1)S(1)}, u32[]{:S(2)}, u32[]{:S(2)}) async-start(bf16[12,40,160]{2,1,0:T(8,128)(2,1)} %bitcast.31), calls=%async_computation.4 | async-start | bytes 491520 | tf_op jit(solution)/shard_map/all_to_all | solution.py:30
  170.3 15.0 %all-to-all-start.5 = ((bf16[8,40,160]{2,1,0:T(8,128)(2,1)}), bf16[8,40,160]{2,1,0:T(8,128)(2,1)S(1)}, u32[]{:S(2)}, u32[]{:S(2)}) async-start(bf16[8,40,160]{2,1,0:T(8,128)(2,1)} %broadcast_in_dim.17), calls=%async_computation.5 | async-start | bytes 327680 | tf_op jit(solution)/shard_map/all_to_all | solution.py:30
  185.3 22.5 %all-to-all-start.2 = ((bf16[24,32,640]{2,1,0:T(8,128)(2,1)}), bf16[24,32,640]{2,1,0:T(8,128)(2,1)S(1)}, u32[]{:S(2)}, u32[]{:S(2)}) async-start(bf16[24,32,640]{2,1,0:T(8,128)(2,1)} %route.1), calls=%async_computation.2 | async-start | bytes 1966080 | tf_op jit(solution)/shard_map/all_to_all | solution.py:30

commit v4 on v3

v4 whole, which is shorter than its diff:
```python
import functools
import math

import jax
import jax.numpy as jnp
from jax import lax
from jax.experimental import pallas as pl
from jax.experimental.pallas import tpu as pltpu
from jax.sharding import Mesh
from jax.sharding import PartitionSpec as P

HD = 80
LANES = 128
SPLIT = (3, 4, 2, 4, 8)
AXES = ("zl", "x", "c", "zh", "y")
BF16 = jnp.bfloat16
F32 = jnp.float32


def core_swap(array):
    return lax.ppermute(array, "c", [(0, 1), (1, 0)])


def ring_x(array, step):
    count = lax.axis_size("x")
    return lax.ppermute(array, "x", [(i, (i + step) % count) for i in range(count)])


def exchange(array, axes):
    return lax.all_to_all(array, axes, split_axis=0, concat_axis=0, tiled=True)


def spread(array, axes):
    count = lax.axis_size(axes)
    return exchange(jnp.broadcast_to(array[None], (count,) + array.shape), axes)


def dot(a, b, dims):
    return lax.dot_general(a, b, (dims, ((), ())), preferred_element_type=F32)


def partner(array):
    quarter = HD // 4
    lane = lax.broadcasted_iota(jnp.int32, array.shape, 1)
    front = lax.rem(lane, 2 * quarter) < quarter
    ahead = pltpu.roll(array, LANES - quarter, 1)
    behind = pltpu.roll(array, quarter, 1)
    return jnp.where(front, -ahead, behind)


def head_kernel(
    patch_len,
    group,
    position,
    counts,
    order,
    weight_hbm,
    own_hbm,
    other_hbm,
    turned_hbm,
    cos_hbm,
    sin_hbm,
    values_hbm,
    upstream_hbm,
    context_ref,
    grad_ref,
    weight_ref,
    own_ref,
    other_ref,
    turned_ref,
    cos_ref,
    sin_ref,
    values_ref,
    upstream_ref,
    full_ref,
    proj_ref,
    dproj_ref,
    arrivals,
):
    rows = turned_ref.shape[1]
    windows = rows // patch_len
    head = order[position]
    strip, strips = weight_ref.shape[0], weight_ref.shape[1] // (2 * HD)
    moves = (
        (weight_hbm, weight_ref),
        (own_hbm, own_ref),
        (other_hbm, other_ref),
        (cos_hbm, cos_ref),
        (sin_hbm, sin_ref),
        (values_hbm.at[head], values_ref),
        (upstream_hbm.at[head], upstream_ref),
        (turned_hbm, turned_ref),
    )
    copies = [
        pltpu.make_async_copy(source, target, arrivals.at[at])
        for at, (source, target) in enumerate(moves)
    ]
    for copy in copies:
        copy.start()
    scale = 1.0 / math.sqrt(HD)
    full_ref[...] = jnp.zeros_like(full_ref)
    copies[0].wait()
    for z in range(strips):
        span, at = pl.ds(z * strip, strip), z * 2 * HD
        full_ref[span, pl.ds(0, HD)] = weight_ref[:, pl.ds(at, HD)]
        full_ref[span, pl.ds(LANES, HD)] = weight_ref[:, pl.ds(at + HD, HD)]
    half = rows // 2
    copies[1].wait()
    proj_ref[:half, :] = dot(own_ref[...], full_ref[...], ((1,), (0,)))
    copies[2].wait()
    proj_ref[half:, :] = dot(other_ref[...], full_ref[...], ((1,), (0,)))
    for copy in copies[3:7]:
        copy.wait()
    block = group * patch_len
    row_at = lax.broadcasted_iota(jnp.int32, (block, block), 0)
    key_at = lax.broadcasted_iota(jnp.int32, (block, block), 1)
    row_win, key_win = row_at // patch_len, key_at // patch_len
    row_one = lax.broadcasted_iota(jnp.int32, (block, 1), 0)
    same = row_win == key_win
    for start in range(0, windows, group * 3):
        firsts = [first for first in range(start, min(windows, start + group * 3), group)]
        spans = [pl.ds(first * patch_len, block) for first in firsts]
        each = range(len(firsts))
        masks, lives = [], []
        for first in firsts:
            key_count = jnp.full((block, block), counts[first], jnp.int32)
            row_count = jnp.full((block, 1), counts[first], jnp.int32)
            for later in range(1, group):
                count = counts[first + later]
                key_count = jnp.where(key_win == later, count, key_count)
                row_count = jnp.where(row_one // patch_len == later, count, row_count)
            masks.append(same & (key_at - key_win * patch_len < key_count))
            live = row_one - row_one // patch_len * patch_len < row_count
            lives.append(live.astype(F32))
        cosines, sines = [cos_ref[s, :] for s in spans], [sin_ref[s, :] for s in spans]
        q = [proj_ref[s, pl.ds(0, LANES)] for s in spans]
        k = [proj_ref[s, pl.ds(LANES, LANES)] for s in spans]
        q = [(q[i] * cosines[i] + partner(q[i]) * sines[i]).astype(BF16) for i in each]
        k = [(k[i] * cosines[i] + partner(k[i]) * sines[i]).astype(BF16) for i in each]
        scores = [dot(q[i], k[i], ((1,), (1,))) * scale for i in each]
        v = [values_ref[s, :] for s in spans]
        dprobs = [dot(upstream_ref[spans[i], :], v[i], ((1,), (1,))) for i in each]
        scores = [jnp.where(masks[i], scores[i], -1e30) for i in each]
        tops = [jnp.max(scores[i], axis=1, keepdims=True) for i in each]
        exps = [jnp.exp(scores[i] - tops[i]) for i in each]
        sums = [jnp.sum(exps[i], axis=1, keepdims=True) for i in each]
        probs = [exps[i] * (lives[i] / sums[i]) for i in each]
        context = [dot(probs[i].astype(BF16), v[i], ((1,), (0,))) for i in each]
        delta = [jnp.sum(probs[i] * dprobs[i], axis=1, keepdims=True) for i in each]
        dscores = [(probs[i] * (dprobs[i] - delta[i]) * scale).astype(BF16) for i in each]
        dquery = [dot(dscores[i], k[i], ((1,), (0,))) for i in each]
        dkey = [dot(dscores[i], q[i], ((0,), (0,))) for i in each]
        for i in each:
            context_ref[spans[i], :] = context[i].astype(BF16)
            back = dquery[i] * cosines[i] - partner(dquery[i]) * sines[i]
            dproj_ref[spans[i], pl.ds(0, LANES)] = back.astype(BF16)
            back = dkey[i] * cosines[i] - partner(dkey[i]) * sines[i]
            dproj_ref[spans[i], pl.ds(LANES, LANES)] = back.astype(BF16)
    copies[7].wait()
    for z in range(strips):
        at = z * 2 * HD
        part = dot(turned_ref[pl.ds(z * strip, strip), :], dproj_ref[...], ((1,), (0,)))
        part = part.astype(BF16)
        grad_ref[:, pl.ds(at, HD)] = part[:, :HD]
        grad_ref[:, pl.ds(at + HD, HD)] = part[:, LANES : LANES + HD]


def one_head(position, counts, order, weight, own, other, turned, tables, cotangents, patch_len):
    model_width, rows = turned.shape
    windows = rows // patch_len
    group = math.gcd(windows, max(1, 128 // patch_len))
    vmem = pl.BlockSpec(memory_space=pltpu.VMEM)
    smem = pl.BlockSpec(memory_space=pltpu.SMEM)
    return pl.pallas_call(
        functools.partial(head_kernel, patch_len, group, position),
        in_specs=[smem, smem] + [pl.BlockSpec(memory_space=pltpu.HBM)] * 8,
        out_specs=[vmem] * 2,
        out_shape=[
            jax.ShapeDtypeStruct((rows, LANES), BF16),
            jax.ShapeDtypeStruct(weight.shape, BF16),
        ],
        scratch_shapes=[
            pltpu.VMEM(weight.shape, BF16),
            pltpu.VMEM(own.shape, BF16),
            pltpu.VMEM(other.shape, BF16),
            pltpu.VMEM(turned.shape, BF16),
            pltpu.VMEM((rows, LANES), F32),
            pltpu.VMEM((rows, LANES), F32),
            pltpu.VMEM((rows, LANES), BF16),
            pltpu.VMEM((rows, LANES), BF16),
            pltpu.VMEM((model_width, 2 * LANES), BF16),
            pltpu.VMEM((rows, 2 * LANES), F32),
            pltpu.VMEM((rows, 2 * LANES), BF16),
            pltpu.SemaphoreType.DMA((8,)),
        ],
        compiler_params=pltpu.CompilerParams(vmem_limit_bytes=60 * 1024 * 1024),
        cost_estimate=pl.CostEstimate(
            flops=4_000_000_000, bytes_accessed=8_000_000, transcendentals=rows * 128
        ),
        name="one_head",
    )(counts, order, weight, own, other, turned, *tables, *cotangents)


def prepare_kernel(
    order,
    own_ref,
    other_ref,
    own_v_ref,
    other_v_ref,
    own_u_ref,
    other_u_ref,
    turned_ref,
    values_ref,
    upstream_ref,
):
    heads, rows = values_ref.shape[0], own_ref.shape[0]
    is_first = order[heads] == 0
    turned_ref[:, :rows] = jnp.transpose(own_ref[...])
    turned_ref[:, rows:] = jnp.transpose(other_ref[...])
    values_ref[...] = jnp.zeros_like(values_ref)
    upstream_ref[...] = jnp.zeros_like(upstream_ref)
    pairs = ((own_v_ref, other_v_ref, values_ref), (own_u_ref, other_u_ref, upstream_ref))
    for own, other, out in pairs:
        for at, source in ((0, own), (rows, other)):
            for head in range(heads):
                low = source[:, pl.ds(head * HD, HD)]
                high = source[:, pl.ds((heads + head) * HD, HD)]
                out[head, pl.ds(at, rows), pl.ds(0, HD)] = jnp.where(is_first, low, high)


def prepare(order, patches, values, upstream, heads):
    rows, model_width = patches[0].shape
    vmem = pl.BlockSpec(memory_space=pltpu.VMEM)
    smem = pl.BlockSpec(memory_space=pltpu.SMEM)
    spread_heads = jax.ShapeDtypeStruct((heads, 2 * rows, LANES), BF16)
    return pl.pallas_call(
        prepare_kernel,
        in_specs=[smem] + [vmem] * 6,
        out_specs=[vmem] * 3,
        out_shape=[
            jax.ShapeDtypeStruct((model_width, 2 * rows), BF16),
            spread_heads,
            spread_heads,
        ],
        compiler_params=pltpu.CompilerParams(vmem_limit_bytes=60 * 1024 * 1024),
        cost_estimate=pl.CostEstimate(flops=0, bytes_accessed=10_000_000, transcendentals=0),
        name="prepare",
    )(order, *patches, *values, *upstream)


def route_kernel(patch_len, dest, order, stack_ref, routed_ref):
    heads = stack_ref.shape[0]
    windows = stack_ref.shape[1] // patch_len // 2
    routed_ref[...] = jnp.zeros_like(routed_ref)
    for source in range(2):
        first = order[heads + source] * windows
        for window in range(windows):
            here = first + window
            rows = pl.ds(pl.multiple_of(here * patch_len, patch_len), patch_len)
            slot = dest[here]
            for head in range(heads):
                lanes = pl.ds((source * heads + head) * HD, HD)
                routed_ref[slot, :, lanes] = stack_ref[order[head], rows, :][:, :HD]


def route(dest, order, stack, slots, patch_len):
    heads = stack.shape[0]
    vmem = pl.BlockSpec(memory_space=pltpu.VMEM)
    smem = pl.BlockSpec(memory_space=pltpu.SMEM)
    return pl.pallas_call(
        functools.partial(route_kernel, patch_len),
        in_specs=[smem, smem, vmem],
        out_specs=vmem,
        out_shape=jax.ShapeDtypeStruct((slots, patch_len, 2 * heads * HD), BF16),
        compiler_params=pltpu.CompilerParams(vmem_limit_bytes=60 * 1024 * 1024),
        name="route",
    )(dest, order, stack)


def settle_kernel(arrived_ref, placed_ref):
    half = arrived_ref.shape[2] // 2
    for pair in range(0, arrived_ref.shape[0], 2):
        for source in range(2):
            lanes = pl.ds(source * half, half)
            for core in range(2):
                out = pl.ds(core * half, half)
                placed_ref[pair + source, :, out] = arrived_ref[pair + core, :, lanes]


def settle(arrived):
    vmem = pl.BlockSpec(memory_space=pltpu.VMEM)
    return pl.pallas_call(
        settle_kernel,
        in_specs=[vmem],
        out_specs=vmem,
        out_shape=jax.ShapeDtypeStruct(arrived.shape, BF16),
        compiler_params=pltpu.CompilerParams(vmem_limit_bytes=60 * 1024 * 1024),
        name="settle",
    )(arrived)


def rotary_tables(coords):
    quarter = HD // 4
    windows, _, patch_len = coords.shape
    lane = jnp.arange(LANES, dtype=jnp.int32)
    frequency = 10000.0 ** (-(lane % quarter).astype(F32) / quarter)
    position = coords.astype(F32)
    by_row = (lane < HD // 2)[None, None, :]
    position = jnp.where(by_row, position[:, 0, :, None], position[:, 1, :, None])
    angles = (position * frequency).reshape(windows * patch_len, LANES)
    used = (lane < HD)[None, :]
    return jnp.where(used, jnp.cos(angles), 0.0), jnp.where(used, jnp.sin(angles), 0.0)


def after(first, arrays):
    return lax.optimization_barrier((first, arrays))[1]


def per_device(patches, values, upstream, coords, counts, dest, weight):
    core, here = lax.axis_index("c"), lax.axis_index("x")
    nx, ny, nz = lax.axis_size("x"), lax.axis_size("y"), lax.axis_size("zh")
    slots = lax.axis_size(("zl", "x", "c"))
    window_count, patch_len, model_width = patches.shape
    value_width = values.shape[-1]
    row_total = window_count * patch_len
    depth = weight.shape[0]
    steps = [0, nx - 1, 1] + list(range(2, nx - 1))

    head = core * nx + here
    slice_q = lax.dynamic_slice_in_dim(weight, head * HD, HD, axis=1)
    slice_k = lax.dynamic_slice_in_dim(weight, value_width + head * HD, HD, axis=1)
    own_w = jnp.concatenate([slice_q, slice_k], axis=1)
    own_w = jnp.broadcast_to(own_w[None], (nz,) + own_w.shape)
    patches, values, upstream, coords, counts, dest = after(
        own_w, (patches, values, upstream, coords, counts, dest)
    )
    own_w = exchange(own_w, "zh")
    own_w = jnp.transpose(own_w, (1, 0, 2)).reshape(depth, nz * 2 * HD)
    own_w = spread(own_w, "y").reshape(ny * depth, nz * 2 * HD)

    patches = patches.reshape(row_total, model_width)
    values = values.reshape(row_total, value_width)
    upstream = upstream.reshape(row_total, value_width)
    other_patches = core_swap(patches)
    small = jnp.concatenate([coords.reshape(window_count, -1), counts[:, None], dest], axis=1)
    small = jnp.concatenate([small, core_swap(small)], axis=0)
    both_coords = small[:, : 2 * patch_len].reshape(2 * window_count, 2, patch_len)
    both_counts, both_dest = small[:, 2 * patch_len], small[:, 2 * patch_len + 1]
    tables = rotary_tables(both_coords)
    order = [lax.rem(here + step, nx) for step in steps]
    place = [jnp.int32(0)] * nx
    for at, head_at in enumerate(order):
        place = [jnp.where(head_at == h, at, place[h]) for h in range(nx)]
    place = jnp.stack(place + [core, 1 - core]).astype(jnp.int32)
    order = jnp.stack(order + [core]).astype(jnp.int32)
    turned, value_heads, upstream_heads = prepare(
        order,
        (patches, other_patches),
        (values, core_swap(values)),
        (upstream, core_swap(upstream)),
        nx,
    )

    own_w = after((turned, tables), own_w)
    weights = [own_w] + [ring_x(own_w, -step) for step in steps[1:]]
    contexts, grads = [], []
    for at, step in enumerate(steps):
        at_weight = weights[at]
        if at:
            at_weight = after((contexts[-1], grads[1 : at - 1]), at_weight)
        context, grad = one_head(
            at,
            both_counts,
            order,
            at_weight,
            patches,
            other_patches,
            turned,
            tables,
            (value_heads, upstream_heads),
            patch_len,
        )
        contexts.append(context)
        grads.append(ring_x(grad, step) if step else grad)

    stack = after(grads[:-1], jnp.stack(contexts))
    routed = route(both_dest, place, stack, slots, patch_len)
    arrived = exchange(routed, ("zl", "x", "c"))
    total = grads[0].astype(F32)
    for grad in grads[1:]:
        total = total + grad.astype(F32)
    total = after(arrived, total.astype(BF16))
    placed = settle(arrived)

    total = exchange(total.reshape(ny, depth, nz * 2 * HD), "y")
    total = jnp.sum(total.astype(F32), axis=0).astype(BF16)
    total = jnp.transpose(total.reshape(depth, nz, 2 * HD), (1, 0, 2))
    copies = lax.axis_size("zl")
    total = jnp.broadcast_to(total[None], (copies,) + total.shape)
    total = exchange(total.reshape(copies * nz, depth, 2 * HD), ("zl", "zh"))
    total = jnp.sum(total.astype(F32), axis=0).astype(BF16)
    total = spread(total, ("x", "c")).reshape(nx, 2, depth, 2, HD)
    grad_weight = jnp.transpose(total, (2, 3, 1, 0, 4)).reshape(depth, 2 * value_width)
    return (placed, grad_weight.astype(F32))


def solution(mesh):
    fine = Mesh(mesh.devices.reshape(SPLIT), AXES)
    return jax.shard_map(
        per_device,
        mesh=fine,
        in_specs=(
            P(AXES, None, None),
            P(AXES, None, None),
            P(AXES, None, None),
            P(AXES, None, None),
            P(AXES),
            P(AXES, None),
            P(("zh", "y"), None),
        ),
        out_specs=(P(AXES, None, None), P(("zh", "y"), None)),
        check_vma=False,
    )
```

time: 211 us -> 190 us (0.900)
  blocking collectives: 13.3 us -> 38.6 us
  local copies, waits for them, and re-layouts: 36.3 us -> 13.4 us
  waiting for transfers between devices: 38.4 us -> 25.2 us
  starting transfers between devices: 77.1 us -> 66.9 us
  Pallas kernels: 33.6 us -> 38.6 us
  other arithmetic: 9.03 us -> 5.03 us
    all_to_all x5 -> x4, waiting for transfers between devices: 38.4 us -> 6.85 us  [exchange(): return lax.all_to_all(array, axes, split_axis=0, concat_axis=0, tiled=True)]
    all_to_all x1 -> x2, blocking collectives: 13.3 us -> 38.6 us  [exchange(): return lax.all_to_all(array, axes, split_axis=0, concat_axis=0, tiled=True)]
    ppermute x6, waiting for transfers between devices: 0.02 us -> 18.4 us  [ring_x(): lax.ppermute(array, 'x', [(i, (i + step) % count) for i in range(count)])]
    dynamic_slice x11 -> x0, local copies, waits for them, and re-layouts: 12 us -> none  [the longest x9 9.88 us: head_major(): lax.dynamic_index_in_dim(both, at, axis=1, keepdims=False)]
    ppermute x4, starting transfers between devices: 18.9 us -> 9.09 us  [core_swap(): return lax.ppermute(array, 'c', [(0, 1), (1, 0)])]
    concatenate x3 -> x0, local copies, waits for them, and re-layouts: 6.02 us -> none  [the longest x1 3.97 us: per_device(): both = jnp.concatenate([flat, core_swap(flat)], axis=0)]
    unnamed x41 -> x26, local copies, waits for them, and re-layouts: 8.79 us -> 4.16 us
    pallas_call x4 -> x5, Pallas kernels: 30.5 us -> 33.6 us  [the longest x4 28.3 us: one_head(): pl.pallas_call(functools.partial(head_kernel, patch_len, group, position)...]
  transfers between devices with their start and end apart: 15 -> 14, of which waited for: 4 -> 3; matrix products, arithmetic and copies ran while one was open for 15% -> 5% of each run, Pallas kernels for 15% -> 19%
where the time goes in v4:
time: 190 us; the launch traced here: 189 us
  starting transfers between devices  66.9 us (35%)
  Pallas kernels  38.6 us (20%)
  blocking collectives  38.6 us (20%)
  waiting for transfers between devices  25.2 us (13%)
  local copies, waits for them, and re-layouts  13.4 us (7%)
  other arithmetic  5.03 us (3%)
    all_to_all x2, blocking collectives, exchange(): return lax.all_to_all(array, axes, split_axis=0, concat_axis=0, tiled=True)  38.6 us
    all_to_all x4, starting transfers between devices, exchange(): return lax.all_to_all(array, axes, split_axis=0, concat_axis=0, tiled=True)  37 us
    pallas_call x4, Pallas kernels, one_head(): pl.pallas_call(functools.partial(head_kernel, patch_len, group, position)...  28.3 us
    ppermute x6, starting transfers between devices, ring_x(): lax.ppermute(array, 'x', [(i, (i + step) % count) for i in range(count)])  20.8 us
    ppermute x6, waiting for transfers between devices, ring_x(): lax.ppermute(array, 'x', [(i, (i + step) % count) for i in range(count)])  18.4 us
    ppermute x4, starting transfers between devices, core_swap(): return lax.ppermute(array, 'c', [(0, 1), (1, 0)])  9.09 us
    all_to_all x4, waiting for transfers between devices, exchange(): return lax.all_to_all(array, axes, split_axis=0, concat_axis=0, tiled=True)  6.85 us
    pallas_call x1, Pallas kernels, prepare(): pl.pallas_call(prepare_kernel, in_specs=[smem] + [vmem] * 6, out_specs=[v...  5.35 us
  transfers between devices with their start and end apart: 14, of which 3 were waited for; matrix products, arithmetic and copies ran while one was open for 5% of the time, Pallas kernels for 19%

profile of v4, /device:TPU:1, one launch (start us, length us, event | category | flops | bytes accessed | tf_op | source)
XLA Modules:
  0.0 188.8 jit_solution(5543037359235573072)
XLA Ops:
  0.6 0.8 constant_dynamic-slice_fusion.1
  1.6 0.6 broadcast_in_dim.77
  2.2 15.0 %all-to-all-start = ((bf16[4,40,160]{2,1,0:T(8,128)(2,1)}), bf16[4,40,160]{2,1,0:T(8,128)(2,1)S(1)}, u32[]{:S(2)}, u32[]{:S(2)}) async-start(bf16[4,40,160]{2,1,0:T(8,128)(2,1)} %broadcast_in_dim.77), calls=%async_computation | async-start | bytes 163840 | tf_op jit(solution)/shard_map/all_to_all | solution.py:30
  17.2 2.9 %collective-permute-start.1 = (bf16[384,1280]{1,0:T(8,128)(2,1)}, bf16[384,1280]{1,0:T(8,128)(2,1)S(1)}, u32[]{:S(2)}, u32[]{:S(2)}) collective-permute-start(bf16[384,1280]{1,0:T(8,128)(2,1)} %bitcast.27), channel_id=1, source_target_pairs={{0,32},{32,0},{1,33},{33,1},{2,34},{34,2},{3,35},{35,3},{4,36},{36... | collective-permute-start | bytes 2949128 | tf_op jit(solution)/shard_map/ppermute | solution.py:21
  20.1 0.7 copy.34
  20.9 0.8 reshape.68
  21.6 0.7 copy.35
  22.5 1.9 %collective-permute-start = (s32[12,66]{1,0:T(8,128)S(1)}, s32[12,66]{1,0:T(8,128)S(1)}, u32[]{:S(2)}, u32[]{:S(2)}) collective-permute-start(s32[12,66]{1,0:T(8,128)S(1)} %pad_add_fusion.1), channel_id=1, source_target_pairs={{0,32},{32,0},{1,33},{33,1},{2,34},{34,2},{3,35},{35,3},{4,36},{36... | collective-permute-start | bytes 9512 | tf_op jit(solution)/shard_map/ppermute | solution.py:21
  24.4 2.4 %collective-permute-start.2 = (bf16[384,640]{1,0:T(8,128)(2,1)}, bf16[384,640]{1,0:T(8,128)(2,1)S(1)}, u32[]{:S(2)}, u32[]{:S(2)}) collective-permute-start(bf16[384,640]{1,0:T(8,128)(2,1)} %bitcast.33), channel_id=1, source_target_pairs={{0,32},{32,0},{1,33},{33,1},{2,34},{34,2},{3,35},{35,3},{4,36},{36... | collective-permute-start | bytes 1474568 | tf_op jit(solution)/shard_map/ppermute | solution.py:21
  26.8 1.9 %collective-permute-start.3 = (bf16[384,640]{1,0:T(8,128)(2,1)}, bf16[384,640]{1,0:T(8,128)(2,1)S(1)}, u32[]{:S(2)}, u32[]{:S(2)}) collective-permute-start(bf16[384,640]{1,0:T(8,128)(2,1)} %bitcast.35), channel_id=1, source_target_pairs={{0,32},{32,0},{1,33},{33,1},{2,34},{34,2},{3,35},{35,3},{4,36},{36... | collective-permute-start | bytes 1474568 | tf_op jit(solution)/shard_map/ppermute | solution.py:21
  28.9 0.8 broadcast_in_dim.87
  29.7 6.8 %all-to-all-start.1 = ((bf16[8,40,640]{2,1,0:T(8,128)(2,1)}), bf16[8,40,640]{2,1,0:T(8,128)(2,1)S(1)}, u32[]{:S(2)}, u32[]{:S(2)}) async-start(bf16[8,40,640]{2,1,0:T(8,128)(2,1)} %broadcast_in_dim.87), calls=%async_computation.1 | async-start | bytes 819200 | tf_op jit(solution)/shard_map/all_to_all | solution.py:30
  36.6 0.6 stack.63.order
  37.6 2.5 %sine_select_fusion = (f32[768,128]{1,0:T(8,128)}, f32[768,128]{1,0:T(8,128)}) fusion(f32[128]{0:T(128)S(1)} %fusion.3, f32[768]{0:T(1024)S(1)} %broadcast_in_dim.83, f32[768]{0:T(1024)S(1)} %broadcast_in_dim.81, pred[128]{0:T(512)(128)(4,1)S(1)} %get-tuple-element.56, pred[128]{0:T(512)(128)(4,1)S(1)} %get-tuple-element.57), kind=kLoop, calls=%fused_computation.2 | loop fusion | flops 393216 | bytes 793344 | tf_op jit(solution)/shard_map/jit(_where)/select_n | solution.py:312
  40.2 0.7 copy-done.2
  40.9 0.2 copy-done.3
  41.1 0.9 copy-done.1
  42.0 5.3 %prepare.1 = (bf16[1280,768]{1,0:T(8,128)(2,1)}, bf16[4,768,128]{2,1,0:T(8,128)(2,1)}, bf16[4,768,128]{2,1,0:T(8,128)(2,1)}) custom-call(s32[5]{0:T(128)} %stack.63.order, bf16[384,1280]{1,0:T(8,128)(2,1)} %bitcast.28, bf16[384,1280]{1,0:T(8,128)(2,1)} %copy-done.1, bf16[384,640]{1,0:T(8,128)(2,1)} %bitcast.34, bf16[384,640]{1,0:T(8,128)(2,1)} %copy-done.2, ...), custom_call_target="tpu_custom_call" | custom-call | bytes 10000000 | tf_op jit(solution)/shard_map/prepare/pallas_call | solution.py:236
  47.4 3.7 %all-to-all-done.1 = bf16[8,40,640]{2,1,0:T(8,128)(2,1)S(1)} async-done(((bf16[8,40,640]{2,1,0:T(8,128)(2,1)}), bf16[8,40,640]{2,1,0:T(8,128)(2,1)S(1)}, u32[]{:S(2)}, u32[]{:S(2)}) %all-to-all-start.1) | async-done | bytes 409632 | tf_op jit(solution)/shard_map/all_to_all | solution.py:30
  51.1 3.1 %collective-permute-start.4 = (bf16[320,640]{1,0:T(8,128)(2,1)S(1)}, bf16[320,640]{1,0:T(8,128)(2,1)S(1)}, u32[]{:S(2)}, u32[]{:S(2)}) collective-permute-start(bf16[320,640]{1,0:T(8,128)(2,1)S(1)} %bitcast.37), channel_id=1, source_target_pairs={{0,64},{64,128},{128,192},{192,0},{1,65},{65,129},{129,193},{193,1... | collective-permute-start | bytes 1228808 | tf_op jit(solution)/shard_map/ppermute | solution.py:26
  54.2 0.7 slice_reduce_fusion.2
  54.9 4.4 %collective-permute-start.8 = (bf16[320,640]{1,0:T(8,128)(2,1)S(1)}, bf16[320,640]{1,0:T(8,128)(2,1)S(1)}, u32[]{:S(2)}, u32[]{:S(2)}) collective-permute-start(bf16[320,640]{1,0:T(8,128)(2,1)S(1)} %bitcast.38), channel_id=1, source_target_pairs={{0,128},{64,192},{128,0},{192,64},{1,129},{65,193},{129,1},{193,65... | collective-permute-start | bytes 1228808 | tf_op jit(solution)/shard_map/ppermute | solution.py:26
  59.3 3.0 %collective-permute-start.6 = (bf16[320,640]{1,0:T(8,128)(2,1)S(1)}, bf16[320,640]{1,0:T(8,128)(2,1)S(1)}, u32[]{:S(2)}, u32[]{:S(2)}) collective-permute-start(bf16[320,640]{1,0:T(8,128)(2,1)S(1)} %bitcast.39), channel_id=1, source_target_pairs={{0,192},{64,0},{128,64},{192,128},{1,193},{65,1},{129,65},{193,129... | collective-permute-start | bytes 1228808 | tf_op jit(solution)/shard_map/ppermute | solution.py:26
  62.3 7.0 %one_head.4 = (bf16[768,128]{1,0:T(8,128)(2,1)}, bf16[320,640]{1,0:T(8,128)(2,1)}) custom-call(s32[24]{0:T(128)} %get-tuple-element.50.counts, s32[5]{0:T(128)} %stack.63.order, bf16[320,640]{1,0:T(8,128)(2,1)} %bitcast.40, bf16[384,1280]{1,0:T(8,128)(2,1)} %bitcast.29, bf16[384,1280]{1,0:T(8,128)(2,1)} %copy-done.1, ...), custom_call_target="tpu_custom_call" | custom-call | flops 4000000000 | bytes 8000000 | tf_op jit(solution)/shard_map/one_head/pallas_call | solution.py:174
  69.4 0.8 copy-done.12
  70.1 7.0 %one_head.5 = (bf16[768,128]{1,0:T(8,128)(2,1)}, bf16[320,640]{1,0:T(8,128)(2,1)}) custom-call(s32[24]{0:T(128)} %get-tuple-element.50.counts, s32[5]{0:T(128)} %stack.63.order, bf16[320,640]{1,0:T(8,128)(2,1)} %copy-done.12, bf16[384,1280]{1,0:T(8,128)(2,1)} %bitcast.30, bf16[384,1280]{1,0:T(8,128)(2,1)} %copy-done.1, ...), custom_call_target="tpu_custom_call" | custom-call | flops 4000000000 | bytes 8000000 | tf_op jit(solution)/shard_map/one_head/pallas_call | solution.py:174
  77.2 2.1 %collective-permute-start.5 = (bf16[320,640]{1,0:T(8,128)(2,1)}, bf16[320,640]{1,0:T(8,128)(2,1)S(1)}, u32[]{:S(2)}, u32[]{:S(2)}) collective-permute-start(bf16[320,640]{1,0:T(8,128)(2,1)} %get-tuple-element.38), channel_id=1, source_target_pairs={{0,192},{64,0},{128,64},{192,128},{1,193},{65,1},{129,65},{193,129... | collective-permute-start | bytes 1228808 | tf_op jit(solution)/shard_map/ppermute | solution.py:26
  79.4 0.7 stack.58.order
  80.0 0.8 copy-done.10
  80.8 7.1 %one_head.6 = (bf16[768,128]{1,0:T(8,128)(2,1)}, bf16[320,640]{1,0:T(8,128)(2,1)}) custom-call(s32[24]{0:T(128)} %get-tuple-element.50.counts, s32[5]{0:T(128)} %stack.63.order, bf16[320,640]{1,0:T(8,128)(2,1)} %copy-done.10, bf16[384,1280]{1,0:T(8,128)(2,1)} %bitcast.31, bf16[384,1280]{1,0:T(8,128)(2,1)} %copy-done.1, ...), custom_call_target="tpu_custom_call" | custom-call | flops 4000000000 | bytes 8000000 | tf_op jit(solution)/shard_map/one_head/pallas_call | solution.py:174
  87.8 3.4 %collective-permute-start.7 = (bf16[320,640]{1,0:T(8,128)(2,1)}, bf16[320,640]{1,0:T(8,128)(2,1)S(1)}, u32[]{:S(2)}, u32[]{:S(2)}) collective-permute-start(bf16[320,640]{1,0:T(8,128)(2,1)} %get-tuple-element.41), channel_id=1, source_target_pairs={{0,64},{64,128},{128,192},{192,0},{1,65},{65,129},{129,193},{193,1... | collective-permute-start | bytes 1228808 | tf_op jit(solution)/shard_map/ppermute | solution.py:26
  91.2 0.7 copy-done.9
  92.0 7.2 %one_head.7 = (bf16[768,128]{1,0:T(8,128)(2,1)}, bf16[320,640]{1,0:T(8,128)(2,1)}) custom-call(s32[24]{0:T(128)} %get-tuple-element.50.counts, s32[5]{0:T(128)} %stack.63.order, bf16[320,640]{1,0:T(8,128)(2,1)} %copy-done.9, bf16[384,1280]{1,0:T(8,128)(2,1)} %bitcast.32, bf16[384,1280]{1,0:T(8,128)(2,1)} %copy-done.1, ...), custom_call_target="tpu_custom_call" | custom-call | flops 4000000000 | bytes 8000000 | tf_op jit(solution)/shard_map/one_head/pallas_call | solution.py:174
  99.2 1.9 %pad_maximum_fusion.stack_ref = bf16[4,768,128]{2,1,0:T(8,128)(2,1)} fusion(bf16[1,768,128]{2,1,0:T(8,128)(2,1)} %bitcast.46, bf16[1,768,128]{2,1,0:T(8,128)(2,1)S(1)} %bitcast.45, bf16[1,768,128]{2,1,0:T(8,128)(2,1)S(1)} %bitcast.44, bf16[1,768,128]{2,1,0:T(8,128)(2,1)S(1)} %bitcast.43), kind=kLoop, calls=%fused_computation.1 | loop fusion | flops 1179648 | bytes 1572864 | tf_op jit(solution)/shard_map/stack | solution.py:386
  101.1 2.6 %route.1 = bf16[24,32,640]{2,1,0:T(8,128)(2,1)} custom-call(s32[24]{0:T(128)} %get-tuple-element.51.dest, s32[6]{0:T(128)} %stack.58.order, bf16[4,768,128]{2,1,0:T(8,128)(2,1)} %pad_maximum_fusion.stack_ref), custom_call_target="tpu_custom_call" | custom-call | tf_op jit(solution)/shard_map/route/pallas_call | solution.py:270
  103.7 6.7 %all-to-all-start.2 = ((bf16[24,32,640]{2,1,0:T(8,128)(2,1)}), bf16[24,32,640]{2,1,0:T(8,128)(2,1)S(1)}, u32[]{:S(2)}, u32[]{:S(2)}) async-start(bf16[24,32,640]{2,1,0:T(8,128)(2,1)} %route.1), calls=%async_computation.2 | async-start | bytes 1966080 | tf_op jit(solution)/shard_map/all_to_all | solution.py:30
  110.4 4.8 %collective-permute-start.9 = (bf16[320,640]{1,0:T(8,128)(2,1)S(1)}, bf16[320,640]{1,0:T(8,128)(2,1)S(1)}, u32[]{:S(2)}, u32[]{:S(2)}) collective-permute-start(bf16[320,640]{1,0:T(8,128)(2,1)S(1)} %copy-done.11), channel_id=1, source_target_pairs={{0,128},{64,192},{128,0},{192,64},{1,129},{65,193},{129,1},{193,65... | collective-permute-start | bytes 1228808 | tf_op jit(solution)/shard_map/ppermute | solution.py:26
  115.2 18.4 %collective-permute-done.9 = bf16[320,640]{1,0:T(8,128)(2,1)S(1)} collective-permute-done((bf16[320,640]{1,0:T(8,128)(2,1)S(1)}, bf16[320,640]{1,0:T(8,128)(2,1)S(1)}, u32[]{:S(2)}, u32[]{:S(2)}) %collective-permute-start.9) | collective-permute-done | bytes 409632 | tf_op jit(solution)/shard_map/ppermute | solution.py:26
  133.6 0.2 add_convert_fusion
  133.8 16.1 %all_to_all.30 = bf16[8,40,640]{2,1,0:T(8,128)(2,1)S(1)} all-to-all(bf16[8,40,640]{2,1,0:T(8,128)(2,1)S(1)} %bitcast.24), channel_id=1, replica_groups=mesh['zl'=3,'x'=4,'c'=2,'zh'=4,'y'=8] {'y'}, dimensions={0} | all-to-all | bytes 819200 | tf_op jit(solution)/shard_map/all_to_all | solution.py:30
  150.1 22.5 %all_to_all.31 = bf16[12,40,160]{2,1,0:T(8,128)(2,1)S(1)} all-to-all(bf16[12,40,160]{2,1,0:T(8,128)(2,1)S(1)} %bitcast.26), channel_id=1, replica_groups=mesh['zl'=3,'x'=4,'c'=2,'zh'=4,'y'=8] {'zl','zh'}, dimensions={0} | all-to-all | bytes 307200 | tf_op jit(solution)/shard_map/all_to_all | solution.py:30
  172.7 0.7 broadcast_in_dim.89
  173.3 8.4 %all-to-all-start.5 = ((bf16[8,40,160]{2,1,0:T(8,128)(2,1)}), bf16[8,40,160]{2,1,0:T(8,128)(2,1)S(1)}, u32[]{:S(2)}, u32[]{:S(2)}) async-start(bf16[8,40,160]{2,1,0:T(8,128)(2,1)} %broadcast_in_dim.89), calls=%async_computation.5 | async-start | bytes 327680 | tf_op jit(solution)/shard_map/all_to_all | solution.py:30
  181.8 2.4 %settle.1 = bf16[24,32,640]{2,1,0:T(8,128)(2,1)} custom-call(bf16[24,32,640]{2,1,0:T(8,128)(2,1)} %copy-done), custom_call_target="tpu_custom_call" | custom-call | tf_op jit(solution)/shard_map/settle/pallas_call | solution.py:292
  184.2 3.2 %all-to-all-done.5 = bf16[8,40,160]{2,1,0:T(8,128)(2,1)S(1)} async-done(((bf16[8,40,160]{2,1,0:T(8,128)(2,1)}), bf16[8,40,160]{2,1,0:T(8,128)(2,1)S(1)}, u32[]{:S(2)}, u32[]{:S(2)}) %all-to-all-start.5) | async-done | bytes 102432 | tf_op jit(solution)/shard_map/all_to_all | solution.py:30
  187.4 0.3 reshape.77
  187.6 0.2 copy.38
  187.8 1.0 reshape.76
  (48 shorter events, 1.0 us)
Async XLA Ops:
  2.2 26.5 %all-to-all-start = ((bf16[4,40,160]{2,1,0:T(8,128)(2,1)}), bf16[4,40,160]{2,1,0:T(8,128)(2,1)S(1)}, u32[]{:S(2)}, u32[]{:S(2)}) async-start(bf16[4,40,160]{2,1,0:T(8,128)(2,1)} %broadcast_in_dim.77), calls=%async_computation | async-start | bytes 163840 | tf_op jit(solution)/shard_map/all_to_all | solution.py:30
  17.2 22.9 %collective-permute-start.1 = (bf16[384,1280]{1,0:T(8,128)(2,1)}, bf16[384,1280]{1,0:T(8,128)(2,1)S(1)}, u32[]{:S(2)}, u32[]{:S(2)}) collective-permute-start(bf16[384,1280]{1,0:T(8,128)(2,1)} %bitcast.27), channel_id=1, source_target_pairs={{0,32},{32,0},{1,33},{33,1},{2,34},{34,2},{3,35},{35,3},{4,36},{36... | collective-permute-start | bytes 2949128 | tf_op jit(solution)/shard_map/ppermute | solution.py:21
  22.5 14.7 %collective-permute-start = (s32[12,66]{1,0:T(8,128)S(1)}, s32[12,66]{1,0:T(8,128)S(1)}, u32[]{:S(2)}, u32[]{:S(2)}) collective-permute-start(s32[12,66]{1,0:T(8,128)S(1)} %pad_add_fusion.1), channel_id=1, source_target_pairs={{0,32},{32,0},{1,33},{33,1},{2,34},{34,2},{3,35},{35,3},{4,36},{36... | collective-permute-start | bytes 9512 | tf_op jit(solution)/shard_map/ppermute | solution.py:21
  24.4 15.8 %collective-permute-start.2 = (bf16[384,640]{1,0:T(8,128)(2,1)}, bf16[384,640]{1,0:T(8,128)(2,1)S(1)}, u32[]{:S(2)}, u32[]{:S(2)}) collective-permute-start(bf16[384,640]{1,0:T(8,128)(2,1)} %bitcast.33), channel_id=1, source_target_pairs={{0,32},{32,0},{1,33},{33,1},{2,34},{34,2},{3,35},{35,3},{4,36},{36... | collective-permute-start | bytes 1474568 | tf_op jit(solution)/shard_map/ppermute | solution.py:21
  26.8 13.3 %collective-permute-start.3 = (bf16[384,640]{1,0:T(8,128)(2,1)}, bf16[384,640]{1,0:T(8,128)(2,1)S(1)}, u32[]{:S(2)}, u32[]{:S(2)}) collective-permute-start(bf16[384,640]{1,0:T(8,128)(2,1)} %bitcast.35), channel_id=1, source_target_pairs={{0,32},{32,0},{1,33},{33,1},{2,34},{34,2},{3,35},{35,3},{4,36},{36... | collective-permute-start | bytes 1474568 | tf_op jit(solution)/shard_map/ppermute | solution.py:21
  29.7 21.4 %all-to-all-start.1 = ((bf16[8,40,640]{2,1,0:T(8,128)(2,1)}), bf16[8,40,640]{2,1,0:T(8,128)(2,1)S(1)}, u32[]{:S(2)}, u32[]{:S(2)}) async-start(bf16[8,40,640]{2,1,0:T(8,128)(2,1)} %broadcast_in_dim.87), calls=%async_computation.1 | async-start | bytes 819200 | tf_op jit(solution)/shard_map/all_to_all | solution.py:30
  40.1 0.8 copy-start.2
  40.1 1.0 copy-start.3
  41.1 0.9 copy-start.1
  51.1 11.3 %copy-start.4 = (bf16[8,40,640]{2,1,0:T(8,128)(2,1)}, bf16[8,40,640]{2,1,0:T(8,128)(2,1)S(1)}, u32[]{:S(2)}) copy-start(bf16[8,40,640]{2,1,0:T(8,128)(2,1)S(1)} %all-to-all-done.1) | copy-start | bytes 1228804
  51.1 18.3 %collective-permute-start.4 = (bf16[320,640]{1,0:T(8,128)(2,1)S(1)}, bf16[320,640]{1,0:T(8,128)(2,1)S(1)}, u32[]{:S(2)}, u32[]{:S(2)}) collective-permute-start(bf16[320,640]{1,0:T(8,128)(2,1)S(1)} %bitcast.37), channel_id=1, source_target_pairs={{0,64},{64,128},{128,192},{192,0},{1,65},{65,129},{129,193},{193,1... | collective-permute-start | bytes 1228808 | tf_op jit(solution)/shard_map/ppermute | solution.py:26
  54.9 36.3 %collective-permute-start.8 = (bf16[320,640]{1,0:T(8,128)(2,1)S(1)}, bf16[320,640]{1,0:T(8,128)(2,1)S(1)}, u32[]{:S(2)}, u32[]{:S(2)}) collective-permute-start(bf16[320,640]{1,0:T(8,128)(2,1)S(1)} %bitcast.38), channel_id=1, source_target_pairs={{0,128},{64,192},{128,0},{192,64},{1,129},{65,193},{129,1},{193,65... | collective-permute-start | bytes 1228808 | tf_op jit(solution)/shard_map/ppermute | solution.py:26
  59.3 20.7 %collective-permute-start.6 = (bf16[320,640]{1,0:T(8,128)(2,1)S(1)}, bf16[320,640]{1,0:T(8,128)(2,1)S(1)}, u32[]{:S(2)}, u32[]{:S(2)}) collective-permute-start(bf16[320,640]{1,0:T(8,128)(2,1)S(1)} %bitcast.39), channel_id=1, source_target_pairs={{0,192},{64,0},{128,64},{192,128},{1,193},{65,1},{129,65},{193,129... | collective-permute-start | bytes 1228808 | tf_op jit(solution)/shard_map/ppermute | solution.py:26
  69.4 0.8 copy-start.12
  77.2 14.0 %collective-permute-start.5 = (bf16[320,640]{1,0:T(8,128)(2,1)}, bf16[320,640]{1,0:T(8,128)(2,1)S(1)}, u32[]{:S(2)}, u32[]{:S(2)}) collective-permute-start(bf16[320,640]{1,0:T(8,128)(2,1)} %get-tuple-element.38), channel_id=1, source_target_pairs={{0,192},{64,0},{128,64},{192,128},{1,193},{65,1},{129,65},{193,129... | collective-permute-start | bytes 1228808 | tf_op jit(solution)/shard_map/ppermute | solution.py:26
  80.0 0.8 copy-start.10
  87.8 13.3 %collective-permute-start.7 = (bf16[320,640]{1,0:T(8,128)(2,1)}, bf16[320,640]{1,0:T(8,128)(2,1)S(1)}, u32[]{:S(2)}, u32[]{:S(2)}) collective-permute-start(bf16[320,640]{1,0:T(8,128)(2,1)} %get-tuple-element.41), channel_id=1, source_target_pairs={{0,64},{64,128},{128,192},{192,0},{1,65},{65,129},{129,193},{193,1... | collective-permute-start | bytes 1228808 | tf_op jit(solution)/shard_map/ppermute | solution.py:26
  91.2 0.8 copy-start.9
  92.0 7.2 %copy-start.6 = (bf16[768,128]{1,0:T(8,128)(2,1)S(1)}, bf16[768,128]{1,0:T(8,128)(2,1)}, u32[]{:S(2)}) copy-start(bf16[768,128]{1,0:T(8,128)(2,1)} %get-tuple-element.36) | copy-start | bytes 589828
  92.0 7.2 %copy-start.7 = (bf16[768,128]{1,0:T(8,128)(2,1)S(1)}, bf16[768,128]{1,0:T(8,128)(2,1)}, u32[]{:S(2)}) copy-start(bf16[768,128]{1,0:T(8,128)(2,1)} %get-tuple-element.39) | copy-start | bytes 589828
  92.0 7.2 %copy-start.8 = (bf16[768,128]{1,0:T(8,128)(2,1)S(1)}, bf16[768,128]{1,0:T(8,128)(2,1)}, u32[]{:S(2)}) copy-start(bf16[768,128]{1,0:T(8,128)(2,1)} %get-tuple-element.42) | copy-start | bytes 589828
  101.1 9.3 %copy-start.11 = (bf16[320,640]{1,0:T(8,128)(2,1)S(1)}, bf16[320,640]{1,0:T(8,128)(2,1)}, u32[]{:S(2)}) copy-start(bf16[320,640]{1,0:T(8,128)(2,1)} %get-tuple-element.46) | copy-start | bytes 1228804
  101.1 32.5 %copy-start.5 = (bf16[320,640]{1,0:T(8,128)(2,1)S(1)}, bf16[320,640]{1,0:T(8,128)(2,1)}, u32[]{:S(2)}) copy-start(bf16[320,640]{1,0:T(8,128)(2,1)} %get-tuple-element.35) | copy-start | bytes 1228804
  103.7 30.1 %all-to-all-start.2 = ((bf16[24,32,640]{2,1,0:T(8,128)(2,1)}), bf16[24,32,640]{2,1,0:T(8,128)(2,1)S(1)}, u32[]{:S(2)}, u32[]{:S(2)}) async-start(bf16[24,32,640]{2,1,0:T(8,128)(2,1)} %route.1), calls=%async_computation.2 | async-start | bytes 1966080 | tf_op jit(solution)/shard_map/all_to_all | solution.py:30
  110.4 23.2 %collective-permute-start.9 = (bf16[320,640]{1,0:T(8,128)(2,1)S(1)}, bf16[320,640]{1,0:T(8,128)(2,1)S(1)}, u32[]{:S(2)}, u32[]{:S(2)}) collective-permute-start(bf16[320,640]{1,0:T(8,128)(2,1)S(1)} %copy-done.11), channel_id=1, source_target_pairs={{0,128},{64,192},{128,0},{192,64},{1,129},{65,193},{129,1},{193,65... | collective-permute-start | bytes 1228808 | tf_op jit(solution)/shard_map/ppermute | solution.py:26
  133.8 48.0 %copy-start = (bf16[24,32,640]{2,1,0:T(8,128)(2,1)}, bf16[24,32,640]{2,1,0:T(8,128)(2,1)S(1)}, u32[]{:S(2)}) copy-start(bf16[24,32,640]{2,1,0:T(8,128)(2,1)S(1)} %all-to-all-done.2.arrived_ref) | copy-start | bytes 2949124
  173.3 14.0 %all-to-all-start.5 = ((bf16[8,40,160]{2,1,0:T(8,128)(2,1)}), bf16[8,40,160]{2,1,0:T(8,128)(2,1)S(1)}, u32[]{:S(2)}, u32[]{:S(2)}) async-start(bf16[8,40,160]{2,1,0:T(8,128)(2,1)} %broadcast_in_dim.89), calls=%async_computation.5 | async-start | bytes 327680 | tf_op jit(solution)/shard_map/all_to_all | solution.py:30

commit v5 on v3

v5 whole, which is shorter than its diff:
```python
import functools
import math

import jax
import jax.numpy as jnp
from jax import lax
from jax.experimental import pallas as pl
from jax.experimental.pallas import tpu as pltpu
from jax.sharding import Mesh
from jax.sharding import PartitionSpec as P

HD = 80
LANES = 128
POSITIONS = 32
EXTRA = 16
SPLIT = (3, 4, 2, 4, 8)
AXES = ("zl", "x", "c", "zh", "y")
GROUP = ("x", "c")
PEERS = ("zl", "x", "c")
BF16 = jnp.bfloat16
F32 = jnp.float32
VMEM_BYTES = 60 * 1024 * 1024


def exchange(array, axes):
    return lax.all_to_all(array, axes, split_axis=0, concat_axis=0, tiled=True)


def spread(array, axes):
    count = lax.axis_size(axes)
    return exchange(jnp.broadcast_to(array[None], (count,) + array.shape), axes)


def after(first, arrays):
    return lax.optimization_barrier((first, arrays))[1]


def dot(a, b, dims):
    return lax.dot_general(a, b, (dims, ((), ())), preferred_element_type=F32)


def head_of(place, cores, heads):
    return place % cores * (heads // cores) + place // cores


def partner(array):
    quarter = HD // 4
    lane = lax.broadcasted_iota(jnp.int32, array.shape, 1)
    front = lax.rem(lane, 2 * quarter) < quarter
    ahead = pltpu.roll(array, LANES - quarter, 1)
    behind = pltpu.roll(array, quarter, 1)
    return jnp.where(front, -ahead, behind)


def pack_kernel(cores, values_ref, upstream_ref, notes_ref, packed_ref):
    heads, rows = packed_ref.shape[0], values_ref.shape[0]
    parts = packed_ref.shape[2] // (2 * HD)
    depth = rows // parts
    for place in range(heads):
        lanes = pl.ds(head_of(place, cores, heads) * HD, HD)
        for part in range(parts):
            span, at = pl.ds(part * depth, depth), part * 2 * HD
            packed_ref[place, :depth, pl.ds(at, HD)] = values_ref[span, lanes]
            packed_ref[place, :depth, pl.ds(at + HD, HD)] = upstream_ref[span, lanes]
        packed_ref[place, depth:, :] = notes_ref[...]


def pack(values, upstream, notes, heads, cores):
    rows, width = values.shape
    parts = width // (2 * HD)
    vmem = pl.BlockSpec(memory_space=pltpu.VMEM)
    return pl.pallas_call(
        functools.partial(pack_kernel, cores),
        in_specs=[vmem] * 3,
        out_specs=vmem,
        out_shape=jax.ShapeDtypeStruct((heads, rows // parts + EXTRA, width), BF16),
        compiler_params=pltpu.CompilerParams(vmem_limit_bytes=VMEM_BYTES),
        name="pack",
    )(values, upstream, notes)


def head_kernel(
    patch_len,
    group,
    weight_ref,
    table_ref,
    patches_ref,
    packed_ref,
    context_ref,
    grad_ref,
    full_ref,
    sum_ref,
    dproj_ref,
    values_ref,
    upstream_ref,
):
    step = pl.program_id(0)
    rows = patches_ref.shape[1]
    block = group * patch_len
    strip, strips = weight_ref.shape[0], weight_ref.shape[1] // (2 * HD)
    scale = 1.0 / math.sqrt(HD)

    @pl.when(step == 0)
    def _():
        full_ref[...] = jnp.zeros_like(full_ref)
        sum_ref[...] = jnp.zeros_like(sum_ref)
        values_ref[...] = jnp.zeros_like(values_ref)
        upstream_ref[...] = jnp.zeros_like(upstream_ref)
        for z in range(strips):
            span, at = pl.ds(z * strip, strip), z * 2 * HD
            full_ref[span, pl.ds(0, HD)] = weight_ref[:, pl.ds(at, HD)]
            full_ref[span, pl.ds(LANES, HD)] = weight_ref[:, pl.ds(at + HD, HD)]

    depth = packed_ref.shape[1] - EXTRA
    for part in range(rows // depth):
        span, at = pl.ds(part * depth, depth), part * 2 * HD
        values_ref[span, pl.ds(0, HD)] = packed_ref[0, :depth, pl.ds(at, HD)]
        upstream_ref[span, pl.ds(0, HD)] = packed_ref[0, :depth, pl.ds(at + HD, HD)]
    notes = packed_ref[0, depth:, :rows].astype(F32)
    live_keys = notes[2:3, :]
    kind = lax.broadcasted_iota(jnp.int32, (3 * POSITIONS, rows), 0)
    wanted = lax.rem(kind, POSITIONS).astype(F32)
    row_at, col_at = notes[0:1, :], notes[1:2, :]
    by_row = jnp.where(row_at == wanted, 1.0, 0.0)
    by_col = jnp.where(col_at == wanted, 1.0, 0.0)
    chosen = jnp.where(kind < POSITIONS, by_row, jnp.where(kind < 2 * POSITIONS, by_col, live_keys))
    chosen = chosen.astype(BF16)
    tables = dot(chosen, table_ref[0], ((0,), (0,)))
    tables += dot(chosen, table_ref[1], ((0,), (0,)))
    tables += dot(chosen, table_ref[2], ((0,), (0,)))

    proj = dot(patches_ref[0], full_ref[...], ((1,), (0,)))
    row_win = lax.broadcasted_iota(jnp.int32, (block, block), 0) // patch_len
    key_win = lax.broadcasted_iota(jnp.int32, (block, block), 1) // patch_len
    same = row_win == key_win
    starts = list(range(0, rows, block))
    each = range(len(starts))
    cosines = [tables[s : s + block, :LANES] for s in starts]
    sines = [tables[s : s + block, LANES:] for s in starts]
    masks = [same & (live_keys[:, s : s + block] > 0.5) for s in starts]
    lives = [cosine[:, HD : HD + 1] for cosine in cosines]
    q = [proj[s : s + block, :LANES] for s in starts]
    k = [proj[s : s + block, LANES:] for s in starts]
    q = [(q[i] * cosines[i] + partner(q[i]) * sines[i]).astype(BF16) for i in each]
    k = [(k[i] * cosines[i] + partner(k[i]) * sines[i]).astype(BF16) for i in each]
    scores = [dot(q[i], k[i], ((1,), (1,))) * scale for i in each]
    v = [values_ref[s : s + block, :] for s in starts]
    dprobs = [dot(upstream_ref[s : s + block, :], v[i], ((1,), (1,))) for i, s in enumerate(starts)]
    scores = [jnp.where(masks[i], scores[i], -1e30) for i in each]
    tops = [jnp.max(scores[i], axis=1, keepdims=True) for i in each]
    exps = [jnp.exp(scores[i] - tops[i]) for i in each]
    sums = [jnp.sum(exps[i], axis=1, keepdims=True) for i in each]
    probs = [exps[i] * (lives[i] / sums[i]) for i in each]
    context = [dot(probs[i].astype(BF16), v[i], ((1,), (0,))) for i in each]
    delta = [jnp.sum(probs[i] * dprobs[i], axis=1, keepdims=True) for i in each]
    dscores = [(probs[i] * (dprobs[i] - delta[i]) * scale).astype(BF16) for i in each]
    dquery = [dot(dscores[i], k[i], ((1,), (0,))) for i in each]
    dkey = [dot(dscores[i], q[i], ((0,), (0,))) for i in each]
    for i, s in enumerate(starts):
        span = pl.ds(s, block)
        context_ref[span, :] = context[i].astype(BF16)
        back = dquery[i] * cosines[i] - partner(dquery[i]) * sines[i]
        dproj_ref[span, pl.ds(0, LANES)] = back.astype(BF16)
        back = dkey[i] * cosines[i] - partner(dkey[i]) * sines[i]
        dproj_ref[span, pl.ds(LANES, LANES)] = back.astype(BF16)
    sum_ref[...] += dot(dproj_ref[...], patches_ref[0], ((0,), (0,)))

    @pl.when(step == pl.num_programs(0) - 1)
    def _():
        for z in range(strips):
            at = z * 2 * HD
            part = jnp.transpose(sum_ref[:, z * strip : (z + 1) * strip]).astype(BF16)
            grad_ref[:, pl.ds(at, HD)] = part[:, :HD]
            grad_ref[:, pl.ds(at + HD, HD)] = part[:, LANES : LANES + HD]


def one_head(weight, table, patches, packed, patch_len):
    sources, rows, model_width = patches.shape
    group = math.gcd(rows // patch_len, max(1, 128 // patch_len))
    return pl.pallas_call(
        functools.partial(head_kernel, patch_len, group),
        grid=(sources,),
        in_specs=[
            pl.BlockSpec(weight.shape, lambda s: (0, 0)),
            pl.BlockSpec(table.shape, lambda s: (0, 0, 0)),
            pl.BlockSpec((1, rows, model_width), lambda s: (s, 0, 0)),
            pl.BlockSpec((1,) + packed.shape[1:], lambda s: (s, 0, 0)),
        ],
        out_specs=[
            pl.BlockSpec((rows, LANES), lambda s: (s, 0)),
            pl.BlockSpec(weight.shape, lambda s: (0, 0)),
        ],
        out_shape=[
            jax.ShapeDtypeStruct((sources * rows, LANES), BF16),
            jax.ShapeDtypeStruct(weight.shape, BF16),
        ],
        scratch_shapes=[
            pltpu.VMEM((model_width, 2 * LANES), BF16),
            pltpu.VMEM((2 * LANES, model_width), F32),
            pltpu.VMEM((rows, 2 * LANES), BF16),
            pltpu.VMEM((rows, LANES), BF16),
            pltpu.VMEM((rows, LANES), BF16),
        ],
        compiler_params=pltpu.CompilerParams(vmem_limit_bytes=VMEM_BYTES),
        cost_estimate=pl.CostEstimate(
            flops=20_000_000_000, bytes_accessed=12_000_000, transcendentals=3_000_000
        ),
        name="one_head",
    )(weight, table, patches, packed)


def route_kernel(patch_len, dest, context_ref, routed_ref):
    routed_ref[...] = jnp.zeros_like(routed_ref)
    sources = routed_ref.shape[2] // HD
    windows = context_ref.shape[0] // patch_len // sources
    for source in range(sources):
        for window in range(windows):
            at = source * windows + window
            rows = context_ref[pl.ds(at * patch_len, patch_len), :]
            routed_ref[dest[at], :patch_len, pl.ds(source * HD, HD)] = rows[:, :HD]


def route(dest, context, slots, patch_len, chunk, sources):
    vmem = pl.BlockSpec(memory_space=pltpu.VMEM)
    return pl.pallas_call(
        functools.partial(route_kernel, patch_len),
        in_specs=[pl.BlockSpec(memory_space=pltpu.SMEM), vmem],
        out_specs=vmem,
        out_shape=jax.ShapeDtypeStruct((slots, patch_len + chunk, sources * HD), BF16),
        compiler_params=pltpu.CompilerParams(vmem_limit_bytes=VMEM_BYTES),
        name="route",
    )(dest, context)


def fold_kernel(parts_ref, folded_ref):
    total = parts_ref[0].astype(F32)
    for at in range(1, parts_ref.shape[0]):
        total += parts_ref[at].astype(F32)
    total = total.astype(BF16)
    depth, width = total.shape
    folded_ref[...] = jnp.zeros_like(folded_ref)
    chunk = folded_ref.shape[1]
    for at in range(0, depth, chunk):
        count = min(chunk, depth - at)
        lanes = pl.ds(at // chunk * width, width)
        folded_ref[:, :count, lanes] = jnp.broadcast_to(
            total[at : at + count][None], (folded_ref.shape[0], count, width)
        )


def fold(parts, slots, chunk, width):
    vmem = pl.BlockSpec(memory_space=pltpu.VMEM)
    return pl.pallas_call(
        fold_kernel,
        in_specs=[vmem],
        out_specs=vmem,
        out_shape=jax.ShapeDtypeStruct((slots, chunk, width), BF16),
        compiler_params=pltpu.CompilerParams(vmem_limit_bytes=VMEM_BYTES),
        name="fold",
    )(parts)


def settle_kernel(cores, patch_len, arrived_ref, placed_ref, grad_ref):
    heads = arrived_ref.shape[2] // HD
    copies = arrived_ref.shape[0] // heads
    depth, chunk = grad_ref.shape[0], arrived_ref.shape[1] - patch_len
    for place in range(heads):
        head = head_of(place, cores, heads)
        out = pl.ds(head * HD, HD)
        for copy in range(copies):
            for source in range(heads):
                rows = arrived_ref[copy * heads + place, :patch_len, pl.ds(source * HD, HD)]
                placed_ref[copy * heads + source, :, out] = rows
        total = arrived_ref[place, patch_len:, :].astype(F32)
        for copy in range(1, copies):
            total += arrived_ref[copy * heads + place, patch_len:, :].astype(F32)
        for at in range(0, depth, chunk):
            count = min(chunk, depth - at)
            lanes = at // chunk * 2 * HD
            span = pl.ds(at, count)
            grad_ref[span, out] = total[:count, lanes : lanes + HD]
            other = pl.ds((heads + head) * HD, HD)
            grad_ref[span, other] = total[:count, lanes + HD : lanes + 2 * HD]


def settle(arrived, patch_len, depth, cores):
    slots, _, width = arrived.shape
    vmem = pl.BlockSpec(memory_space=pltpu.VMEM)
    return pl.pallas_call(
        functools.partial(settle_kernel, cores, patch_len),
        in_specs=[vmem],
        out_specs=[vmem, vmem],
        out_shape=[
            jax.ShapeDtypeStruct((slots, patch_len, width), BF16),
            jax.ShapeDtypeStruct((depth, 2 * width), F32),
        ],
        compiler_params=pltpu.CompilerParams(vmem_limit_bytes=VMEM_BYTES),
        name="settle",
    )(arrived)


def rotary_table():
    quarter = HD // 4
    lane = jnp.arange(LANES, dtype=jnp.int32)[None, :]
    kind = jnp.arange(3 * POSITIONS, dtype=jnp.int32)[:, None]
    frequency = 10000.0 ** (-(lane % quarter).astype(F32) / quarter)
    angles = (kind % POSITIONS).astype(F32) * frequency
    by_row = (kind < POSITIONS) & (lane < HD // 2)
    by_col = (kind >= POSITIONS) & (kind < 2 * POSITIONS) & (lane >= HD // 2) & (lane < HD)
    used = by_row | by_col
    flag = (kind == 2 * POSITIONS) & (lane == HD)
    cosine = jnp.where(used, jnp.cos(angles), jnp.where(flag, 1.0, 0.0))
    left = jnp.concatenate([cosine, jnp.where(used, jnp.sin(angles), 0.0)], axis=1)
    terms = []
    for _ in range(3):
        term = lax.reduce_precision(left, 8, 7)
        terms.append(term.astype(BF16))
        left = left - term
    return jnp.stack(terms)


def per_device(patches, values, upstream, coords, counts, dest, weight):
    core, here = lax.axis_index("c"), lax.axis_index("x")
    nx, nc = lax.axis_size("x"), lax.axis_size("c")
    ny, nz = lax.axis_size("y"), lax.axis_size("zh")
    heads = nx * nc
    slots = lax.axis_size(PEERS)
    window_count, patch_len, model_width = patches.shape
    value_width = values.shape[-1]
    row_total = window_count * patch_len
    depth = weight.shape[0]
    chunk = -(-depth * 2 * HD // value_width)
    chunk = -(-chunk // EXTRA) * EXTRA

    gathered = lax.all_gather(patches.reshape(row_total, model_width), GROUP, axis=0)
    head = core * nx + here
    slice_q = lax.dynamic_slice_in_dim(weight, head * HD, HD, axis=1)
    slice_k = lax.dynamic_slice_in_dim(weight, value_width + head * HD, HD, axis=1)
    own_w = jnp.concatenate([slice_q, slice_k], axis=1)
    own_w = jnp.broadcast_to(own_w[None], (nz,) + own_w.shape)
    values, upstream, coords, counts, dest = after(
        own_w, (values, upstream, coords, counts, dest)
    )
    own_w = exchange(own_w, "zh")
    own_w = jnp.transpose(own_w, (1, 0, 2)).reshape(depth, nz * 2 * HD)
    own_w = spread(own_w, "y").reshape(ny * depth, nz * 2 * HD)

    live = jnp.arange(patch_len, dtype=jnp.int32)[None, :] < counts[:, None]
    notes = jnp.stack(
        [
            coords[:, 0, :].reshape(row_total),
            coords[:, 1, :].reshape(row_total),
            live.astype(jnp.int32).reshape(row_total),
            jnp.pad(dest[:, 0], (0, row_total - window_count)),
        ]
    )
    notes = jnp.pad(notes, ((0, EXTRA - 4), (0, value_width - row_total))).astype(BF16)
    values = values.reshape(row_total, value_width)
    upstream = upstream.reshape(row_total, value_width)
    packed = exchange(pack(values, upstream, notes, heads, nc), GROUP)
    all_dest = packed[:, packed.shape[1] - EXTRA + 3, :window_count]
    all_dest = all_dest.astype(jnp.int32).reshape(heads * window_count)

    context, grad = one_head(own_w, rotary_table(), gathered, packed, patch_len)
    routed = route(all_dest, context, slots, patch_len, chunk, heads)

    grad = exchange(grad.reshape(ny, depth, nz * 2 * HD), "y")
    grad = jnp.sum(grad.astype(F32), axis=0).astype(BF16)
    grad = jnp.transpose(grad.reshape(depth, nz, 2 * HD), (1, 0, 2))
    folded = fold(exchange(grad, "zh"), slots, chunk, value_width)
    routed = lax.dynamic_update_slice(routed, folded, (0, patch_len, 0))
    arrived = exchange(routed, PEERS)
    return tuple(settle(arrived, patch_len, depth, nc))


def solution(mesh):
    fine = Mesh(mesh.devices.reshape(SPLIT), AXES)
    return jax.shard_map(
        per_device,
        mesh=fine,
        in_specs=(
            P(AXES, None, None),
            P(AXES, None, None),
            P(AXES, None, None),
            P(AXES, None, None),
            P(AXES),
            P(AXES, None),
            P(("zh", "y"), None),
        ),
        out_specs=(P(AXES, None, None), P(("zh", "y"), None)),
        check_vma=False,
    )
```

time: 211 us -> 198 us (0.938)
  blocking collectives: 13.3 us -> 52.9 us
  starting transfers between devices: 77.1 us -> 42 us
  local copies, waits for them, and re-layouts: 36.3 us -> 7.73 us
  between operations: 1.19 us -> 14.2 us
  other arithmetic: 9.03 us -> 2.6 us
  waiting for transfers between devices: 38.4 us -> 44.5 us
    all_to_all x1 -> x2, blocking collectives: 13.3 us -> 52.9 us  [exchange(): return lax.all_to_all(array, axes, split_axis=0, concat_axis=0, tiled=True)]
    ppermute x10 -> x0, starting transfers between devices: 37.4 us -> none  [the longest x4 18.9 us: core_swap(): return lax.ppermute(array, 'c', [(0, 1), (1, 0)])]
    dynamic_slice x11 -> x0, local copies, waits for them, and re-layouts: 12 us -> none  [the longest x9 9.88 us: head_major(): lax.dynamic_index_in_dim(both, at, axis=1, keepdims=False)]
    unnamed x41 -> x12, local copies, waits for them, and re-layouts: 8.79 us -> 1.72 us
    concatenate x3 -> x0, local copies, waits for them, and re-layouts: 6.02 us -> none  [the longest x1 3.97 us: per_device(): both = jnp.concatenate([flat, core_swap(flat)], axis=0)]
    all_to_all x5 -> x4, waiting for transfers between devices: 38.4 us -> 43.8 us  [exchange(): return lax.all_to_all(array, axes, split_axis=0, concat_axis=0, tiled=True)]
    transpose x1 -> x0, other arithmetic: 3.02 us -> none  [per_device(): turned = jnp.transpose(both)]
    all_to_all x5 -> x4, starting transfers between devices: 39.7 us -> 42 us  [exchange(): return lax.all_to_all(array, axes, split_axis=0, concat_axis=0, tiled=True)]
  transfers between devices with their start and end apart: 15 -> 5, of which waited for: 4 -> 4; matrix products, arithmetic and copies ran while one was open for 15% -> 3% of each run, Pallas kernels for 15% -> 3%
where the time goes in v5:
time: 198 us; the launch traced here: 197 us
  blocking collectives  52.9 us (27%)
  waiting for transfers between devices  44.5 us (22%)
  starting transfers between devices  42 us (21%)
  Pallas kernels  32.8 us (17%)
  between operations  14.2 us (7%)
  local copies, waits for them, and re-layouts  7.73 us (4%)
  other arithmetic  2.6 us (1%)
    all_to_all x2, blocking collectives, exchange(): return lax.all_to_all(array, axes, split_axis=0, concat_axis=0, tiled=True)  52.9 us
    all_to_all x4, waiting for transfers between devices, exchange(): return lax.all_to_all(array, axes, split_axis=0, concat_axis=0, tiled=True)  43.8 us
    all_to_all x4, starting transfers between devices, exchange(): return lax.all_to_all(array, axes, split_axis=0, concat_axis=0, tiled=True)  42 us
    pallas_call x1, Pallas kernels, one_head(): pl.pallas_call(functools.partial(head_kernel, patch_len, group), grid=(so...  22 us
  transfers between devices with their start and end apart: 5, of which 4 were waited for; matrix products, arithmetic and copies ran while one was open for 3% of the time, Pallas kernels for 3%

profile of v5, /device:TPU:1, one launch (start us, length us, event | category | flops | bytes accessed | tf_op | source)
XLA Modules:
  0.0 196.7 jit_solution(12303334707263521378)
XLA Ops:
  7.2 0.0 all-gather.2.cloned.1.call-start
  7.2 0.0 copy-start.5
  7.2 0.0 copy-start.4
  7.2 0.0 copy-start.3
  7.2 0.7 all-gather.2.cloned.1.call-update
  7.9 0.8 constant_dynamic-slice_fusion.1
  8.7 0.1 pad_maximum_fusion.2
  8.8 0.6 broadcast_in_dim.15
  9.5 15.0 %all-to-all-start.1 = ((bf16[4,40,160]{2,1,0:T(8,128)(2,1)}), bf16[4,40,160]{2,1,0:T(8,128)(2,1)S(1)}, u32[]{:S(2)}, u32[]{:S(2)}) async-start(bf16[4,40,160]{2,1,0:T(8,128)(2,1)} %broadcast_in_dim.15), calls=%async_computation.1 | async-start | bytes 163840 | tf_op jit(solution)/shard_map/all_to_all | solution.py:26
  24.5 9.6 %all-to-all-done.1 = bf16[4,40,160]{2,1,0:T(8,128)(2,1)S(1)} async-done(((bf16[4,40,160]{2,1,0:T(8,128)(2,1)}), bf16[4,40,160]{2,1,0:T(8,128)(2,1)S(1)}, u32[]{:S(2)}, u32[]{:S(2)}) %all-to-all-start.1) | async-done | bytes 51232 | tf_op jit(solution)/shard_map/all_to_all | solution.py:26
  34.1 0.1 broadcast_in_dim.28
  34.2 0.8 broadcast_in_dim.29
  35.0 6.8 %all-to-all-start.2 = ((bf16[8,40,640]{2,1,0:T(8,128)(2,1)}), bf16[8,40,640]{2,1,0:T(8,128)(2,1)S(1)}, u32[]{:S(2)}, u32[]{:S(2)}) async-start(bf16[8,40,640]{2,1,0:T(8,128)(2,1)} %broadcast_in_dim.29), calls=%async_computation.2 | async-start | bytes 819200 | tf_op jit(solution)/shard_map/all_to_all | solution.py:26
  41.8 0.0 copy-done.5
  41.9 0.0 copy-done.4
  41.9 0.1 convert_convert_fusion
  42.0 0.1 reshape.678
  42.1 0.0 copy-done.3
  42.1 0.1 stack_reshape_squeeze.8
  42.2 0.1 stack_reshape_squeeze.9
  42.3 0.6 fusion.14.notes_ref
  42.9 3.0 %pack.1 = bf16[8,112,640]{2,1,0:T(8,128)(2,1)} custom-call(bf16[384,640]{1,0:T(8,128)(2,1)} %bitcast.16, bf16[384,640]{1,0:T(8,128)(2,1)} %bitcast.17, bf16[16,640]{1,0:T(8,128)(2,1)} %fusion.14.notes_ref), custom_call_target="tpu_custom_call" | custom-call | tf_op jit(solution)/shard_map/pack/pallas_call | solution.py:72
  46.0 7.6 %all-to-all-done.2 = bf16[8,40,640]{2,1,0:T(8,128)(2,1)S(1)} async-done(((bf16[8,40,640]{2,1,0:T(8,128)(2,1)}), bf16[8,40,640]{2,1,0:T(8,128)(2,1)S(1)}, u32[]{:S(2)}, u32[]{:S(2)}) %all-to-all-start.2) | async-done | bytes 409632 | tf_op jit(solution)/shard_map/all_to_all | solution.py:26
  53.6 0.0 copy-start.1
  53.6 8.5 %all-to-all-start = ((bf16[8,112,640]{2,1,0:T(8,128)(2,1)}), bf16[8,112,640]{2,1,0:T(8,128)(2,1)S(1)}, u32[]{:S(2)}, u32[]{:S(2)}) async-start(bf16[8,112,640]{2,1,0:T(8,128)(2,1)} %pack.1), calls=%async_computation | async-start | bytes 2293760 | tf_op jit(solution)/shard_map/all_to_all | solution.py:26
  62.2 0.3 fusion.3
  62.5 0.7 pad_maximum_fusion.table_ref
  63.2 0.0 copy-done.1
  63.2 21.2 %all-to-all-done.packed_ref = bf16[8,112,640]{2,1,0:T(8,128)(2,1)S(1)} async-done(((bf16[8,112,640]{2,1,0:T(8,128)(2,1)}), bf16[8,112,640]{2,1,0:T(8,128)(2,1)S(1)}, u32[]{:S(2)}, u32[]{:S(2)}) %all-to-all-start) | async-done | bytes 1146912 | tf_op jit(solution)/shard_map/all_to_all | solution.py:26
  84.4 0.0 copy-start
  84.4 0.0 all-gather.2.cloned.1.call-done.patches_ref
  84.4 1.1 copy-done
  85.5 22.0 %one_head.1 = (bf16[3072,128]{1,0:T(8,128)(2,1)}, bf16[320,640]{1,0:T(8,128)(2,1)}) custom-call(bf16[320,640]{1,0:T(8,128)(2,1)} %bitcast.18, bf16[3,96,256]{2,1,0:T(8,128)(2,1)} %pad_maximum_fusion.table_ref, bf16[8,384,1280]{2,1,0:T(8,128)(2,1)} %all-gather.2.cloned.1.call-done.patches_ref, bf16[8,112,640]{2,1,0:T(8,128)(2,1)} %copy-done), custom_call_target="tpu_custom_call" | custom-call | flops 20000000000 | bytes 12000000 | tf_op jit(solution)/shard_map/one_head/pallas_call | solution.py:180
  107.5 20.1 %all_to_all.30 = bf16[8,40,640]{2,1,0:T(8,128)(2,1)S(1)} all-to-all(bf16[8,40,640]{2,1,0:T(8,128)(2,1)} %bitcast.19), channel_id=1, replica_groups=mesh['zl'=3,'x'=4,'c'=2,'zh'=4,'y'=8] {'y'}, dimensions={0} | all-to-all | bytes 819200 | tf_op jit(solution)/shard_map/all_to_all | solution.py:26
  127.6 0.1 reduce_sum.12
  127.7 0.1 reshape.675
  127.8 0.6 copy.14
  128.4 11.5 %all-to-all-start.4 = ((bf16[4,40,160]{2,1,0:T(8,128)(2,1)}), bf16[4,40,160]{2,1,0:T(8,128)(2,1)S(1)}, u32[]{:S(2)}, u32[]{:S(2)}) async-start(bf16[4,40,160]{2,1,0:T(8,128)(2,1)} %bitcast.14), calls=%async_computation.4 | async-start | bytes 163840 | tf_op jit(solution)/shard_map/all_to_all | solution.py:26
  140.0 0.7 fusion.18
  140.7 0.6 reshape.677.dest
  141.3 2.8 %route.1 = bf16[24,48,640]{2,1,0:T(8,128)(2,1)} custom-call(s32[96]{0:T(128)} %reshape.677.dest, bf16[3072,128]{1,0:T(8,128)(2,1)} %get-tuple-element.14.context_ref), custom_call_target="tpu_custom_call" | custom-call | tf_op jit(solution)/shard_map/route/pallas_call | solution.py:225
  144.1 5.4 %all-to-all-done.4.parts_ref = bf16[4,40,160]{2,1,0:T(8,128)(2,1)S(1)} async-done(((bf16[4,40,160]{2,1,0:T(8,128)(2,1)}), bf16[4,40,160]{2,1,0:T(8,128)(2,1)S(1)}, u32[]{:S(2)}, u32[]{:S(2)}) %all-to-all-start.4) | async-done | bytes 51232 | tf_op jit(solution)/shard_map/all_to_all | solution.py:26
  149.5 0.0 copy-start.2
  149.5 0.6 copy-done.2
  150.1 1.8 fold.1
  151.9 1.9 constant_dynamic-update-slice_fusion
  153.8 32.8 %all_to_all.31.arrived_ref = bf16[24,48,640]{2,1,0:T(8,128)(2,1)} all-to-all(bf16[24,48,640]{2,1,0:T(8,128)(2,1)} %constant_dynamic-update-slice_fusion), channel_id=1, replica_groups=mesh['zl'=3,'x'=4,'c'=2,'zh'=4,'y'=8] {'zl','x','c'}, dimensions={0} | all-to-all | bytes 2949120 | tf_op jit(solution)/shard_map/all_to_all | solution.py:26
  186.6 3.3 %settle.1 = (bf16[24,32,640]{2,1,0:T(8,128)(2,1)}, f32[40,1280]{1,0:T(8,128)}) custom-call(bf16[24,48,640]{2,1,0:T(8,128)(2,1)} %all_to_all.31.arrived_ref), custom_call_target="tpu_custom_call" | custom-call | tf_op jit(solution)/shard_map/settle/pallas_call | solution.py:289
  (13 shorter events, 0.2 us)
Async XLA Ops:
  7.2 77.3 %all-gather.2.cloned.1.call-start = ((), (), s32[]{:S(2)}) async-start(), calls=%async_computation.6 | async-start | bytes 8847360 | tf_op jit(solution)/shard_map/all_gather | solution.py:335
  7.2 34.6 %copy-start.5 = (s32[12,1]{0,1:T(1,128)S(1)}, s32[12,1]{0,1:T(1,128)}, u32[]{:S(2)}) copy-start(s32[12,1]{0,1:T(1,128)} %param.12) | copy-start | bytes 148
  7.2 34.7 %copy-start.4 = (s32[12]{0:T(128)S(1)}, s32[12]{0:T(128)}, u32[]{:S(2)}) copy-start(s32[12]{0:T(128)} %param.11) | copy-start | bytes 148
  7.2 34.8 %copy-start.3 = (s32[12,2,32]{2,1,0:T(2,128)S(1)}, s32[12,2,32]{2,1,0:T(2,128)}, u32[]{:S(2)}) copy-start(s32[12,2,32]{2,1,0:T(2,128)} %param.10) | copy-start | bytes 9220
  9.5 24.6 %all-to-all-start.1 = ((bf16[4,40,160]{2,1,0:T(8,128)(2,1)}), bf16[4,40,160]{2,1,0:T(8,128)(2,1)S(1)}, u32[]{:S(2)}, u32[]{:S(2)}) async-start(bf16[4,40,160]{2,1,0:T(8,128)(2,1)} %broadcast_in_dim.15), calls=%async_computation.1 | async-start | bytes 163840 | tf_op jit(solution)/shard_map/all_to_all | solution.py:26
  35.0 18.6 %all-to-all-start.2 = ((bf16[8,40,640]{2,1,0:T(8,128)(2,1)}), bf16[8,40,640]{2,1,0:T(8,128)(2,1)S(1)}, u32[]{:S(2)}, u32[]{:S(2)}) async-start(bf16[8,40,640]{2,1,0:T(8,128)(2,1)} %broadcast_in_dim.29), calls=%async_computation.2 | async-start | bytes 819200 | tf_op jit(solution)/shard_map/all_to_all | solution.py:26
  53.6 9.6 %copy-start.1 = (bf16[8,40,640]{2,1,0:T(8,128)(2,1)}, bf16[8,40,640]{2,1,0:T(8,128)(2,1)S(1)}, u32[]{:S(2)}) copy-start(bf16[8,40,640]{2,1,0:T(8,128)(2,1)S(1)} %all-to-all-done.2) | copy-start | bytes 1228804
  53.6 30.8 %all-to-all-start = ((bf16[8,112,640]{2,1,0:T(8,128)(2,1)}), bf16[8,112,640]{2,1,0:T(8,128)(2,1)S(1)}, u32[]{:S(2)}, u32[]{:S(2)}) async-start(bf16[8,112,640]{2,1,0:T(8,128)(2,1)} %pack.1), calls=%async_computation | async-start | bytes 2293760 | tf_op jit(solution)/shard_map/all_to_all | solution.py:26
  84.4 1.1 copy-start
  128.4 21.1 %all-to-all-start.4 = ((bf16[4,40,160]{2,1,0:T(8,128)(2,1)}), bf16[4,40,160]{2,1,0:T(8,128)(2,1)S(1)}, u32[]{:S(2)}, u32[]{:S(2)}) async-start(bf16[4,40,160]{2,1,0:T(8,128)(2,1)} %bitcast.14), calls=%async_computation.4 | async-start | bytes 163840 | tf_op jit(solution)/shard_map/all_to_all | solution.py:26
  149.5 0.6 copy-start.2
Sparse Core Ops, SparseCore 0:
  10.4 71.8 all-gather.1

commit v6 on v5

v6 whole, which is shorter than its diff:
```python
import functools
import math

import jax
import jax.numpy as jnp
from jax import lax
from jax.experimental import pallas as pl
from jax.experimental.pallas import tpu as pltpu
from jax.sharding import Mesh
from jax.sharding import PartitionSpec as P

HD = 80
LANES = 128
POSITIONS = 32
EXTRA = 16
SPLIT = (3, 4, 2, 4, 8)
AXES = ("zl", "x", "c", "zh", "y")
PEERS = ("zl", "x", "c")
BF16 = jnp.bfloat16
F32 = jnp.float32
VMEM_BYTES = 60 * 1024 * 1024


def core_swap(array):
    return lax.ppermute(array, "c", [(0, 1), (1, 0)])


def ring_x(array, step):
    count = lax.axis_size("x")
    if step == 0:
        return array
    return lax.ppermute(array, "x", [(i, (i + step) % count) for i in range(count)])


def exchange(array, axes):
    return lax.all_to_all(array, axes, split_axis=0, concat_axis=0, tiled=True)


def spread(array, axes):
    count = lax.axis_size(axes)
    return exchange(jnp.broadcast_to(array[None], (count,) + array.shape), axes)


def after(first, arrays):
    return lax.optimization_barrier((first, arrays))[1]


def dot(a, b, dims):
    return lax.dot_general(a, b, (dims, ((), ())), preferred_element_type=F32)


def head_of(place, cores, heads):
    return place % cores * (heads // cores) + place // cores


def partner(array):
    quarter = HD // 4
    lane = lax.broadcasted_iota(jnp.int32, array.shape, 1)
    front = lax.rem(lane, 2 * quarter) < quarter
    ahead = pltpu.roll(array, LANES - quarter, 1)
    behind = pltpu.roll(array, quarter, 1)
    return jnp.where(front, -ahead, behind)


def ring_steps(count):
    return [0, count - 1, 1] + list(range(2, count - 1))


def pack_kernel(where, values_ref, upstream_ref, notes_ref, *packed_refs):
    count = len(packed_refs)
    steps = ring_steps(count)
    rows, width = values_ref.shape
    parts = width // (2 * HD)
    depth = rows // parts
    kinds = width // HD // count
    for here in range(count):

        @pl.when(where[0] == here)
        def _():
            for packed_ref, step in zip(packed_refs, steps):
                for kind in range(kinds):
                    head = kind * count + (here + step) % count
                    lanes = pl.ds(head * HD, HD)
                    for part in range(parts):
                        span, at = pl.ds(part * depth, depth), part * 2 * HD
                        out = pl.ds(kind * depth, depth)
                        packed_ref[out, pl.ds(at, HD)] = values_ref[span, lanes]
                        packed_ref[out, pl.ds(at + HD, HD)] = upstream_ref[span, lanes]

    for packed_ref in packed_refs:
        packed_ref[kinds * depth :, :] = notes_ref[...]


def pack(where, values, upstream, notes, count):
    rows, width = values.shape
    parts = width // (2 * HD)
    kinds = width // HD // count
    vmem = pl.BlockSpec(memory_space=pltpu.VMEM)
    piece = jax.ShapeDtypeStruct((kinds * rows // parts + EXTRA, width), BF16)
    return pl.pallas_call(
        pack_kernel,
        in_specs=[pl.BlockSpec(memory_space=pltpu.SMEM)] + [vmem] * 3,
        out_specs=[vmem] * count,
        out_shape=[piece] * count,
        compiler_params=pltpu.CompilerParams(vmem_limit_bytes=VMEM_BYTES),
        name="pack",
    )(where, values, upstream, notes)


def heads_kernel(patch_len, group, sources, first, last, where, own_hbm, other_hbm, *refs):
    refs = list(refs)
    take = lambda count: [refs.pop(0) for _ in range(count)]
    table_hbm = take(1)[0]
    patches_hbm, packed_hbm = take(sources), take(sources)
    total_hbm = [] if first else take(1)
    context_refs = take(sources)
    results = take(2 if last else 1)
    own_ref, other_ref, table_ref = take(3)
    patches_refs, packed_refs = take(sources), take(sources)
    full_ref, sum_ref, dproj_ref, values_ref, upstream_ref, arrivals = take(6)
    moves = [(own_hbm, own_ref), (other_hbm, other_ref), (table_hbm, table_ref)]
    for at in range(sources):
        moves.append((patches_hbm[at], patches_refs[at]))
        moves.append((packed_hbm[at], packed_refs[at]))
    if not first:
        moves.append((total_hbm[0], sum_ref))
    copies = [
        pltpu.make_async_copy(source, target, arrivals.at[at])
        for at, (source, target) in enumerate(moves)
    ]
    for copy in copies:
        copy.start()
    strip, strips = own_ref.shape[0], own_ref.shape[1] // (2 * HD)
    rows = patches_refs[0].shape[0]
    block = group * patch_len
    scale = 1.0 / math.sqrt(HD)
    full_ref[...] = jnp.zeros_like(full_ref)
    values_ref[...] = jnp.zeros_like(values_ref)
    upstream_ref[...] = jnp.zeros_like(upstream_ref)
    is_first = where[1] == 0
    copies[0].wait()
    copies[1].wait()
    for z in range(strips):
        span = pl.ds(z * strip, strip)
        for part in range(2):
            lanes = pl.ds((2 * z + part) * HD, HD)
            own, other = own_ref[:, lanes], other_ref[:, lanes]
            full_ref[span, pl.ds(part * LANES, HD)] = jnp.where(is_first, own, other)
            full_ref[span, pl.ds((2 + part) * LANES, HD)] = jnp.where(is_first, other, own)
    copies[2].wait()
    row_win = lax.broadcasted_iota(jnp.int32, (block, block), 0) // patch_len
    key_win = lax.broadcasted_iota(jnp.int32, (block, block), 1) // patch_len
    same = row_win == key_win
    kind = lax.broadcasted_iota(jnp.int32, (3 * POSITIONS, rows), 0)
    wanted = lax.rem(kind, POSITIONS).astype(F32)
    starts = [at for at in range(0, rows, block)]
    chains = [(head, at) for head in range(2) for at in range(len(starts))]
    each = range(len(chains))
    for source in range(sources):
        patches_ref, packed_ref = patches_refs[source], packed_refs[source]
        copies[3 + 2 * source].wait()
        proj = dot(patches_ref[...], full_ref[...], ((1,), (0,)))
        copies[4 + 2 * source].wait()
        depth = (packed_ref.shape[0] - EXTRA) // 2
        notes = packed_ref[2 * depth :, :rows].astype(F32)
        live_keys = notes[2:3, :]
        by_row = jnp.where(notes[0:1, :] == wanted, 1.0, 0.0)
        by_col = jnp.where(notes[1:2, :] == wanted, 1.0, 0.0)
        chosen = jnp.where(kind < 2 * POSITIONS, by_col, live_keys)
        chosen = jnp.where(kind < POSITIONS, by_row, chosen).astype(BF16)
        tables = dot(chosen, table_ref[0], ((0,), (0,)))
        tables += dot(chosen, table_ref[1], ((0,), (0,)))
        tables += dot(chosen, table_ref[2], ((0,), (0,)))
        for head in range(2):
            out, come = pl.ds(head * LANES, HD), pl.ds(head * depth, depth)
            for part in range(rows // depth):
                span, at = pl.ds(part * depth, depth), part * 2 * HD
                values_ref[span, out] = packed_ref[come, pl.ds(at, HD)]
                upstream_ref[span, out] = packed_ref[come, pl.ds(at + HD, HD)]
        cosines = [tables[s : s + block, :LANES] for s in starts]
        sines = [tables[s : s + block, LANES:] for s in starts]
        masks = [same & (live_keys[:, s : s + block] > 0.5) for s in starts]
        lives = [cosine[:, HD : HD + 1] for cosine in cosines]
        spans = [pl.ds(starts[at], block) for _, at in chains]
        lanes = [pl.ds(head * LANES, LANES) for head, _ in chains]
        blocks = [at for _, at in chains]
        q = [proj[starts[at] : starts[at] + block, 2 * h * LANES :][:, :LANES] for h, at in chains]
        k = [
            proj[starts[at] : starts[at] + block, (2 * h + 1) * LANES :][:, :LANES]
            for h, at in chains
        ]
        turn = lambda x, at: x * cosines[at] + partner(x) * sines[at]
        q = [turn(q[i], blocks[i]).astype(BF16) for i in each]
        k = [turn(k[i], blocks[i]).astype(BF16) for i in each]
        scores = [dot(q[i], k[i], ((1,), (1,))) * scale for i in each]
        v = [values_ref[spans[i], lanes[i]] for i in each]
        dprobs = [dot(upstream_ref[spans[i], lanes[i]], v[i], ((1,), (1,))) for i in each]
        scores = [jnp.where(masks[blocks[i]], scores[i], -1e30) for i in each]
        tops = [jnp.max(scores[i], axis=1, keepdims=True) for i in each]
        exps = [jnp.exp(scores[i] - tops[i]) for i in each]
        sums = [jnp.sum(exps[i], axis=1, keepdims=True) for i in each]
        probs = [exps[i] * (lives[blocks[i]] / sums[i]) for i in each]
        context = [dot(probs[i].astype(BF16), v[i], ((1,), (0,))) for i in each]
        delta = [jnp.sum(probs[i] * dprobs[i], axis=1, keepdims=True) for i in each]
        dscores = [(probs[i] * (dprobs[i] - delta[i]) * scale).astype(BF16) for i in each]
        dquery = [dot(dscores[i], k[i], ((1,), (0,))) for i in each]
        dkey = [dot(dscores[i], q[i], ((0,), (0,))) for i in each]
        back = lambda x, at: (x * cosines[at] - partner(x) * sines[at]).astype(BF16)
        for i in each:
            context_refs[source][spans[i], lanes[i]] = context[i].astype(BF16)
            at = 2 * chains[i][0] * LANES
            dproj_ref[spans[i], pl.ds(at, LANES)] = back(dquery[i], blocks[i])
            dproj_ref[spans[i], pl.ds(at + LANES, LANES)] = back(dkey[i], blocks[i])
        grown = dot(dproj_ref[...], patches_ref[...], ((0,), (0,)))
        if first and source == 0:
            sum_ref[...] = grown
        else:
            if source == 0:
                copies[-1].wait()
            sum_ref[...] += grown
    if not last:
        results[0][...] = sum_ref[...]
        return
    for z in range(strips):
        part = jnp.transpose(sum_ref[:, z * strip : (z + 1) * strip]).astype(BF16)
        for at in range(2):
            low = part[:, at * LANES : at * LANES + HD]
            high = part[:, (2 + at) * LANES : (2 + at) * LANES + HD]
            lanes = pl.ds((2 * z + at) * HD, HD)
            results[0][:, lanes] = jnp.where(is_first, low, high)
            results[1][:, lanes] = jnp.where(is_first, high, low)


def some_heads(where, weights, table, patches, packed, total, last, patch_len):
    sources = len(patches)
    rows, model_width = patches[0].shape
    group = math.gcd(rows // patch_len, max(1, 128 // patch_len))
    vmem = pl.BlockSpec(memory_space=pltpu.VMEM)
    hbm = pl.BlockSpec(memory_space=pltpu.HBM)
    carried = [] if total is None else [total]
    sum_shape = jax.ShapeDtypeStruct((4 * LANES, model_width), F32)
    grad_shape = jax.ShapeDtypeStruct(weights[0].shape, BF16)
    results = [grad_shape] * 2 if last else [sum_shape]
    moves = 3 + 2 * sources + len(carried)
    return pl.pallas_call(
        functools.partial(heads_kernel, patch_len, group, sources, total is None, last),
        in_specs=[pl.BlockSpec(memory_space=pltpu.SMEM)] + [hbm] * moves,
        out_specs=[vmem] * (sources + len(results)),
        out_shape=[jax.ShapeDtypeStruct((rows, 2 * LANES), BF16)] * sources + results,
        scratch_shapes=[pltpu.VMEM(weights[0].shape, BF16)] * 2
        + [pltpu.VMEM(table.shape, BF16)]
        + [pltpu.VMEM(patches[0].shape, BF16)] * sources
        + [pltpu.VMEM(packed[0].shape, BF16)] * sources
        + [
            pltpu.VMEM((model_width, 4 * LANES), BF16),
            pltpu.VMEM(sum_shape.shape, F32),
            pltpu.VMEM((rows, 4 * LANES), BF16),
            pltpu.VMEM((rows, 2 * LANES), BF16),
            pltpu.VMEM((rows, 2 * LANES), BF16),
            pltpu.SemaphoreType.DMA((moves,)),
        ],
        compiler_params=pltpu.CompilerParams(vmem_limit_bytes=VMEM_BYTES),
        cost_estimate=pl.CostEstimate(
            flops=5_000_000_000 * sources,
            bytes_accessed=3_000_000 * sources,
            transcendentals=800_000 * sources,
        ),
        name="heads",
    )(where, *weights, table, *patches, *packed, *carried)


def route_kernel(patch_len, dest, *refs):
    context_refs, routed_ref = refs[:-1], refs[-1]
    routed_ref[...] = jnp.zeros_like(routed_ref)
    windows = context_refs[0].shape[0] // patch_len
    for source, context_ref in enumerate(context_refs):
        for window in range(windows):
            slot = dest[source * windows + window]
            rows = context_ref[pl.ds(window * patch_len, patch_len), :]
            for head in range(2):
                lanes = pl.ds((2 * source + head) * HD, HD)
                routed_ref[slot, :patch_len, lanes] = rows[:, head * LANES : head * LANES + HD]


def route(dest, contexts, slots, patch_len, chunk):
    vmem = pl.BlockSpec(memory_space=pltpu.VMEM)
    width = 2 * HD * len(contexts)
    return pl.pallas_call(
        functools.partial(route_kernel, patch_len),
        in_specs=[pl.BlockSpec(memory_space=pltpu.SMEM)] + [vmem] * len(contexts),
        out_specs=vmem,
        out_shape=jax.ShapeDtypeStruct((slots, patch_len + chunk, width), BF16),
        compiler_params=pltpu.CompilerParams(vmem_limit_bytes=VMEM_BYTES),
        name="route",
    )(dest, *contexts)


def fold_kernel(parts_ref, folded_ref):
    total = parts_ref[0].astype(F32)
    for at in range(1, parts_ref.shape[0]):
        total += parts_ref[at].astype(F32)
    total = total.astype(BF16)
    depth, width = total.shape
    folded_ref[...] = jnp.zeros_like(folded_ref)
    chunk = folded_ref.shape[1]
    for at in range(0, depth, chunk):
        count = min(chunk, depth - at)
        lanes = pl.ds(at // chunk * width, width)
        folded_ref[:, :count, lanes] = jnp.broadcast_to(
            total[at : at + count][None], (folded_ref.shape[0], count, width)
        )


def fold(parts, slots, chunk, width):
    vmem = pl.BlockSpec(memory_space=pltpu.VMEM)
    return pl.pallas_call(
        fold_kernel,
        in_specs=[vmem],
        out_specs=vmem,
        out_shape=jax.ShapeDtypeStruct((slots, chunk, width), BF16),
        compiler_params=pltpu.CompilerParams(vmem_limit_bytes=VMEM_BYTES),
        name="fold",
    )(parts)


def settle_kernel(cores, patch_len, arrived_ref, placed_ref, grad_ref):
    heads = arrived_ref.shape[2] // HD
    copies = arrived_ref.shape[0] // heads
    depth, chunk = grad_ref.shape[0], arrived_ref.shape[1] - patch_len
    for place in range(heads):
        head = head_of(place, cores, heads)
        out = pl.ds(head * HD, HD)
        count = heads // cores
        here, core = place // cores, place % cores
        for copy in range(copies):
            for at, step in enumerate(ring_steps(count)):
                source = copy * heads + (here - step) % count * cores + core
                for kind in range(cores):
                    lanes = pl.ds((cores * at + kind) * HD, HD)
                    rows = arrived_ref[copy * heads + place, :patch_len, lanes]
                    placed_ref[source, :, pl.ds((kind * count + here) * HD, HD)] = rows
        total = arrived_ref[place, patch_len:, :].astype(F32)
        for copy in range(1, copies):
            total += arrived_ref[copy * heads + place, patch_len:, :].astype(F32)
        for at in range(0, depth, chunk):
            count = min(chunk, depth - at)
            lanes = at // chunk * 2 * HD
            span = pl.ds(at, count)
            grad_ref[span, out] = total[:count, lanes : lanes + HD]
            other = pl.ds((heads + head) * HD, HD)
            grad_ref[span, other] = total[:count, lanes + HD : lanes + 2 * HD]


def settle(arrived, patch_len, depth, cores):
    slots, _, width = arrived.shape
    vmem = pl.BlockSpec(memory_space=pltpu.VMEM)
    return pl.pallas_call(
        functools.partial(settle_kernel, cores, patch_len),
        in_specs=[vmem],
        out_specs=[vmem, vmem],
        out_shape=[
            jax.ShapeDtypeStruct((slots, patch_len, width), BF16),
            jax.ShapeDtypeStruct((depth, 2 * width), F32),
        ],
        compiler_params=pltpu.CompilerParams(vmem_limit_bytes=VMEM_BYTES),
        name="settle",
    )(arrived)


def rotary_table():
    quarter = HD // 4
    lane = jnp.arange(LANES, dtype=jnp.int32)[None, :]
    kind = jnp.arange(3 * POSITIONS, dtype=jnp.int32)[:, None]
    frequency = 10000.0 ** (-(lane % quarter).astype(F32) / quarter)
    angles = (kind % POSITIONS).astype(F32) * frequency
    by_row = (kind < POSITIONS) & (lane < HD // 2)
    by_col = (kind >= POSITIONS) & (kind < 2 * POSITIONS) & (lane >= HD // 2) & (lane < HD)
    used = by_row | by_col
    flag = (kind == 2 * POSITIONS) & (lane == HD)
    cosine = jnp.where(used, jnp.cos(angles), jnp.where(flag, 1.0, 0.0))
    left = jnp.concatenate([cosine, jnp.where(used, jnp.sin(angles), 0.0)], axis=1)
    terms = []
    for _ in range(3):
        term = lax.reduce_precision(left, 8, 7)
        terms.append(term.astype(BF16))
        left = left - term
    return jnp.stack(terms)


def per_device(patches, values, upstream, coords, counts, dest, weight):
    core, here = lax.axis_index("c"), lax.axis_index("x")
    nx, nc = lax.axis_size("x"), lax.axis_size("c")
    ny, nz = lax.axis_size("y"), lax.axis_size("zh")
    heads = nx * nc
    slots = lax.axis_size(PEERS)
    window_count, patch_len, model_width = patches.shape
    value_width = values.shape[-1]
    row_total = window_count * patch_len
    depth = weight.shape[0]
    chunk = -(-depth * 2 * HD // value_width)
    chunk = -(-chunk // EXTRA) * EXTRA

    head = core * nx + here
    slice_q = lax.dynamic_slice_in_dim(weight, head * HD, HD, axis=1)
    slice_k = lax.dynamic_slice_in_dim(weight, value_width + head * HD, HD, axis=1)
    own_w = jnp.concatenate([slice_q, slice_k], axis=1)
    own_w = jnp.broadcast_to(own_w[None], (nz,) + own_w.shape)
    patches, values, upstream, coords, counts, dest = after(
        own_w, (patches, values, upstream, coords, counts, dest)
    )
    own_w = exchange(own_w, "zh")
    own_w = jnp.transpose(own_w, (1, 0, 2)).reshape(depth, nz * 2 * HD)
    own_w = spread(own_w, "y").reshape(ny * depth, nz * 2 * HD)

    live = jnp.arange(patch_len, dtype=jnp.int32)[None, :] < counts[:, None]
    notes = jnp.stack(
        [
            coords[:, 0, :].reshape(row_total),
            coords[:, 1, :].reshape(row_total),
            live.astype(jnp.int32).reshape(row_total),
            jnp.pad(dest[:, 0], (0, row_total - window_count)),
        ]
    )
    notes = jnp.pad(notes, ((0, EXTRA - 4), (0, value_width - row_total))).astype(BF16)
    values = values.reshape(row_total, value_width)
    upstream = upstream.reshape(row_total, value_width)
    steps = ring_steps(nx)
    where = jnp.stack([here, core]).astype(jnp.int32)
    patches = patches.reshape(row_total, model_width)
    all_patches = [ring_x(patches, step) for step in steps]
    packed = pack(where, values, upstream, notes, nx)
    packed = [ring_x(piece, step) for piece, step in zip(packed, steps)]
    note_at = packed[0].shape[0] - EXTRA + 3
    all_dest = jnp.concatenate([piece[note_at, :window_count] for piece in packed])
    all_dest = all_dest.astype(jnp.int32)

    weights = (own_w, core_swap(own_w))
    table = rotary_table()
    early = len(steps) - 1
    *contexts, total = some_heads(
        where, weights, table, all_patches[:early], packed[:early], None, False, patch_len
    )
    context, grad, sent = some_heads(
        where, weights, table, all_patches[early:], packed[early:], total, True, patch_len
    )
    routed = route(all_dest, contexts + [context], slots, patch_len, chunk)

    grad = (grad.astype(F32) + core_swap(sent).astype(F32)).astype(BF16)
    grad = exchange(grad.reshape(ny, depth, nz * 2 * HD), "y")
    grad = jnp.sum(grad.astype(F32), axis=0).astype(BF16)
    grad = jnp.transpose(grad.reshape(depth, nz, 2 * HD), (1, 0, 2))
    folded = fold(exchange(grad, "zh"), slots, chunk, value_width)
    routed = lax.dynamic_update_slice(routed, folded, (0, patch_len, 0))
    arrived = exchange(routed, PEERS)
    return tuple(settle(arrived, patch_len, depth, nc))


def solution(mesh):
    fine = Mesh(mesh.devices.reshape(SPLIT), AXES)
    return jax.shard_map(
        per_device,
        mesh=fine,
        in_specs=(
            P(AXES, None, None),
            P(AXES, None, None),
            P(AXES, None, None),
            P(AXES, None, None),
            P(AXES),
            P(AXES, None),
            P(("zh", "y"), None),
        ),
        out_specs=(P(AXES, None, None), P(("zh", "y"), None)),
        check_vma=False,
    )
```

time: 198 us -> 184 us (0.929)
  starting transfers between devices: 42 us -> 66.1 us
  blocking collectives: 52.9 us -> 32.7 us
  waiting for transfers between devices: 44.5 us -> 29.4 us
  between operations: 14.2 us -> 0.89 us
  other arithmetic: 2.6 us -> 7.05 us
  local copies, waits for them, and re-layouts: 7.73 us -> 10.8 us
  Pallas kernels: 32.8 us -> 35.7 us
    ppermute x0 -> x8, starting transfers between devices: none -> 29.4 us  [the longest x6 19.7 us: ring_x(): lax.ppermute(array, 'x', [(i, (i + step) % count) for i in range(count)])]
    all_to_all x4, waiting for transfers between devices: 43.8 us -> 20.6 us  [exchange(): return lax.all_to_all(array, axes, split_axis=0, concat_axis=0, tiled=True)]
    all_to_all x2 -> x1, blocking collectives: 52.9 us -> 32.7 us  [exchange(): return lax.all_to_all(array, axes, split_axis=0, concat_axis=0, tiled=True)]
    ppermute x0 -> x8, waiting for transfers between devices: none -> 8.84 us  [the longest x6 7.28 us: ring_x(): lax.ppermute(array, 'x', [(i, (i + step) % count) for i in range(count)])]
    all_to_all x4, starting transfers between devices: 42 us -> 36.7 us  [exchange(): return lax.all_to_all(array, axes, split_axis=0, concat_axis=0, tiled=True)]
    pallas_call x2 -> x3, Pallas kernels: 25 us -> 27.8 us  [the longest x2 24.8 us: some_heads(): pl.pallas_call(functools.partial(heads_kernel, patch_len, group, sources,...]
    squeeze x0 -> x4, local copies, waits for them, and re-layouts: none -> 2.68 us  [per_device(): piece[note_at, :window_count]]
    another operation x2 -> x3, other arithmetic: 0.08 us -> 2.09 us
  transfers between devices with their start and end apart: 5 -> 12, of which waited for: 4 -> 6; matrix products, arithmetic and copies ran while one was open for 3% -> 5% of each run, Pallas kernels for 3% -> 12%
where the time goes in v6:
time: 184 us; the launch traced here: 183 us
  starting transfers between devices  66.1 us (36%)
  Pallas kernels  35.7 us (19%)
  blocking collectives  32.7 us (18%)
  waiting for transfers between devices  29.4 us (16%)
  local copies, waits for them, and re-layouts  10.8 us (6%)
  other arithmetic  7.05 us (4%)
    all_to_all x4, starting transfers between devices, exchange(): return lax.all_to_all(array, axes, split_axis=0, concat_axis=0, tiled=True)  36.7 us
    all_to_all x1, blocking collectives, exchange(): return lax.all_to_all(array, axes, split_axis=0, concat_axis=0, tiled=True)  32.7 us
    pallas_call x2, Pallas kernels, some_heads(): pl.pallas_call(functools.partial(heads_kernel, patch_len, group, sources,...  24.8 us
    all_to_all x4, waiting for transfers between devices, exchange(): return lax.all_to_all(array, axes, split_axis=0, concat_axis=0, tiled=True)  20.6 us
    ppermute x6, starting transfers between devices, ring_x(): lax.ppermute(array, 'x', [(i, (i + step) % count) for i in range(count)])  19.7 us
    ppermute x2, starting transfers between devices, core_swap(): return lax.ppermute(array, 'c', [(0, 1), (1, 0)])  9.7 us
    ppermute x6, waiting for transfers between devices, ring_x(): lax.ppermute(array, 'x', [(i, (i + step) % count) for i in range(count)])  7.28 us
  transfers between devices with their start and end apart: 12, of which 6 were waited for; matrix products, arithmetic and copies ran while one was open for 5% of the time, Pallas kernels for 12%

profile of v6, /device:TPU:1, one launch (start us, length us, event | category | flops | bytes accessed | tf_op | source)
XLA Modules:
  0.0 182.7 jit_solution(3287784150572206872)
XLA Ops:
  0.6 0.8 constant_dynamic-slice_fusion.1
  1.6 0.6 broadcast_in_dim.15
  2.2 15.0 %all-to-all-start = ((bf16[4,40,160]{2,1,0:T(8,128)(2,1)}), bf16[4,40,160]{2,1,0:T(8,128)(2,1)S(1)}, u32[]{:S(2)}, u32[]{:S(2)}) async-start(bf16[4,40,160]{2,1,0:T(8,128)(2,1)} %broadcast_in_dim.15), calls=%async_computation | async-start | bytes 163840 | tf_op jit(solution)/shard_map/all_to_all | solution.py:36
  17.2 4.4 %collective-permute-start.4 = (bf16[384,1280]{1,0:T(8,128)(2,1)}, bf16[384,1280]{1,0:T(8,128)(2,1)S(1)}, u32[]{:S(2)}, u32[]{:S(2)}) collective-permute-start(bf16[384,1280]{1,0:T(8,128)(2,1)} %bitcast.31), channel_id=1, source_target_pairs={{0,192},{64,0},{128,64},{192,128},{1,193},{65,1},{129,65},{193,129... | collective-permute-start | bytes 2949128 | tf_op jit(solution)/shard_map/ppermute | solution.py:32
  21.6 1.9 %collective-permute-start.5 = (bf16[384,1280]{1,0:T(8,128)(2,1)}, bf16[384,1280]{1,0:T(8,128)(2,1)S(1)}, u32[]{:S(2)}, u32[]{:S(2)}) collective-permute-start(bf16[384,1280]{1,0:T(8,128)(2,1)} %bitcast.32), channel_id=1, source_target_pairs={{0,64},{64,128},{128,192},{192,0},{1,65},{65,129},{129,193},{193,1... | collective-permute-start | bytes 2949128 | tf_op jit(solution)/shard_map/ppermute | solution.py:32
  23.5 0.7 convert_bitcast_fusion
  24.2 0.7 convert_convert_fusion
  24.9 0.7 convert.22
  26.0 0.6 fusion.14.notes_ref
  26.6 0.2 all-to-all-done
  27.0 0.8 broadcast_in_dim.29
  27.8 6.8 %all-to-all-start.1 = ((bf16[8,40,640]{2,1,0:T(8,128)(2,1)}), bf16[8,40,640]{2,1,0:T(8,128)(2,1)S(1)}, u32[]{:S(2)}, u32[]{:S(2)}) async-start(bf16[8,40,640]{2,1,0:T(8,128)(2,1)} %broadcast_in_dim.29), calls=%async_computation.1 | async-start | bytes 819200 | tf_op jit(solution)/shard_map/all_to_all | solution.py:36
  34.6 0.7 pad_add_fusion.where
  35.2 3.0 %pack.1 = (bf16[208,640]{1,0:T(8,128)(2,1)}, bf16[208,640]{1,0:T(8,128)(2,1)}, bf16[208,640]{1,0:T(8,128)(2,1)}, bf16[208,640]{1,0:T(8,128)(2,1)}) custom-call(s32[2]{0:T(128)} %pad_add_fusion.where, bf16[384,640]{1,0:T(8,128)(2,1)} %bitcast.25, bf16[384,640]{1,0:T(8,128)(2,1)} %bitcast.26, bf16[16,640]{1,0:T(8,128)(2,1)} %fusion.14.notes_ref), custom_call_target="tpu_custom_call" | custom-call | tf_op jit(solution)/shard_map/pack/pallas_call | solution.py:100
  38.2 3.1 %collective-permute-start.1 = (bf16[208,640]{1,0:T(8,128)(2,1)}, bf16[208,640]{1,0:T(8,128)(2,1)}, u32[]{:S(2)}, u32[]{:S(2)}) collective-permute-start(bf16[208,640]{1,0:T(8,128)(2,1)} %get-tuple-element.26), channel_id=1, source_target_pairs={{0,64},{64,128},{128,192},{192,0},{1,65},{65,129},{129,193},{193,1... | collective-permute-start | bytes 798728 | tf_op jit(solution)/shard_map/ppermute | solution.py:32
  41.3 3.4 %collective-permute-start = (bf16[208,640]{1,0:T(8,128)(2,1)}, bf16[208,640]{1,0:T(8,128)(2,1)}, u32[]{:S(2)}, u32[]{:S(2)}) collective-permute-start(bf16[208,640]{1,0:T(8,128)(2,1)} %get-tuple-element.25), channel_id=1, source_target_pairs={{0,192},{64,0},{128,64},{192,128},{1,193},{65,1},{129,65},{193,129... | collective-permute-start | bytes 798728 | tf_op jit(solution)/shard_map/ppermute | solution.py:32
  44.8 1.5 all-to-all-done.1
  46.3 6.1 %collective-permute-start.3 = (bf16[320,640]{1,0:T(8,128)(2,1)S(1)}, bf16[320,640]{1,0:T(8,128)(2,1)S(1)}, u32[]{:S(2)}, u32[]{:S(2)}) collective-permute-start(bf16[320,640]{1,0:T(8,128)(2,1)S(1)} %bitcast.27), channel_id=1, source_target_pairs={{0,32},{32,0},{1,33},{33,1},{2,34},{34,2},{3,35},{35,3},{4,36},{36... | collective-permute-start | bytes 1228808 | tf_op jit(solution)/shard_map/ppermute | solution.py:25
  52.5 0.3 fusion.3
  52.8 0.7 pad_maximum_fusion.refs_0_
  53.5 4.6 %collective-permute-start.6 = (bf16[384,1280]{1,0:T(8,128)(2,1)S(1)}, bf16[384,1280]{1,0:T(8,128)(2,1)}, u32[]{:S(2)}, u32[]{:S(2)}) collective-permute-start(bf16[384,1280]{1,0:T(8,128)(2,1)S(1)} %bitcast.34), channel_id=1, source_target_pairs={{0,128},{64,192},{128,0},{192,64},{1,129},{65,193},{129,1},{193,65... | collective-permute-start | bytes 2949128 | tf_op jit(solution)/shard_map/ppermute | solution.py:32
  58.1 2.3 %collective-permute-start.2 = (bf16[208,640]{1,0:T(8,128)(2,1)}, bf16[208,640]{1,0:T(8,128)(2,1)S(1)}, u32[]{:S(2)}, u32[]{:S(2)}) collective-permute-start(bf16[208,640]{1,0:T(8,128)(2,1)} %get-tuple-element.27), channel_id=1, source_target_pairs={{0,128},{64,192},{128,0},{192,64},{1,129},{65,193},{129,1},{193,65... | collective-permute-start | bytes 798728 | tf_op jit(solution)/shard_map/ppermute | solution.py:32
  60.5 0.9 copy-done.3
  61.4 0.3 copy-done.4
  61.8 0.2 copy-done.5
  61.9 15.9 %heads.2 = (bf16[384,256]{1,0:T(8,128)(2,1)}, bf16[384,256]{1,0:T(8,128)(2,1)}, bf16[384,256]{1,0:T(8,128)(2,1)}, f32[512,1280]{1,0:T(8,128)}) custom-call(s32[2]{0:T(128)} %pad_add_fusion.where, bf16[320,640]{1,0:T(8,128)(2,1)} %bitcast.28, bf16[320,640]{1,0:T(8,128)(2,1)} %copy-done.5, bf16[3,96,256]{2,1,0:T(8,128)(2,1)} %pad_maximum_fusion.refs_0_, ...), custom_call_target="tpu_custom_call" | custom-call | flops 15000000512 | bytes 9000000 | tf_op jit(solution)/shard_map/heads/pallas_call | solution.py:245
  77.8 7.3 %collective-permute-done.2.refs_2_ = bf16[208,640]{1,0:T(8,128)(2,1)S(1)} collective-permute-done((bf16[208,640]{1,0:T(8,128)(2,1)}, bf16[208,640]{1,0:T(8,128)(2,1)S(1)}, u32[]{:S(2)}, u32[]{:S(2)}) %collective-permute-start.2) | collective-permute-done | bytes 266272 | tf_op jit(solution)/shard_map/ppermute | solution.py:32
  85.1 0.7 copy-done.6
  85.8 8.9 %heads.3 = (bf16[384,256]{1,0:T(8,128)(2,1)}, bf16[320,640]{1,0:T(8,128)(2,1)}, bf16[320,640]{1,0:T(8,128)(2,1)}) custom-call(s32[2]{0:T(128)} %pad_add_fusion.where, bf16[320,640]{1,0:T(8,128)(2,1)} %bitcast.29, bf16[320,640]{1,0:T(8,128)(2,1)} %copy-done.5, bf16[3,96,256]{2,1,0:T(8,128)(2,1)} %pad_maximum_fusion.refs_0_, ...), custom_call_target="tpu_custom_call" | custom-call | flops 5000000000 | bytes 3000000 | tf_op jit(solution)/shard_map/heads/pallas_call | solution.py:245
  94.7 3.6 %collective-permute-start.7 = (bf16[320,640]{1,0:T(8,128)(2,1)}, bf16[320,640]{1,0:T(8,128)(2,1)S(1)}, u32[]{:S(2)}, u32[]{:S(2)}) collective-permute-start(bf16[320,640]{1,0:T(8,128)(2,1)} %get-tuple-element.35), channel_id=1, source_target_pairs={{0,32},{32,0},{1,33},{33,1},{2,34},{34,2},{3,35},{35,3},{4,36},{36... | collective-permute-start | bytes 1228808 | tf_op jit(solution)/shard_map/ppermute | solution.py:25
  98.3 1.6 collective-permute-done.7
  99.8 1.9 %add_convert_fusion = bf16[320,640]{1,0:T(8,128)(2,1)} fusion(bf16[320,640]{1,0:T(8,128)(2,1)S(1)} %collective-permute-done.7, bf16[320,640]{1,0:T(8,128)(2,1)} %get-tuple-element.34), kind=kLoop, calls=%fused_computation | loop fusion | flops 819200 | bytes 1228800 | tf_op jit(solution)/shard_map/convert_element_type | solution.py:448
  101.7 6.1 %all-to-all-start.2 = ((bf16[8,40,640]{2,1,0:T(8,128)(2,1)}), bf16[8,40,640]{2,1,0:T(8,128)(2,1)S(1)}, u32[]{:S(2)}, u32[]{:S(2)}) async-start(bf16[8,40,640]{2,1,0:T(8,128)(2,1)} %bitcast.14), calls=%async_computation.2 | async-start | bytes 819200 | tf_op jit(solution)/shard_map/all_to_all | solution.py:36
  107.8 0.7 slice_bitcast_fusion.3
  108.4 0.7 slice_bitcast_fusion
  109.1 0.7 slice_bitcast_fusion.1
  109.8 13.5 %all-to-all-done.2 = bf16[8,40,640]{2,1,0:T(8,128)(2,1)S(1)} async-done(((bf16[8,40,640]{2,1,0:T(8,128)(2,1)}), bf16[8,40,640]{2,1,0:T(8,128)(2,1)S(1)}, u32[]{:S(2)}, u32[]{:S(2)}) %all-to-all-start.2) | async-done | bytes 409632 | tf_op jit(solution)/shard_map/all_to_all | solution.py:36
  123.4 0.6 copy.14
  124.1 8.8 %all-to-all-start.3 = ((bf16[4,40,160]{2,1,0:T(8,128)(2,1)}), bf16[4,40,160]{2,1,0:T(8,128)(2,1)S(1)}, u32[]{:S(2)}, u32[]{:S(2)}) async-start(bf16[4,40,160]{2,1,0:T(8,128)(2,1)} %bitcast.24), calls=%async_computation.3 | async-start | bytes 163840 | tf_op jit(solution)/shard_map/all_to_all | solution.py:36
  132.8 0.7 slice_bitcast_fusion.2
  133.5 0.7 maximum_convert_fusion.dest
  134.2 2.9 %route.1 = bf16[24,48,640]{2,1,0:T(8,128)(2,1)} custom-call(s32[48]{0:T(128)} %maximum_convert_fusion.dest, bf16[384,256]{1,0:T(8,128)(2,1)} %get-tuple-element.29.refs_0_, bf16[384,256]{1,0:T(8,128)(2,1)} %get-tuple-element.30.refs_1_, bf16[384,256]{1,0:T(8,128)(2,1)} %get-tuple-element.31.refs_2_, bf16[384,256]{1,0:T(8,128)(2,1)} %get-tuple-element.33.refs_3_), custom_call_target="tpu_custom_call" | custom-call | tf_op jit(solution)/shard_map/route/pallas_call | solution.py:288
  137.0 5.4 %all-to-all-done.3.parts_ref = bf16[4,40,160]{2,1,0:T(8,128)(2,1)S(1)} async-done(((bf16[4,40,160]{2,1,0:T(8,128)(2,1)}), bf16[4,40,160]{2,1,0:T(8,128)(2,1)S(1)}, u32[]{:S(2)}, u32[]{:S(2)}) %all-to-all-start.3) | async-done | bytes 51232 | tf_op jit(solution)/shard_map/all_to_all | solution.py:36
  142.4 0.6 copy-done.1
  143.1 1.8 fold.1
  144.8 1.9 %constant_dynamic-update-slice_fusion = bf16[24,48,640]{2,1,0:T(8,128)(2,1)} fusion(bf16[24,48,640]{2,1,0:T(8,128)(2,1)} %route.1, bf16[24,16,640]{2,1,0:T(8,128)(2,1)} %fold.1), kind=kLoop, calls=%fused_computation.39 | loop fusion | bytes 983040 | tf_op jit(solution)/shard_map/dynamic_update_slice | solution.py:453
  146.8 32.7 %all_to_all.25.arrived_ref = bf16[24,48,640]{2,1,0:T(8,128)(2,1)} all-to-all(bf16[24,48,640]{2,1,0:T(8,128)(2,1)} %constant_dynamic-update-slice_fusion), channel_id=1, replica_groups=mesh['zl'=3,'x'=4,'c'=2,'zh'=4,'y'=8] {'zl','x','c'}, dimensions={0} | all-to-all | bytes 2949120 | tf_op jit(solution)/shard_map/all_to_all | solution.py:36
  179.4 3.3 %settle.1 = (bf16[24,32,640]{2,1,0:T(8,128)(2,1)}, f32[40,1280]{1,0:T(8,128)}) custom-call(bf16[24,48,640]{2,1,0:T(8,128)(2,1)} %all_to_all.25.arrived_ref), custom_call_target="tpu_custom_call" | custom-call | tf_op jit(solution)/shard_map/settle/pallas_call | solution.py:357
  (33 shorter events, 0.8 us)
Async XLA Ops:
  2.2 24.6 %all-to-all-start = ((bf16[4,40,160]{2,1,0:T(8,128)(2,1)}), bf16[4,40,160]{2,1,0:T(8,128)(2,1)S(1)}, u32[]{:S(2)}, u32[]{:S(2)}) async-start(bf16[4,40,160]{2,1,0:T(8,128)(2,1)} %broadcast_in_dim.15), calls=%async_computation | async-start | bytes 163840 | tf_op jit(solution)/shard_map/all_to_all | solution.py:36
  17.2 43.2 %collective-permute-start.4 = (bf16[384,1280]{1,0:T(8,128)(2,1)}, bf16[384,1280]{1,0:T(8,128)(2,1)S(1)}, u32[]{:S(2)}, u32[]{:S(2)}) collective-permute-start(bf16[384,1280]{1,0:T(8,128)(2,1)} %bitcast.31), channel_id=1, source_target_pairs={{0,192},{64,0},{128,64},{192,128},{1,193},{65,1},{129,65},{193,129... | collective-permute-start | bytes 2949128 | tf_op jit(solution)/shard_map/ppermute | solution.py:32
  21.6 38.9 %collective-permute-start.5 = (bf16[384,1280]{1,0:T(8,128)(2,1)}, bf16[384,1280]{1,0:T(8,128)(2,1)S(1)}, u32[]{:S(2)}, u32[]{:S(2)}) collective-permute-start(bf16[384,1280]{1,0:T(8,128)(2,1)} %bitcast.32), channel_id=1, source_target_pairs={{0,64},{64,128},{128,192},{192,0},{1,65},{65,129},{129,193},{193,1... | collective-permute-start | bytes 2949128 | tf_op jit(solution)/shard_map/ppermute | solution.py:32
  27.0 26.5 %copy-start.2 = (bf16[12,32,1280]{2,1,0:T(8,128)(2,1)S(1)}, bf16[12,32,1280]{2,1,0:T(8,128)(2,1)}, u32[]{:S(2)}) copy-start(bf16[12,32,1280]{2,1,0:T(8,128)(2,1)} %param.7) | copy-start | bytes 2949124
  27.8 18.6 %all-to-all-start.1 = ((bf16[8,40,640]{2,1,0:T(8,128)(2,1)}), bf16[8,40,640]{2,1,0:T(8,128)(2,1)S(1)}, u32[]{:S(2)}, u32[]{:S(2)}) async-start(bf16[8,40,640]{2,1,0:T(8,128)(2,1)} %broadcast_in_dim.29), calls=%async_computation.1 | async-start | bytes 819200 | tf_op jit(solution)/shard_map/all_to_all | solution.py:36
  38.2 15.3 %collective-permute-start.1 = (bf16[208,640]{1,0:T(8,128)(2,1)}, bf16[208,640]{1,0:T(8,128)(2,1)}, u32[]{:S(2)}, u32[]{:S(2)}) collective-permute-start(bf16[208,640]{1,0:T(8,128)(2,1)} %get-tuple-element.26), channel_id=1, source_target_pairs={{0,64},{64,128},{128,192},{192,0},{1,65},{65,129},{129,193},{193,1... | collective-permute-start | bytes 798728 | tf_op jit(solution)/shard_map/ppermute | solution.py:32
  41.3 16.8 %collective-permute-start = (bf16[208,640]{1,0:T(8,128)(2,1)}, bf16[208,640]{1,0:T(8,128)(2,1)}, u32[]{:S(2)}, u32[]{:S(2)}) collective-permute-start(bf16[208,640]{1,0:T(8,128)(2,1)} %get-tuple-element.25), channel_id=1, source_target_pairs={{0,192},{64,0},{128,64},{192,128},{1,193},{65,1},{129,65},{193,129... | collective-permute-start | bytes 798728 | tf_op jit(solution)/shard_map/ppermute | solution.py:32
  46.3 14.2 %copy-start = (bf16[8,40,640]{2,1,0:T(8,128)(2,1)}, bf16[8,40,640]{2,1,0:T(8,128)(2,1)S(1)}, u32[]{:S(2)}) copy-start(bf16[8,40,640]{2,1,0:T(8,128)(2,1)S(1)} %all-to-all-done.1) | copy-start | bytes 1228804
  46.3 14.2 %collective-permute-start.3 = (bf16[320,640]{1,0:T(8,128)(2,1)S(1)}, bf16[320,640]{1,0:T(8,128)(2,1)S(1)}, u32[]{:S(2)}, u32[]{:S(2)}) collective-permute-start(bf16[320,640]{1,0:T(8,128)(2,1)S(1)} %bitcast.27), channel_id=1, source_target_pairs={{0,32},{32,0},{1,33},{33,1},{2,34},{34,2},{3,35},{35,3},{4,36},{36... | collective-permute-start | bytes 1228808 | tf_op jit(solution)/shard_map/ppermute | solution.py:25
  53.5 31.6 %collective-permute-start.6 = (bf16[384,1280]{1,0:T(8,128)(2,1)S(1)}, bf16[384,1280]{1,0:T(8,128)(2,1)}, u32[]{:S(2)}, u32[]{:S(2)}) collective-permute-start(bf16[384,1280]{1,0:T(8,128)(2,1)S(1)} %bitcast.34), channel_id=1, source_target_pairs={{0,128},{64,192},{128,0},{192,64},{1,129},{65,193},{129,1},{193,65... | collective-permute-start | bytes 2949128 | tf_op jit(solution)/shard_map/ppermute | solution.py:32
  58.1 27.0 %collective-permute-start.2 = (bf16[208,640]{1,0:T(8,128)(2,1)}, bf16[208,640]{1,0:T(8,128)(2,1)S(1)}, u32[]{:S(2)}, u32[]{:S(2)}) collective-permute-start(bf16[208,640]{1,0:T(8,128)(2,1)} %get-tuple-element.27), channel_id=1, source_target_pairs={{0,128},{64,192},{128,0},{192,64},{1,129},{65,193},{129,1},{193,65... | collective-permute-start | bytes 798728 | tf_op jit(solution)/shard_map/ppermute | solution.py:32
  60.5 0.9 copy-start.3
  60.5 1.3 copy-start.4
  60.5 1.4 copy-start.5
  85.1 0.7 copy-start.6
  94.7 5.1 %collective-permute-start.7 = (bf16[320,640]{1,0:T(8,128)(2,1)}, bf16[320,640]{1,0:T(8,128)(2,1)S(1)}, u32[]{:S(2)}, u32[]{:S(2)}) collective-permute-start(bf16[320,640]{1,0:T(8,128)(2,1)} %get-tuple-element.35), channel_id=1, source_target_pairs={{0,32},{32,0},{1,33},{33,1},{2,34},{34,2},{3,35},{35,3},{4,36},{36... | collective-permute-start | bytes 1228808 | tf_op jit(solution)/shard_map/ppermute | solution.py:25
  101.7 21.6 %all-to-all-start.2 = ((bf16[8,40,640]{2,1,0:T(8,128)(2,1)}), bf16[8,40,640]{2,1,0:T(8,128)(2,1)S(1)}, u32[]{:S(2)}, u32[]{:S(2)}) async-start(bf16[8,40,640]{2,1,0:T(8,128)(2,1)} %bitcast.14), calls=%async_computation.2 | async-start | bytes 819200 | tf_op jit(solution)/shard_map/all_to_all | solution.py:36
  124.1 18.3 %all-to-all-start.3 = ((bf16[4,40,160]{2,1,0:T(8,128)(2,1)}), bf16[4,40,160]{2,1,0:T(8,128)(2,1)S(1)}, u32[]{:S(2)}, u32[]{:S(2)}) async-start(bf16[4,40,160]{2,1,0:T(8,128)(2,1)} %bitcast.24), calls=%async_computation.3 | async-start | bytes 163840 | tf_op jit(solution)/shard_map/all_to_all | solution.py:36
  142.4 0.6 copy-start.1

commit v7 on v6

--- a/solution.py
+++ b/solution.py
@@ -25,11 +25,11 @@
     return lax.ppermute(array, "c", [(0, 1), (1, 0)])
 
 
-def ring_x(array, step):
-    count = lax.axis_size("x")
+def ring(array, axis, step):
+    count = lax.axis_size(axis)
     if step == 0:
         return array
-    return lax.ppermute(array, "x", [(i, (i + step) % count) for i in range(count)])
+    return lax.ppermute(array, axis, [(i, (i + step) % count) for i in range(count)])
 
 
 def exchange(array, axes):
@@ -116,7 +116,9 @@
     context_refs = take(sources)
     results = take(2 if last else 1)
     own_ref, other_ref, table_ref = take(3)
-    patches_refs, packed_refs = take(sources), take(sources)
+    whole_ref, packed_refs = take(1)[0], take(sources)
+    rows = whole_ref.shape[0] // sources
+    patches_refs = [whole_ref.at[pl.ds(at * rows, rows), :] for at in range(sources)]
     full_ref, sum_ref, dproj_ref, values_ref, upstream_ref, arrivals = take(6)
     moves = [(own_hbm, own_ref), (other_hbm, other_ref), (table_hbm, table_ref)]
     for at in range(sources):
@@ -131,7 +133,6 @@
     for copy in copies:
         copy.start()
     strip, strips = own_ref.shape[0], own_ref.shape[1] // (2 * HD)
-    rows = patches_refs[0].shape[0]
     block = group * patch_len
     scale = 1.0 / math.sqrt(HD)
     full_ref[...] = jnp.zeros_like(full_ref)
@@ -209,15 +210,12 @@
         for i in each:
             context_refs[source][spans[i], lanes[i]] = context[i].astype(BF16)
             at = 2 * chains[i][0] * LANES
-            dproj_ref[spans[i], pl.ds(at, LANES)] = back(dquery[i], blocks[i])
-            dproj_ref[spans[i], pl.ds(at + LANES, LANES)] = back(dkey[i], blocks[i])
-        grown = dot(dproj_ref[...], patches_ref[...], ((0,), (0,)))
-        if first and source == 0:
-            sum_ref[...] = grown
-        else:
-            if source == 0:
-                copies[-1].wait()
-            sum_ref[...] += grown
+            here = pl.ds(source * rows + starts[blocks[i]], block)
+            dproj_ref[here, pl.ds(at, LANES)] = back(dquery[i], blocks[i])
+            dproj_ref[here, pl.ds(at + LANES, LANES)] = back(dkey[i], blocks[i])
+    sum_ref[...] = dot(dproj_ref[...], whole_ref[...], ((0,), (0,)))
+    if not first:
+        copies[-1].wait()
     if not last:
         results[0][...] = sum_ref[...]
         return
@@ -249,12 +247,12 @@
         out_shape=[jax.ShapeDtypeStruct((rows, 2 * LANES), BF16)] * sources + results,
         scratch_shapes=[pltpu.VMEM(weights[0].shape, BF16)] * 2
         + [pltpu.VMEM(table.shape, BF16)]
-        + [pltpu.VMEM(patches[0].shape, BF16)] * sources
+        + [pltpu.VMEM((sources * rows, model_width), BF16)]
         + [pltpu.VMEM(packed[0].shape, BF16)] * sources
         + [
             pltpu.VMEM((model_width, 4 * LANES), BF16),
             pltpu.VMEM(sum_shape.shape, F32),
-            pltpu.VMEM((rows, 4 * LANES), BF16),
+            pltpu.VMEM((sources * rows, 4 * LANES), BF16),
             pltpu.VMEM((rows, 2 * LANES), BF16),
             pltpu.VMEM((rows, 2 * LANES), BF16),
             pltpu.SemaphoreType.DMA((moves,)),
@@ -269,101 +267,129 @@
     )(where, *weights, table, *patches, *packed, *carried)
 
 
-def route_kernel(patch_len, dest, *refs):
+def route_kernel(patch_len, slot_of, *refs):
     context_refs, routed_ref = refs[:-1], refs[-1]
     routed_ref[...] = jnp.zeros_like(routed_ref)
     windows = context_refs[0].shape[0] // patch_len
     for source, context_ref in enumerate(context_refs):
         for window in range(windows):
-            slot = dest[source * windows + window]
+            slot = slot_of[source * windows + window]
             rows = context_ref[pl.ds(window * patch_len, patch_len), :]
             for head in range(2):
                 lanes = pl.ds((2 * source + head) * HD, HD)
-                routed_ref[slot, :patch_len, lanes] = rows[:, head * LANES : head * LANES + HD]
-
-
-def route(dest, contexts, slots, patch_len, chunk):
+                routed_ref[slot, :, lanes] = rows[:, head * LANES : head * LANES + HD]
+
+
+def route(slot_of, contexts, slots, patch_len):
     vmem = pl.BlockSpec(memory_space=pltpu.VMEM)
     width = 2 * HD * len(contexts)
     return pl.pallas_call(
         functools.partial(route_kernel, patch_len),
         in_specs=[pl.BlockSpec(memory_space=pltpu.SMEM)] + [vmem] * len(contexts),
         out_specs=vmem,
-        out_shape=jax.ShapeDtypeStruct((slots, patch_len + chunk, width), BF16),
+        out_shape=jax.ShapeDtypeStruct((slots, patch_len, width), BF16),
         compiler_params=pltpu.CompilerParams(vmem_limit_bytes=VMEM_BYTES),
         name="route",
-    )(dest, *contexts)
-
-
-def fold_kernel(parts_ref, folded_ref):
-    total = parts_ref[0].astype(F32)
-    for at in range(1, parts_ref.shape[0]):
-        total += parts_ref[at].astype(F32)
-    total = total.astype(BF16)
-    depth, width = total.shape
-    folded_ref[...] = jnp.zeros_like(folded_ref)
-    chunk = folded_ref.shape[1]
-    for at in range(0, depth, chunk):
-        count = min(chunk, depth - at)
-        lanes = pl.ds(at // chunk * width, width)
-        folded_ref[:, :count, lanes] = jnp.broadcast_to(
-            total[at : at + count][None], (folded_ref.shape[0], count, width)
-        )
-
-
-def fold(parts, slots, chunk, width):
-    vmem = pl.BlockSpec(memory_space=pltpu.VMEM)
-    return pl.pallas_call(
-        fold_kernel,
+    )(slot_of, *contexts)
+
+
+def join_kernel(kept_ref, got_ref, *out_refs):
+    count = out_refs[0].shape[1]
+    for at, out_ref in enumerate(out_refs):
+        out_ref[0] = kept_ref[pl.ds(at * count, count)]
+        out_ref[1] = got_ref[pl.ds(at * count, count)]
+
+
+def join(kept, got, nx):
+    slots, patch_len, width = kept.shape
+    vmem = pl.BlockSpec(memory_space=pltpu.VMEM)
+    piece = jax.ShapeDtypeStruct((2, slots // nx, patch_len, width), BF16)
+    return pl.pallas_call(
+        join_kernel,
+        in_specs=[vmem] * 2,
+        out_specs=[vmem] * nx,
+        out_shape=[piece] * nx,
+        compiler_params=pltpu.CompilerParams(vmem_limit_bytes=VMEM_BYTES),
+        name="join",
+    )(kept, got)
+
+
+def regroup_kernel(where, *refs):
+    inputs = [ref for ref in refs if ref.shape[0] == 2]
+    outputs = refs[len(inputs) :]
+    copies = len(outputs)
+    for step, out_ref in enumerate(outputs):
+        target = lax.rem(where[2] + step, copies)
+        for at, ref in enumerate(inputs):
+            for kind in range(2):
+                out_ref[at, kind] = ref[kind, target]
+
+
+def regroup(where, pieces):
+    _, copies, patch_len, width = pieces[0].shape
+    vmem = pl.BlockSpec(memory_space=pltpu.VMEM)
+    piece = jax.ShapeDtypeStruct((len(pieces), 2, patch_len, width), BF16)
+    return pl.pallas_call(
+        regroup_kernel,
+        in_specs=[pl.BlockSpec(memory_space=pltpu.SMEM)] + [vmem] * len(pieces),
+        out_specs=[vmem] * copies,
+        out_shape=[piece] * copies,
+        compiler_params=pltpu.CompilerParams(vmem_limit_bytes=VMEM_BYTES),
+        name="regroup",
+    )(where, *pieces)
+
+
+def settle_kernel(where, places, *refs):
+    arrived_refs, placed_ref = refs[:-1], refs[-1]
+    copies, nx = len(arrived_refs), arrived_refs[0].shape[0]
+    steps = ring_steps(nx)
+    for step, arrived_ref in enumerate(arrived_refs):
+        copy = lax.rem(where[2] + copies - step, copies)
+        for swap in range(2):
+            core = where[1] if swap == 0 else 1 - where[1]
+            for sender in range(nx):
+                at = places[sender]
+                for source in range(nx):
+                    lane = 2 * steps.index((sender - source) % nx)
+                    slot = (copy * nx + source) * 2 + core
+                    for kind in range(2):
+                        rows = arrived_ref[at, swap, :, pl.ds((lane + kind) * HD, HD)]
+                        placed_ref[slot, :, pl.ds((kind * nx + sender) * HD, HD)] = rows
+
+
+def settle(where, places, arrived):
+    nx, _, patch_len, width = arrived[0].shape
+    vmem = pl.BlockSpec(memory_space=pltpu.VMEM)
+    smem = pl.BlockSpec(memory_space=pltpu.SMEM)
+    return pl.pallas_call(
+        settle_kernel,
+        in_specs=[smem, smem] + [vmem] * len(arrived),
+        out_specs=vmem,
+        out_shape=jax.ShapeDtypeStruct((len(arrived) * nx * 2, patch_len, width), BF16),
+        compiler_params=pltpu.CompilerParams(vmem_limit_bytes=VMEM_BYTES),
+        name="settle",
+    )(where, places, *arrived)
+
+
+def finish_kernel(cores, arrived_ref, grad_ref):
+    heads = arrived_ref.shape[0]
+    for place in range(heads):
+        head = head_of(place, cores, heads)
+        part = arrived_ref[place].astype(F32)
+        grad_ref[:, pl.ds(head * HD, HD)] = part[:, :HD]
+        grad_ref[:, pl.ds((heads + head) * HD, HD)] = part[:, HD:]
+
+
+def finish(arrived, cores):
+    heads, depth, width = arrived.shape
+    vmem = pl.BlockSpec(memory_space=pltpu.VMEM)
+    return pl.pallas_call(
+        functools.partial(finish_kernel, cores),
         in_specs=[vmem],
         out_specs=vmem,
-        out_shape=jax.ShapeDtypeStruct((slots, chunk, width), BF16),
-        compiler_params=pltpu.CompilerParams(vmem_limit_bytes=VMEM_BYTES),
-        name="fold",
-    )(parts)
-
-
-def settle_kernel(cores, patch_len, arrived_ref, placed_ref, grad_ref):
-    heads = arrived_ref.shape[2] // HD
-    copies = arrived_ref.shape[0] // heads
-    depth, chunk = grad_ref.shape[0], arrived_ref.shape[1] - patch_len
-    for place in range(heads):
-        head = head_of(place, cores, heads)
-        out = pl.ds(head * HD, HD)
-        count = heads // cores
-        here, core = place // cores, place % cores
-        for copy in range(copies):
-            for at, step in enumerate(ring_steps(count)):
-                source = copy * heads + (here - step) % count * cores + core
-                for kind in range(cores):
-                    lanes = pl.ds((cores * at + kind) * HD, HD)
-                    rows = arrived_ref[copy * heads + place, :patch_len, lanes]
-                    placed_ref[source, :, pl.ds((kind * count + here) * HD, HD)] = rows
-        total = arrived_ref[place, patch_len:, :].astype(F32)
-        for copy in range(1, copies):
-            total += arrived_ref[copy * heads + place, patch_len:, :].astype(F32)
-        for at in range(0, depth, chunk):
-            count = min(chunk, depth - at)
-            lanes = at // chunk * 2 * HD
-            span = pl.ds(at, count)
-            grad_ref[span, out] = total[:count, lanes : lanes + HD]
-            other = pl.ds((heads + head) * HD, HD)
-            grad_ref[span, other] = total[:count, lanes + HD : lanes + 2 * HD]
-
-
-def settle(arrived, patch_len, depth, cores):
-    slots, _, width = arrived.shape
-    vmem = pl.BlockSpec(memory_space=pltpu.VMEM)
-    return pl.pallas_call(
-        functools.partial(settle_kernel, cores, patch_len),
-        in_specs=[vmem],
-        out_specs=[vmem, vmem],
-        out_shape=[
-            jax.ShapeDtypeStruct((slots, patch_len, width), BF16),
-            jax.ShapeDtypeStruct((depth, 2 * width), F32),
-        ],
-        compiler_params=pltpu.CompilerParams(vmem_limit_bytes=VMEM_BYTES),
-        name="settle",
+        out_shape=jax.ShapeDtypeStruct((depth, heads * width), F32),
+        compiler_params=pltpu.CompilerParams(vmem_limit_bytes=VMEM_BYTES),
+        name="finish",
     )(arrived)
 
 
@@ -388,8 +414,8 @@
 
 
 def per_device(patches, values, upstream, coords, counts, dest, weight):
-    core, here = lax.axis_index("c"), lax.axis_index("x")
-    nx, nc = lax.axis_size("x"), lax.axis_size("c")
+    core, here, copy = lax.axis_index("c"), lax.axis_index("x"), lax.axis_index("zl")
+    nx, nc, copies = lax.axis_size("x"), lax.axis_size("c"), lax.axis_size("zl")
     ny, nz = lax.axis_size("y"), lax.axis_size("zh")
     heads = nx * nc
     slots = lax.axis_size(PEERS)
@@ -397,8 +423,6 @@
     value_width = values.shape[-1]
     row_total = window_count * patch_len
     depth = weight.shape[0]
-    chunk = -(-depth * 2 * HD // value_width)
-    chunk = -(-chunk // EXTRA) * EXTRA
 
     head = core * nx + here
     slice_q = lax.dynamic_slice_in_dim(weight, head * HD, HD, axis=1)
@@ -425,34 +449,45 @@
     values = values.reshape(row_total, value_width)
     upstream = upstream.reshape(row_total, value_width)
     steps = ring_steps(nx)
-    where = jnp.stack([here, core]).astype(jnp.int32)
+    where = jnp.stack([here, core, copy]).astype(jnp.int32)
     patches = patches.reshape(row_total, model_width)
-    all_patches = [ring_x(patches, step) for step in steps]
+    all_patches = [ring(patches, "x", step) for step in steps]
     packed = pack(where, values, upstream, notes, nx)
-    packed = [ring_x(piece, step) for piece, step in zip(packed, steps)]
+    packed = [ring(piece, "x", step) for piece, step in zip(packed, steps)]
     note_at = packed[0].shape[0] - EXTRA + 3
     all_dest = jnp.concatenate([piece[note_at, :window_count] for piece in packed])
     all_dest = all_dest.astype(jnp.int32)
 
     weights = (own_w, core_swap(own_w))
     table = rotary_table()
-    early = len(steps) - 1
-    *contexts, total = some_heads(
-        where, weights, table, all_patches[:early], packed[:early], None, False, patch_len
+    *contexts, grad, sent = some_heads(
+        where, weights, table, all_patches, packed, None, True, patch_len
     )
-    context, grad, sent = some_heads(
-        where, weights, table, all_patches[early:], packed[early:], total, True, patch_len
-    )
-    routed = route(all_dest, contexts + [context], slots, patch_len, chunk)
+    step_of = lax.rem(all_dest // nc + nx - here, nx)
+    slot_of = jnp.zeros_like(step_of)
+    for at, step in enumerate(steps):
+        slot_of = jnp.where(step_of == step, at, slot_of)
+    away = jnp.where(lax.rem(all_dest, nc) == core, 0, nx)
+    slot_of = (away + slot_of) * copies + all_dest // (nc * nx)
+    routed = route(slot_of, contexts, slots, patch_len)
+    half = slots // 2
+    pieces = join(routed[:half], core_swap(routed[half:]), nx)
+    pieces = [ring(piece, "x", step) for piece, step in zip(pieces, steps)]
+    pieces = regroup(where, pieces)
+    pieces = [ring(piece, "zl", step) for step, piece in enumerate(pieces)]
+    places = [lax.rem(here - sender + nx, nx) for sender in range(nx)]
+    places = [sum(jnp.where(at == steps[k], k, 0) for k in range(nx)) for at in places]
+    places = jnp.stack(places).astype(jnp.int32)
+    placed = settle(where, places, pieces)
 
     grad = (grad.astype(F32) + core_swap(sent).astype(F32)).astype(BF16)
     grad = exchange(grad.reshape(ny, depth, nz * 2 * HD), "y")
     grad = jnp.sum(grad.astype(F32), axis=0).astype(BF16)
     grad = jnp.transpose(grad.reshape(depth, nz, 2 * HD), (1, 0, 2))
-    folded = fold(exchange(grad, "zh"), slots, chunk, value_width)
-    routed = lax.dynamic_update_slice(routed, folded, (0, patch_len, 0))
-    arrived = exchange(routed, PEERS)
-    return tuple(settle(arrived, patch_len, depth, nc))
+    grad = jnp.broadcast_to(grad[None], (copies,) + grad.shape)
+    grad = exchange(grad.reshape(copies * nz, depth, 2 * HD), ("zl", "zh"))
+    grad = jnp.sum(grad.astype(F32), axis=0).astype(BF16)
+    return (placed, finish(spread(grad, ("x", "c")), nc))
 
 
 def solution(mesh):

time: 184 us -> 175 us (0.951)
  blocking collectives: 32.7 us -> 0 us
  starting transfers between devices: 66.1 us -> 94.1 us
  Pallas kernels: 35.7 us -> 31.6 us
  local copies, waits for them, and re-layouts: 10.8 us -> 14.4 us
  other arithmetic: 7.05 us -> 4.65 us
  waiting for transfers between devices: 29.4 us -> 27.3 us
    all_to_all x1 -> x0, blocking collectives: 32.7 us -> none  [exchange(): return lax.all_to_all(array, axes, split_axis=0, concat_axis=0, tiled=True)]
    ppermute x6 -> x11, starting transfers between devices: 19.7 us -> 34 us  [ring(): lax.ppermute(array, axis, [(i, (i + step) % count) for i in range(count)])]
    all_to_all x4 -> x5, waiting for transfers between devices: 20.6 us -> 7.13 us  [exchange(): return lax.all_to_all(array, axes, split_axis=0, concat_axis=0, tiled=True)]
    all_to_all x4 -> x5, starting transfers between devices: 36.7 us -> 49 us  [exchange(): return lax.all_to_all(array, axes, split_axis=0, concat_axis=0, tiled=True)]
    ppermute x6 -> x11, waiting for transfers between devices: 7.28 us -> 18.7 us  [ring(): lax.ppermute(array, axis, [(i, (i + step) % count) for i in range(count)])]
    pallas_call x2 -> x1, Pallas kernels: 24.8 us -> 16.8 us  [some_heads(): pl.pallas_call(functools.partial(heads_kernel, patch_len, group, sources,...]
    pallas_call x2 -> x4, Pallas kernels: 5.03 us -> 9.16 us  [the longest x1 2.9 us: settle(): pl.pallas_call(settle_kernel, in_specs=[smem, smem] + [vmem] * len(arrive...]
    unnamed x14 -> x36, local copies, waits for them, and re-layouts: 2.72 us -> 6.55 us
  transfers between devices with their start and end apart: 12 -> 19, of which waited for: 6 -> 7; matrix products, arithmetic and copies ran while one was open for 5% -> 6% of each run, Pallas kernels for 12% -> 8%
where the time goes in v7:
time: 175 us; the launch traced here: 173 us
  starting transfers between devices  94.1 us (54%)
  Pallas kernels  31.6 us (18%)
  waiting for transfers between devices  27.3 us (16%)
  local copies, waits for them, and re-layouts  14.4 us (8%)
  other arithmetic  4.65 us (3%)
    all_to_all x5, starting transfers between devices, exchange(): return lax.all_to_all(array, axes, split_axis=0, concat_axis=0, tiled=True)  49 us
    ppermute x11, starting transfers between devices, ring(): lax.ppermute(array, axis, [(i, (i + step) % count) for i in range(count)])  34 us
    ppermute x11, waiting for transfers between devices, ring(): lax.ppermute(array, axis, [(i, (i + step) % count) for i in range(count)])  18.7 us
    pallas_call x1, Pallas kernels, some_heads(): pl.pallas_call(functools.partial(heads_kernel, patch_len, group, sources,...  16.8 us
    ppermute x3, starting transfers between devices, core_swap(): return lax.ppermute(array, 'c', [(0, 1), (1, 0)])  11.1 us
    all_to_all x5, waiting for transfers between devices, exchange(): return lax.all_to_all(array, axes, split_axis=0, concat_axis=0, tiled=True)  7.13 us
    unnamed x36, local copies, waits for them, and re-layouts  6.55 us
  transfers between devices with their start and end apart: 19, of which 7 were waited for; matrix products, arithmetic and copies ran while one was open for 6% of the time, Pallas kernels for 8%

profile of v7, /device:TPU:1, one launch (start us, length us, event | category | flops | bytes accessed | tf_op | source)
XLA Modules:
  0.0 173.2 jit_solution(15649311479875659097)
XLA Ops:
  0.6 0.8 constant_dynamic-slice_fusion.1
  2.2 5.3 %collective-permute-start.4 = (bf16[384,1280]{1,0:T(8,128)(2,1)}, bf16[384,1280]{1,0:T(8,128)(2,1)S(1)}, u32[]{:S(2)}, u32[]{:S(2)}) collective-permute-start(bf16[384,1280]{1,0:T(8,128)(2,1)} %bitcast.35), channel_id=1, source_target_pairs={{0,192},{64,0},{128,64},{192,128},{1,193},{65,1},{129,65},{193,129... | collective-permute-start | bytes 2949128 | tf_op jit(solution)/shard_map/ppermute | solution.py:32
  7.5 1.9 %collective-permute-start.5 = (bf16[384,1280]{1,0:T(8,128)(2,1)}, bf16[384,1280]{1,0:T(8,128)(2,1)S(1)}, u32[]{:S(2)}, u32[]{:S(2)}) collective-permute-start(bf16[384,1280]{1,0:T(8,128)(2,1)} %bitcast.36), channel_id=1, source_target_pairs={{0,64},{64,128},{128,192},{192,0},{1,65},{65,129},{129,193},{193,1... | collective-permute-start | bytes 2949128 | tf_op jit(solution)/shard_map/ppermute | solution.py:32
  9.5 3.6 %collective-permute-start.6 = (bf16[384,1280]{1,0:T(8,128)(2,1)}, bf16[384,1280]{1,0:T(8,128)(2,1)S(1)}, u32[]{:S(2)}, u32[]{:S(2)}) collective-permute-start(bf16[384,1280]{1,0:T(8,128)(2,1)} %bitcast.37), channel_id=1, source_target_pairs={{0,128},{64,192},{128,0},{192,64},{1,129},{65,193},{129,1},{193,65... | collective-permute-start | bytes 2949128 | tf_op jit(solution)/shard_map/ppermute | solution.py:32
  13.1 14.2 %all-to-all-start = ((bf16[4,40,160]{2,1,0:T(8,128)(2,1)}), bf16[4,40,160]{2,1,0:T(8,128)(2,1)S(1)}, u32[]{:S(2)}, u32[]{:S(2)}) async-start(bf16[4,40,160]{2,1,0:T(8,128)(2,1)} %broadcast_in_dim.50), calls=%async_computation | async-start | bytes 163840 | tf_op jit(solution)/shard_map/all_to_all | solution.py:36
  30.1 3.0 %pack.1 = (bf16[208,640]{1,0:T(8,128)(2,1)}, bf16[208,640]{1,0:T(8,128)(2,1)}, bf16[208,640]{1,0:T(8,128)(2,1)}, bf16[208,640]{1,0:T(8,128)(2,1)}) custom-call(s32[3]{0:T(128)} %pad_add_fusion.where, bf16[384,640]{1,0:T(8,128)(2,1)} %bitcast.29, bf16[384,640]{1,0:T(8,128)(2,1)} %bitcast.30, bf16[16,640]{1,0:T(8,128)(2,1)} %fusion.14.notes_ref), custom_call_target="tpu_custom_call" | custom-call | tf_op jit(solution)/shard_map/pack/pallas_call | solution.py:100
  33.1 2.8 %collective-permute-start = (bf16[208,640]{1,0:T(8,128)(2,1)}, bf16[208,640]{1,0:T(8,128)(2,1)}, u32[]{:S(2)}, u32[]{:S(2)}) collective-permute-start(bf16[208,640]{1,0:T(8,128)(2,1)} %get-tuple-element.31), channel_id=1, source_target_pairs={{0,192},{64,0},{128,64},{192,128},{1,193},{65,1},{129,65},{193,129... | collective-permute-start | bytes 798728 | tf_op jit(solution)/shard_map/ppermute | solution.py:32
  36.0 4.3 %collective-permute-start.2 = (bf16[208,640]{1,0:T(8,128)(2,1)}, bf16[208,640]{1,0:T(8,128)(2,1)}, u32[]{:S(2)}, u32[]{:S(2)}) collective-permute-start(bf16[208,640]{1,0:T(8,128)(2,1)} %get-tuple-element.33), channel_id=1, source_target_pairs={{0,128},{64,192},{128,0},{192,64},{1,129},{65,193},{129,1},{193,65... | collective-permute-start | bytes 798728 | tf_op jit(solution)/shard_map/ppermute | solution.py:32
  40.5 0.8 broadcast_in_dim.53
  41.3 6.8 %all-to-all-start.1 = ((bf16[8,40,640]{2,1,0:T(8,128)(2,1)}), bf16[8,40,640]{2,1,0:T(8,128)(2,1)S(1)}, u32[]{:S(2)}, u32[]{:S(2)}) async-start(bf16[8,40,640]{2,1,0:T(8,128)(2,1)} %broadcast_in_dim.53), calls=%async_computation.1 | async-start | bytes 819200 | tf_op jit(solution)/shard_map/all_to_all | solution.py:36
  48.4 0.7 slice_bitcast_fusion.3
  49.1 7.7 %collective-permute-done.refs_6_ = bf16[208,640]{1,0:T(8,128)(2,1)} collective-permute-done((bf16[208,640]{1,0:T(8,128)(2,1)}, bf16[208,640]{1,0:T(8,128)(2,1)}, u32[]{:S(2)}, u32[]{:S(2)}) %collective-permute-start) | collective-permute-done | bytes 266272 | tf_op jit(solution)/shard_map/ppermute | solution.py:32
  56.8 3.2 %all-to-all-done.1 = bf16[8,40,640]{2,1,0:T(8,128)(2,1)S(1)} async-done(((bf16[8,40,640]{2,1,0:T(8,128)(2,1)}), bf16[8,40,640]{2,1,0:T(8,128)(2,1)S(1)}, u32[]{:S(2)}, u32[]{:S(2)}) %all-to-all-start.1) | async-done | bytes 409632 | tf_op jit(solution)/shard_map/all_to_all | solution.py:36
  60.0 6.0 %collective-permute-start.3 = (bf16[320,640]{1,0:T(8,128)(2,1)S(1)}, bf16[320,640]{1,0:T(8,128)(2,1)S(1)}, u32[]{:S(2)}, u32[]{:S(2)}) collective-permute-start(bf16[320,640]{1,0:T(8,128)(2,1)S(1)} %bitcast.31), channel_id=1, source_target_pairs={{0,32},{32,0},{1,33},{33,1},{2,34},{34,2},{3,35},{35,3},{4,36},{36... | collective-permute-start | bytes 1228808 | tf_op jit(solution)/shard_map/ppermute | solution.py:25
  66.0 2.1 %collective-permute-start.1 = (bf16[208,640]{1,0:T(8,128)(2,1)}, bf16[208,640]{1,0:T(8,128)(2,1)S(1)}, u32[]{:S(2)}, u32[]{:S(2)}) collective-permute-start(bf16[208,640]{1,0:T(8,128)(2,1)} %get-tuple-element.32), channel_id=1, source_target_pairs={{0,64},{64,128},{128,192},{192,0},{1,65},{65,129},{129,193},{193,1... | collective-permute-start | bytes 798728 | tf_op jit(solution)/shard_map/ppermute | solution.py:32
  68.1 0.7 pad_maximum_fusion.refs_0_
  68.8 0.7 slice_bitcast_fusion
  69.5 7.9 %collective-permute-done.1.refs_7_ = bf16[208,640]{1,0:T(8,128)(2,1)S(1)} collective-permute-done((bf16[208,640]{1,0:T(8,128)(2,1)}, bf16[208,640]{1,0:T(8,128)(2,1)S(1)}, u32[]{:S(2)}, u32[]{:S(2)}) %collective-permute-start.1) | collective-permute-done | bytes 266272 | tf_op jit(solution)/shard_map/ppermute | solution.py:32
  77.4 0.7 copy-done.16
  79.0 0.8 copy-done.15
  79.8 16.8 %heads.1 = (bf16[384,256]{1,0:T(8,128)(2,1)}, bf16[384,256]{1,0:T(8,128)(2,1)}, bf16[384,256]{1,0:T(8,128)(2,1)}, bf16[384,256]{1,0:T(8,128)(2,1)}, bf16[320,640]{1,0:T(8,128)(2,1)}, /*index=5*/bf16[320,640]{1,0:T(8,128)(2,1)}) custom-call(s32[3]{0:T(128)} %pad_add_fusion.where, bf16[320,640]{1,0:T(8,128)(2,1)} %bitcast.32, bf16[320,640]{1,0:T(8,128)(2,1)} %copy-done.15, ...), custom_call_target="tpu_custom_call" | custom-call | flops 20000000000 | bytes 12000000 | tf_op jit(solution)/shard_map/heads/pallas_call | solution.py:243
  96.6 2.9 %collective-permute-start.13 = (bf16[320,640]{1,0:T(8,128)(2,1)}, bf16[320,640]{1,0:T(8,128)(2,1)S(1)}, u32[]{:S(2)}, u32[]{:S(2)}) collective-permute-start(bf16[320,640]{1,0:T(8,128)(2,1)} %get-tuple-element.47), channel_id=1, source_target_pairs={{0,32},{32,0},{1,33},{33,1},{2,34},{34,2},{3,35},{35,3},{4,36},{36... | collective-permute-start | bytes 1228808 | tf_op jit(solution)/shard_map/ppermute | solution.py:25
  99.5 0.7 slice_bitcast_fusion.1
  100.2 0.7 slice_bitcast_fusion.2
  101.5 2.7 %route.1 = bf16[24,32,640]{2,1,0:T(8,128)(2,1)} custom-call(s32[48]{0:T(128)} %multiply_add_fusion.slot_of, bf16[384,256]{1,0:T(8,128)(2,1)} %get-tuple-element.35.refs_0_, bf16[384,256]{1,0:T(8,128)(2,1)} %get-tuple-element.36.refs_1_, bf16[384,256]{1,0:T(8,128)(2,1)} %get-tuple-element.37.refs_2_, bf16[384,256]{1,0:T(8,128)(2,1)} %get-tuple-element.38.refs_3_), custom_call_target="tpu_custom_call" | custom-call | tf_op jit(solution)/shard_map/route/pallas_call | solution.py:286
  104.2 0.9 add_convert_fusion
  105.1 5.8 %all-to-all-start.2 = ((bf16[8,40,640]{2,1,0:T(8,128)(2,1)}), bf16[8,40,640]{2,1,0:T(8,128)(2,1)S(1)}, u32[]{:S(2)}, u32[]{:S(2)}) async-start(bf16[8,40,640]{2,1,0:T(8,128)(2,1)} %bitcast.19), calls=%async_computation.2 | async-start | bytes 819200 | tf_op jit(solution)/shard_map/all_to_all | solution.py:36
  110.9 0.9 fusion.25
  111.7 2.2 %collective-permute-start.7 = (bf16[12,32,640]{2,1,0:T(8,128)(2,1)S(1)}, bf16[12,32,640]{2,1,0:T(8,128)(2,1)S(1)}, u32[]{:S(2)}, u32[]{:S(2)}) collective-permute-start(bf16[12,32,640]{2,1,0:T(8,128)(2,1)S(1)} %get-tuple-element.50), channel_id=1, source_target_pairs={{0,32},{32,0},{1,33},{33,1},{2,34},{34,2},{3,35},{35,3},{4,36},{36... | collective-permute-start | bytes 1474568 | tf_op jit(solution)/shard_map/ppermute | solution.py:25
  113.9 1.5 collective-permute-done.7.got_ref
  115.5 0.8 copy-done.2
  116.3 2.2 %join.1 = (bf16[2,3,32,640]{3,2,1,0:T(8,128)(2,1)}, bf16[2,3,32,640]{3,2,1,0:T(8,128)(2,1)}, bf16[2,3,32,640]{3,2,1,0:T(8,128)(2,1)}, bf16[2,3,32,640]{3,2,1,0:T(8,128)(2,1)}) custom-call(bf16[12,32,640]{2,1,0:T(8,128)(2,1)} %get-tuple-element.51.kept_ref, bf16[12,32,640]{2,1,0:T(8,128)(2,1)} %copy-done.2), custom_call_target="tpu_custom_call" | custom-call | tf_op jit(solution)/shard_map/join/pallas_call | solution.py:307
  118.4 2.4 %collective-permute-start.10 = (bf16[2,3,32,640]{3,2,1,0:T(8,128)(2,1)}, bf16[2,3,32,640]{3,2,1,0:T(8,128)(2,1)S(1)}, u32[]{:S(2)}, u32[]{:S(2)}) collective-permute-start(bf16[2,3,32,640]{3,2,1,0:T(8,128)(2,1)} %get-tuple-element.42), channel_id=1, source_target_pairs={{0,128},{64,192},{128,0},{192,64},{1,129},{65,193},{129,1},{193,65... | collective-permute-start | bytes 737288 | tf_op jit(solution)/shard_map/ppermute | solution.py:32
  120.9 2.8 %collective-permute-start.8 = (bf16[2,3,32,640]{3,2,1,0:T(8,128)(2,1)}, bf16[2,3,32,640]{3,2,1,0:T(8,128)(2,1)S(1)}, u32[]{:S(2)}, u32[]{:S(2)}) collective-permute-start(bf16[2,3,32,640]{3,2,1,0:T(8,128)(2,1)} %get-tuple-element.40), channel_id=1, source_target_pairs={{0,192},{64,0},{128,64},{192,128},{1,193},{65,1},{129,65},{193,129... | collective-permute-start | bytes 737288 | tf_op jit(solution)/shard_map/ppermute | solution.py:32
  123.7 2.5 %collective-permute-start.9 = (bf16[2,3,32,640]{3,2,1,0:T(8,128)(2,1)}, bf16[2,3,32,640]{3,2,1,0:T(8,128)(2,1)S(1)}, u32[]{:S(2)}, u32[]{:S(2)}) collective-permute-start(bf16[2,3,32,640]{3,2,1,0:T(8,128)(2,1)} %get-tuple-element.41), channel_id=1, source_target_pairs={{0,64},{64,128},{128,192},{192,0},{1,65},{65,129},{129,193},{193,1... | collective-permute-start | bytes 737288 | tf_op jit(solution)/shard_map/ppermute | solution.py:32
  126.6 0.7 broadcast_in_dim.56
  127.3 14.9 %all-to-all-start.3 = ((bf16[12,40,160]{2,1,0:T(8,128)(2,1)}), bf16[12,40,160]{2,1,0:T(8,128)(2,1)S(1)}, u32[]{:S(2)}, u32[]{:S(2)}) async-start(bf16[12,40,160]{2,1,0:T(8,128)(2,1)} %bitcast.21), calls=%async_computation.3 | async-start | bytes 491520 | tf_op jit(solution)/shard_map/all_to_all | solution.py:36
  143.1 2.4 %regroup.1 = (bf16[4,2,32,640]{3,2,1,0:T(8,128)(2,1)}, bf16[4,2,32,640]{3,2,1,0:T(8,128)(2,1)}, bf16[4,2,32,640]{3,2,1,0:T(8,128)(2,1)}) custom-call(s32[3]{0:T(128)} %pad_add_fusion.where, bf16[2,3,32,640]{3,2,1,0:T(8,128)(2,1)} %get-tuple-element.39.refs_0_, bf16[2,3,32,640]{3,2,1,0:T(8,128)(2,1)} %copy-done.8, bf16[2,3,32,640]{3,2,1,0:T(8,128)(2,1)} %copy-done.9, ...), custom_call_target="tpu_custom_call" | custom-call | tf_op jit(solution)/shard_map/regroup/pallas_call | solution.py:332
  145.4 3.3 %collective-permute-start.11 = (bf16[4,2,32,640]{3,2,1,0:T(8,128)(2,1)}, bf16[4,2,32,640]{3,2,1,0:T(8,128)(2,1)S(1)}, u32[]{:S(2)}, u32[]{:S(2)}) collective-permute-start(bf16[4,2,32,640]{3,2,1,0:T(8,128)(2,1)} %get-tuple-element.44), channel_id=1, source_target_pairs={{0,256},{256,512},{512,0},{1,257},{257,513},{513,1},{2,258},{258,5... | collective-permute-start | bytes 983048 | tf_op jit(solution)/shard_map/ppermute | solution.py:32
  148.8 2.8 %collective-permute-start.12 = (bf16[4,2,32,640]{3,2,1,0:T(8,128)(2,1)}, bf16[4,2,32,640]{3,2,1,0:T(8,128)(2,1)S(1)}, u32[]{:S(2)}, u32[]{:S(2)}) collective-permute-start(bf16[4,2,32,640]{3,2,1,0:T(8,128)(2,1)} %get-tuple-element.45), channel_id=1, source_target_pairs={{0,512},{256,0},{512,256},{1,513},{257,1},{513,257},{2,514},{258,2... | collective-permute-start | bytes 983048 | tf_op jit(solution)/shard_map/ppermute | solution.py:32
  151.7 3.8 %all-to-all-done.3 = bf16[12,40,160]{2,1,0:T(8,128)(2,1)S(1)} async-done(((bf16[12,40,160]{2,1,0:T(8,128)(2,1)}), bf16[12,40,160]{2,1,0:T(8,128)(2,1)S(1)}, u32[]{:S(2)}, u32[]{:S(2)}) %all-to-all-start.3) | async-done | bytes 153632 | tf_op jit(solution)/shard_map/all_to_all | solution.py:36
  155.5 0.7 broadcast_in_dim.57
  156.2 7.3 %all-to-all-start.4 = ((bf16[8,40,160]{2,1,0:T(8,128)(2,1)}), bf16[8,40,160]{2,1,0:T(8,128)(2,1)S(1)}, u32[]{:S(2)}, u32[]{:S(2)}) async-start(bf16[8,40,160]{2,1,0:T(8,128)(2,1)} %broadcast_in_dim.57), calls=%async_computation.4 | async-start | bytes 327680 | tf_op jit(solution)/shard_map/all_to_all | solution.py:36
  164.1 3.0 %collective-permute-done.12.refs_2_ = bf16[4,2,32,640]{3,2,1,0:T(8,128)(2,1)S(1)} collective-permute-done((bf16[4,2,32,640]{3,2,1,0:T(8,128)(2,1)}, bf16[4,2,32,640]{3,2,1,0:T(8,128)(2,1)S(1)}, u32[]{:S(2)}, u32[]{:S(2)}) %collective-permute-start.12) | collective-permute-done | bytes 327712 | tf_op jit(solution)/shard_map/ppermute | solution.py:32
  167.2 0.7 copy-done.6
  167.9 2.9 %settle.1 = bf16[24,32,640]{2,1,0:T(8,128)(2,1)} custom-call(s32[3]{0:T(128)} %pad_add_fusion.where, s32[4]{0:T(128)} %pad_add_fusion.1.places, bf16[4,2,32,640]{3,2,1,0:T(8,128)(2,1)} %get-tuple-element.43.refs_0_, bf16[4,2,32,640]{3,2,1,0:T(8,128)(2,1)} %copy-done.5, bf16[4,2,32,640]{3,2,1,0:T(8,128)(2,1)} %copy-done.6), custom_call_target="tpu_custom_call" | custom-call | tf_op jit(solution)/shard_map/settle/pallas_call | solution.py:364
  170.8 0.7 copy-done.1
  171.5 1.7 finish.1
  (73 shorter events, 7.5 us)
Async XLA Ops:
  2.2 25.1 %copy-start.10 = (s32[12,2,32]{2,1,0:T(2,128)S(1)}, s32[12,2,32]{2,1,0:T(2,128)}, u32[]{:S(2)}) copy-start(s32[12,2,32]{2,1,0:T(2,128)} %param.10) | copy-start | bytes 9220
  2.2 75.1 %collective-permute-start.4 = (bf16[384,1280]{1,0:T(8,128)(2,1)}, bf16[384,1280]{1,0:T(8,128)(2,1)S(1)}, u32[]{:S(2)}, u32[]{:S(2)}) collective-permute-start(bf16[384,1280]{1,0:T(8,128)(2,1)} %bitcast.35), channel_id=1, source_target_pairs={{0,192},{64,0},{128,64},{192,128},{1,193},{65,1},{129,65},{193,129... | collective-permute-start | bytes 2949128 | tf_op jit(solution)/shard_map/ppermute | solution.py:32
  7.5 69.8 %collective-permute-start.5 = (bf16[384,1280]{1,0:T(8,128)(2,1)}, bf16[384,1280]{1,0:T(8,128)(2,1)S(1)}, u32[]{:S(2)}, u32[]{:S(2)}) collective-permute-start(bf16[384,1280]{1,0:T(8,128)(2,1)} %bitcast.36), channel_id=1, source_target_pairs={{0,64},{64,128},{128,192},{192,0},{1,65},{65,129},{129,193},{193,1... | collective-permute-start | bytes 2949128 | tf_op jit(solution)/shard_map/ppermute | solution.py:32
  9.5 67.9 %collective-permute-start.6 = (bf16[384,1280]{1,0:T(8,128)(2,1)}, bf16[384,1280]{1,0:T(8,128)(2,1)S(1)}, u32[]{:S(2)}, u32[]{:S(2)}) collective-permute-start(bf16[384,1280]{1,0:T(8,128)(2,1)} %bitcast.37), channel_id=1, source_target_pairs={{0,128},{64,192},{128,0},{192,64},{1,129},{65,193},{129,1},{193,65... | collective-permute-start | bytes 2949128 | tf_op jit(solution)/shard_map/ppermute | solution.py:32
  13.1 27.2 %all-to-all-start = ((bf16[4,40,160]{2,1,0:T(8,128)(2,1)}), bf16[4,40,160]{2,1,0:T(8,128)(2,1)S(1)}, u32[]{:S(2)}, u32[]{:S(2)}) async-start(bf16[4,40,160]{2,1,0:T(8,128)(2,1)} %broadcast_in_dim.50), calls=%async_computation | async-start | bytes 163840 | tf_op jit(solution)/shard_map/all_to_all | solution.py:36
  27.5 0.7 copy-start.11
  28.2 0.7 copy-start.17
  33.1 23.7 %collective-permute-start = (bf16[208,640]{1,0:T(8,128)(2,1)}, bf16[208,640]{1,0:T(8,128)(2,1)}, u32[]{:S(2)}, u32[]{:S(2)}) collective-permute-start(bf16[208,640]{1,0:T(8,128)(2,1)} %get-tuple-element.31), channel_id=1, source_target_pairs={{0,192},{64,0},{128,64},{192,128},{1,193},{65,1},{129,65},{193,129... | collective-permute-start | bytes 798728 | tf_op jit(solution)/shard_map/ppermute | solution.py:32
  36.0 30.0 %collective-permute-start.2 = (bf16[208,640]{1,0:T(8,128)(2,1)}, bf16[208,640]{1,0:T(8,128)(2,1)}, u32[]{:S(2)}, u32[]{:S(2)}) collective-permute-start(bf16[208,640]{1,0:T(8,128)(2,1)} %get-tuple-element.33), channel_id=1, source_target_pairs={{0,128},{64,192},{128,0},{192,64},{1,129},{65,193},{129,1},{193,65... | collective-permute-start | bytes 798728 | tf_op jit(solution)/shard_map/ppermute | solution.py:32
  41.3 18.7 %all-to-all-start.1 = ((bf16[8,40,640]{2,1,0:T(8,128)(2,1)}), bf16[8,40,640]{2,1,0:T(8,128)(2,1)S(1)}, u32[]{:S(2)}, u32[]{:S(2)}) async-start(bf16[8,40,640]{2,1,0:T(8,128)(2,1)} %broadcast_in_dim.53), calls=%async_computation.1 | async-start | bytes 819200 | tf_op jit(solution)/shard_map/all_to_all | solution.py:36
  60.0 18.1 %copy-start.3 = (bf16[8,40,640]{2,1,0:T(8,128)(2,1)}, bf16[8,40,640]{2,1,0:T(8,128)(2,1)S(1)}, u32[]{:S(2)}) copy-start(bf16[8,40,640]{2,1,0:T(8,128)(2,1)S(1)} %all-to-all-done.1) | copy-start | bytes 1228804
  60.0 18.1 %collective-permute-start.3 = (bf16[320,640]{1,0:T(8,128)(2,1)S(1)}, bf16[320,640]{1,0:T(8,128)(2,1)S(1)}, u32[]{:S(2)}, u32[]{:S(2)}) collective-permute-start(bf16[320,640]{1,0:T(8,128)(2,1)S(1)} %bitcast.31), channel_id=1, source_target_pairs={{0,32},{32,0},{1,33},{33,1},{2,34},{34,2},{3,35},{35,3},{4,36},{36... | collective-permute-start | bytes 1228808 | tf_op jit(solution)/shard_map/ppermute | solution.py:25
  66.0 11.3 %collective-permute-start.1 = (bf16[208,640]{1,0:T(8,128)(2,1)}, bf16[208,640]{1,0:T(8,128)(2,1)S(1)}, u32[]{:S(2)}, u32[]{:S(2)}) collective-permute-start(bf16[208,640]{1,0:T(8,128)(2,1)} %get-tuple-element.32), channel_id=1, source_target_pairs={{0,64},{64,128},{128,192},{192,0},{1,65},{65,129},{129,193},{193,1... | collective-permute-start | bytes 798728 | tf_op jit(solution)/shard_map/ppermute | solution.py:32
  77.3 0.7 copy-start.16
  77.4 1.0 copy-start.12
  77.4 1.3 copy-start.13
  78.1 1.0 copy-start.14
  79.0 0.8 copy-start.15
  96.6 7.6 %collective-permute-start.13 = (bf16[320,640]{1,0:T(8,128)(2,1)}, bf16[320,640]{1,0:T(8,128)(2,1)S(1)}, u32[]{:S(2)}, u32[]{:S(2)}) collective-permute-start(bf16[320,640]{1,0:T(8,128)(2,1)} %get-tuple-element.47), channel_id=1, source_target_pairs={{0,32},{32,0},{1,33},{33,1},{2,34},{34,2},{3,35},{35,3},{4,36},{36... | collective-permute-start | bytes 1228808 | tf_op jit(solution)/shard_map/ppermute | solution.py:25
  101.5 2.7 %copy-start.4 = (bf16[320,640]{1,0:T(8,128)(2,1)S(1)}, bf16[320,640]{1,0:T(8,128)(2,1)}, u32[]{:S(2)}) copy-start(bf16[320,640]{1,0:T(8,128)(2,1)} %get-tuple-element.46) | copy-start | bytes 1228804
  104.2 6.7 %copy-start = (bf16[24,32,640]{2,1,0:T(8,128)(2,1)S(1)}, bf16[24,32,640]{2,1,0:T(8,128)(2,1)}, u32[]{:S(2)}) copy-start(bf16[24,32,640]{2,1,0:T(8,128)(2,1)} %route.1) | copy-start | bytes 2949124
  105.1 21.3 %all-to-all-start.2 = ((bf16[8,40,640]{2,1,0:T(8,128)(2,1)}), bf16[8,40,640]{2,1,0:T(8,128)(2,1)S(1)}, u32[]{:S(2)}, u32[]{:S(2)}) async-start(bf16[8,40,640]{2,1,0:T(8,128)(2,1)} %bitcast.19), calls=%async_computation.2 | async-start | bytes 819200 | tf_op jit(solution)/shard_map/all_to_all | solution.py:36
  111.7 3.7 %collective-permute-start.7 = (bf16[12,32,640]{2,1,0:T(8,128)(2,1)S(1)}, bf16[12,32,640]{2,1,0:T(8,128)(2,1)S(1)}, u32[]{:S(2)}, u32[]{:S(2)}) collective-permute-start(bf16[12,32,640]{2,1,0:T(8,128)(2,1)S(1)} %get-tuple-element.50), channel_id=1, source_target_pairs={{0,32},{32,0},{1,33},{33,1},{2,34},{34,2},{3,35},{35,3},{4,36},{36... | collective-permute-start | bytes 1474568 | tf_op jit(solution)/shard_map/ppermute | solution.py:25
  115.5 0.8 copy-start.2
  118.4 23.8 %collective-permute-start.10 = (bf16[2,3,32,640]{3,2,1,0:T(8,128)(2,1)}, bf16[2,3,32,640]{3,2,1,0:T(8,128)(2,1)S(1)}, u32[]{:S(2)}, u32[]{:S(2)}) collective-permute-start(bf16[2,3,32,640]{3,2,1,0:T(8,128)(2,1)} %get-tuple-element.42), channel_id=1, source_target_pairs={{0,128},{64,192},{128,0},{192,64},{1,129},{65,193},{129,1},{193,65... | collective-permute-start | bytes 737288 | tf_op jit(solution)/shard_map/ppermute | solution.py:32
  120.9 21.3 %collective-permute-start.8 = (bf16[2,3,32,640]{3,2,1,0:T(8,128)(2,1)}, bf16[2,3,32,640]{3,2,1,0:T(8,128)(2,1)S(1)}, u32[]{:S(2)}, u32[]{:S(2)}) collective-permute-start(bf16[2,3,32,640]{3,2,1,0:T(8,128)(2,1)} %get-tuple-element.40), channel_id=1, source_target_pairs={{0,192},{64,0},{128,64},{192,128},{1,193},{65,1},{129,65},{193,129... | collective-permute-start | bytes 737288 | tf_op jit(solution)/shard_map/ppermute | solution.py:32
  123.7 18.5 %collective-permute-start.9 = (bf16[2,3,32,640]{3,2,1,0:T(8,128)(2,1)}, bf16[2,3,32,640]{3,2,1,0:T(8,128)(2,1)S(1)}, u32[]{:S(2)}, u32[]{:S(2)}) collective-permute-start(bf16[2,3,32,640]{3,2,1,0:T(8,128)(2,1)} %get-tuple-element.41), channel_id=1, source_target_pairs={{0,64},{64,128},{128,192},{192,0},{1,65},{65,129},{129,193},{193,1... | collective-permute-start | bytes 737288 | tf_op jit(solution)/shard_map/ppermute | solution.py:32
  127.3 28.1 %all-to-all-start.3 = ((bf16[12,40,160]{2,1,0:T(8,128)(2,1)}), bf16[12,40,160]{2,1,0:T(8,128)(2,1)S(1)}, u32[]{:S(2)}, u32[]{:S(2)}) async-start(bf16[12,40,160]{2,1,0:T(8,128)(2,1)} %bitcast.21), calls=%async_computation.3 | async-start | bytes 491520 | tf_op jit(solution)/shard_map/all_to_all | solution.py:36
  142.2 0.7 copy-start.7
  142.2 0.8 copy-start.8
  142.2 0.8 copy-start.9
  145.4 18.7 %collective-permute-start.11 = (bf16[4,2,32,640]{3,2,1,0:T(8,128)(2,1)}, bf16[4,2,32,640]{3,2,1,0:T(8,128)(2,1)S(1)}, u32[]{:S(2)}, u32[]{:S(2)}) collective-permute-start(bf16[4,2,32,640]{3,2,1,0:T(8,128)(2,1)} %get-tuple-element.44), channel_id=1, source_target_pairs={{0,256},{256,512},{512,0},{1,257},{257,513},{513,1},{2,258},{258,5... | collective-permute-start | bytes 983048 | tf_op jit(solution)/shard_map/ppermute | solution.py:32
  148.8 18.4 %collective-permute-start.12 = (bf16[4,2,32,640]{3,2,1,0:T(8,128)(2,1)}, bf16[4,2,32,640]{3,2,1,0:T(8,128)(2,1)S(1)}, u32[]{:S(2)}, u32[]{:S(2)}) collective-permute-start(bf16[4,2,32,640]{3,2,1,0:T(8,128)(2,1)} %get-tuple-element.45), channel_id=1, source_target_pairs={{0,512},{256,0},{512,256},{1,513},{257,1},{513,257},{2,514},{258,2... | collective-permute-start | bytes 983048 | tf_op jit(solution)/shard_map/ppermute | solution.py:32
  156.2 14.7 %all-to-all-start.4 = ((bf16[8,40,160]{2,1,0:T(8,128)(2,1)}), bf16[8,40,160]{2,1,0:T(8,128)(2,1)S(1)}, u32[]{:S(2)}, u32[]{:S(2)}) async-start(bf16[8,40,160]{2,1,0:T(8,128)(2,1)} %broadcast_in_dim.57), calls=%async_computation.4 | async-start | bytes 327680 | tf_op jit(solution)/shard_map/all_to_all | solution.py:36
  164.1 3.0 %copy-start.5 = (bf16[4,2,32,640]{3,2,1,0:T(8,128)(2,1)}, bf16[4,2,32,640]{3,2,1,0:T(8,128)(2,1)S(1)}, u32[]{:S(2)}) copy-start(bf16[4,2,32,640]{3,2,1,0:T(8,128)(2,1)S(1)} %collective-permute-done.11.refs_1_) | copy-start | bytes 983044
  167.2 0.7 copy-start.6
  170.8 0.7 copy-start.1

commit v8 on v7

--- a/solution.py
+++ b/solution.py
@@ -66,72 +66,120 @@
     return [0, count - 1, 1] + list(range(2, count - 1))
 
 
-def pack_kernel(where, values_ref, upstream_ref, notes_ref, *packed_refs):
+def pack_kernel(
+    where,
+    counts,
+    dest,
+    coords_ref,
+    patches_ref,
+    values_ref,
+    upstream_ref,
+    own_ref,
+    left_ref,
+    right_ref,
+    far_ref,
+    notes_ref,
+):
+    packed_refs = (own_ref, left_ref, right_ref, far_ref)
     count = len(packed_refs)
     steps = ring_steps(count)
     rows, width = values_ref.shape
+    windows, _, patch_len = coords_ref.shape
+    lane = lax.broadcasted_iota(jnp.int32, (1, width), 1)
+    live = jnp.zeros((1, width), jnp.int32)
+    slot = jnp.zeros((1, width), jnp.int32)
+    notes_ref[...] = jnp.zeros_like(notes_ref)
+    for window in range(windows):
+        at = window * patch_len
+        for axis in range(2):
+            coord = coords_ref[window, axis : axis + 1, :].astype(F32)
+            notes_ref[axis : axis + 1, at : at + patch_len] = coord
+        live = jnp.where((lane >= at) & (lane < at + counts[window]), 1, live)
+        slot = jnp.where(lane == window, dest[window, 0], slot)
+    notes_ref[2:3, :] = live.astype(F32)
+    notes_ref[3:4, :] = slot.astype(F32)
+    for packed_ref in (left_ref, right_ref):
+        packed_ref[:rows, :] = patches_ref[:, :width]
+        packed_ref[rows : 2 * rows, :] = patches_ref[:, width:]
     parts = width // (2 * HD)
     depth = rows // parts
     kinds = width // HD // count
+    tops = [ref.shape[0] - EXTRA - kinds * depth for ref in packed_refs]
     for here in range(count):
 
         @pl.when(where[0] == here)
         def _():
-            for packed_ref, step in zip(packed_refs, steps):
+            for packed_ref, step, top in zip(packed_refs, steps, tops):
                 for kind in range(kinds):
                     head = kind * count + (here + step) % count
                     lanes = pl.ds(head * HD, HD)
                     for part in range(parts):
                         span, at = pl.ds(part * depth, depth), part * 2 * HD
-                        out = pl.ds(kind * depth, depth)
+                        out = pl.ds(top + kind * depth, depth)
                         packed_ref[out, pl.ds(at, HD)] = values_ref[span, lanes]
                         packed_ref[out, pl.ds(at + HD, HD)] = upstream_ref[span, lanes]
 
+    notes = notes_ref[...].astype(BF16)
     for packed_ref in packed_refs:
-        packed_ref[kinds * depth :, :] = notes_ref[...]
-
-
-def pack(where, values, upstream, notes, count):
+        packed_ref[packed_ref.shape[0] - EXTRA :, :] = notes
+
+
+def pack(where, counts, dest, coords, patches, values, upstream, count):
     rows, width = values.shape
-    parts = width // (2 * HD)
-    kinds = width // HD // count
-    vmem = pl.BlockSpec(memory_space=pltpu.VMEM)
-    piece = jax.ShapeDtypeStruct((kinds * rows // parts + EXTRA, width), BF16)
+    depth = width // HD // count * rows // (width // (2 * HD)) + EXTRA
+    vmem = pl.BlockSpec(memory_space=pltpu.VMEM)
+    smem = pl.BlockSpec(memory_space=pltpu.SMEM)
+    small = jax.ShapeDtypeStruct((depth, width), BF16)
+    large = jax.ShapeDtypeStruct((2 * rows + depth, width), BF16)
     return pl.pallas_call(
         pack_kernel,
-        in_specs=[pl.BlockSpec(memory_space=pltpu.SMEM)] + [vmem] * 3,
-        out_specs=[vmem] * count,
-        out_shape=[piece] * count,
+        in_specs=[smem] * 3 + [vmem] * 4,
+        out_specs=[vmem] * 4,
+        out_shape=[small, large, large, small],
+        scratch_shapes=[pltpu.VMEM((EXTRA, width), F32)],
         compiler_params=pltpu.CompilerParams(vmem_limit_bytes=VMEM_BYTES),
         name="pack",
-    )(where, values, upstream, notes)
-
-
-def heads_kernel(patch_len, group, sources, first, last, where, own_hbm, other_hbm, *refs):
+    )(where, counts, dest, coords, patches, values, upstream)
+
+
+def heads_kernel(patch_len, group, where, *refs):
     refs = list(refs)
     take = lambda count: [refs.pop(0) for _ in range(count)]
-    table_hbm = take(1)[0]
-    patches_hbm, packed_hbm = take(sources), take(sources)
-    total_hbm = [] if first else take(1)
-    context_refs = take(sources)
-    results = take(2 if last else 1)
-    own_ref, other_ref, table_ref = take(3)
-    whole_ref, packed_refs = take(1)[0], take(sources)
-    rows = whole_ref.shape[0] // sources
+    own_hbm, other_hbm, table_hbm, patches_hbm, packed_hbm = take(5)
+    left_hbm, right_hbm, low_hbm, high_hbm, far_hbm = take(5)
+    context_refs = take(4)
+    results = take(2)
+    own_ref, other_ref, table_ref, whole_ref = take(4)
+    packed_refs = take(4)
+    full_ref, sum_ref, dproj_ref, values_ref, upstream_ref, arrivals = take(6)
+    sources = len(packed_refs)
+    rows, width = patches_hbm.shape[0], packed_hbm.shape[1]
+    depth = packed_hbm.shape[0]
     patches_refs = [whole_ref.at[pl.ds(at * rows, rows), :] for at in range(sources)]
-    full_ref, sum_ref, dproj_ref, values_ref, upstream_ref, arrivals = take(6)
+    halves = [[ref.at[:, pl.ds(at * width, width)] for at in range(2)] for ref in patches_refs]
     moves = [(own_hbm, own_ref), (other_hbm, other_ref), (table_hbm, table_ref)]
-    for at in range(sources):
-        moves.append((patches_hbm[at], patches_refs[at]))
-        moves.append((packed_hbm[at], packed_refs[at]))
-    if not first:
-        moves.append((total_hbm[0], sum_ref))
-    copies = [
-        pltpu.make_async_copy(source, target, arrivals.at[at])
-        for at, (source, target) in enumerate(moves)
-    ]
-    for copy in copies:
-        copy.start()
+    waits = [[(patches_hbm, patches_refs[0])], [(packed_hbm, packed_refs[0])]]
+    for at, source_hbm in ((1, left_hbm), (2, right_hbm)):
+        cut = [source_hbm.at[pl.ds(half * rows, rows), :] for half in range(2)]
+        waits.append(list(zip(cut, halves[at])))
+        waits.append([(source_hbm.at[pl.ds(2 * rows, depth), :], packed_refs[at])])
+    waits.append([(low_hbm, halves[3][0]), (high_hbm, halves[3][1])])
+    waits.append([(far_hbm, packed_refs[3])])
+    waits = [[move] for move in moves] + waits
+    number = 0
+    copies = []
+    for moves in waits:
+        copies.append([])
+        for source, target in moves:
+            copy = pltpu.make_async_copy(source, target, arrivals.at[number])
+            copy.start()
+            copies[-1].append(copy)
+            number += 1
+
+    def arrive(at):
+        for copy in copies[at]:
+            copy.wait()
+
     strip, strips = own_ref.shape[0], own_ref.shape[1] // (2 * HD)
     block = group * patch_len
     scale = 1.0 / math.sqrt(HD)
@@ -139,8 +187,8 @@
     values_ref[...] = jnp.zeros_like(values_ref)
     upstream_ref[...] = jnp.zeros_like(upstream_ref)
     is_first = where[1] == 0
-    copies[0].wait()
-    copies[1].wait()
+    arrive(0)
+    arrive(1)
     for z in range(strips):
         span = pl.ds(z * strip, strip)
         for part in range(2):
@@ -148,7 +196,7 @@
             own, other = own_ref[:, lanes], other_ref[:, lanes]
             full_ref[span, pl.ds(part * LANES, HD)] = jnp.where(is_first, own, other)
             full_ref[span, pl.ds((2 + part) * LANES, HD)] = jnp.where(is_first, other, own)
-    copies[2].wait()
+    arrive(2)
     row_win = lax.broadcasted_iota(jnp.int32, (block, block), 0) // patch_len
     key_win = lax.broadcasted_iota(jnp.int32, (block, block), 1) // patch_len
     same = row_win == key_win
@@ -159,9 +207,9 @@
     each = range(len(chains))
     for source in range(sources):
         patches_ref, packed_ref = patches_refs[source], packed_refs[source]
-        copies[3 + 2 * source].wait()
+        arrive(3 + 2 * source)
         proj = dot(patches_ref[...], full_ref[...], ((1,), (0,)))
-        copies[4 + 2 * source].wait()
+        arrive(4 + 2 * source)
         depth = (packed_ref.shape[0] - EXTRA) // 2
         notes = packed_ref[2 * depth :, :rows].astype(F32)
         live_keys = notes[2:3, :]
@@ -214,11 +262,6 @@
             dproj_ref[here, pl.ds(at, LANES)] = back(dquery[i], blocks[i])
             dproj_ref[here, pl.ds(at + LANES, LANES)] = back(dkey[i], blocks[i])
     sum_ref[...] = dot(dproj_ref[...], whole_ref[...], ((0,), (0,)))
-    if not first:
-        copies[-1].wait()
-    if not last:
-        results[0][...] = sum_ref[...]
-        return
     for z in range(strips):
         part = jnp.transpose(sum_ref[:, z * strip : (z + 1) * strip]).astype(BF16)
         for at in range(2):
@@ -229,65 +272,65 @@
             results[1][:, lanes] = jnp.where(is_first, high, low)
 
 
-def some_heads(where, weights, table, patches, packed, total, last, patch_len):
-    sources = len(patches)
-    rows, model_width = patches[0].shape
+def some_heads(where, weights, table, arrays, patch_len):
+    rows, model_width = arrays[0].shape
+    piece = arrays[1].shape
     group = math.gcd(rows // patch_len, max(1, 128 // patch_len))
     vmem = pl.BlockSpec(memory_space=pltpu.VMEM)
     hbm = pl.BlockSpec(memory_space=pltpu.HBM)
-    carried = [] if total is None else [total]
-    sum_shape = jax.ShapeDtypeStruct((4 * LANES, model_width), F32)
     grad_shape = jax.ShapeDtypeStruct(weights[0].shape, BF16)
-    results = [grad_shape] * 2 if last else [sum_shape]
-    moves = 3 + 2 * sources + len(carried)
-    return pl.pallas_call(
-        functools.partial(heads_kernel, patch_len, group, sources, total is None, last),
-        in_specs=[pl.BlockSpec(memory_space=pltpu.SMEM)] + [hbm] * moves,
-        out_specs=[vmem] * (sources + len(results)),
-        out_shape=[jax.ShapeDtypeStruct((rows, 2 * LANES), BF16)] * sources + results,
+    return pl.pallas_call(
+        functools.partial(heads_kernel, patch_len, group),
+        in_specs=[pl.BlockSpec(memory_space=pltpu.SMEM)] + [hbm] * (3 + len(arrays)),
+        out_specs=[vmem] * 6,
+        out_shape=[jax.ShapeDtypeStruct((rows, 2 * LANES), BF16)] * 4 + [grad_shape] * 2,
         scratch_shapes=[pltpu.VMEM(weights[0].shape, BF16)] * 2
-        + [pltpu.VMEM(table.shape, BF16)]
-        + [pltpu.VMEM((sources * rows, model_width), BF16)]
-        + [pltpu.VMEM(packed[0].shape, BF16)] * sources
+        + [pltpu.VMEM(table.shape, BF16), pltpu.VMEM((4 * rows, model_width), BF16)]
+        + [pltpu.VMEM(piece, BF16)] * 4
         + [
             pltpu.VMEM((model_width, 4 * LANES), BF16),
-            pltpu.VMEM(sum_shape.shape, F32),
-            pltpu.VMEM((sources * rows, 4 * LANES), BF16),
+            pltpu.VMEM((4 * LANES, model_width), F32),
+            pltpu.VMEM((4 * rows, 4 * LANES), BF16),
             pltpu.VMEM((rows, 2 * LANES), BF16),
             pltpu.VMEM((rows, 2 * LANES), BF16),
-            pltpu.SemaphoreType.DMA((moves,)),
+            pltpu.SemaphoreType.DMA((14,)),
         ],
         compiler_params=pltpu.CompilerParams(vmem_limit_bytes=VMEM_BYTES),
         cost_estimate=pl.CostEstimate(
-            flops=5_000_000_000 * sources,
-            bytes_accessed=3_000_000 * sources,
-            transcendentals=800_000 * sources,
+            flops=20_000_000_000, bytes_accessed=12_000_000, transcendentals=3_000_000
         ),
         name="heads",
-    )(where, *weights, table, *patches, *packed, *carried)
+    )(where, *weights, table, *arrays)
 
 
 def route_kernel(patch_len, slot_of, *refs):
-    context_refs, routed_ref = refs[:-1], refs[-1]
-    routed_ref[...] = jnp.zeros_like(routed_ref)
+    context_refs, routed_refs = refs[:-2], refs[-2:]
+    half = routed_refs[0].shape[0]
+    for routed_ref in routed_refs:
+        routed_ref[...] = jnp.zeros_like(routed_ref)
     windows = context_refs[0].shape[0] // patch_len
     for source, context_ref in enumerate(context_refs):
         for window in range(windows):
             slot = slot_of[source * windows + window]
             rows = context_ref[pl.ds(window * patch_len, patch_len), :]
-            for head in range(2):
-                lanes = pl.ds((2 * source + head) * HD, HD)
-                routed_ref[slot, :, lanes] = rows[:, head * LANES : head * LANES + HD]
+            for away, routed_ref in enumerate(routed_refs):
+
+                @pl.when((slot >= half) == (away == 1))
+                def _():
+                    for head in range(2):
+                        lanes = pl.ds((2 * source + head) * HD, HD)
+                        here = rows[:, head * LANES : head * LANES + HD]
+                        routed_ref[slot - away * half, :, lanes] = here
 
 
 def route(slot_of, contexts, slots, patch_len):
     vmem = pl.BlockSpec(memory_space=pltpu.VMEM)
-    width = 2 * HD * len(contexts)
+    piece = jax.ShapeDtypeStruct((slots // 2, patch_len, 2 * HD * len(contexts)), BF16)
     return pl.pallas_call(
         functools.partial(route_kernel, patch_len),
         in_specs=[pl.BlockSpec(memory_space=pltpu.SMEM)] + [vmem] * len(contexts),
-        out_specs=vmem,
-        out_shape=jax.ShapeDtypeStruct((slots, patch_len, width), BF16),
+        out_specs=[vmem] * 2,
+        out_shape=[piece] * 2,
         compiler_params=pltpu.CompilerParams(vmem_limit_bytes=VMEM_BYTES),
         name="route",
     )(slot_of, *contexts)
@@ -424,54 +467,50 @@
     row_total = window_count * patch_len
     depth = weight.shape[0]
 
+    where = jnp.stack([here, core, copy]).astype(jnp.int32)
+    steps = ring_steps(nx)
+    patches = patches.reshape(row_total, model_width)
+    values = values.reshape(row_total, value_width)
+    upstream = upstream.reshape(row_total, value_width)
+    own, left, right, far = pack(where, counts, dest, coords, patches, values, upstream, nx)
+    left, right = ring(left, "x", steps[1]), ring(right, "x", steps[2])
+
     head = core * nx + here
     slice_q = lax.dynamic_slice_in_dim(weight, head * HD, HD, axis=1)
     slice_k = lax.dynamic_slice_in_dim(weight, value_width + head * HD, HD, axis=1)
     own_w = jnp.concatenate([slice_q, slice_k], axis=1)
-    own_w = jnp.broadcast_to(own_w[None], (nz,) + own_w.shape)
-    patches, values, upstream, coords, counts, dest = after(
-        own_w, (patches, values, upstream, coords, counts, dest)
-    )
-    own_w = exchange(own_w, "zh")
+    own_w = spread(own_w, "zh")
+    far = ring(after(own_w, far), "x", steps[3])
     own_w = jnp.transpose(own_w, (1, 0, 2)).reshape(depth, nz * 2 * HD)
     own_w = spread(own_w, "y").reshape(ny * depth, nz * 2 * HD)
-
-    live = jnp.arange(patch_len, dtype=jnp.int32)[None, :] < counts[:, None]
-    notes = jnp.stack(
-        [
-            coords[:, 0, :].reshape(row_total),
-            coords[:, 1, :].reshape(row_total),
-            live.astype(jnp.int32).reshape(row_total),
-            jnp.pad(dest[:, 0], (0, row_total - window_count)),
-        ]
-    )
-    notes = jnp.pad(notes, ((0, EXTRA - 4), (0, value_width - row_total))).astype(BF16)
-    values = values.reshape(row_total, value_width)
-    upstream = upstream.reshape(row_total, value_width)
-    steps = ring_steps(nx)
-    where = jnp.stack([here, core, copy]).astype(jnp.int32)
-    patches = patches.reshape(row_total, model_width)
-    all_patches = [ring(patches, "x", step) for step in steps]
-    packed = pack(where, values, upstream, notes, nx)
-    packed = [ring(piece, "x", step) for piece, step in zip(packed, steps)]
-    note_at = packed[0].shape[0] - EXTRA + 3
-    all_dest = jnp.concatenate([piece[note_at, :window_count] for piece in packed])
-    all_dest = all_dest.astype(jnp.int32)
-
     weights = (own_w, core_swap(own_w))
-    table = rotary_table()
-    *contexts, grad, sent = some_heads(
-        where, weights, table, all_patches, packed, None, True, patch_len
-    )
+    left, right, far = after(own_w, (left, right, far))
+    low = ring(right[:row_total], "x", steps[2])
+    high = ring(left[row_total : 2 * row_total], "x", steps[1])
+
+    all_dest = [dest[:, 0]]
+    for piece in (left, right, far):
+        at = piece.shape[0] - EXTRA + 3
+        all_dest.append(piece[at, :window_count].astype(jnp.int32))
+    all_dest = jnp.concatenate(all_dest)
     step_of = lax.rem(all_dest // nc + nx - here, nx)
     slot_of = jnp.zeros_like(step_of)
     for at, step in enumerate(steps):
         slot_of = jnp.where(step_of == step, at, slot_of)
     away = jnp.where(lax.rem(all_dest, nc) == core, 0, nx)
     slot_of = (away + slot_of) * copies + all_dest // (nc * nx)
-    routed = route(slot_of, contexts, slots, patch_len)
-    half = slots // 2
-    pieces = join(routed[:half], core_swap(routed[half:]), nx)
+
+    *contexts, grad, sent = some_heads(
+        after(slot_of, where),
+        weights,
+        rotary_table(),
+        (patches, own, left, right, low, high, far),
+        patch_len,
+    )
+    grad = (grad.astype(F32) + core_swap(sent).astype(F32)).astype(BF16)
+    contexts = after(grad, contexts)
+    kept, sent = route(slot_of, contexts, slots, patch_len)
+    pieces = join(kept, core_swap(sent), nx)
     pieces = [ring(piece, "x", step) for piece, step in zip(pieces, steps)]
     pieces = regroup(where, pieces)
     pieces = [ring(piece, "zl", step) for step, piece in enumerate(pieces)]
@@ -480,7 +519,6 @@
     places = jnp.stack(places).astype(jnp.int32)
     placed = settle(where, places, pieces)
 
-    grad = (grad.astype(F32) + core_swap(sent).astype(F32)).astype(BF16)
     grad = exchange(grad.reshape(ny, depth, nz * 2 * HD), "y")
     grad = jnp.sum(grad.astype(F32), axis=0).astype(BF16)
     grad = jnp.transpose(grad.reshape(depth, nz, 2 * HD), (1, 0, 2))

time: 175 us -> 174 us (level)
  starting transfers between devices: 94.1 us -> 79.8 us
  waiting for transfers between devices: 27.3 us -> 41.5 us
  local copies, waits for them, and re-layouts: 14.4 us -> 9.11 us
  Pallas kernels: 31.6 us -> 35.8 us
    all_to_all x5, starting transfers between devices: 49 us -> 33.8 us  [exchange(): return lax.all_to_all(array, axes, split_axis=0, concat_axis=0, tiled=True)]
    all_to_all x5, waiting for transfers between devices: 7.13 us -> 16.3 us  [exchange(): return lax.all_to_all(array, axes, split_axis=0, concat_axis=0, tiled=True)]
    ppermute x11 -> x10, waiting for transfers between devices: 18.7 us -> 21.8 us  [ring(): lax.ppermute(array, axis, [(i, (i + step) % count) for i in range(count)])]
    pallas_call x1, Pallas kernels: 2.68 us -> 5.81 us  [route(): pl.pallas_call(functools.partial(route_kernel, patch_len), in_specs=[pl.B...]
    squeeze x4 -> x0, local copies, waits for them, and re-layouts: 2.71 us -> none  [per_device(): piece[note_at, :window_count]]
    ppermute x3, waiting for transfers between devices: 1.55 us -> 3.43 us  [core_swap(): return lax.ppermute(array, 'c', [(0, 1), (1, 0)])]
    unnamed x36 -> x33, local copies, waits for them, and re-layouts: 6.55 us -> 5.1 us
    ppermute x11 -> x10, starting transfers between devices: 34 us -> 34.9 us  [ring(): lax.ppermute(array, axis, [(i, (i + step) % count) for i in range(count)])]
  transfers between devices with their start and end apart: 19 -> 18, of which waited for: 7 -> 8; matrix products, arithmetic and copies ran while one was open for 6% -> 4% of each run, Pallas kernels for 8% -> 8%
where the time goes in v8:
time: 174 us; the launch traced here: 172 us
  starting transfers between devices  79.8 us (46%)
  waiting for transfers between devices  41.5 us (24%)
  Pallas kernels  35.8 us (21%)
  local copies, waits for them, and re-layouts  9.11 us (5%)
  other arithmetic  5.03 us (3%)
    ppermute x10, starting transfers between devices, ring(): lax.ppermute(array, axis, [(i, (i + step) % count) for i in range(count)])  34.9 us
    all_to_all x5, starting transfers between devices, exchange(): return lax.all_to_all(array, axes, split_axis=0, concat_axis=0, tiled=True)  33.8 us
    ppermute x10, waiting for transfers between devices, ring(): lax.ppermute(array, axis, [(i, (i + step) % count) for i in range(count)])  21.8 us
    pallas_call x1, Pallas kernels, some_heads(): pl.pallas_call(functools.partial(heads_kernel, patch_len, group), in_spec...  16.8 us
    all_to_all x5, waiting for transfers between devices, exchange(): return lax.all_to_all(array, axes, split_axis=0, concat_axis=0, tiled=True)  16.3 us
    ppermute x3, starting transfers between devices, core_swap(): return lax.ppermute(array, 'c', [(0, 1), (1, 0)])  11 us
    pallas_call x1, Pallas kernels, route(): pl.pallas_call(functools.partial(route_kernel, patch_len), in_specs=[pl.B...  5.81 us
    unnamed x33, local copies, waits for them, and re-layouts  5.1 us
  transfers between devices with their start and end apart: 18, of which 8 were waited for; matrix products, arithmetic and copies ran while one was open for 4% of the time, Pallas kernels for 8%

profile of v8, /device:TPU:1, one launch (start us, length us, event | category | flops | bytes accessed | tf_op | source)
XLA Modules:
  0.0 172.4 jit_solution(5902807892609157295)
XLA Ops:
  0.6 1.3 copy.19.dest
  2.6 4.1 %pack.1 = (bf16[208,640]{1,0:T(8,128)(2,1)}, bf16[976,640]{1,0:T(8,128)(2,1)}, bf16[976,640]{1,0:T(8,128)(2,1)}, bf16[208,640]{1,0:T(8,128)(2,1)}) custom-call(s32[3]{0:T(128)} %pad_add_fusion.where, s32[12]{0:T(128)} %counts.1, s32[12,1]{1,0:T(8,128)} %copy.19.dest, s32[12,2,32]{2,1,0:T(2,128)} %coords_ref.1, bf16[384,1280]{1,0:T(8,128)(2,1)} %bitcast.29, ...), custom_call_target="tpu_custom_call" | custom-call | tf_op jit(solution)/shard_map/pack/pallas_call | solution.py:134
  6.7 5.3 %collective-permute-start = (bf16[976,640]{1,0:T(8,128)(2,1)}, bf16[976,640]{1,0:T(8,128)(2,1)S(1)}, u32[]{:S(2)}, u32[]{:S(2)}) collective-permute-start(bf16[976,640]{1,0:T(8,128)(2,1)} %get-tuple-element.30), channel_id=1, source_target_pairs={{0,192},{64,0},{128,64},{192,128},{1,193},{65,1},{129,65},{193,129... | collective-permute-start | bytes 3747848 | tf_op jit(solution)/shard_map/ppermute | solution.py:32
  12.0 1.9 %collective-permute-start.1 = (bf16[976,640]{1,0:T(8,128)(2,1)}, bf16[976,640]{1,0:T(8,128)(2,1)S(1)}, u32[]{:S(2)}, u32[]{:S(2)}) collective-permute-start(bf16[976,640]{1,0:T(8,128)(2,1)} %get-tuple-element.31), channel_id=1, source_target_pairs={{0,64},{64,128},{128,192},{192,0},{1,65},{65,129},{129,193},{193,1... | collective-permute-start | bytes 3747848 | tf_op jit(solution)/shard_map/ppermute | solution.py:32
  14.0 0.8 constant_dynamic-slice_fusion.1
  14.9 0.6 broadcast_in_dim.48
  15.5 14.2 %all-to-all-start = ((bf16[4,40,160]{2,1,0:T(8,128)(2,1)}), bf16[4,40,160]{2,1,0:T(8,128)(2,1)S(1)}, u32[]{:S(2)}, u32[]{:S(2)}) async-start(bf16[4,40,160]{2,1,0:T(8,128)(2,1)} %broadcast_in_dim.48), calls=%async_computation | async-start | bytes 163840 | tf_op jit(solution)/shard_map/all_to_all | solution.py:36
  29.8 9.5 %all-to-all-done = bf16[4,40,160]{2,1,0:T(8,128)(2,1)S(1)} async-done(((bf16[4,40,160]{2,1,0:T(8,128)(2,1)}), bf16[4,40,160]{2,1,0:T(8,128)(2,1)S(1)}, u32[]{:S(2)}, u32[]{:S(2)}) %all-to-all-start) | async-done | bytes 51232 | tf_op jit(solution)/shard_map/all_to_all | solution.py:36
  39.5 0.8 broadcast_in_dim.50
  40.2 6.8 %all-to-all-start.1 = ((bf16[8,40,640]{2,1,0:T(8,128)(2,1)}), bf16[8,40,640]{2,1,0:T(8,128)(2,1)S(1)}, u32[]{:S(2)}, u32[]{:S(2)}) async-start(bf16[8,40,640]{2,1,0:T(8,128)(2,1)} %broadcast_in_dim.50), calls=%async_computation.1 | async-start | bytes 819200 | tf_op jit(solution)/shard_map/all_to_all | solution.py:36
  47.1 4.0 %collective-permute-start.2 = (bf16[208,640]{1,0:T(8,128)(2,1)S(1)}, bf16[208,640]{1,0:T(8,128)(2,1)S(1)}, u32[]{:S(2)}, u32[]{:S(2)}) collective-permute-start(bf16[208,640]{1,0:T(8,128)(2,1)S(1)} %copy-done.15), channel_id=1, source_target_pairs={{0,128},{64,192},{128,0},{192,64},{1,129},{65,193},{129,1},{193,65... | collective-permute-start | bytes 798728 | tf_op jit(solution)/shard_map/ppermute | solution.py:32
  51.4 0.7 pad_maximum_fusion.refs_2_
  52.1 6.7 %all-to-all-done.1 = bf16[8,40,640]{2,1,0:T(8,128)(2,1)S(1)} async-done(((bf16[8,40,640]{2,1,0:T(8,128)(2,1)}), bf16[8,40,640]{2,1,0:T(8,128)(2,1)S(1)}, u32[]{:S(2)}, u32[]{:S(2)}) %all-to-all-start.1) | async-done | bytes 409632 | tf_op jit(solution)/shard_map/all_to_all | solution.py:36
  58.8 6.1 %collective-permute-start.3 = (bf16[320,640]{1,0:T(8,128)(2,1)S(1)}, bf16[320,640]{1,0:T(8,128)(2,1)S(1)}, u32[]{:S(2)}, u32[]{:S(2)}) collective-permute-start(bf16[320,640]{1,0:T(8,128)(2,1)S(1)} %bitcast.33), channel_id=1, source_target_pairs={{0,32},{32,0},{1,33},{33,1},{2,34},{34,2},{3,35},{35,3},{4,36},{36... | collective-permute-start | bytes 1228808 | tf_op jit(solution)/shard_map/ppermute | solution.py:25
  65.1 2.4 %collective-permute-start.4 = (bf16[384,640]{1,0:T(8,128)(2,1)S(1)}, bf16[384,640]{1,0:T(8,128)(2,1)S(1)}, u32[]{:S(2)}, u32[]{:S(2)}) collective-permute-start(bf16[384,640]{1,0:T(8,128)(2,1)S(1)} %slice.18), channel_id=1, source_target_pairs={{0,64},{64,128},{128,192},{192,0},{1,65},{65,129},{129,193},{193,1... | collective-permute-start | bytes 1474568 | tf_op jit(solution)/shard_map/ppermute | solution.py:32
  67.6 4.6 %collective-permute-start.5 = (bf16[384,640]{1,0:T(8,128)(2,1)S(1)}, bf16[384,640]{1,0:T(8,128)(2,1)S(1)}, u32[]{:S(2)}, u32[]{:S(2)}) collective-permute-start(bf16[384,640]{1,0:T(8,128)(2,1)S(1)} %slice.19), channel_id=1, source_target_pairs={{0,192},{64,0},{128,64},{192,128},{1,193},{65,1},{129,65},{193,129... | collective-permute-start | bytes 1474568 | tf_op jit(solution)/shard_map/ppermute | solution.py:32
  72.2 0.7 multiply_add_fusion.slot_of
  72.9 8.7 %collective-permute-done.4.refs_7_ = bf16[384,640]{1,0:T(8,128)(2,1)S(1)} collective-permute-done((bf16[384,640]{1,0:T(8,128)(2,1)S(1)}, bf16[384,640]{1,0:T(8,128)(2,1)S(1)}, u32[]{:S(2)}, u32[]{:S(2)}) %collective-permute-start.4) | collective-permute-done | bytes 491552 | tf_op jit(solution)/shard_map/ppermute | solution.py:32
  81.6 1.0 collective-permute-done.5.refs_8_
  82.6 0.8 copy-done.13
  83.4 16.8 %heads.1 = (bf16[384,256]{1,0:T(8,128)(2,1)}, bf16[384,256]{1,0:T(8,128)(2,1)}, bf16[384,256]{1,0:T(8,128)(2,1)}, bf16[384,256]{1,0:T(8,128)(2,1)}, bf16[320,640]{1,0:T(8,128)(2,1)}, /*index=5*/bf16[320,640]{1,0:T(8,128)(2,1)}) custom-call(s32[3]{0:T(128)} %pad_add_fusion.where, bf16[320,640]{1,0:T(8,128)(2,1)} %bitcast.34, bf16[320,640]{1,0:T(8,128)(2,1)} %copy-done.14, ...), custom_call_target="tpu_custom_call" | custom-call | flops 20000000000 | bytes 12000000 | tf_op jit(solution)/shard_map/heads/pallas_call | solution.py:282
  100.2 2.7 %collective-permute-start.6 = (bf16[320,640]{1,0:T(8,128)(2,1)}, bf16[320,640]{1,0:T(8,128)(2,1)S(1)}, u32[]{:S(2)}, u32[]{:S(2)}) collective-permute-start(bf16[320,640]{1,0:T(8,128)(2,1)} %get-tuple-element.40), channel_id=1, source_target_pairs={{0,32},{32,0},{1,33},{33,1},{2,34},{34,2},{3,35},{35,3},{4,36},{36... | collective-permute-start | bytes 1228808 | tf_op jit(solution)/shard_map/ppermute | solution.py:25
  102.9 1.7 collective-permute-done.6
  104.6 1.9 %add_convert_fusion = bf16[320,640]{1,0:T(8,128)(2,1)} fusion(bf16[320,640]{1,0:T(8,128)(2,1)S(1)} %collective-permute-done.6, bf16[320,640]{1,0:T(8,128)(2,1)} %get-tuple-element.39), kind=kLoop, calls=%fused_computation | loop fusion | flops 819200 | bytes 1228800 | tf_op jit(solution)/shard_map/convert_element_type | solution.py:510
  106.5 3.5 %all-to-all-start.2 = ((bf16[8,40,640]{2,1,0:T(8,128)(2,1)}), bf16[8,40,640]{2,1,0:T(8,128)(2,1)S(1)}, u32[]{:S(2)}, u32[]{:S(2)}) async-start(bf16[8,40,640]{2,1,0:T(8,128)(2,1)} %bitcast.18), calls=%async_computation.2 | async-start | bytes 819200 | tf_op jit(solution)/shard_map/all_to_all | solution.py:36
  109.9 5.8 %route.1 = (bf16[12,32,640]{2,1,0:T(8,128)(2,1)}, bf16[12,32,640]{2,1,0:T(8,128)(2,1)}) custom-call(s32[48]{0:T(128)} %multiply_add_fusion.slot_of, bf16[384,256]{1,0:T(8,128)(2,1)} %get-tuple-element.45.refs_0_, bf16[384,256]{1,0:T(8,128)(2,1)} %get-tuple-element.46.refs_1_, bf16[384,256]{1,0:T(8,128)(2,1)} %get-tuple-element.47.refs_2_, ...), custom_call_target="tpu_custom_call" | custom-call | tf_op jit(solution)/shard_map/route/pallas_call | solution.py:329
  115.7 2.2 %collective-permute-start.7 = (bf16[12,32,640]{2,1,0:T(8,128)(2,1)}, bf16[12,32,640]{2,1,0:T(8,128)(2,1)S(1)}, u32[]{:S(2)}, u32[]{:S(2)}) collective-permute-start(bf16[12,32,640]{2,1,0:T(8,128)(2,1)} %get-tuple-element.50), channel_id=1, source_target_pairs={{0,32},{32,0},{1,33},{33,1},{2,34},{34,2},{3,35},{35,3},{4,36},{36... | collective-permute-start | bytes 1474568 | tf_op jit(solution)/shard_map/ppermute | solution.py:25
  117.9 1.8 %collective-permute-done.7.got_ref = bf16[12,32,640]{2,1,0:T(8,128)(2,1)S(1)} collective-permute-done((bf16[12,32,640]{2,1,0:T(8,128)(2,1)}, bf16[12,32,640]{2,1,0:T(8,128)(2,1)S(1)}, u32[]{:S(2)}, u32[]{:S(2)}) %collective-permute-start.7) | collective-permute-done | bytes 491552 | tf_op jit(solution)/shard_map/ppermute | solution.py:25
  119.7 0.8 copy-done.1
  120.5 2.2 %join.1 = (bf16[2,3,32,640]{3,2,1,0:T(8,128)(2,1)}, bf16[2,3,32,640]{3,2,1,0:T(8,128)(2,1)}, bf16[2,3,32,640]{3,2,1,0:T(8,128)(2,1)}, bf16[2,3,32,640]{3,2,1,0:T(8,128)(2,1)}) custom-call(bf16[12,32,640]{2,1,0:T(8,128)(2,1)} %get-tuple-element.49.kept_ref, bf16[12,32,640]{2,1,0:T(8,128)(2,1)} %copy-done.1), custom_call_target="tpu_custom_call" | custom-call | tf_op jit(solution)/shard_map/join/pallas_call | solution.py:350
  122.6 5.3 %collective-permute-start.8 = (bf16[2,3,32,640]{3,2,1,0:T(8,128)(2,1)}, bf16[2,3,32,640]{3,2,1,0:T(8,128)(2,1)S(1)}, u32[]{:S(2)}, u32[]{:S(2)}) collective-permute-start(bf16[2,3,32,640]{3,2,1,0:T(8,128)(2,1)} %get-tuple-element.52), channel_id=1, source_target_pairs={{0,192},{64,0},{128,64},{192,128},{1,193},{65,1},{129,65},{193,129... | collective-permute-start | bytes 737288 | tf_op jit(solution)/shard_map/ppermute | solution.py:32
  128.0 1.9 %collective-permute-start.9 = (bf16[2,3,32,640]{3,2,1,0:T(8,128)(2,1)}, bf16[2,3,32,640]{3,2,1,0:T(8,128)(2,1)S(1)}, u32[]{:S(2)}, u32[]{:S(2)}) collective-permute-start(bf16[2,3,32,640]{3,2,1,0:T(8,128)(2,1)} %get-tuple-element.53), channel_id=1, source_target_pairs={{0,64},{64,128},{128,192},{192,0},{1,65},{65,129},{129,193},{193,1... | collective-permute-start | bytes 737288 | tf_op jit(solution)/shard_map/ppermute | solution.py:32
  129.9 3.3 %collective-permute-start.10 = (bf16[2,3,32,640]{3,2,1,0:T(8,128)(2,1)}, bf16[2,3,32,640]{3,2,1,0:T(8,128)(2,1)S(1)}, u32[]{:S(2)}, u32[]{:S(2)}) collective-permute-start(bf16[2,3,32,640]{3,2,1,0:T(8,128)(2,1)} %get-tuple-element.54), channel_id=1, source_target_pairs={{0,128},{64,192},{128,0},{192,64},{1,129},{65,193},{129,1},{193,65... | collective-permute-start | bytes 737288 | tf_op jit(solution)/shard_map/ppermute | solution.py:32
  133.4 0.7 broadcast_in_dim.54
  134.1 3.8 %all-to-all-start.3 = ((bf16[12,40,160]{2,1,0:T(8,128)(2,1)}), bf16[12,40,160]{2,1,0:T(8,128)(2,1)S(1)}, u32[]{:S(2)}, u32[]{:S(2)}) async-start(bf16[12,40,160]{2,1,0:T(8,128)(2,1)} %bitcast.20), calls=%async_computation.3 | async-start | bytes 491520 | tf_op jit(solution)/shard_map/all_to_all | solution.py:36
  138.0 5.5 %collective-permute-done.9.refs_2_ = bf16[2,3,32,640]{3,2,1,0:T(8,128)(2,1)S(1)} collective-permute-done((bf16[2,3,32,640]{3,2,1,0:T(8,128)(2,1)}, bf16[2,3,32,640]{3,2,1,0:T(8,128)(2,1)S(1)}, u32[]{:S(2)}, u32[]{:S(2)}) %collective-permute-start.9) | collective-permute-done | bytes 245792 | tf_op jit(solution)/shard_map/ppermute | solution.py:32
  143.4 0.7 copy-done.6
  144.2 2.3 %regroup.1 = (bf16[4,2,32,640]{3,2,1,0:T(8,128)(2,1)}, bf16[4,2,32,640]{3,2,1,0:T(8,128)(2,1)}, bf16[4,2,32,640]{3,2,1,0:T(8,128)(2,1)}) custom-call(s32[3]{0:T(128)} %pad_add_fusion.where, bf16[2,3,32,640]{3,2,1,0:T(8,128)(2,1)} %get-tuple-element.51.refs_0_, bf16[2,3,32,640]{3,2,1,0:T(8,128)(2,1)} %copy-done.5, bf16[2,3,32,640]{3,2,1,0:T(8,128)(2,1)} %copy-done.6, ...), custom_call_target="tpu_custom_call" | custom-call | tf_op jit(solution)/shard_map/regroup/pallas_call | solution.py:375
  146.6 2.7 %collective-permute-start.11 = (bf16[4,2,32,640]{3,2,1,0:T(8,128)(2,1)}, bf16[4,2,32,640]{3,2,1,0:T(8,128)(2,1)S(1)}, u32[]{:S(2)}, u32[]{:S(2)}) collective-permute-start(bf16[4,2,32,640]{3,2,1,0:T(8,128)(2,1)} %get-tuple-element.56), channel_id=1, source_target_pairs={{0,256},{256,512},{512,0},{1,257},{257,513},{513,1},{2,258},{258,5... | collective-permute-start | bytes 983048 | tf_op jit(solution)/shard_map/ppermute | solution.py:32
  149.2 3.5 %collective-permute-start.12 = (bf16[4,2,32,640]{3,2,1,0:T(8,128)(2,1)}, bf16[4,2,32,640]{3,2,1,0:T(8,128)(2,1)S(1)}, u32[]{:S(2)}, u32[]{:S(2)}) collective-permute-start(bf16[4,2,32,640]{3,2,1,0:T(8,128)(2,1)} %get-tuple-element.57), channel_id=1, source_target_pairs={{0,512},{256,0},{512,256},{1,513},{257,1},{513,257},{2,514},{258,2... | collective-permute-start | bytes 983048 | tf_op jit(solution)/shard_map/ppermute | solution.py:32
  152.9 0.7 broadcast_in_dim.55
  153.6 5.5 %all-to-all-start.4 = ((bf16[8,40,160]{2,1,0:T(8,128)(2,1)}), bf16[8,40,160]{2,1,0:T(8,128)(2,1)S(1)}, u32[]{:S(2)}, u32[]{:S(2)}) async-start(bf16[8,40,160]{2,1,0:T(8,128)(2,1)} %broadcast_in_dim.55), calls=%async_computation.4 | async-start | bytes 327680 | tf_op jit(solution)/shard_map/all_to_all | solution.py:36
  159.0 0.7 pad_add_fusion.1.places
  159.7 6.6 %collective-permute-done.12.refs_2_ = bf16[4,2,32,640]{3,2,1,0:T(8,128)(2,1)S(1)} collective-permute-done((bf16[4,2,32,640]{3,2,1,0:T(8,128)(2,1)}, bf16[4,2,32,640]{3,2,1,0:T(8,128)(2,1)S(1)}, u32[]{:S(2)}, u32[]{:S(2)}) %collective-permute-start.12) | collective-permute-done | bytes 327712 | tf_op jit(solution)/shard_map/ppermute | solution.py:32
  166.3 0.7 copy-done.4
  167.1 2.9 %settle.1 = bf16[24,32,640]{2,1,0:T(8,128)(2,1)} custom-call(s32[3]{0:T(128)} %pad_add_fusion.where, s32[4]{0:T(128)} %pad_add_fusion.1.places, bf16[4,2,32,640]{3,2,1,0:T(8,128)(2,1)} %get-tuple-element.55.refs_0_, bf16[4,2,32,640]{3,2,1,0:T(8,128)(2,1)} %copy-done.3, bf16[4,2,32,640]{3,2,1,0:T(8,128)(2,1)} %copy-done.4), custom_call_target="tpu_custom_call" | custom-call | tf_op jit(solution)/shard_map/settle/pallas_call | solution.py:407
  170.0 0.7 copy-done
  170.6 1.7 finish.1
  (57 shorter events, 1.7 us)
Async XLA Ops:
  6.7 40.4 %copy-start.15 = (bf16[208,640]{1,0:T(8,128)(2,1)S(1)}, bf16[208,640]{1,0:T(8,128)(2,1)}, u32[]{:S(2)}) copy-start(bf16[208,640]{1,0:T(8,128)(2,1)} %get-tuple-element.33) | copy-start | bytes 798724
  6.7 58.3 %collective-permute-start = (bf16[976,640]{1,0:T(8,128)(2,1)}, bf16[976,640]{1,0:T(8,128)(2,1)S(1)}, u32[]{:S(2)}, u32[]{:S(2)}) collective-permute-start(bf16[976,640]{1,0:T(8,128)(2,1)} %get-tuple-element.30), channel_id=1, source_target_pairs={{0,192},{64,0},{128,64},{192,128},{1,193},{65,1},{129,65},{193,129... | collective-permute-start | bytes 3747848 | tf_op jit(solution)/shard_map/ppermute | solution.py:32
  12.0 53.0 %collective-permute-start.1 = (bf16[976,640]{1,0:T(8,128)(2,1)}, bf16[976,640]{1,0:T(8,128)(2,1)S(1)}, u32[]{:S(2)}, u32[]{:S(2)}) collective-permute-start(bf16[976,640]{1,0:T(8,128)(2,1)} %get-tuple-element.31), channel_id=1, source_target_pairs={{0,64},{64,128},{128,192},{192,0},{1,65},{65,129},{129,193},{193,1... | collective-permute-start | bytes 3747848 | tf_op jit(solution)/shard_map/ppermute | solution.py:32
  15.5 23.8 %all-to-all-start = ((bf16[4,40,160]{2,1,0:T(8,128)(2,1)}), bf16[4,40,160]{2,1,0:T(8,128)(2,1)S(1)}, u32[]{:S(2)}, u32[]{:S(2)}) async-start(bf16[4,40,160]{2,1,0:T(8,128)(2,1)} %broadcast_in_dim.48), calls=%async_computation | async-start | bytes 163840 | tf_op jit(solution)/shard_map/all_to_all | solution.py:36
  40.2 18.6 %all-to-all-start.1 = ((bf16[8,40,640]{2,1,0:T(8,128)(2,1)}), bf16[8,40,640]{2,1,0:T(8,128)(2,1)S(1)}, u32[]{:S(2)}, u32[]{:S(2)}) async-start(bf16[8,40,640]{2,1,0:T(8,128)(2,1)} %broadcast_in_dim.50), calls=%async_computation.1 | async-start | bytes 819200 | tf_op jit(solution)/shard_map/all_to_all | solution.py:36
  47.1 17.9 %collective-permute-start.2 = (bf16[208,640]{1,0:T(8,128)(2,1)S(1)}, bf16[208,640]{1,0:T(8,128)(2,1)S(1)}, u32[]{:S(2)}, u32[]{:S(2)}) collective-permute-start(bf16[208,640]{1,0:T(8,128)(2,1)S(1)} %copy-done.15), channel_id=1, source_target_pairs={{0,128},{64,192},{128,0},{192,64},{1,129},{65,193},{129,1},{193,65... | collective-permute-start | bytes 798728 | tf_op jit(solution)/shard_map/ppermute | solution.py:32
  51.4 20.8 %copy-start.10 = (s32[12,1]{0,1:T(1,128)S(1)}, s32[12,1]{0,1:T(1,128)}, u32[]{:S(2)}) copy-start(s32[12,1]{0,1:T(1,128)} %param.12) | copy-start | bytes 148
  58.8 24.6 %copy-start.2 = (bf16[8,40,640]{2,1,0:T(8,128)(2,1)}, bf16[8,40,640]{2,1,0:T(8,128)(2,1)S(1)}, u32[]{:S(2)}) copy-start(bf16[8,40,640]{2,1,0:T(8,128)(2,1)S(1)} %all-to-all-done.1) | copy-start | bytes 1228804
  58.8 14.1 %collective-permute-start.3 = (bf16[320,640]{1,0:T(8,128)(2,1)S(1)}, bf16[320,640]{1,0:T(8,128)(2,1)S(1)}, u32[]{:S(2)}, u32[]{:S(2)}) collective-permute-start(bf16[320,640]{1,0:T(8,128)(2,1)S(1)} %bitcast.33), channel_id=1, source_target_pairs={{0,32},{32,0},{1,33},{33,1},{2,34},{34,2},{3,35},{35,3},{4,36},{36... | collective-permute-start | bytes 1228808 | tf_op jit(solution)/shard_map/ppermute | solution.py:25
  65.0 18.4 %copy-start.11 = (bf16[208,640]{1,0:T(8,128)(2,1)}, bf16[208,640]{1,0:T(8,128)(2,1)S(1)}, u32[]{:S(2)}) copy-start(bf16[208,640]{1,0:T(8,128)(2,1)S(1)} %collective-permute-done.2.refs_9_) | copy-start | bytes 798724
  65.0 18.4 %copy-start.9 = (bf16[976,640]{1,0:T(8,128)(2,1)}, bf16[976,640]{1,0:T(8,128)(2,1)S(1)}, u32[]{:S(2)}) copy-start(bf16[976,640]{1,0:T(8,128)(2,1)S(1)} %collective-permute-done.refs_5_) | copy-start | bytes 3747844
  65.0 18.4 %copy-start.8 = (bf16[976,640]{1,0:T(8,128)(2,1)}, bf16[976,640]{1,0:T(8,128)(2,1)S(1)}, u32[]{:S(2)}) copy-start(bf16[976,640]{1,0:T(8,128)(2,1)S(1)} %collective-permute-done.1.refs_6_) | copy-start | bytes 3747844
  65.1 16.5 %collective-permute-start.4 = (bf16[384,640]{1,0:T(8,128)(2,1)S(1)}, bf16[384,640]{1,0:T(8,128)(2,1)S(1)}, u32[]{:S(2)}, u32[]{:S(2)}) collective-permute-start(bf16[384,640]{1,0:T(8,128)(2,1)S(1)} %slice.18), channel_id=1, source_target_pairs={{0,64},{64,128},{128,192},{192,0},{1,65},{65,129},{129,193},{193,1... | collective-permute-start | bytes 1474568 | tf_op jit(solution)/shard_map/ppermute | solution.py:32
  67.6 15.0 %collective-permute-start.5 = (bf16[384,640]{1,0:T(8,128)(2,1)S(1)}, bf16[384,640]{1,0:T(8,128)(2,1)S(1)}, u32[]{:S(2)}, u32[]{:S(2)}) collective-permute-start(bf16[384,640]{1,0:T(8,128)(2,1)S(1)} %slice.19), channel_id=1, source_target_pairs={{0,192},{64,0},{128,64},{192,128},{1,193},{65,1},{129,65},{193,129... | collective-permute-start | bytes 1474568 | tf_op jit(solution)/shard_map/ppermute | solution.py:32
  72.9 9.7 %copy-start.14 = (bf16[320,640]{1,0:T(8,128)(2,1)}, bf16[320,640]{1,0:T(8,128)(2,1)S(1)}, u32[]{:S(2)}) copy-start(bf16[320,640]{1,0:T(8,128)(2,1)S(1)} %collective-permute-done.3.refs_1_) | copy-start | bytes 1228804
  81.6 1.8 %copy-start.12 = (bf16[384,640]{1,0:T(8,128)(2,1)}, bf16[384,640]{1,0:T(8,128)(2,1)S(1)}, u32[]{:S(2)}) copy-start(bf16[384,640]{1,0:T(8,128)(2,1)S(1)} %collective-permute-done.4.refs_7_) | copy-start | bytes 1474564
  82.6 0.8 copy-start.13
  100.2 4.4 %collective-permute-start.6 = (bf16[320,640]{1,0:T(8,128)(2,1)}, bf16[320,640]{1,0:T(8,128)(2,1)S(1)}, u32[]{:S(2)}, u32[]{:S(2)}) collective-permute-start(bf16[320,640]{1,0:T(8,128)(2,1)} %get-tuple-element.40), channel_id=1, source_target_pairs={{0,32},{32,0},{1,33},{33,1},{2,34},{34,2},{3,35},{35,3},{4,36},{36... | collective-permute-start | bytes 1228808 | tf_op jit(solution)/shard_map/ppermute | solution.py:25
  106.5 26.7 %all-to-all-start.2 = ((bf16[8,40,640]{2,1,0:T(8,128)(2,1)}), bf16[8,40,640]{2,1,0:T(8,128)(2,1)S(1)}, u32[]{:S(2)}, u32[]{:S(2)}) async-start(bf16[8,40,640]{2,1,0:T(8,128)(2,1)} %bitcast.18), calls=%async_computation.2 | async-start | bytes 819200 | tf_op jit(solution)/shard_map/all_to_all | solution.py:36
  115.7 4.0 %collective-permute-start.7 = (bf16[12,32,640]{2,1,0:T(8,128)(2,1)}, bf16[12,32,640]{2,1,0:T(8,128)(2,1)S(1)}, u32[]{:S(2)}, u32[]{:S(2)}) collective-permute-start(bf16[12,32,640]{2,1,0:T(8,128)(2,1)} %get-tuple-element.50), channel_id=1, source_target_pairs={{0,32},{32,0},{1,33},{33,1},{2,34},{34,2},{3,35},{35,3},{4,36},{36... | collective-permute-start | bytes 1474568 | tf_op jit(solution)/shard_map/ppermute | solution.py:25
  119.7 0.8 copy-start.1
  122.6 15.3 %collective-permute-start.8 = (bf16[2,3,32,640]{3,2,1,0:T(8,128)(2,1)}, bf16[2,3,32,640]{3,2,1,0:T(8,128)(2,1)S(1)}, u32[]{:S(2)}, u32[]{:S(2)}) collective-permute-start(bf16[2,3,32,640]{3,2,1,0:T(8,128)(2,1)} %get-tuple-element.52), channel_id=1, source_target_pairs={{0,192},{64,0},{128,64},{192,128},{1,193},{65,1},{129,65},{193,129... | collective-permute-start | bytes 737288 | tf_op jit(solution)/shard_map/ppermute | solution.py:32
  128.0 15.5 %collective-permute-start.9 = (bf16[2,3,32,640]{3,2,1,0:T(8,128)(2,1)}, bf16[2,3,32,640]{3,2,1,0:T(8,128)(2,1)S(1)}, u32[]{:S(2)}, u32[]{:S(2)}) collective-permute-start(bf16[2,3,32,640]{3,2,1,0:T(8,128)(2,1)} %get-tuple-element.53), channel_id=1, source_target_pairs={{0,64},{64,128},{128,192},{192,0},{1,65},{65,129},{129,193},{193,1... | collective-permute-start | bytes 737288 | tf_op jit(solution)/shard_map/ppermute | solution.py:32
  129.9 13.5 %collective-permute-start.10 = (bf16[2,3,32,640]{3,2,1,0:T(8,128)(2,1)}, bf16[2,3,32,640]{3,2,1,0:T(8,128)(2,1)S(1)}, u32[]{:S(2)}, u32[]{:S(2)}) collective-permute-start(bf16[2,3,32,640]{3,2,1,0:T(8,128)(2,1)} %get-tuple-element.54), channel_id=1, source_target_pairs={{0,128},{64,192},{128,0},{192,64},{1,129},{65,193},{129,1},{193,65... | collective-permute-start | bytes 737288 | tf_op jit(solution)/shard_map/ppermute | solution.py:32
  134.1 18.7 %all-to-all-start.3 = ((bf16[12,40,160]{2,1,0:T(8,128)(2,1)}), bf16[12,40,160]{2,1,0:T(8,128)(2,1)S(1)}, u32[]{:S(2)}, u32[]{:S(2)}) async-start(bf16[12,40,160]{2,1,0:T(8,128)(2,1)} %bitcast.20), calls=%async_computation.3 | async-start | bytes 491520 | tf_op jit(solution)/shard_map/all_to_all | solution.py:36
  138.0 5.5 %copy-start.5 = (bf16[2,3,32,640]{3,2,1,0:T(8,128)(2,1)}, bf16[2,3,32,640]{3,2,1,0:T(8,128)(2,1)S(1)}, u32[]{:S(2)}) copy-start(bf16[2,3,32,640]{3,2,1,0:T(8,128)(2,1)S(1)} %collective-permute-done.8.refs_1_) | copy-start | bytes 737284
  143.4 0.7 copy-start.6
  143.4 0.8 copy-start.7
  146.6 13.1 %collective-permute-start.11 = (bf16[4,2,32,640]{3,2,1,0:T(8,128)(2,1)}, bf16[4,2,32,640]{3,2,1,0:T(8,128)(2,1)S(1)}, u32[]{:S(2)}, u32[]{:S(2)}) collective-permute-start(bf16[4,2,32,640]{3,2,1,0:T(8,128)(2,1)} %get-tuple-element.56), channel_id=1, source_target_pairs={{0,256},{256,512},{512,0},{1,257},{257,513},{513,1},{2,258},{258,5... | collective-permute-start | bytes 983048 | tf_op jit(solution)/shard_map/ppermute | solution.py:32
  149.2 17.1 %collective-permute-start.12 = (bf16[4,2,32,640]{3,2,1,0:T(8,128)(2,1)}, bf16[4,2,32,640]{3,2,1,0:T(8,128)(2,1)S(1)}, u32[]{:S(2)}, u32[]{:S(2)}) collective-permute-start(bf16[4,2,32,640]{3,2,1,0:T(8,128)(2,1)} %get-tuple-element.57), channel_id=1, source_target_pairs={{0,512},{256,0},{512,256},{1,513},{257,1},{513,257},{2,514},{258,2... | collective-permute-start | bytes 983048 | tf_op jit(solution)/shard_map/ppermute | solution.py:32
  153.6 16.4 %all-to-all-start.4 = ((bf16[8,40,160]{2,1,0:T(8,128)(2,1)}), bf16[8,40,160]{2,1,0:T(8,128)(2,1)S(1)}, u32[]{:S(2)}, u32[]{:S(2)}) async-start(bf16[8,40,160]{2,1,0:T(8,128)(2,1)} %broadcast_in_dim.55), calls=%async_computation.4 | async-start | bytes 327680 | tf_op jit(solution)/shard_map/all_to_all | solution.py:36
  159.7 6.6 %copy-start.3 = (bf16[4,2,32,640]{3,2,1,0:T(8,128)(2,1)}, bf16[4,2,32,640]{3,2,1,0:T(8,128)(2,1)S(1)}, u32[]{:S(2)}) copy-start(bf16[4,2,32,640]{3,2,1,0:T(8,128)(2,1)S(1)} %collective-permute-done.11.refs_1_) | copy-start | bytes 983044
  166.3 0.7 copy-start.4
  170.0 0.7 copy-start

commit v9 on v8

--- a/solution.py
+++ b/solution.py
@@ -98,7 +98,7 @@
         slot = jnp.where(lane == window, dest[window, 0], slot)
     notes_ref[2:3, :] = live.astype(F32)
     notes_ref[3:4, :] = slot.astype(F32)
-    for packed_ref in (left_ref, right_ref):
+    for packed_ref in packed_refs[1:]:
         packed_ref[:rows, :] = patches_ref[:, :width]
         packed_ref[rows : 2 * rows, :] = patches_ref[:, width:]
     parts = width // (2 * HD)
@@ -135,7 +135,7 @@
         pack_kernel,
         in_specs=[smem] * 3 + [vmem] * 4,
         out_specs=[vmem] * 4,
-        out_shape=[small, large, large, small],
+        out_shape=[small, large, large, large],
         scratch_shapes=[pltpu.VMEM((EXTRA, width), F32)],
         compiler_params=pltpu.CompilerParams(vmem_limit_bytes=VMEM_BYTES),
         name="pack",
@@ -146,7 +146,7 @@
     refs = list(refs)
     take = lambda count: [refs.pop(0) for _ in range(count)]
     own_hbm, other_hbm, table_hbm, patches_hbm, packed_hbm = take(5)
-    left_hbm, right_hbm, low_hbm, high_hbm, far_hbm = take(5)
+    remote_hbm = take(3)
     context_refs = take(4)
     results = take(2)
     own_ref, other_ref, table_ref, whole_ref = take(4)
@@ -159,12 +159,10 @@
     halves = [[ref.at[:, pl.ds(at * width, width)] for at in range(2)] for ref in patches_refs]
     moves = [(own_hbm, own_ref), (other_hbm, other_ref), (table_hbm, table_ref)]
     waits = [[(patches_hbm, patches_refs[0])], [(packed_hbm, packed_refs[0])]]
-    for at, source_hbm in ((1, left_hbm), (2, right_hbm)):
+    for at, source_hbm in enumerate(remote_hbm, 1):
         cut = [source_hbm.at[pl.ds(half * rows, rows), :] for half in range(2)]
         waits.append(list(zip(cut, halves[at])))
         waits.append([(source_hbm.at[pl.ds(2 * rows, depth), :], packed_refs[at])])
-    waits.append([(low_hbm, halves[3][0]), (high_hbm, halves[3][1])])
-    waits.append([(far_hbm, packed_refs[3])])
     waits = [[move] for move in moves] + waits
     number = 0
     copies = []
@@ -304,89 +302,78 @@
 
 
 def route_kernel(patch_len, slot_of, *refs):
-    context_refs, routed_refs = refs[:-2], refs[-2:]
-    half = routed_refs[0].shape[0]
-    for routed_ref in routed_refs:
-        routed_ref[...] = jnp.zeros_like(routed_ref)
+    context_refs, routed_refs, table_ref = refs[:4], refs[4:-1], refs[-1]
+    table_ref[...] = jnp.zeros_like(table_ref)
     windows = context_refs[0].shape[0] // patch_len
     for source, context_ref in enumerate(context_refs):
         for window in range(windows):
             slot = slot_of[source * windows + window]
             rows = context_ref[pl.ds(window * patch_len, patch_len), :]
-            for away, routed_ref in enumerate(routed_refs):
-
-                @pl.when((slot >= half) == (away == 1))
-                def _():
-                    for head in range(2):
-                        lanes = pl.ds((2 * source + head) * HD, HD)
-                        here = rows[:, head * LANES : head * LANES + HD]
-                        routed_ref[slot - away * half, :, lanes] = here
+            for head in range(2):
+                lanes = pl.ds((2 * source + head) * HD, HD)
+                table_ref[slot, :, lanes] = rows[:, head * LANES : head * LANES + HD]
+    for at, routed_ref in enumerate(routed_refs):
+        count = routed_ref.shape[0]
+        routed_ref[...] = table_ref[pl.ds(at * count, count)]
 
 
 def route(slot_of, contexts, slots, patch_len):
+    count = len(contexts)
     vmem = pl.BlockSpec(memory_space=pltpu.VMEM)
-    piece = jax.ShapeDtypeStruct((slots // 2, patch_len, 2 * HD * len(contexts)), BF16)
+    shape = (patch_len, 2 * HD * count)
     return pl.pallas_call(
         functools.partial(route_kernel, patch_len),
-        in_specs=[pl.BlockSpec(memory_space=pltpu.SMEM)] + [vmem] * len(contexts),
-        out_specs=[vmem] * 2,
-        out_shape=[piece] * 2,
+        in_specs=[pl.BlockSpec(memory_space=pltpu.SMEM)] + [vmem] * count,
+        out_specs=[vmem] * count,
+        out_shape=[jax.ShapeDtypeStruct((slots // count,) + shape, BF16)] * count,
+        scratch_shapes=[pltpu.VMEM((slots,) + shape, BF16)],
         compiler_params=pltpu.CompilerParams(vmem_limit_bytes=VMEM_BYTES),
         name="route",
     )(slot_of, *contexts)
 
 
-def join_kernel(kept_ref, got_ref, *out_refs):
-    count = out_refs[0].shape[1]
-    for at, out_ref in enumerate(out_refs):
-        out_ref[0] = kept_ref[pl.ds(at * count, count)]
-        out_ref[1] = got_ref[pl.ds(at * count, count)]
-
-
-def join(kept, got, nx):
-    slots, patch_len, width = kept.shape
+def regroup_kernel(count, where, *refs):
+    inputs, outputs = refs[:count], refs[count:]
+    copies = len(outputs) // 2
+    for step in range(copies):
+        target = lax.rem(where[2] + step, copies)
+        for swap in range(2):
+            core = where[1] if swap == 0 else 1 - where[1]
+            for at, ref in enumerate(inputs):
+                outputs[2 * step + swap][at] = ref[2 * target + core]
+
+
+def regroup(where, pieces):
+    slots, patch_len, width = pieces[0].shape
     vmem = pl.BlockSpec(memory_space=pltpu.VMEM)
-    piece = jax.ShapeDtypeStruct((2, slots // nx, patch_len, width), BF16)
+    piece = jax.ShapeDtypeStruct((len(pieces), patch_len, width), BF16)
     return pl.pallas_call(
-        join_kernel,
-        in_specs=[vmem] * 2,
-        out_specs=[vmem] * nx,
-        out_shape=[piece] * nx,
-        compiler_params=pltpu.CompilerParams(vmem_limit_bytes=VMEM_BYTES),
-        name="join",
-    )(kept, got)
-
-
-def regroup_kernel(where, *refs):
-    inputs = [ref for ref in refs if ref.shape[0] == 2]
-    outputs = refs[len(inputs) :]
-    copies = len(outputs)
-    for step, out_ref in enumerate(outputs):
-        target = lax.rem(where[2] + step, copies)
-        for at, ref in enumerate(inputs):
-            for kind in range(2):
-                out_ref[at, kind] = ref[kind, target]
-
-
-def regroup(where, pieces):
-    _, copies, patch_len, width = pieces[0].shape
-    vmem = pl.BlockSpec(memory_space=pltpu.VMEM)
-    piece = jax.ShapeDtypeStruct((len(pieces), 2, patch_len, width), BF16)
-    return pl.pallas_call(
-        regroup_kernel,
+        functools.partial(regroup_kernel, len(pieces)),
         in_specs=[pl.BlockSpec(memory_space=pltpu.SMEM)] + [vmem] * len(pieces),
-        out_specs=[vmem] * copies,
-        out_shape=[piece] * copies,
+        out_specs=[vmem] * slots,
+        out_shape=[piece] * slots,
         compiler_params=pltpu.CompilerParams(vmem_limit_bytes=VMEM_BYTES),
         name="regroup",
     )(where, *pieces)
 
 
+def hop(array, step, swap):
+    copies, cores = lax.axis_size("zl"), lax.axis_size("c")
+    if step == 0 and swap == 0:
+        return array
+    pairs = [
+        (z * cores + c, (z + step) % copies * cores + (c + swap) % cores)
+        for z in range(copies)
+        for c in range(cores)
+    ]
+    return lax.ppermute(array, ("zl", "c"), pairs)
+
+
 def settle_kernel(where, places, *refs):
     arrived_refs, placed_ref = refs[:-1], refs[-1]
-    copies, nx = len(arrived_refs), arrived_refs[0].shape[0]
+    copies, nx = len(arrived_refs) // 2, arrived_refs[0].shape[0]
     steps = ring_steps(nx)
-    for step, arrived_ref in enumerate(arrived_refs):
+    for step in range(copies):
         copy = lax.rem(where[2] + copies - step, copies)
         for swap in range(2):
             core = where[1] if swap == 0 else 1 - where[1]
@@ -396,19 +383,20 @@
                     lane = 2 * steps.index((sender - source) % nx)
                     slot = (copy * nx + source) * 2 + core
                     for kind in range(2):
-                        rows = arrived_ref[at, swap, :, pl.ds((lane + kind) * HD, HD)]
+                        here = pl.ds((lane + kind) * HD, HD)
+                        rows = arrived_refs[2 * step + swap][at, :, here]
                         placed_ref[slot, :, pl.ds((kind * nx + sender) * HD, HD)] = rows
 
 
 def settle(where, places, arrived):
-    nx, _, patch_len, width = arrived[0].shape
+    nx, patch_len, width = arrived[0].shape
     vmem = pl.BlockSpec(memory_space=pltpu.VMEM)
     smem = pl.BlockSpec(memory_space=pltpu.SMEM)
     return pl.pallas_call(
         settle_kernel,
         in_specs=[smem, smem] + [vmem] * len(arrived),
         out_specs=vmem,
-        out_shape=jax.ShapeDtypeStruct((len(arrived) * nx * 2, patch_len, width), BF16),
+        out_shape=jax.ShapeDtypeStruct((len(arrived) * nx, patch_len, width), BF16),
         compiler_params=pltpu.CompilerParams(vmem_limit_bytes=VMEM_BYTES),
         name="settle",
     )(where, places, *arrived)
@@ -474,19 +462,17 @@
     upstream = upstream.reshape(row_total, value_width)
     own, left, right, far = pack(where, counts, dest, coords, patches, values, upstream, nx)
     left, right = ring(left, "x", steps[1]), ring(right, "x", steps[2])
+    far = ring(far, "x", steps[3])
 
     head = core * nx + here
     slice_q = lax.dynamic_slice_in_dim(weight, head * HD, HD, axis=1)
     slice_k = lax.dynamic_slice_in_dim(weight, value_width + head * HD, HD, axis=1)
     own_w = jnp.concatenate([slice_q, slice_k], axis=1)
     own_w = spread(own_w, "zh")
-    far = ring(after(own_w, far), "x", steps[3])
     own_w = jnp.transpose(own_w, (1, 0, 2)).reshape(depth, nz * 2 * HD)
     own_w = spread(own_w, "y").reshape(ny * depth, nz * 2 * HD)
     weights = (own_w, core_swap(own_w))
     left, right, far = after(own_w, (left, right, far))
-    low = ring(right[:row_total], "x", steps[2])
-    high = ring(left[row_total : 2 * row_total], "x", steps[1])
 
     all_dest = [dest[:, 0]]
     for piece in (left, right, far):
@@ -497,23 +483,22 @@
     slot_of = jnp.zeros_like(step_of)
     for at, step in enumerate(steps):
         slot_of = jnp.where(step_of == step, at, slot_of)
-    away = jnp.where(lax.rem(all_dest, nc) == core, 0, nx)
-    slot_of = (away + slot_of) * copies + all_dest // (nc * nx)
+    slot_of = (slot_of * copies + all_dest // (nc * nx)) * nc + lax.rem(all_dest, nc)
 
     *contexts, grad, sent = some_heads(
         after(slot_of, where),
         weights,
         rotary_table(),
-        (patches, own, left, right, low, high, far),
+        (patches, own, left, right, far),
         patch_len,
     )
     grad = (grad.astype(F32) + core_swap(sent).astype(F32)).astype(BF16)
-    contexts = after(grad, contexts)
-    kept, sent = route(slot_of, contexts, slots, patch_len)
-    pieces = join(kept, core_swap(sent), nx)
+    pieces = route(slot_of, contexts, slots, patch_len)
+    grad = after(pieces, grad)
     pieces = [ring(piece, "x", step) for piece, step in zip(pieces, steps)]
+    crossed = pieces
     pieces = regroup(where, pieces)
-    pieces = [ring(piece, "zl", step) for step, piece in enumerate(pieces)]
+    pieces = [hop(piece, at // 2, at % 2) for at, piece in enumerate(pieces)]
     places = [lax.rem(here - sender + nx, nx) for sender in range(nx)]
     places = [sum(jnp.where(at == steps[k], k, 0) for k in range(nx)) for at in places]
     places = jnp.stack(places).astype(jnp.int32)
@@ -522,7 +507,7 @@
     grad = exchange(grad.reshape(ny, depth, nz * 2 * HD), "y")
     grad = jnp.sum(grad.astype(F32), axis=0).astype(BF16)
     grad = jnp.transpose(grad.reshape(depth, nz, 2 * HD), (1, 0, 2))
-    grad = jnp.broadcast_to(grad[None], (copies,) + grad.shape)
+    grad = jnp.broadcast_to(after(crossed, grad)[None], (copies,) + grad.shape)
     grad = exchange(grad.reshape(copies * nz, depth, 2 * HD), ("zl", "zh"))
     grad = jnp.sum(grad.astype(F32), axis=0).astype(BF16)
     return (placed, finish(spread(grad, ("x", "c")), nc))

time: 174 us -> 172 us (0.989)
  starting transfers between devices: 79.8 us -> 91.5 us
  waiting for transfers between devices: 41.5 us -> 34.1 us
  Pallas kernels: 35.8 us -> 31.1 us
    ppermute x10 -> x6, waiting for transfers between devices: 21.8 us -> 1.92 us  [ring(): lax.ppermute(array, axis, [(i, (i + step) % count) for i in range(count)])]
    ppermute x10 -> x6, starting transfers between devices: 34.9 us -> 18.2 us  [ring(): lax.ppermute(array, axis, [(i, (i + step) % count) for i in range(count)])]
    ppermute x0 -> x5, starting transfers between devices: none -> 15.6 us  [hop(): return lax.ppermute(array, ('zl', 'c'), pairs)]
    all_to_all x5, starting transfers between devices: 33.8 us -> 46.1 us  [exchange(): return lax.all_to_all(array, axes, split_axis=0, concat_axis=0, tiled=True)]
    all_to_all x5, waiting for transfers between devices: 16.3 us -> 28.3 us  [exchange(): return lax.all_to_all(array, axes, split_axis=0, concat_axis=0, tiled=True)]
    ppermute x0 -> x5, waiting for transfers between devices: none -> 3.9 us  [hop(): return lax.ppermute(array, ('zl', 'c'), pairs)]
    ppermute x3 -> x2, waiting for transfers between devices: 3.43 us -> 0.01 us  [core_swap(): return lax.ppermute(array, 'c', [(0, 1), (1, 0)])]
    pallas_call x1, Pallas kernels: 5.81 us -> 2.67 us  [route(): pl.pallas_call(functools.partial(route_kernel, patch_len), in_specs=[pl.B...]
  transfers between devices with their start and end apart: 18 -> 18, of which waited for: 8 -> 7; matrix products, arithmetic and copies ran while one was open for 4% -> 4% of each run, Pallas kernels for 8% -> 5%
where the time goes in v9:
time: 172 us; the launch traced here: 171 us
  starting transfers between devices  91.5 us (53%)
  waiting for transfers between devices  34.1 us (20%)
  Pallas kernels  31.1 us (18%)
  local copies, waits for them, and re-layouts  7.43 us (4%)
  other arithmetic  5.79 us (3%)
    all_to_all x5, starting transfers between devices, exchange(): return lax.all_to_all(array, axes, split_axis=0, concat_axis=0, tiled=True)  46.1 us
    all_to_all x5, waiting for transfers between devices, exchange(): return lax.all_to_all(array, axes, split_axis=0, concat_axis=0, tiled=True)  28.3 us
    ppermute x6, starting transfers between devices, ring(): lax.ppermute(array, axis, [(i, (i + step) % count) for i in range(count)])  18.2 us
    pallas_call x1, Pallas kernels, some_heads(): pl.pallas_call(functools.partial(heads_kernel, patch_len, group), in_spec...  16.8 us
    ppermute x5, starting transfers between devices, hop(): return lax.ppermute(array, ('zl', 'c'), pairs)  15.6 us
    ppermute x2, starting transfers between devices, core_swap(): return lax.ppermute(array, 'c', [(0, 1), (1, 0)])  11.6 us
    pallas_call x1, Pallas kernels, pack(): pl.pallas_call(pack_kernel, in_specs=[smem] * 3 + [vmem] * 4, out_specs=[...  4.51 us
    ppermute x5, waiting for transfers between devices, hop(): return lax.ppermute(array, ('zl', 'c'), pairs)  3.9 us
  transfers between devices with their start and end apart: 18, of which 7 were waited for; matrix products, arithmetic and copies ran while one was open for 4% of the time, Pallas kernels for 5%

profile of v9, /device:TPU:1, one launch (start us, length us, event | category | flops | bytes accessed | tf_op | source)
XLA Modules:
  0.0 171.0 jit_solution(5091184661233674741)
XLA Ops:
  0.6 1.3 copy.19.dest
  2.0 0.7 pad_add_fusion.where
  2.6 4.5 %pack.1 = (bf16[208,640]{1,0:T(8,128)(2,1)}, bf16[976,640]{1,0:T(8,128)(2,1)}, bf16[976,640]{1,0:T(8,128)(2,1)}, bf16[976,640]{1,0:T(8,128)(2,1)}) custom-call(s32[3]{0:T(128)} %pad_add_fusion.where, s32[12]{0:T(128)} %counts.1, s32[12,1]{1,0:T(8,128)} %copy.19.dest, s32[12,2,32]{2,1,0:T(2,128)} %coords_ref.1, bf16[384,1280]{1,0:T(8,128)(2,1)} %bitcast.29, ...), custom_call_target="tpu_custom_call" | custom-call | tf_op jit(solution)/shard_map/pack/pallas_call | solution.py:134
  7.2 5.2 %collective-permute-start = (bf16[976,640]{1,0:T(8,128)(2,1)}, bf16[976,640]{1,0:T(8,128)(2,1)}, u32[]{:S(2)}, u32[]{:S(2)}) collective-permute-start(bf16[976,640]{1,0:T(8,128)(2,1)} %get-tuple-element.28), channel_id=1, source_target_pairs={{0,192},{64,0},{128,64},{192,128},{1,193},{65,1},{129,65},{193,129... | collective-permute-start | bytes 3747848 | tf_op jit(solution)/shard_map/ppermute | solution.py:32
  12.4 1.9 %collective-permute-start.1 = (bf16[976,640]{1,0:T(8,128)(2,1)}, bf16[976,640]{1,0:T(8,128)(2,1)S(1)}, u32[]{:S(2)}, u32[]{:S(2)}) collective-permute-start(bf16[976,640]{1,0:T(8,128)(2,1)} %get-tuple-element.29), channel_id=1, source_target_pairs={{0,64},{64,128},{128,192},{192,0},{1,65},{65,129},{129,193},{193,1... | collective-permute-start | bytes 3747848 | tf_op jit(solution)/shard_map/ppermute | solution.py:32
  14.3 3.6 %collective-permute-start.2 = (bf16[976,640]{1,0:T(8,128)(2,1)}, bf16[976,640]{1,0:T(8,128)(2,1)S(1)}, u32[]{:S(2)}, u32[]{:S(2)}) collective-permute-start(bf16[976,640]{1,0:T(8,128)(2,1)} %get-tuple-element.30), channel_id=1, source_target_pairs={{0,128},{64,192},{128,0},{192,64},{1,129},{65,193},{129,1},{193,65... | collective-permute-start | bytes 3747848 | tf_op jit(solution)/shard_map/ppermute | solution.py:32
  17.9 0.8 constant_dynamic-slice_fusion.1
  18.9 0.6 broadcast_in_dim.42
  19.5 14.2 %all-to-all-start = ((bf16[4,40,160]{2,1,0:T(8,128)(2,1)}), bf16[4,40,160]{2,1,0:T(8,128)(2,1)S(1)}, u32[]{:S(2)}, u32[]{:S(2)}) async-start(bf16[4,40,160]{2,1,0:T(8,128)(2,1)} %broadcast_in_dim.42), calls=%async_computation | async-start | bytes 163840 | tf_op jit(solution)/shard_map/all_to_all | solution.py:36
  33.8 9.9 %all-to-all-done = bf16[4,40,160]{2,1,0:T(8,128)(2,1)S(1)} async-done(((bf16[4,40,160]{2,1,0:T(8,128)(2,1)}), bf16[4,40,160]{2,1,0:T(8,128)(2,1)S(1)}, u32[]{:S(2)}, u32[]{:S(2)}) %all-to-all-start) | async-done | bytes 51232 | tf_op jit(solution)/shard_map/all_to_all | solution.py:36
  43.7 0.1 broadcast_in_dim.43
  43.8 0.8 broadcast_in_dim.44
  44.6 6.8 %all-to-all-start.1 = ((bf16[8,40,640]{2,1,0:T(8,128)(2,1)}), bf16[8,40,640]{2,1,0:T(8,128)(2,1)S(1)}, u32[]{:S(2)}, u32[]{:S(2)}) async-start(bf16[8,40,640]{2,1,0:T(8,128)(2,1)} %broadcast_in_dim.44), calls=%async_computation.1 | async-start | bytes 819200 | tf_op jit(solution)/shard_map/all_to_all | solution.py:36
  51.4 0.3 fusion.3
  51.7 0.7 pad_maximum_fusion.refs_2_
  52.4 10.4 %all-to-all-done.1 = bf16[8,40,640]{2,1,0:T(8,128)(2,1)S(1)} async-done(((bf16[8,40,640]{2,1,0:T(8,128)(2,1)}), bf16[8,40,640]{2,1,0:T(8,128)(2,1)S(1)}, u32[]{:S(2)}, u32[]{:S(2)}) %all-to-all-start.1) | async-done | bytes 409632 | tf_op jit(solution)/shard_map/all_to_all | solution.py:36
  62.8 6.7 %collective-permute-start.3 = (bf16[320,640]{1,0:T(8,128)(2,1)S(1)}, bf16[320,640]{1,0:T(8,128)(2,1)S(1)}, u32[]{:S(2)}, u32[]{:S(2)}) collective-permute-start(bf16[320,640]{1,0:T(8,128)(2,1)S(1)} %bitcast.33), channel_id=1, source_target_pairs={{0,32},{32,0},{1,33},{33,1},{2,34},{34,2},{3,35},{35,3},{4,36},{36... | collective-permute-start | bytes 1228808 | tf_op jit(solution)/shard_map/ppermute | solution.py:25
  69.6 0.7 bitcast_convert_fusion.2
  70.3 0.7 multiply_add_fusion.slot_of
  71.0 0.7 copy-done.13
  71.7 16.8 %heads.1 = (bf16[384,256]{1,0:T(8,128)(2,1)}, bf16[384,256]{1,0:T(8,128)(2,1)}, bf16[384,256]{1,0:T(8,128)(2,1)}, bf16[384,256]{1,0:T(8,128)(2,1)}, bf16[320,640]{1,0:T(8,128)(2,1)}, /*index=5*/bf16[320,640]{1,0:T(8,128)(2,1)}) custom-call(s32[3]{0:T(128)} %pad_add_fusion.where, bf16[320,640]{1,0:T(8,128)(2,1)} %bitcast.34, bf16[320,640]{1,0:T(8,128)(2,1)} %copy-done.13, ...), custom_call_target="tpu_custom_call" | custom-call | flops 20000000000 | bytes 12000000 | tf_op jit(solution)/shard_map/heads/pallas_call | solution.py:280
  88.6 4.9 %collective-permute-start.12 = (bf16[320,640]{1,0:T(8,128)(2,1)}, bf16[320,640]{1,0:T(8,128)(2,1)S(1)}, u32[]{:S(2)}, u32[]{:S(2)}) collective-permute-start(bf16[320,640]{1,0:T(8,128)(2,1)} %get-tuple-element.51), channel_id=1, source_target_pairs={{0,32},{32,0},{1,33},{33,1},{2,34},{34,2},{3,35},{35,3},{4,36},{36... | collective-permute-start | bytes 1228808 | tf_op jit(solution)/shard_map/ppermute | solution.py:25
  93.5 2.7 %route.1 = (bf16[6,32,640]{2,1,0:T(8,128)(2,1)}, bf16[6,32,640]{2,1,0:T(8,128)(2,1)}, bf16[6,32,640]{2,1,0:T(8,128)(2,1)}, bf16[6,32,640]{2,1,0:T(8,128)(2,1)}) custom-call(s32[48]{0:T(128)} %multiply_add_fusion.slot_of, bf16[384,256]{1,0:T(8,128)(2,1)} %get-tuple-element.36.refs_0_, bf16[384,256]{1,0:T(8,128)(2,1)} %get-tuple-element.37.refs_1_, ...), custom_call_target="tpu_custom_call" | custom-call | tf_op jit(solution)/shard_map/route/pallas_call | solution.py:324
  96.2 1.9 %add_convert_fusion = bf16[320,640]{1,0:T(8,128)(2,1)} fusion(bf16[320,640]{1,0:T(8,128)(2,1)S(1)} %collective-permute-done.12, bf16[320,640]{1,0:T(8,128)(2,1)} %get-tuple-element.50), kind=kLoop, calls=%fused_computation | loop fusion | flops 819200 | bytes 1228800 | tf_op jit(solution)/shard_map/convert_element_type | solution.py:495
  98.1 6.8 %all-to-all-start.2 = ((bf16[8,40,640]{2,1,0:T(8,128)(2,1)}), bf16[8,40,640]{2,1,0:T(8,128)(2,1)S(1)}, u32[]{:S(2)}, u32[]{:S(2)}) async-start(bf16[8,40,640]{2,1,0:T(8,128)(2,1)} %bitcast.18), calls=%async_computation.2 | async-start | bytes 819200 | tf_op jit(solution)/shard_map/all_to_all | solution.py:36
  105.0 1.9 %collective-permute-start.4 = (bf16[6,32,640]{2,1,0:T(8,128)(2,1)S(1)}, bf16[6,32,640]{2,1,0:T(8,128)(2,1)S(1)}, u32[]{:S(2)}, u32[]{:S(2)}) collective-permute-start(bf16[6,32,640]{2,1,0:T(8,128)(2,1)S(1)} %copy-done.16), channel_id=1, source_target_pairs={{0,192},{64,0},{128,64},{192,128},{1,193},{65,1},{129,65},{193,129... | collective-permute-start | bytes 737288 | tf_op jit(solution)/shard_map/ppermute | solution.py:32
  106.9 3.4 %collective-permute-start.5 = (bf16[6,32,640]{2,1,0:T(8,128)(2,1)S(1)}, bf16[6,32,640]{2,1,0:T(8,128)(2,1)S(1)}, u32[]{:S(2)}, u32[]{:S(2)}) collective-permute-start(bf16[6,32,640]{2,1,0:T(8,128)(2,1)S(1)} %copy-done.15), channel_id=1, source_target_pairs={{0,64},{64,128},{128,192},{192,0},{1,65},{65,129},{129,193},{193,1... | collective-permute-start | bytes 737288 | tf_op jit(solution)/shard_map/ppermute | solution.py:32
  110.3 2.1 %collective-permute-start.6 = (bf16[6,32,640]{2,1,0:T(8,128)(2,1)S(1)}, bf16[6,32,640]{2,1,0:T(8,128)(2,1)S(1)}, u32[]{:S(2)}, u32[]{:S(2)}) collective-permute-start(bf16[6,32,640]{2,1,0:T(8,128)(2,1)S(1)} %copy-done.14), channel_id=1, source_target_pairs={{0,128},{64,192},{128,0},{192,64},{1,129},{65,193},{129,1},{193,65... | collective-permute-start | bytes 737288 | tf_op jit(solution)/shard_map/ppermute | solution.py:32
  112.4 8.0 %all-to-all-done.2 = bf16[8,40,640]{2,1,0:T(8,128)(2,1)S(1)} async-done(((bf16[8,40,640]{2,1,0:T(8,128)(2,1)}), bf16[8,40,640]{2,1,0:T(8,128)(2,1)S(1)}, u32[]{:S(2)}, u32[]{:S(2)}) %all-to-all-start.2) | async-done | bytes 409632 | tf_op jit(solution)/shard_map/all_to_all | solution.py:36
  120.5 0.1 reshape.658
  120.7 1.8 %collective-permute-done.5.refs_2_ = bf16[6,32,640]{2,1,0:T(8,128)(2,1)S(1)} collective-permute-done((bf16[6,32,640]{2,1,0:T(8,128)(2,1)S(1)}, bf16[6,32,640]{2,1,0:T(8,128)(2,1)S(1)}, u32[]{:S(2)}, u32[]{:S(2)}) %collective-permute-start.5) | collective-permute-done | bytes 245792 | tf_op jit(solution)/shard_map/ppermute | solution.py:32
  122.5 0.8 broadcast_in_dim.47
  123.3 14.9 %all-to-all-start.3 = ((bf16[12,40,160]{2,1,0:T(8,128)(2,1)}), bf16[12,40,160]{2,1,0:T(8,128)(2,1)S(1)}, u32[]{:S(2)}, u32[]{:S(2)}) async-start(bf16[12,40,160]{2,1,0:T(8,128)(2,1)} %bitcast.20), calls=%async_computation.3 | async-start | bytes 491520 | tf_op jit(solution)/shard_map/all_to_all | solution.py:36
  138.3 2.4 %regroup.1 = (bf16[4,32,640]{2,1,0:T(8,128)(2,1)}, bf16[4,32,640]{2,1,0:T(8,128)(2,1)}, bf16[4,32,640]{2,1,0:T(8,128)(2,1)}, bf16[4,32,640]{2,1,0:T(8,128)(2,1)}...) custom-call(s32[3]{0:T(128)} %pad_add_fusion.where, bf16[6,32,640]{2,1,0:T(8,128)(2,1)} %get-tuple-element.40.refs_0_, ...), custom_call_target="tpu_custom_call" | custom-call | tf_op jit(solution)/shard_map/regroup/pallas_call | solution.py:350
  140.6 3.3 %collective-permute-start.7 = (bf16[4,32,640]{2,1,0:T(8,128)(2,1)}, bf16[4,32,640]{2,1,0:T(8,128)(2,1)S(1)}, u32[]{:S(2)}, u32[]{:S(2)}) collective-permute-start(bf16[4,32,640]{2,1,0:T(8,128)(2,1)} %get-tuple-element.45), channel_id=1, source_target_pairs={{0,32},{32,0},{256,288},{288,256},{512,544},{544,512},{1,33},{33,1... | collective-permute-start | bytes 491528 | tf_op jit(solution)/shard_map/ppermute | solution.py:369
  143.9 3.6 %collective-permute-start.8 = (bf16[4,32,640]{2,1,0:T(8,128)(2,1)}, bf16[4,32,640]{2,1,0:T(8,128)(2,1)S(1)}, u32[]{:S(2)}, u32[]{:S(2)}) collective-permute-start(bf16[4,32,640]{2,1,0:T(8,128)(2,1)} %get-tuple-element.46), channel_id=1, source_target_pairs={{0,256},{32,288},{256,512},{288,544},{512,0},{544,32},{1,257},{33,... | collective-permute-start | bytes 491528 | tf_op jit(solution)/shard_map/ppermute | solution.py:369
  147.5 3.3 %collective-permute-start.9 = (bf16[4,32,640]{2,1,0:T(8,128)(2,1)}, bf16[4,32,640]{2,1,0:T(8,128)(2,1)S(1)}, u32[]{:S(2)}, u32[]{:S(2)}) collective-permute-start(bf16[4,32,640]{2,1,0:T(8,128)(2,1)} %get-tuple-element.47), channel_id=1, source_target_pairs={{0,288},{32,256},{256,544},{288,512},{512,32},{544,0},{1,289},{33,... | collective-permute-start | bytes 491528 | tf_op jit(solution)/shard_map/ppermute | solution.py:369
  150.8 3.1 %collective-permute-start.10 = (bf16[4,32,640]{2,1,0:T(8,128)(2,1)}, bf16[4,32,640]{2,1,0:T(8,128)(2,1)S(1)}, u32[]{:S(2)}, u32[]{:S(2)}) collective-permute-start(bf16[4,32,640]{2,1,0:T(8,128)(2,1)} %get-tuple-element.48), channel_id=1, source_target_pairs={{0,512},{32,544},{256,0},{288,32},{512,256},{544,288},{1,513},{33,... | collective-permute-start | bytes 491528 | tf_op jit(solution)/shard_map/ppermute | solution.py:369
  153.9 2.3 %collective-permute-start.11 = (bf16[4,32,640]{2,1,0:T(8,128)(2,1)}, bf16[4,32,640]{2,1,0:T(8,128)(2,1)S(1)}, u32[]{:S(2)}, u32[]{:S(2)}) collective-permute-start(bf16[4,32,640]{2,1,0:T(8,128)(2,1)} %get-tuple-element.49), channel_id=1, source_target_pairs={{0,544},{32,512},{256,32},{288,0},{512,288},{544,256},{1,545},{33,... | collective-permute-start | bytes 491528 | tf_op jit(solution)/shard_map/ppermute | solution.py:369
  156.3 0.7 broadcast_in_dim.48
  157.0 3.4 %all-to-all-start.4 = ((bf16[8,40,160]{2,1,0:T(8,128)(2,1)}), bf16[8,40,160]{2,1,0:T(8,128)(2,1)S(1)}, u32[]{:S(2)}, u32[]{:S(2)}) async-start(bf16[8,40,160]{2,1,0:T(8,128)(2,1)} %broadcast_in_dim.48), calls=%async_computation.4 | async-start | bytes 327680 | tf_op jit(solution)/shard_map/all_to_all | solution.py:36
  160.4 0.6 pad_add_fusion.1.places
  161.1 0.3 collective-permute-done.10.refs_4_
  161.4 3.6 %collective-permute-done.11.refs_5_ = bf16[4,32,640]{2,1,0:T(8,128)(2,1)S(1)} collective-permute-done((bf16[4,32,640]{2,1,0:T(8,128)(2,1)}, bf16[4,32,640]{2,1,0:T(8,128)(2,1)S(1)}, u32[]{:S(2)}, u32[]{:S(2)}) %collective-permute-start.11) | collective-permute-done | bytes 163872 | tf_op jit(solution)/shard_map/ppermute | solution.py:369
  165.0 0.6 copy-done.9
  165.6 3.0 %settle.1 = bf16[24,32,640]{2,1,0:T(8,128)(2,1)} custom-call(s32[3]{0:T(128)} %pad_add_fusion.where, s32[4]{0:T(128)} %pad_add_fusion.1.places, bf16[4,32,640]{2,1,0:T(8,128)(2,1)} %get-tuple-element.44.refs_0_, bf16[4,32,640]{2,1,0:T(8,128)(2,1)} %copy-done.5, bf16[4,32,640]{2,1,0:T(8,128)(2,1)} %copy-done.6, bf16[4,32,640]{2,1,0:T(8,128)(2,1)} %copy-done.7, ...), custom_call_target="tpu_custom_call" | custom-call | tf_op jit(solution)/shard_map/settle/pallas_call | solution.py:395
  168.7 0.7 copy-done
  169.3 1.7 %finish.1 = f32[40,1280]{1,0:T(8,128)} custom-call(bf16[8,40,160]{2,1,0:T(8,128)(2,1)} %copy-done), custom_call_target="tpu_custom_call" | custom-call | tf_op jit(solution)/shard_map/finish/pallas_call | solution.py:417
  (56 shorter events, 0.5 us)
Async XLA Ops:
  7.2 62.3 %collective-permute-start = (bf16[976,640]{1,0:T(8,128)(2,1)}, bf16[976,640]{1,0:T(8,128)(2,1)}, u32[]{:S(2)}, u32[]{:S(2)}) collective-permute-start(bf16[976,640]{1,0:T(8,128)(2,1)} %get-tuple-element.28), channel_id=1, source_target_pairs={{0,192},{64,0},{128,64},{192,128},{1,193},{65,1},{129,65},{193,129... | collective-permute-start | bytes 3747848 | tf_op jit(solution)/shard_map/ppermute | solution.py:32
  12.4 57.1 %collective-permute-start.1 = (bf16[976,640]{1,0:T(8,128)(2,1)}, bf16[976,640]{1,0:T(8,128)(2,1)S(1)}, u32[]{:S(2)}, u32[]{:S(2)}) collective-permute-start(bf16[976,640]{1,0:T(8,128)(2,1)} %get-tuple-element.29), channel_id=1, source_target_pairs={{0,64},{64,128},{128,192},{192,0},{1,65},{65,129},{129,193},{193,1... | collective-permute-start | bytes 3747848 | tf_op jit(solution)/shard_map/ppermute | solution.py:32
  14.3 55.3 %collective-permute-start.2 = (bf16[976,640]{1,0:T(8,128)(2,1)}, bf16[976,640]{1,0:T(8,128)(2,1)S(1)}, u32[]{:S(2)}, u32[]{:S(2)}) collective-permute-start(bf16[976,640]{1,0:T(8,128)(2,1)} %get-tuple-element.30), channel_id=1, source_target_pairs={{0,128},{64,192},{128,0},{192,64},{1,129},{65,193},{129,1},{193,65... | collective-permute-start | bytes 3747848 | tf_op jit(solution)/shard_map/ppermute | solution.py:32
  18.9 51.4 %copy-start.10 = (s32[12,1]{0,1:T(1,128)S(1)}, s32[12,1]{0,1:T(1,128)}, u32[]{:S(2)}) copy-start(s32[12,1]{0,1:T(1,128)} %param.12) | copy-start | bytes 148
  19.5 24.1 %all-to-all-start = ((bf16[4,40,160]{2,1,0:T(8,128)(2,1)}), bf16[4,40,160]{2,1,0:T(8,128)(2,1)S(1)}, u32[]{:S(2)}, u32[]{:S(2)}) async-start(bf16[4,40,160]{2,1,0:T(8,128)(2,1)} %broadcast_in_dim.42), calls=%async_computation | async-start | bytes 163840 | tf_op jit(solution)/shard_map/all_to_all | solution.py:36
  44.6 18.2 %all-to-all-start.1 = ((bf16[8,40,640]{2,1,0:T(8,128)(2,1)}), bf16[8,40,640]{2,1,0:T(8,128)(2,1)S(1)}, u32[]{:S(2)}, u32[]{:S(2)}) async-start(bf16[8,40,640]{2,1,0:T(8,128)(2,1)} %broadcast_in_dim.44), calls=%async_computation.1 | async-start | bytes 819200 | tf_op jit(solution)/shard_map/all_to_all | solution.py:36
  62.8 8.2 %copy-start.1 = (bf16[8,40,640]{2,1,0:T(8,128)(2,1)}, bf16[8,40,640]{2,1,0:T(8,128)(2,1)S(1)}, u32[]{:S(2)}) copy-start(bf16[8,40,640]{2,1,0:T(8,128)(2,1)S(1)} %all-to-all-done.1) | copy-start | bytes 1228804
  62.8 8.2 %collective-permute-start.3 = (bf16[320,640]{1,0:T(8,128)(2,1)S(1)}, bf16[320,640]{1,0:T(8,128)(2,1)S(1)}, u32[]{:S(2)}, u32[]{:S(2)}) collective-permute-start(bf16[320,640]{1,0:T(8,128)(2,1)S(1)} %bitcast.33), channel_id=1, source_target_pairs={{0,32},{32,0},{1,33},{33,1},{2,34},{34,2},{3,35},{35,3},{4,36},{36... | collective-permute-start | bytes 1228808 | tf_op jit(solution)/shard_map/ppermute | solution.py:25
  69.5 1.5 copy-start.11
  69.6 1.4 copy-start.12
  71.0 0.8 copy-start.13
  88.6 7.6 %collective-permute-start.12 = (bf16[320,640]{1,0:T(8,128)(2,1)}, bf16[320,640]{1,0:T(8,128)(2,1)S(1)}, u32[]{:S(2)}, u32[]{:S(2)}) collective-permute-start(bf16[320,640]{1,0:T(8,128)(2,1)} %get-tuple-element.51), channel_id=1, source_target_pairs={{0,32},{32,0},{1,33},{33,1},{2,34},{34,2},{3,35},{35,3},{4,36},{36... | collective-permute-start | bytes 1228808 | tf_op jit(solution)/shard_map/ppermute | solution.py:25
  96.2 8.8 %copy-start.16 = (bf16[6,32,640]{2,1,0:T(8,128)(2,1)S(1)}, bf16[6,32,640]{2,1,0:T(8,128)(2,1)}, u32[]{:S(2)}) copy-start(bf16[6,32,640]{2,1,0:T(8,128)(2,1)} %get-tuple-element.41) | copy-start | bytes 737284
  96.2 10.7 %copy-start.15 = (bf16[6,32,640]{2,1,0:T(8,128)(2,1)S(1)}, bf16[6,32,640]{2,1,0:T(8,128)(2,1)}, u32[]{:S(2)}) copy-start(bf16[6,32,640]{2,1,0:T(8,128)(2,1)} %get-tuple-element.42) | copy-start | bytes 737284
  96.2 14.1 %copy-start.14 = (bf16[6,32,640]{2,1,0:T(8,128)(2,1)S(1)}, bf16[6,32,640]{2,1,0:T(8,128)(2,1)}, u32[]{:S(2)}) copy-start(bf16[6,32,640]{2,1,0:T(8,128)(2,1)} %get-tuple-element.43) | copy-start | bytes 737284
  98.1 22.3 %all-to-all-start.2 = ((bf16[8,40,640]{2,1,0:T(8,128)(2,1)}), bf16[8,40,640]{2,1,0:T(8,128)(2,1)S(1)}, u32[]{:S(2)}, u32[]{:S(2)}) async-start(bf16[8,40,640]{2,1,0:T(8,128)(2,1)} %bitcast.18), calls=%async_computation.2 | async-start | bytes 819200 | tf_op jit(solution)/shard_map/all_to_all | solution.py:36
  105.0 15.7 %collective-permute-start.4 = (bf16[6,32,640]{2,1,0:T(8,128)(2,1)S(1)}, bf16[6,32,640]{2,1,0:T(8,128)(2,1)S(1)}, u32[]{:S(2)}, u32[]{:S(2)}) collective-permute-start(bf16[6,32,640]{2,1,0:T(8,128)(2,1)S(1)} %copy-done.16), channel_id=1, source_target_pairs={{0,192},{64,0},{128,64},{192,128},{1,193},{65,1},{129,65},{193,129... | collective-permute-start | bytes 737288 | tf_op jit(solution)/shard_map/ppermute | solution.py:32
  106.9 15.6 %collective-permute-start.5 = (bf16[6,32,640]{2,1,0:T(8,128)(2,1)S(1)}, bf16[6,32,640]{2,1,0:T(8,128)(2,1)S(1)}, u32[]{:S(2)}, u32[]{:S(2)}) collective-permute-start(bf16[6,32,640]{2,1,0:T(8,128)(2,1)S(1)} %copy-done.15), channel_id=1, source_target_pairs={{0,64},{64,128},{128,192},{192,0},{1,65},{65,129},{129,193},{193,1... | collective-permute-start | bytes 737288 | tf_op jit(solution)/shard_map/ppermute | solution.py:32
  110.3 12.3 %collective-permute-start.6 = (bf16[6,32,640]{2,1,0:T(8,128)(2,1)S(1)}, bf16[6,32,640]{2,1,0:T(8,128)(2,1)S(1)}, u32[]{:S(2)}, u32[]{:S(2)}) collective-permute-start(bf16[6,32,640]{2,1,0:T(8,128)(2,1)S(1)} %copy-done.14), channel_id=1, source_target_pairs={{0,128},{64,192},{128,0},{192,64},{1,129},{65,193},{129,1},{193,65... | collective-permute-start | bytes 737288 | tf_op jit(solution)/shard_map/ppermute | solution.py:32
  120.7 17.6 %copy-start.2 = (bf16[6,32,640]{2,1,0:T(8,128)(2,1)}, bf16[6,32,640]{2,1,0:T(8,128)(2,1)S(1)}, u32[]{:S(2)}) copy-start(bf16[6,32,640]{2,1,0:T(8,128)(2,1)S(1)} %collective-permute-done.4.refs_1_) | copy-start | bytes 737284
  122.5 15.7 %copy-start.3 = (bf16[6,32,640]{2,1,0:T(8,128)(2,1)}, bf16[6,32,640]{2,1,0:T(8,128)(2,1)S(1)}, u32[]{:S(2)}) copy-start(bf16[6,32,640]{2,1,0:T(8,128)(2,1)S(1)} %collective-permute-done.5.refs_2_) | copy-start | bytes 737284
  122.5 15.7 %copy-start.4 = (bf16[6,32,640]{2,1,0:T(8,128)(2,1)}, bf16[6,32,640]{2,1,0:T(8,128)(2,1)S(1)}, u32[]{:S(2)}) copy-start(bf16[6,32,640]{2,1,0:T(8,128)(2,1)S(1)} %collective-permute-done.6.refs_3_) | copy-start | bytes 737284
  123.3 32.9 %all-to-all-start.3 = ((bf16[12,40,160]{2,1,0:T(8,128)(2,1)}), bf16[12,40,160]{2,1,0:T(8,128)(2,1)S(1)}, u32[]{:S(2)}, u32[]{:S(2)}) async-start(bf16[12,40,160]{2,1,0:T(8,128)(2,1)} %bitcast.20), calls=%async_computation.3 | async-start | bytes 491520 | tf_op jit(solution)/shard_map/all_to_all | solution.py:36
  140.6 20.4 %collective-permute-start.7 = (bf16[4,32,640]{2,1,0:T(8,128)(2,1)}, bf16[4,32,640]{2,1,0:T(8,128)(2,1)S(1)}, u32[]{:S(2)}, u32[]{:S(2)}) collective-permute-start(bf16[4,32,640]{2,1,0:T(8,128)(2,1)} %get-tuple-element.45), channel_id=1, source_target_pairs={{0,32},{32,0},{256,288},{288,256},{512,544},{544,512},{1,33},{33,1... | collective-permute-start | bytes 491528 | tf_op jit(solution)/shard_map/ppermute | solution.py:369
  143.9 17.1 %collective-permute-start.8 = (bf16[4,32,640]{2,1,0:T(8,128)(2,1)}, bf16[4,32,640]{2,1,0:T(8,128)(2,1)S(1)}, u32[]{:S(2)}, u32[]{:S(2)}) collective-permute-start(bf16[4,32,640]{2,1,0:T(8,128)(2,1)} %get-tuple-element.46), channel_id=1, source_target_pairs={{0,256},{32,288},{256,512},{288,544},{512,0},{544,32},{1,257},{33,... | collective-permute-start | bytes 491528 | tf_op jit(solution)/shard_map/ppermute | solution.py:369
  147.5 13.5 %collective-permute-start.9 = (bf16[4,32,640]{2,1,0:T(8,128)(2,1)}, bf16[4,32,640]{2,1,0:T(8,128)(2,1)S(1)}, u32[]{:S(2)}, u32[]{:S(2)}) collective-permute-start(bf16[4,32,640]{2,1,0:T(8,128)(2,1)} %get-tuple-element.47), channel_id=1, source_target_pairs={{0,288},{32,256},{256,544},{288,512},{512,32},{544,0},{1,289},{33,... | collective-permute-start | bytes 491528 | tf_op jit(solution)/shard_map/ppermute | solution.py:369
  150.8 10.6 %collective-permute-start.10 = (bf16[4,32,640]{2,1,0:T(8,128)(2,1)}, bf16[4,32,640]{2,1,0:T(8,128)(2,1)S(1)}, u32[]{:S(2)}, u32[]{:S(2)}) collective-permute-start(bf16[4,32,640]{2,1,0:T(8,128)(2,1)} %get-tuple-element.48), channel_id=1, source_target_pairs={{0,512},{32,544},{256,0},{288,32},{512,256},{544,288},{1,513},{33,... | collective-permute-start | bytes 491528 | tf_op jit(solution)/shard_map/ppermute | solution.py:369
  153.9 11.1 %collective-permute-start.11 = (bf16[4,32,640]{2,1,0:T(8,128)(2,1)}, bf16[4,32,640]{2,1,0:T(8,128)(2,1)S(1)}, u32[]{:S(2)}, u32[]{:S(2)}) collective-permute-start(bf16[4,32,640]{2,1,0:T(8,128)(2,1)} %get-tuple-element.49), channel_id=1, source_target_pairs={{0,544},{32,512},{256,32},{288,0},{512,288},{544,256},{1,545},{33,... | collective-permute-start | bytes 491528 | tf_op jit(solution)/shard_map/ppermute | solution.py:369
  157.0 11.7 %all-to-all-start.4 = ((bf16[8,40,160]{2,1,0:T(8,128)(2,1)}), bf16[8,40,160]{2,1,0:T(8,128)(2,1)S(1)}, u32[]{:S(2)}, u32[]{:S(2)}) async-start(bf16[8,40,160]{2,1,0:T(8,128)(2,1)} %broadcast_in_dim.48), calls=%async_computation.4 | async-start | bytes 327680 | tf_op jit(solution)/shard_map/all_to_all | solution.py:36
  161.0 3.9 %copy-start.5 = (bf16[4,32,640]{2,1,0:T(8,128)(2,1)}, bf16[4,32,640]{2,1,0:T(8,128)(2,1)S(1)}, u32[]{:S(2)}) copy-start(bf16[4,32,640]{2,1,0:T(8,128)(2,1)S(1)} %collective-permute-done.7.refs_1_) | copy-start | bytes 491524
  161.0 3.9 %copy-start.6 = (bf16[4,32,640]{2,1,0:T(8,128)(2,1)}, bf16[4,32,640]{2,1,0:T(8,128)(2,1)S(1)}, u32[]{:S(2)}) copy-start(bf16[4,32,640]{2,1,0:T(8,128)(2,1)S(1)} %collective-permute-done.8.refs_2_) | copy-start | bytes 491524
  161.1 3.9 %copy-start.7 = (bf16[4,32,640]{2,1,0:T(8,128)(2,1)}, bf16[4,32,640]{2,1,0:T(8,128)(2,1)S(1)}, u32[]{:S(2)}) copy-start(bf16[4,32,640]{2,1,0:T(8,128)(2,1)S(1)} %collective-permute-done.9.refs_3_) | copy-start | bytes 491524
  161.4 3.6 %copy-start.8 = (bf16[4,32,640]{2,1,0:T(8,128)(2,1)}, bf16[4,32,640]{2,1,0:T(8,128)(2,1)S(1)}, u32[]{:S(2)}) copy-start(bf16[4,32,640]{2,1,0:T(8,128)(2,1)S(1)} %collective-permute-done.10.refs_4_) | copy-start | bytes 491524
  165.0 0.7 copy-start.9
  168.7 0.7 copy-start

commit v10 on v9

--- a/solution.py
+++ b/solution.py
@@ -98,7 +98,7 @@
         slot = jnp.where(lane == window, dest[window, 0], slot)
     notes_ref[2:3, :] = live.astype(F32)
     notes_ref[3:4, :] = slot.astype(F32)
-    for packed_ref in packed_refs[1:]:
+    for packed_ref in (left_ref, right_ref):
         packed_ref[:rows, :] = patches_ref[:, :width]
         packed_ref[rows : 2 * rows, :] = patches_ref[:, width:]
     parts = width // (2 * HD)
@@ -135,7 +135,7 @@
         pack_kernel,
         in_specs=[smem] * 3 + [vmem] * 4,
         out_specs=[vmem] * 4,
-        out_shape=[small, large, large, large],
+        out_shape=[small, large, large, small],
         scratch_shapes=[pltpu.VMEM((EXTRA, width), F32)],
         compiler_params=pltpu.CompilerParams(vmem_limit_bytes=VMEM_BYTES),
         name="pack",
@@ -146,7 +146,7 @@
     refs = list(refs)
     take = lambda count: [refs.pop(0) for _ in range(count)]
     own_hbm, other_hbm, table_hbm, patches_hbm, packed_hbm = take(5)
-    remote_hbm = take(3)
+    left_hbm, right_hbm, low_hbm, high_hbm, far_hbm = take(5)
     context_refs = take(4)
     results = take(2)
     own_ref, other_ref, table_ref, whole_ref = take(4)
@@ -159,10 +159,12 @@
     halves = [[ref.at[:, pl.ds(at * width, width)] for at in range(2)] for ref in patches_refs]
     moves = [(own_hbm, own_ref), (other_hbm, other_ref), (table_hbm, table_ref)]
     waits = [[(patches_hbm, patches_refs[0])], [(packed_hbm, packed_refs[0])]]
-    for at, source_hbm in enumerate(remote_hbm, 1):
+    for at, source_hbm in ((1, left_hbm), (2, right_hbm)):
         cut = [source_hbm.at[pl.ds(half * rows, rows), :] for half in range(2)]
         waits.append(list(zip(cut, halves[at])))
         waits.append([(source_hbm.at[pl.ds(2 * rows, depth), :], packed_refs[at])])
+    waits.append([(low_hbm, halves[3][0]), (high_hbm, halves[3][1])])
+    waits.append([(far_hbm, packed_refs[3])])
     waits = [[move] for move in moves] + waits
     number = 0
     copies = []
@@ -455,6 +457,11 @@
     row_total = window_count * patch_len
     depth = weight.shape[0]
 
+    head = core * nx + here
+    slice_q = lax.dynamic_slice_in_dim(weight, head * HD, HD, axis=1)
+    slice_k = lax.dynamic_slice_in_dim(weight, value_width + head * HD, HD, axis=1)
+    own_w = jnp.concatenate([slice_q, slice_k], axis=1)
+    own_w = jnp.broadcast_to(own_w[None], (nz,) + own_w.shape)
     where = jnp.stack([here, core, copy]).astype(jnp.int32)
     steps = ring_steps(nx)
     patches = patches.reshape(row_total, model_width)
@@ -462,14 +469,13 @@
     upstream = upstream.reshape(row_total, value_width)
     own, left, right, far = pack(where, counts, dest, coords, patches, values, upstream, nx)
     left, right = ring(left, "x", steps[1]), ring(right, "x", steps[2])
-    far = ring(far, "x", steps[3])
-
-    head = core * nx + here
-    slice_q = lax.dynamic_slice_in_dim(weight, head * HD, HD, axis=1)
-    slice_k = lax.dynamic_slice_in_dim(weight, value_width + head * HD, HD, axis=1)
-    own_w = jnp.concatenate([slice_q, slice_k], axis=1)
-    own_w = spread(own_w, "zh")
+
+    own_w = exchange(own_w, "zh")
+    far = ring(after(own_w, far), "x", steps[3])
     own_w = jnp.transpose(own_w, (1, 0, 2)).reshape(depth, nz * 2 * HD)
+    low, high = right[:row_total], left[row_total : 2 * row_total]
+    own_w = after((low, high), own_w)
+    low, high = ring(low, "x", steps[2]), ring(high, "x", steps[1])
     own_w = spread(own_w, "y").reshape(ny * depth, nz * 2 * HD)
     weights = (own_w, core_swap(own_w))
     left, right, far = after(own_w, (left, right, far))
@@ -489,7 +495,7 @@
         after(slot_of, where),
         weights,
         rotary_table(),
-        (patches, own, left, right, far),
+        (patches, own, left, right, low, high, far),
         patch_len,
     )
     grad = (grad.astype(F32) + core_swap(sent).astype(F32)).astype(BF16)

time: 172 us -> 174 us (1.012)
  starting transfers between devices: 91.5 us -> 101 us
  waiting for transfers between devices: 34.1 us -> 25.3 us
    all_to_all x5, waiting for transfers between devices: 28.3 us -> 15.8 us  [exchange(): return lax.all_to_all(array, axes, split_axis=0, concat_axis=0, tiled=True)]
    ppermute x6 -> x8, starting transfers between devices: 18.2 us -> 28 us  [ring(): lax.ppermute(array, axis, [(i, (i + step) % count) for i in range(count)])]
    ppermute x6 -> x8, waiting for transfers between devices: 1.92 us -> 5.74 us  [ring(): lax.ppermute(array, axis, [(i, (i + step) % count) for i in range(count)])]
    unnamed x35 -> x37, local copies, waits for them, and re-layouts: 3.44 us -> 3.58 us
  transfers between devices with their start and end apart: 18 -> 20, of which waited for: 7 -> 7; matrix products, arithmetic and copies ran while one was open for 4% -> 3% of each run, Pallas kernels for 5% -> 5%
where the time goes in v10:
time: 174 us; the launch traced here: 173 us
  starting transfers between devices  101 us (58%)
  Pallas kernels  30.7 us (18%)
  waiting for transfers between devices  25.3 us (15%)
  local copies, waits for them, and re-layouts  9.09 us (5%)
  other arithmetic  5.7 us (3%)
    all_to_all x5, starting transfers between devices, exchange(): return lax.all_to_all(array, axes, split_axis=0, concat_axis=0, tiled=True)  46.6 us
    ppermute x8, starting transfers between devices, ring(): lax.ppermute(array, axis, [(i, (i + step) % count) for i in range(count)])  28 us
    pallas_call x1, Pallas kernels, some_heads(): pl.pallas_call(functools.partial(heads_kernel, patch_len, group), in_spec...  16.8 us
    ppermute x5, starting transfers between devices, hop(): return lax.ppermute(array, ('zl', 'c'), pairs)  16.1 us
    all_to_all x5, waiting for transfers between devices, exchange(): return lax.all_to_all(array, axes, split_axis=0, concat_axis=0, tiled=True)  15.8 us
    ppermute x2, starting transfers between devices, core_swap(): return lax.ppermute(array, 'c', [(0, 1), (1, 0)])  10.4 us
    ppermute x8, waiting for transfers between devices, ring(): lax.ppermute(array, axis, [(i, (i + step) % count) for i in range(count)])  5.74 us
    pallas_call x1, Pallas kernels, pack(): pl.pallas_call(pack_kernel, in_specs=[smem] * 3 + [vmem] * 4, out_specs=[...  4.1 us
  transfers between devices with their start and end apart: 20, of which 7 were waited for; matrix products, arithmetic and copies ran while one was open for 3% of the time, Pallas kernels for 5%

profile of v10, /device:TPU:1, one launch (start us, length us, event | category | flops | bytes accessed | tf_op | source)
XLA Modules:
  0.0 173.0 jit_solution(2129054510331425300)
XLA Ops:
  0.6 1.3 copy.18.dest
  2.0 0.6 pad_add_fusion.where
  2.6 4.1 %pack.1 = (bf16[208,640]{1,0:T(8,128)(2,1)}, bf16[976,640]{1,0:T(8,128)(2,1)}, bf16[976,640]{1,0:T(8,128)(2,1)}, bf16[208,640]{1,0:T(8,128)(2,1)}) custom-call(s32[3]{0:T(128)} %pad_add_fusion.where, s32[12]{0:T(128)} %counts.1, s32[12,1]{1,0:T(8,128)} %copy.18.dest, s32[12,2,32]{2,1,0:T(2,128)} %coords_ref.1, bf16[384,1280]{1,0:T(8,128)(2,1)} %bitcast.29, ...), custom_call_target="tpu_custom_call" | custom-call | tf_op jit(solution)/shard_map/pack/pallas_call | solution.py:134
  6.7 3.9 %collective-permute-start = (bf16[976,640]{1,0:T(8,128)(2,1)}, bf16[976,640]{1,0:T(8,128)(2,1)S(1)}, u32[]{:S(2)}, u32[]{:S(2)}) collective-permute-start(bf16[976,640]{1,0:T(8,128)(2,1)} %get-tuple-element.30), channel_id=1, source_target_pairs={{0,64},{64,128},{128,192},{192,0},{1,65},{65,129},{129,193},{193,1... | collective-permute-start | bytes 3747848 | tf_op jit(solution)/shard_map/ppermute | solution.py:32
  10.6 3.2 %collective-permute-start.1 = (bf16[976,640]{1,0:T(8,128)(2,1)}, bf16[976,640]{1,0:T(8,128)(2,1)}, u32[]{:S(2)}, u32[]{:S(2)}) collective-permute-start(bf16[976,640]{1,0:T(8,128)(2,1)} %get-tuple-element.31), channel_id=1, source_target_pairs={{0,192},{64,0},{128,64},{192,128},{1,193},{65,1},{129,65},{193,129... | collective-permute-start | bytes 3747848 | tf_op jit(solution)/shard_map/ppermute | solution.py:32
  13.8 0.8 constant_dynamic-slice_fusion.1
  14.7 0.6 broadcast_in_dim.23
  15.4 14.4 %all-to-all-start = ((bf16[4,40,160]{2,1,0:T(8,128)(2,1)}), bf16[4,40,160]{2,1,0:T(8,128)(2,1)S(1)}, u32[]{:S(2)}, u32[]{:S(2)}) async-start(bf16[4,40,160]{2,1,0:T(8,128)(2,1)} %broadcast_in_dim.23), calls=%async_computation | async-start | bytes 163840 | tf_op jit(solution)/shard_map/all_to_all | solution.py:36
  29.8 9.9 %all-to-all-done = bf16[4,40,160]{2,1,0:T(8,128)(2,1)S(1)} async-done(((bf16[4,40,160]{2,1,0:T(8,128)(2,1)}), bf16[4,40,160]{2,1,0:T(8,128)(2,1)S(1)}, u32[]{:S(2)}, u32[]{:S(2)}) %all-to-all-start) | async-done | bytes 51232 | tf_op jit(solution)/shard_map/all_to_all | solution.py:36
  40.0 1.5 slice.21
  41.4 0.8 broadcast_in_dim.24
  42.2 7.3 %all-to-all-start.1 = ((bf16[8,40,640]{2,1,0:T(8,128)(2,1)}), bf16[8,40,640]{2,1,0:T(8,128)(2,1)S(1)}, u32[]{:S(2)}, u32[]{:S(2)}) async-start(bf16[8,40,640]{2,1,0:T(8,128)(2,1)} %broadcast_in_dim.24), calls=%async_computation.1 | async-start | bytes 819200 | tf_op jit(solution)/shard_map/all_to_all | solution.py:36
  49.6 4.4 %collective-permute-start.2 = (bf16[208,640]{1,0:T(8,128)(2,1)}, bf16[208,640]{1,0:T(8,128)(2,1)S(1)}, u32[]{:S(2)}, u32[]{:S(2)}) collective-permute-start(bf16[208,640]{1,0:T(8,128)(2,1)} %get-tuple-element.34), channel_id=1, source_target_pairs={{0,128},{64,192},{128,0},{192,64},{1,129},{65,193},{129,1},{193,65... | collective-permute-start | bytes 798728 | tf_op jit(solution)/shard_map/ppermute | solution.py:32
  54.2 0.7 pad_maximum_fusion.refs_2_
  54.9 2.7 %collective-permute-start.4 = (bf16[384,640]{1,0:T(8,128)(2,1)S(1)}, bf16[384,640]{1,0:T(8,128)(2,1)S(1)}, u32[]{:S(2)}, u32[]{:S(2)}) collective-permute-start(bf16[384,640]{1,0:T(8,128)(2,1)S(1)} %slice.20), channel_id=1, source_target_pairs={{0,64},{64,128},{128,192},{192,0},{1,65},{65,129},{129,193},{193,1... | collective-permute-start | bytes 1474568 | tf_op jit(solution)/shard_map/ppermute | solution.py:32
  57.6 3.8 %collective-permute-start.5 = (bf16[384,640]{1,0:T(8,128)(2,1)S(1)}, bf16[384,640]{1,0:T(8,128)(2,1)}, u32[]{:S(2)}, u32[]{:S(2)}) collective-permute-start(bf16[384,640]{1,0:T(8,128)(2,1)S(1)} %slice.21), channel_id=1, source_target_pairs={{0,192},{64,0},{128,64},{192,128},{1,193},{65,1},{129,65},{193,129... | collective-permute-start | bytes 1474568 | tf_op jit(solution)/shard_map/ppermute | solution.py:32
  61.4 0.5 all-to-all-done.1
  61.9 5.7 %collective-permute-start.3 = (bf16[320,640]{1,0:T(8,128)(2,1)S(1)}, bf16[320,640]{1,0:T(8,128)(2,1)S(1)}, u32[]{:S(2)}, u32[]{:S(2)}) collective-permute-start(bf16[320,640]{1,0:T(8,128)(2,1)S(1)} %bitcast.33), channel_id=1, source_target_pairs={{0,32},{32,0},{1,33},{33,1},{2,34},{34,2},{3,35},{35,3},{4,36},{36... | collective-permute-start | bytes 1228808 | tf_op jit(solution)/shard_map/ppermute | solution.py:25
  67.6 0.7 bitcast_convert_fusion.2
  68.3 0.6 multiply_add_fusion.slot_of
  69.0 1.3 collective-permute-done.4.refs_7_
  70.4 0.7 copy-done.13
  71.2 16.8 %heads.1 = (bf16[384,256]{1,0:T(8,128)(2,1)}, bf16[384,256]{1,0:T(8,128)(2,1)}, bf16[384,256]{1,0:T(8,128)(2,1)}, bf16[384,256]{1,0:T(8,128)(2,1)}, bf16[320,640]{1,0:T(8,128)(2,1)}, /*index=5*/bf16[320,640]{1,0:T(8,128)(2,1)}) custom-call(s32[3]{0:T(128)} %pad_add_fusion.where, bf16[320,640]{1,0:T(8,128)(2,1)} %bitcast.34, bf16[320,640]{1,0:T(8,128)(2,1)} %copy-done.14, ...), custom_call_target="tpu_custom_call" | custom-call | flops 20000000000 | bytes 12000000 | tf_op jit(solution)/shard_map/heads/pallas_call | solution.py:282
  88.0 4.7 %collective-permute-start.14 = (bf16[320,640]{1,0:T(8,128)(2,1)}, bf16[320,640]{1,0:T(8,128)(2,1)S(1)}, u32[]{:S(2)}, u32[]{:S(2)}) collective-permute-start(bf16[320,640]{1,0:T(8,128)(2,1)} %get-tuple-element.55), channel_id=1, source_target_pairs={{0,32},{32,0},{1,33},{33,1},{2,34},{34,2},{3,35},{35,3},{4,36},{36... | collective-permute-start | bytes 1228808 | tf_op jit(solution)/shard_map/ppermute | solution.py:25
  92.7 2.7 %route.1 = (bf16[6,32,640]{2,1,0:T(8,128)(2,1)}, bf16[6,32,640]{2,1,0:T(8,128)(2,1)}, bf16[6,32,640]{2,1,0:T(8,128)(2,1)}, bf16[6,32,640]{2,1,0:T(8,128)(2,1)}) custom-call(s32[48]{0:T(128)} %multiply_add_fusion.slot_of, bf16[384,256]{1,0:T(8,128)(2,1)} %get-tuple-element.40.refs_0_, bf16[384,256]{1,0:T(8,128)(2,1)} %get-tuple-element.41.refs_1_, ...), custom_call_target="tpu_custom_call" | custom-call | tf_op jit(solution)/shard_map/route/pallas_call | solution.py:326
  95.5 1.9 %add_convert_fusion = bf16[320,640]{1,0:T(8,128)(2,1)} fusion(bf16[320,640]{1,0:T(8,128)(2,1)S(1)} %collective-permute-done.14, bf16[320,640]{1,0:T(8,128)(2,1)} %get-tuple-element.54), kind=kLoop, calls=%fused_computation | loop fusion | flops 819200 | bytes 1228800 | tf_op jit(solution)/shard_map/convert_element_type | solution.py:501
  97.4 6.6 %all-to-all-start.2 = ((bf16[8,40,640]{2,1,0:T(8,128)(2,1)}), bf16[8,40,640]{2,1,0:T(8,128)(2,1)S(1)}, u32[]{:S(2)}, u32[]{:S(2)}) async-start(bf16[8,40,640]{2,1,0:T(8,128)(2,1)} %bitcast.18), calls=%async_computation.2 | async-start | bytes 819200 | tf_op jit(solution)/shard_map/all_to_all | solution.py:36
  104.0 5.0 %collective-permute-start.6 = (bf16[6,32,640]{2,1,0:T(8,128)(2,1)S(1)}, bf16[6,32,640]{2,1,0:T(8,128)(2,1)S(1)}, u32[]{:S(2)}, u32[]{:S(2)}) collective-permute-start(bf16[6,32,640]{2,1,0:T(8,128)(2,1)S(1)} %copy-done.17), channel_id=1, source_target_pairs={{0,192},{64,0},{128,64},{192,128},{1,193},{65,1},{129,65},{193,129... | collective-permute-start | bytes 737288 | tf_op jit(solution)/shard_map/ppermute | solution.py:32
  109.0 1.9 %collective-permute-start.7 = (bf16[6,32,640]{2,1,0:T(8,128)(2,1)S(1)}, bf16[6,32,640]{2,1,0:T(8,128)(2,1)S(1)}, u32[]{:S(2)}, u32[]{:S(2)}) collective-permute-start(bf16[6,32,640]{2,1,0:T(8,128)(2,1)S(1)} %copy-done.16), channel_id=1, source_target_pairs={{0,64},{64,128},{128,192},{192,0},{1,65},{65,129},{129,193},{193,1... | collective-permute-start | bytes 737288 | tf_op jit(solution)/shard_map/ppermute | solution.py:32
  111.0 3.1 %collective-permute-start.8 = (bf16[6,32,640]{2,1,0:T(8,128)(2,1)S(1)}, bf16[6,32,640]{2,1,0:T(8,128)(2,1)S(1)}, u32[]{:S(2)}, u32[]{:S(2)}) collective-permute-start(bf16[6,32,640]{2,1,0:T(8,128)(2,1)S(1)} %copy-done.15), channel_id=1, source_target_pairs={{0,128},{64,192},{128,0},{192,64},{1,129},{65,193},{129,1},{193,65... | collective-permute-start | bytes 737288 | tf_op jit(solution)/shard_map/ppermute | solution.py:32
  114.1 5.4 %all-to-all-done.2 = bf16[8,40,640]{2,1,0:T(8,128)(2,1)S(1)} async-done(((bf16[8,40,640]{2,1,0:T(8,128)(2,1)}), bf16[8,40,640]{2,1,0:T(8,128)(2,1)S(1)}, u32[]{:S(2)}, u32[]{:S(2)}) %all-to-all-start.2) | async-done | bytes 409632 | tf_op jit(solution)/shard_map/all_to_all | solution.py:36
  119.7 4.4 %collective-permute-done.7.refs_2_ = bf16[6,32,640]{2,1,0:T(8,128)(2,1)S(1)} collective-permute-done((bf16[6,32,640]{2,1,0:T(8,128)(2,1)S(1)}, bf16[6,32,640]{2,1,0:T(8,128)(2,1)S(1)}, u32[]{:S(2)}, u32[]{:S(2)}) %collective-permute-start.7) | collective-permute-done | bytes 245792 | tf_op jit(solution)/shard_map/ppermute | solution.py:32
  124.1 0.8 broadcast_in_dim.45
  124.9 14.9 %all-to-all-start.3 = ((bf16[12,40,160]{2,1,0:T(8,128)(2,1)}), bf16[12,40,160]{2,1,0:T(8,128)(2,1)S(1)}, u32[]{:S(2)}, u32[]{:S(2)}) async-start(bf16[12,40,160]{2,1,0:T(8,128)(2,1)} %bitcast.20), calls=%async_computation.3 | async-start | bytes 491520 | tf_op jit(solution)/shard_map/all_to_all | solution.py:36
  139.8 2.3 %regroup.1 = (bf16[4,32,640]{2,1,0:T(8,128)(2,1)}, bf16[4,32,640]{2,1,0:T(8,128)(2,1)}, bf16[4,32,640]{2,1,0:T(8,128)(2,1)}, bf16[4,32,640]{2,1,0:T(8,128)(2,1)}...) custom-call(s32[3]{0:T(128)} %pad_add_fusion.where, bf16[6,32,640]{2,1,0:T(8,128)(2,1)} %get-tuple-element.44.refs_0_, ...), custom_call_target="tpu_custom_call" | custom-call | tf_op jit(solution)/shard_map/regroup/pallas_call | solution.py:352
  142.2 3.9 %collective-permute-start.9 = (bf16[4,32,640]{2,1,0:T(8,128)(2,1)}, bf16[4,32,640]{2,1,0:T(8,128)(2,1)S(1)}, u32[]{:S(2)}, u32[]{:S(2)}) collective-permute-start(bf16[4,32,640]{2,1,0:T(8,128)(2,1)} %get-tuple-element.49), channel_id=1, source_target_pairs={{0,32},{32,0},{256,288},{288,256},{512,544},{544,512},{1,33},{33,1... | collective-permute-start | bytes 491528 | tf_op jit(solution)/shard_map/ppermute | solution.py:371
  146.0 3.6 %collective-permute-start.10 = (bf16[4,32,640]{2,1,0:T(8,128)(2,1)}, bf16[4,32,640]{2,1,0:T(8,128)(2,1)S(1)}, u32[]{:S(2)}, u32[]{:S(2)}) collective-permute-start(bf16[4,32,640]{2,1,0:T(8,128)(2,1)} %get-tuple-element.50), channel_id=1, source_target_pairs={{0,256},{32,288},{256,512},{288,544},{512,0},{544,32},{1,257},{33,... | collective-permute-start | bytes 491528 | tf_op jit(solution)/shard_map/ppermute | solution.py:371
  149.6 3.3 %collective-permute-start.11 = (bf16[4,32,640]{2,1,0:T(8,128)(2,1)}, bf16[4,32,640]{2,1,0:T(8,128)(2,1)S(1)}, u32[]{:S(2)}, u32[]{:S(2)}) collective-permute-start(bf16[4,32,640]{2,1,0:T(8,128)(2,1)} %get-tuple-element.51), channel_id=1, source_target_pairs={{0,288},{32,256},{256,544},{288,512},{512,32},{544,0},{1,289},{33,... | collective-permute-start | bytes 491528 | tf_op jit(solution)/shard_map/ppermute | solution.py:371
  152.9 3.1 %collective-permute-start.12 = (bf16[4,32,640]{2,1,0:T(8,128)(2,1)}, bf16[4,32,640]{2,1,0:T(8,128)(2,1)S(1)}, u32[]{:S(2)}, u32[]{:S(2)}) collective-permute-start(bf16[4,32,640]{2,1,0:T(8,128)(2,1)} %get-tuple-element.52), channel_id=1, source_target_pairs={{0,512},{32,544},{256,0},{288,32},{512,256},{544,288},{1,513},{33,... | collective-permute-start | bytes 491528 | tf_op jit(solution)/shard_map/ppermute | solution.py:371
  156.0 2.3 %collective-permute-start.13 = (bf16[4,32,640]{2,1,0:T(8,128)(2,1)}, bf16[4,32,640]{2,1,0:T(8,128)(2,1)S(1)}, u32[]{:S(2)}, u32[]{:S(2)}) collective-permute-start(bf16[4,32,640]{2,1,0:T(8,128)(2,1)} %get-tuple-element.53), channel_id=1, source_target_pairs={{0,544},{32,512},{256,32},{288,0},{512,288},{544,256},{1,545},{33,... | collective-permute-start | bytes 491528 | tf_op jit(solution)/shard_map/ppermute | solution.py:371
  158.4 0.7 broadcast_in_dim.46
  159.1 3.4 %all-to-all-start.4 = ((bf16[8,40,160]{2,1,0:T(8,128)(2,1)}), bf16[8,40,160]{2,1,0:T(8,128)(2,1)S(1)}, u32[]{:S(2)}, u32[]{:S(2)}) async-start(bf16[8,40,160]{2,1,0:T(8,128)(2,1)} %broadcast_in_dim.46), calls=%async_computation.4 | async-start | bytes 327680 | tf_op jit(solution)/shard_map/all_to_all | solution.py:36
  162.5 0.7 pad_add_fusion.1.places
  163.3 3.6 %collective-permute-done.13.refs_5_ = bf16[4,32,640]{2,1,0:T(8,128)(2,1)S(1)} collective-permute-done((bf16[4,32,640]{2,1,0:T(8,128)(2,1)}, bf16[4,32,640]{2,1,0:T(8,128)(2,1)S(1)}, u32[]{:S(2)}, u32[]{:S(2)}) %collective-permute-start.13) | collective-permute-done | bytes 163872 | tf_op jit(solution)/shard_map/ppermute | solution.py:371
  166.9 0.7 copy-done.10
  167.6 3.0 %settle.1 = bf16[24,32,640]{2,1,0:T(8,128)(2,1)} custom-call(s32[3]{0:T(128)} %pad_add_fusion.where, s32[4]{0:T(128)} %pad_add_fusion.1.places, bf16[4,32,640]{2,1,0:T(8,128)(2,1)} %get-tuple-element.48.refs_0_, bf16[4,32,640]{2,1,0:T(8,128)(2,1)} %copy-done.6, bf16[4,32,640]{2,1,0:T(8,128)(2,1)} %copy-done.7, bf16[4,32,640]{2,1,0:T(8,128)(2,1)} %copy-done.8, ...), custom_call_target="tpu_custom_call" | custom-call | tf_op jit(solution)/shard_map/settle/pallas_call | solution.py:397
  170.6 0.7 copy-done
  171.3 1.7 finish.1
  (64 shorter events, 1.2 us)
Async XLA Ops:
  6.7 33.2 %collective-permute-start = (bf16[976,640]{1,0:T(8,128)(2,1)}, bf16[976,640]{1,0:T(8,128)(2,1)S(1)}, u32[]{:S(2)}, u32[]{:S(2)}) collective-permute-start(bf16[976,640]{1,0:T(8,128)(2,1)} %get-tuple-element.30), channel_id=1, source_target_pairs={{0,64},{64,128},{128,192},{192,0},{1,65},{65,129},{129,193},{193,1... | collective-permute-start | bytes 3747848 | tf_op jit(solution)/shard_map/ppermute | solution.py:32
  10.6 29.3 %collective-permute-start.1 = (bf16[976,640]{1,0:T(8,128)(2,1)}, bf16[976,640]{1,0:T(8,128)(2,1)}, u32[]{:S(2)}, u32[]{:S(2)}) collective-permute-start(bf16[976,640]{1,0:T(8,128)(2,1)} %get-tuple-element.31), channel_id=1, source_target_pairs={{0,192},{64,0},{128,64},{192,128},{1,193},{65,1},{129,65},{193,129... | collective-permute-start | bytes 3747848 | tf_op jit(solution)/shard_map/ppermute | solution.py:32
  15.4 24.3 %all-to-all-start = ((bf16[4,40,160]{2,1,0:T(8,128)(2,1)}), bf16[4,40,160]{2,1,0:T(8,128)(2,1)S(1)}, u32[]{:S(2)}, u32[]{:S(2)}) async-start(bf16[4,40,160]{2,1,0:T(8,128)(2,1)} %broadcast_in_dim.23), calls=%async_computation | async-start | bytes 163840 | tf_op jit(solution)/shard_map/all_to_all | solution.py:36
  39.9 28.4 %copy-start.5 = (bf16[976,640]{1,0:T(8,128)(2,1)}, bf16[976,640]{1,0:T(8,128)(2,1)S(1)}, u32[]{:S(2)}) copy-start(bf16[976,640]{1,0:T(8,128)(2,1)S(1)} %collective-permute-done.refs_6_) | copy-start | bytes 3747844
  39.9 28.4 %copy-start.11 = (s32[12,1]{0,1:T(1,128)S(1)}, s32[12,1]{0,1:T(1,128)}, u32[]{:S(2)}) copy-start(s32[12,1]{0,1:T(1,128)} %param.12) | copy-start | bytes 148
  42.2 19.7 %all-to-all-start.1 = ((bf16[8,40,640]{2,1,0:T(8,128)(2,1)}), bf16[8,40,640]{2,1,0:T(8,128)(2,1)S(1)}, u32[]{:S(2)}, u32[]{:S(2)}) async-start(bf16[8,40,640]{2,1,0:T(8,128)(2,1)} %broadcast_in_dim.24), calls=%async_computation.1 | async-start | bytes 819200 | tf_op jit(solution)/shard_map/all_to_all | solution.py:36
  49.6 18.1 %collective-permute-start.2 = (bf16[208,640]{1,0:T(8,128)(2,1)}, bf16[208,640]{1,0:T(8,128)(2,1)S(1)}, u32[]{:S(2)}, u32[]{:S(2)}) collective-permute-start(bf16[208,640]{1,0:T(8,128)(2,1)} %get-tuple-element.34), channel_id=1, source_target_pairs={{0,128},{64,192},{128,0},{192,64},{1,129},{65,193},{129,1},{193,65... | collective-permute-start | bytes 798728 | tf_op jit(solution)/shard_map/ppermute | solution.py:32
  54.9 15.4 %collective-permute-start.4 = (bf16[384,640]{1,0:T(8,128)(2,1)S(1)}, bf16[384,640]{1,0:T(8,128)(2,1)S(1)}, u32[]{:S(2)}, u32[]{:S(2)}) collective-permute-start(bf16[384,640]{1,0:T(8,128)(2,1)S(1)} %slice.20), channel_id=1, source_target_pairs={{0,64},{64,128},{128,192},{192,0},{1,65},{65,129},{129,193},{193,1... | collective-permute-start | bytes 1474568 | tf_op jit(solution)/shard_map/ppermute | solution.py:32
  57.6 12.7 %collective-permute-start.5 = (bf16[384,640]{1,0:T(8,128)(2,1)S(1)}, bf16[384,640]{1,0:T(8,128)(2,1)}, u32[]{:S(2)}, u32[]{:S(2)}) collective-permute-start(bf16[384,640]{1,0:T(8,128)(2,1)S(1)} %slice.21), channel_id=1, source_target_pairs={{0,192},{64,0},{128,64},{192,128},{1,193},{65,1},{129,65},{193,129... | collective-permute-start | bytes 1474568 | tf_op jit(solution)/shard_map/ppermute | solution.py:32
  61.9 8.4 %copy-start.1 = (bf16[8,40,640]{2,1,0:T(8,128)(2,1)}, bf16[8,40,640]{2,1,0:T(8,128)(2,1)S(1)}, u32[]{:S(2)}) copy-start(bf16[8,40,640]{2,1,0:T(8,128)(2,1)S(1)} %all-to-all-done.1) | copy-start | bytes 1228804
  61.9 8.4 %collective-permute-start.3 = (bf16[320,640]{1,0:T(8,128)(2,1)S(1)}, bf16[320,640]{1,0:T(8,128)(2,1)S(1)}, u32[]{:S(2)}, u32[]{:S(2)}) collective-permute-start(bf16[320,640]{1,0:T(8,128)(2,1)S(1)} %bitcast.33), channel_id=1, source_target_pairs={{0,32},{32,0},{1,33},{33,1},{2,34},{34,2},{3,35},{35,3},{4,36},{36... | collective-permute-start | bytes 1228808 | tf_op jit(solution)/shard_map/ppermute | solution.py:25
  67.6 2.7 %copy-start.12 = (bf16[208,640]{1,0:T(8,128)(2,1)}, bf16[208,640]{1,0:T(8,128)(2,1)S(1)}, u32[]{:S(2)}) copy-start(bf16[208,640]{1,0:T(8,128)(2,1)S(1)} %collective-permute-done.2.refs_9_) | copy-start | bytes 798724
  70.3 0.8 copy-start.13
  70.3 0.9 copy-start.14
  88.0 7.4 %collective-permute-start.14 = (bf16[320,640]{1,0:T(8,128)(2,1)}, bf16[320,640]{1,0:T(8,128)(2,1)S(1)}, u32[]{:S(2)}, u32[]{:S(2)}) collective-permute-start(bf16[320,640]{1,0:T(8,128)(2,1)} %get-tuple-element.55), channel_id=1, source_target_pairs={{0,32},{32,0},{1,33},{33,1},{2,34},{34,2},{3,35},{35,3},{4,36},{36... | collective-permute-start | bytes 1228808 | tf_op jit(solution)/shard_map/ppermute | solution.py:25
  95.4 8.6 %copy-start.17 = (bf16[6,32,640]{2,1,0:T(8,128)(2,1)S(1)}, bf16[6,32,640]{2,1,0:T(8,128)(2,1)}, u32[]{:S(2)}) copy-start(bf16[6,32,640]{2,1,0:T(8,128)(2,1)} %get-tuple-element.45) | copy-start | bytes 737284
  95.4 13.6 %copy-start.16 = (bf16[6,32,640]{2,1,0:T(8,128)(2,1)S(1)}, bf16[6,32,640]{2,1,0:T(8,128)(2,1)}, u32[]{:S(2)}) copy-start(bf16[6,32,640]{2,1,0:T(8,128)(2,1)} %get-tuple-element.46) | copy-start | bytes 737284
  95.4 15.5 %copy-start.15 = (bf16[6,32,640]{2,1,0:T(8,128)(2,1)S(1)}, bf16[6,32,640]{2,1,0:T(8,128)(2,1)}, u32[]{:S(2)}) copy-start(bf16[6,32,640]{2,1,0:T(8,128)(2,1)} %get-tuple-element.47) | copy-start | bytes 737284
  97.4 22.1 %all-to-all-start.2 = ((bf16[8,40,640]{2,1,0:T(8,128)(2,1)}), bf16[8,40,640]{2,1,0:T(8,128)(2,1)S(1)}, u32[]{:S(2)}, u32[]{:S(2)}) async-start(bf16[8,40,640]{2,1,0:T(8,128)(2,1)} %bitcast.18), calls=%async_computation.2 | async-start | bytes 819200 | tf_op jit(solution)/shard_map/all_to_all | solution.py:36
  104.0 15.7 %collective-permute-start.6 = (bf16[6,32,640]{2,1,0:T(8,128)(2,1)S(1)}, bf16[6,32,640]{2,1,0:T(8,128)(2,1)S(1)}, u32[]{:S(2)}, u32[]{:S(2)}) collective-permute-start(bf16[6,32,640]{2,1,0:T(8,128)(2,1)S(1)} %copy-done.17), channel_id=1, source_target_pairs={{0,192},{64,0},{128,64},{192,128},{1,193},{65,1},{129,65},{193,129... | collective-permute-start | bytes 737288 | tf_op jit(solution)/shard_map/ppermute | solution.py:32
  109.0 15.1 %collective-permute-start.7 = (bf16[6,32,640]{2,1,0:T(8,128)(2,1)S(1)}, bf16[6,32,640]{2,1,0:T(8,128)(2,1)S(1)}, u32[]{:S(2)}, u32[]{:S(2)}) collective-permute-start(bf16[6,32,640]{2,1,0:T(8,128)(2,1)S(1)} %copy-done.16), channel_id=1, source_target_pairs={{0,64},{64,128},{128,192},{192,0},{1,65},{65,129},{129,193},{193,1... | collective-permute-start | bytes 737288 | tf_op jit(solution)/shard_map/ppermute | solution.py:32
  111.0 13.1 %collective-permute-start.8 = (bf16[6,32,640]{2,1,0:T(8,128)(2,1)S(1)}, bf16[6,32,640]{2,1,0:T(8,128)(2,1)S(1)}, u32[]{:S(2)}, u32[]{:S(2)}) collective-permute-start(bf16[6,32,640]{2,1,0:T(8,128)(2,1)S(1)} %copy-done.15), channel_id=1, source_target_pairs={{0,128},{64,192},{128,0},{192,64},{1,129},{65,193},{129,1},{193,65... | collective-permute-start | bytes 737288 | tf_op jit(solution)/shard_map/ppermute | solution.py:32
  119.7 20.1 %copy-start.2 = (bf16[6,32,640]{2,1,0:T(8,128)(2,1)}, bf16[6,32,640]{2,1,0:T(8,128)(2,1)S(1)}, u32[]{:S(2)}) copy-start(bf16[6,32,640]{2,1,0:T(8,128)(2,1)S(1)} %collective-permute-done.6.refs_1_) | copy-start | bytes 737284
  124.1 15.7 %copy-start.3 = (bf16[6,32,640]{2,1,0:T(8,128)(2,1)}, bf16[6,32,640]{2,1,0:T(8,128)(2,1)S(1)}, u32[]{:S(2)}) copy-start(bf16[6,32,640]{2,1,0:T(8,128)(2,1)S(1)} %collective-permute-done.7.refs_2_) | copy-start | bytes 737284
  124.1 15.7 %copy-start.4 = (bf16[6,32,640]{2,1,0:T(8,128)(2,1)}, bf16[6,32,640]{2,1,0:T(8,128)(2,1)S(1)}, u32[]{:S(2)}) copy-start(bf16[6,32,640]{2,1,0:T(8,128)(2,1)S(1)} %collective-permute-done.8.refs_3_) | copy-start | bytes 737284
  124.9 33.5 %all-to-all-start.3 = ((bf16[12,40,160]{2,1,0:T(8,128)(2,1)}), bf16[12,40,160]{2,1,0:T(8,128)(2,1)S(1)}, u32[]{:S(2)}, u32[]{:S(2)}) async-start(bf16[12,40,160]{2,1,0:T(8,128)(2,1)} %bitcast.20), calls=%async_computation.3 | async-start | bytes 491520 | tf_op jit(solution)/shard_map/all_to_all | solution.py:36
  142.2 21.0 %collective-permute-start.9 = (bf16[4,32,640]{2,1,0:T(8,128)(2,1)}, bf16[4,32,640]{2,1,0:T(8,128)(2,1)S(1)}, u32[]{:S(2)}, u32[]{:S(2)}) collective-permute-start(bf16[4,32,640]{2,1,0:T(8,128)(2,1)} %get-tuple-element.49), channel_id=1, source_target_pairs={{0,32},{32,0},{256,288},{288,256},{512,544},{544,512},{1,33},{33,1... | collective-permute-start | bytes 491528 | tf_op jit(solution)/shard_map/ppermute | solution.py:371
  146.0 17.2 %collective-permute-start.10 = (bf16[4,32,640]{2,1,0:T(8,128)(2,1)}, bf16[4,32,640]{2,1,0:T(8,128)(2,1)S(1)}, u32[]{:S(2)}, u32[]{:S(2)}) collective-permute-start(bf16[4,32,640]{2,1,0:T(8,128)(2,1)} %get-tuple-element.50), channel_id=1, source_target_pairs={{0,256},{32,288},{256,512},{288,544},{512,0},{544,32},{1,257},{33,... | collective-permute-start | bytes 491528 | tf_op jit(solution)/shard_map/ppermute | solution.py:371
  149.6 13.6 %collective-permute-start.11 = (bf16[4,32,640]{2,1,0:T(8,128)(2,1)}, bf16[4,32,640]{2,1,0:T(8,128)(2,1)S(1)}, u32[]{:S(2)}, u32[]{:S(2)}) collective-permute-start(bf16[4,32,640]{2,1,0:T(8,128)(2,1)} %get-tuple-element.51), channel_id=1, source_target_pairs={{0,288},{32,256},{256,544},{288,512},{512,32},{544,0},{1,289},{33,... | collective-permute-start | bytes 491528 | tf_op jit(solution)/shard_map/ppermute | solution.py:371
  152.9 10.4 %collective-permute-start.12 = (bf16[4,32,640]{2,1,0:T(8,128)(2,1)}, bf16[4,32,640]{2,1,0:T(8,128)(2,1)S(1)}, u32[]{:S(2)}, u32[]{:S(2)}) collective-permute-start(bf16[4,32,640]{2,1,0:T(8,128)(2,1)} %get-tuple-element.52), channel_id=1, source_target_pairs={{0,512},{32,544},{256,0},{288,32},{512,256},{544,288},{1,513},{33,... | collective-permute-start | bytes 491528 | tf_op jit(solution)/shard_map/ppermute | solution.py:371
  156.0 10.9 %collective-permute-start.13 = (bf16[4,32,640]{2,1,0:T(8,128)(2,1)}, bf16[4,32,640]{2,1,0:T(8,128)(2,1)S(1)}, u32[]{:S(2)}, u32[]{:S(2)}) collective-permute-start(bf16[4,32,640]{2,1,0:T(8,128)(2,1)} %get-tuple-element.53), channel_id=1, source_target_pairs={{0,544},{32,512},{256,32},{288,0},{512,288},{544,256},{1,545},{33,... | collective-permute-start | bytes 491528 | tf_op jit(solution)/shard_map/ppermute | solution.py:371
  159.1 11.5 %all-to-all-start.4 = ((bf16[8,40,160]{2,1,0:T(8,128)(2,1)}), bf16[8,40,160]{2,1,0:T(8,128)(2,1)S(1)}, u32[]{:S(2)}, u32[]{:S(2)}) async-start(bf16[8,40,160]{2,1,0:T(8,128)(2,1)} %broadcast_in_dim.46), calls=%async_computation.4 | async-start | bytes 327680 | tf_op jit(solution)/shard_map/all_to_all | solution.py:36
  163.2 3.7 %copy-start.6 = (bf16[4,32,640]{2,1,0:T(8,128)(2,1)}, bf16[4,32,640]{2,1,0:T(8,128)(2,1)S(1)}, u32[]{:S(2)}) copy-start(bf16[4,32,640]{2,1,0:T(8,128)(2,1)S(1)} %collective-permute-done.9.refs_1_) | copy-start | bytes 491524
  163.2 3.7 %copy-start.7 = (bf16[4,32,640]{2,1,0:T(8,128)(2,1)}, bf16[4,32,640]{2,1,0:T(8,128)(2,1)S(1)}, u32[]{:S(2)}) copy-start(bf16[4,32,640]{2,1,0:T(8,128)(2,1)S(1)} %collective-permute-done.10.refs_2_) | copy-start | bytes 491524
  163.2 3.7 %copy-start.8 = (bf16[4,32,640]{2,1,0:T(8,128)(2,1)}, bf16[4,32,640]{2,1,0:T(8,128)(2,1)S(1)}, u32[]{:S(2)}) copy-start(bf16[4,32,640]{2,1,0:T(8,128)(2,1)S(1)} %collective-permute-done.11.refs_3_) | copy-start | bytes 491524
  163.3 3.6 %copy-start.9 = (bf16[4,32,640]{2,1,0:T(8,128)(2,1)}, bf16[4,32,640]{2,1,0:T(8,128)(2,1)S(1)}, u32[]{:S(2)}) copy-start(bf16[4,32,640]{2,1,0:T(8,128)(2,1)S(1)} %collective-permute-done.12.refs_4_) | copy-start | bytes 491524
  166.9 0.7 copy-start.10
  170.6 0.7 copy-start

commit v11 on v9

--- a/solution.py
+++ b/solution.py
@@ -142,28 +142,31 @@
     )(where, counts, dest, coords, patches, values, upstream)
 
 
-def heads_kernel(patch_len, group, where, *refs):
+def heads_kernel(patch_len, group, sources, last, where, *refs):
     refs = list(refs)
     take = lambda count: [refs.pop(0) for _ in range(count)]
-    own_hbm, other_hbm, table_hbm, patches_hbm, packed_hbm = take(5)
-    remote_hbm = take(3)
-    context_refs = take(4)
-    results = take(2)
+    own_hbm, other_hbm, table_hbm = take(3)
+    near_hbm = [] if last else take(2)
+    remote_hbm = take(sources - (not last))
+    total_hbm = take(1) if last else []
+    context_refs = take(sources)
+    results = take(2 if last else 1)
     own_ref, other_ref, table_ref, whole_ref = take(4)
-    packed_refs = take(4)
+    packed_refs = take(sources)
     full_ref, sum_ref, dproj_ref, values_ref, upstream_ref, arrivals = take(6)
-    sources = len(packed_refs)
-    rows, width = patches_hbm.shape[0], packed_hbm.shape[1]
-    depth = packed_hbm.shape[0]
+    depth, width = packed_refs[0].shape
+    rows = whole_ref.shape[0] // sources
     patches_refs = [whole_ref.at[pl.ds(at * rows, rows), :] for at in range(sources)]
     halves = [[ref.at[:, pl.ds(at * width, width)] for at in range(2)] for ref in patches_refs]
     moves = [(own_hbm, own_ref), (other_hbm, other_ref), (table_hbm, table_ref)]
-    waits = [[(patches_hbm, patches_refs[0])], [(packed_hbm, packed_refs[0])]]
-    for at, source_hbm in enumerate(remote_hbm, 1):
+    waits = [] if last else [[(near_hbm[0], patches_refs[0])], [(near_hbm[1], packed_refs[0])]]
+    for at, source_hbm in enumerate(remote_hbm, sources - len(remote_hbm)):
         cut = [source_hbm.at[pl.ds(half * rows, rows), :] for half in range(2)]
         waits.append(list(zip(cut, halves[at])))
         waits.append([(source_hbm.at[pl.ds(2 * rows, depth), :], packed_refs[at])])
     waits = [[move] for move in moves] + waits
+    if last:
+        waits.append([(total_hbm[0], sum_ref)])
     number = 0
     copies = []
     for moves in waits:
@@ -259,7 +262,12 @@
             here = pl.ds(source * rows + starts[blocks[i]], block)
             dproj_ref[here, pl.ds(at, LANES)] = back(dquery[i], blocks[i])
             dproj_ref[here, pl.ds(at + LANES, LANES)] = back(dkey[i], blocks[i])
-    sum_ref[...] = dot(dproj_ref[...], whole_ref[...], ((0,), (0,)))
+    grown = dot(dproj_ref[...], whole_ref[...], ((0,), (0,)))
+    if not last:
+        results[0][...] = grown
+        return
+    arrive(-1)
+    sum_ref[...] += grown
     for z in range(strips):
         part = jnp.transpose(sum_ref[:, z * strip : (z + 1) * strip]).astype(BF16)
         for at in range(2):
@@ -270,32 +278,39 @@
             results[1][:, lanes] = jnp.where(is_first, high, low)
 
 
-def some_heads(where, weights, table, arrays, patch_len):
-    rows, model_width = arrays[0].shape
-    piece = arrays[1].shape
+def some_heads(where, weights, table, arrays, total, rows, piece, patch_len):
+    last = total is not None
+    sources = len(arrays) - (not last)
+    model_width = weights[0].size // (2 * HD)
+    arrays = arrays + ((total,) if last else ())
+    moves = 3 + (2 * (not last)) + 3 * (sources - (not last)) + last
     group = math.gcd(rows // patch_len, max(1, 128 // patch_len))
     vmem = pl.BlockSpec(memory_space=pltpu.VMEM)
     hbm = pl.BlockSpec(memory_space=pltpu.HBM)
     grad_shape = jax.ShapeDtypeStruct(weights[0].shape, BF16)
+    sum_shape = jax.ShapeDtypeStruct((4 * LANES, model_width), F32)
     return pl.pallas_call(
-        functools.partial(heads_kernel, patch_len, group),
+        functools.partial(heads_kernel, patch_len, group, sources, last),
         in_specs=[pl.BlockSpec(memory_space=pltpu.SMEM)] + [hbm] * (3 + len(arrays)),
-        out_specs=[vmem] * 6,
-        out_shape=[jax.ShapeDtypeStruct((rows, 2 * LANES), BF16)] * 4 + [grad_shape] * 2,
+        out_specs=[vmem] * (sources + 1 + last),
+        out_shape=[jax.ShapeDtypeStruct((rows, 2 * LANES), BF16)] * sources
+        + ([grad_shape] * 2 if last else [sum_shape]),
         scratch_shapes=[pltpu.VMEM(weights[0].shape, BF16)] * 2
-        + [pltpu.VMEM(table.shape, BF16), pltpu.VMEM((4 * rows, model_width), BF16)]
-        + [pltpu.VMEM(piece, BF16)] * 4
+        + [pltpu.VMEM(table.shape, BF16), pltpu.VMEM((sources * rows, model_width), BF16)]
+        + [pltpu.VMEM(piece, BF16)] * sources
         + [
             pltpu.VMEM((model_width, 4 * LANES), BF16),
             pltpu.VMEM((4 * LANES, model_width), F32),
-            pltpu.VMEM((4 * rows, 4 * LANES), BF16),
+            pltpu.VMEM((sources * rows, 4 * LANES), BF16),
             pltpu.VMEM((rows, 2 * LANES), BF16),
             pltpu.VMEM((rows, 2 * LANES), BF16),
-            pltpu.SemaphoreType.DMA((14,)),
+            pltpu.SemaphoreType.DMA((moves,)),
         ],
         compiler_params=pltpu.CompilerParams(vmem_limit_bytes=VMEM_BYTES),
         cost_estimate=pl.CostEstimate(
-            flops=20_000_000_000, bytes_accessed=12_000_000, transcendentals=3_000_000
+            flops=5_000_000_000 if last else 1_000,
+            bytes_accessed=3_000_000 if last else 1_000,
+            transcendentals=800_000 if last else 0,
         ),
         name="heads",
     )(where, *weights, table, *arrays)
@@ -462,18 +477,29 @@
     upstream = upstream.reshape(row_total, value_width)
     own, left, right, far = pack(where, counts, dest, coords, patches, values, upstream, nx)
     left, right = ring(left, "x", steps[1]), ring(right, "x", steps[2])
-    far = ring(far, "x", steps[3])
 
     head = core * nx + here
     slice_q = lax.dynamic_slice_in_dim(weight, head * HD, HD, axis=1)
     slice_k = lax.dynamic_slice_in_dim(weight, value_width + head * HD, HD, axis=1)
     own_w = jnp.concatenate([slice_q, slice_k], axis=1)
     own_w = spread(own_w, "zh")
+    far = ring(after(own_w, far), "x", steps[3])
     own_w = jnp.transpose(own_w, (1, 0, 2)).reshape(depth, nz * 2 * HD)
     own_w = spread(own_w, "y").reshape(ny * depth, nz * 2 * HD)
     weights = (own_w, core_swap(own_w))
-    left, right, far = after(own_w, (left, right, far))
-
+
+    table = rotary_table()
+    *contexts, total = some_heads(
+        where,
+        weights,
+        table,
+        (patches, own, left, right),
+        None,
+        row_total,
+        own.shape,
+        patch_len,
+    )
+    far = after(total, far)
     all_dest = [dest[:, 0]]
     for piece in (left, right, far):
         at = piece.shape[0] - EXTRA + 3
@@ -485,13 +511,10 @@
         slot_of = jnp.where(step_of == step, at, slot_of)
     slot_of = (slot_of * copies + all_dest // (nc * nx)) * nc + lax.rem(all_dest, nc)
 
-    *contexts, grad, sent = some_heads(
-        after(slot_of, where),
-        weights,
-        rotary_table(),
-        (patches, own, left, right, far),
-        patch_len,
+    context, grad, sent = some_heads(
+        where, weights, table, (far,), total, row_total, own.shape, patch_len
     )
+    contexts = contexts + [context]
     grad = (grad.astype(F32) + core_swap(sent).astype(F32)).astype(BF16)
     pieces = route(slot_of, contexts, slots, patch_len)
     grad = after(pieces, grad)

time: 172 us -> 191 us (1.11)
  starting transfers between devices: 91.5 us -> 99.9 us
  Pallas kernels: 31.1 us -> 37.5 us
    ppermute x2, starting transfers between devices: 11.6 us -> 25.5 us  [core_swap(): return lax.ppermute(array, 'c', [(0, 1), (1, 0)])]
    ppermute x6, waiting for transfers between devices: 1.92 us -> 13.9 us  [ring(): lax.ppermute(array, axis, [(i, (i + step) % count) for i in range(count)])]
    all_to_all x5, waiting for transfers between devices: 28.3 us -> 18 us  [exchange(): return lax.all_to_all(array, axes, split_axis=0, concat_axis=0, tiled=True)]
    pallas_call x1 -> x2, Pallas kernels: 16.8 us -> 23.3 us  [some_heads(): pl.pallas_call(functools.partial(heads_kernel, patch_len, group, sources,...]
    all_to_all x5, starting transfers between devices: 46.1 us -> 41.8 us  [exchange(): return lax.all_to_all(array, axes, split_axis=0, concat_axis=0, tiled=True)]
  transfers between devices with their start and end apart: 18 -> 18, of which waited for: 7 -> 8; matrix products, arithmetic and copies ran while one was open for 4% -> 4% of each run, Pallas kernels for 5% -> 14%
where the time goes in v11:
time: 191 us; the launch traced here: 189 us
  starting transfers between devices  99.9 us (52%)
  Pallas kernels  37.5 us (20%)
  waiting for transfers between devices  36 us (19%)
  local copies, waits for them, and re-layouts  7.72 us (4%)
  other arithmetic  7 us (4%)
    all_to_all x5, starting transfers between devices, exchange(): return lax.all_to_all(array, axes, split_axis=0, concat_axis=0, tiled=True)  41.8 us
    ppermute x2, starting transfers between devices, core_swap(): return lax.ppermute(array, 'c', [(0, 1), (1, 0)])  25.5 us
    pallas_call x2, Pallas kernels, some_heads(): pl.pallas_call(functools.partial(heads_kernel, patch_len, group, sources,...  23.3 us
    all_to_all x5, waiting for transfers between devices, exchange(): return lax.all_to_all(array, axes, split_axis=0, concat_axis=0, tiled=True)  18 us
    ppermute x6, starting transfers between devices, ring(): lax.ppermute(array, axis, [(i, (i + step) % count) for i in range(count)])  17.1 us
    ppermute x5, starting transfers between devices, hop(): return lax.ppermute(array, ('zl', 'c'), pairs)  15.6 us
    ppermute x6, waiting for transfers between devices, ring(): lax.ppermute(array, axis, [(i, (i + step) % count) for i in range(count)])  13.9 us
    pallas_call x1, Pallas kernels, pack(): pl.pallas_call(pack_kernel, in_specs=[smem] * 3 + [vmem] * 4, out_specs=[...  4.47 us
  transfers between devices with their start and end apart: 18, of which 8 were waited for; matrix products, arithmetic and copies ran while one was open for 4% of the time, Pallas kernels for 14%

profile of v11, /device:TPU:1, one launch (start us, length us, event | category | flops | bytes accessed | tf_op | source)
XLA Modules:
  0.0 189.3 jit_solution(14500171227215045352)
XLA Ops:
  0.6 0.8 constant_dynamic-slice_fusion.1
  1.6 0.6 broadcast_in_dim.42
  2.2 15.0 %all-to-all-start = ((bf16[4,40,160]{2,1,0:T(8,128)(2,1)}), bf16[4,40,160]{2,1,0:T(8,128)(2,1)S(1)}, u32[]{:S(2)}, u32[]{:S(2)}) async-start(bf16[4,40,160]{2,1,0:T(8,128)(2,1)} %broadcast_in_dim.42), calls=%async_computation | async-start | bytes 163840 | tf_op jit(solution)/shard_map/all_to_all | solution.py:36
  17.2 0.6 pad_add_fusion.where
  17.9 1.3 copy.18.dest
  19.2 4.5 %pack.1 = (bf16[208,640]{1,0:T(8,128)(2,1)}, bf16[976,640]{1,0:T(8,128)(2,1)}, bf16[976,640]{1,0:T(8,128)(2,1)}, bf16[976,640]{1,0:T(8,128)(2,1)}) custom-call(s32[3]{0:T(128)} %pad_add_fusion.where, s32[12]{0:T(128)} %counts.1, s32[12,1]{1,0:T(8,128)} %copy.18.dest, s32[12,2,32]{2,1,0:T(2,128)} %coords_ref.1, bf16[384,1280]{1,0:T(8,128)(2,1)} %bitcast.33, ...), custom_call_target="tpu_custom_call" | custom-call | tf_op jit(solution)/shard_map/pack/pallas_call | solution.py:134
  23.7 4.4 %collective-permute-start = (bf16[976,640]{1,0:T(8,128)(2,1)}, bf16[976,640]{1,0:T(8,128)(2,1)S(1)}, u32[]{:S(2)}, u32[]{:S(2)}) collective-permute-start(bf16[976,640]{1,0:T(8,128)(2,1)} %get-tuple-element.27), channel_id=1, source_target_pairs={{0,192},{64,0},{128,64},{192,128},{1,193},{65,1},{129,65},{193,129... | collective-permute-start | bytes 3747848 | tf_op jit(solution)/shard_map/ppermute | solution.py:32
  28.1 1.9 %collective-permute-start.1 = (bf16[976,640]{1,0:T(8,128)(2,1)}, bf16[976,640]{1,0:T(8,128)(2,1)S(1)}, u32[]{:S(2)}, u32[]{:S(2)}) collective-permute-start(bf16[976,640]{1,0:T(8,128)(2,1)} %get-tuple-element.28), channel_id=1, source_target_pairs={{0,64},{64,128},{128,192},{192,0},{1,65},{65,129},{129,193},{193,1... | collective-permute-start | bytes 3747848 | tf_op jit(solution)/shard_map/ppermute | solution.py:32
  30.2 0.8 broadcast_in_dim.44
  30.9 6.8 %all-to-all-start.1 = ((bf16[8,40,640]{2,1,0:T(8,128)(2,1)}), bf16[8,40,640]{2,1,0:T(8,128)(2,1)S(1)}, u32[]{:S(2)}, u32[]{:S(2)}) async-start(bf16[8,40,640]{2,1,0:T(8,128)(2,1)} %broadcast_in_dim.44), calls=%async_computation.1 | async-start | bytes 819200 | tf_op jit(solution)/shard_map/all_to_all | solution.py:36
  37.8 3.6 %collective-permute-start.3 = (bf16[976,640]{1,0:T(8,128)(2,1)}, bf16[976,640]{1,0:T(8,128)(2,1)}, u32[]{:S(2)}, u32[]{:S(2)}) collective-permute-start(bf16[976,640]{1,0:T(8,128)(2,1)} %get-tuple-element.32), channel_id=1, source_target_pairs={{0,128},{64,192},{128,0},{192,64},{1,129},{65,193},{129,1},{193,65... | collective-permute-start | bytes 3747848 | tf_op jit(solution)/shard_map/ppermute | solution.py:32
  41.4 9.8 %all-to-all-done.1 = bf16[8,40,640]{2,1,0:T(8,128)(2,1)S(1)} async-done(((bf16[8,40,640]{2,1,0:T(8,128)(2,1)}), bf16[8,40,640]{2,1,0:T(8,128)(2,1)S(1)}, u32[]{:S(2)}, u32[]{:S(2)}) %all-to-all-start.1) | async-done | bytes 409632 | tf_op jit(solution)/shard_map/all_to_all | solution.py:36
  51.2 4.6 %collective-permute-start.2 = (bf16[320,640]{1,0:T(8,128)(2,1)S(1)}, bf16[320,640]{1,0:T(8,128)(2,1)S(1)}, u32[]{:S(2)}, u32[]{:S(2)}) collective-permute-start(bf16[320,640]{1,0:T(8,128)(2,1)S(1)} %bitcast.35), channel_id=1, source_target_pairs={{0,32},{32,0},{1,33},{33,1},{2,34},{34,2},{3,35},{35,3},{4,36},{36... | collective-permute-start | bytes 1228808 | tf_op jit(solution)/shard_map/ppermute | solution.py:25
  56.2 0.7 pad_maximum_fusion.refs_2_
  57.0 3.0 %collective-permute-done.1.refs_6_ = bf16[976,640]{1,0:T(8,128)(2,1)S(1)} collective-permute-done((bf16[976,640]{1,0:T(8,128)(2,1)}, bf16[976,640]{1,0:T(8,128)(2,1)S(1)}, u32[]{:S(2)}, u32[]{:S(2)}) %collective-permute-start.1) | collective-permute-done | bytes 1249312 | tf_op jit(solution)/shard_map/ppermute | solution.py:32
  60.1 1.0 copy-done.1
  61.1 14.3 %heads.2 = (bf16[384,256]{1,0:T(8,128)(2,1)}, bf16[384,256]{1,0:T(8,128)(2,1)}, bf16[384,256]{1,0:T(8,128)(2,1)}, f32[512,1280]{1,0:T(8,128)}) custom-call(s32[3]{0:T(128)} %pad_add_fusion.where, bf16[320,640]{1,0:T(8,128)(2,1)} %bitcast.36, bf16[320,640]{1,0:T(8,128)(2,1)} %copy-done.4, bf16[3,96,256]{2,1,0:T(8,128)(2,1)} %pad_maximum_fusion.refs_2_, ...), custom_call_target="tpu_custom_call" | custom-call | flops 1000 | bytes 1000 | tf_op jit(solution)/shard_map/heads/pallas_call | solution.py:292
  75.4 0.7 fusion.15
  76.0 9.0 %collective-permute-done.3.refs_3_ = bf16[976,640]{1,0:T(8,128)(2,1)} collective-permute-done((bf16[976,640]{1,0:T(8,128)(2,1)}, bf16[976,640]{1,0:T(8,128)(2,1)}, u32[]{:S(2)}, u32[]{:S(2)}) %collective-permute-start.3) | collective-permute-done | bytes 1249312 | tf_op jit(solution)/shard_map/ppermute | solution.py:32
  85.0 9.1 %heads.3 = (bf16[384,256]{1,0:T(8,128)(2,1)}, bf16[320,640]{1,0:T(8,128)(2,1)}, bf16[320,640]{1,0:T(8,128)(2,1)}) custom-call(s32[3]{0:T(128)} %pad_add_fusion.where, bf16[320,640]{1,0:T(8,128)(2,1)} %bitcast.37, bf16[320,640]{1,0:T(8,128)(2,1)} %copy-done.4, bf16[3,96,256]{2,1,0:T(8,128)(2,1)} %pad_maximum_fusion.refs_2_, ...), custom_call_target="tpu_custom_call" | custom-call | flops 5000000000 | bytes 3000000 | tf_op jit(solution)/shard_map/heads/pallas_call | solution.py:292
  94.1 20.9 %collective-permute-start.12 = (bf16[320,640]{1,0:T(8,128)(2,1)}, bf16[320,640]{1,0:T(8,128)(2,1)S(1)}, u32[]{:S(2)}, u32[]{:S(2)}) collective-permute-start(bf16[320,640]{1,0:T(8,128)(2,1)} %get-tuple-element.49), channel_id=1, source_target_pairs={{0,32},{32,0},{1,33},{33,1},{2,34},{34,2},{3,35},{35,3},{4,36},{36... | collective-permute-start | bytes 1228808 | tf_op jit(solution)/shard_map/ppermute | solution.py:25
  115.0 0.7 fusion.14
  115.7 0.7 bitcast_convert_fusion
  116.3 0.6 multiply_add_fusion.slot_of
  117.0 2.7 %route.1 = (bf16[6,32,640]{2,1,0:T(8,128)(2,1)}, bf16[6,32,640]{2,1,0:T(8,128)(2,1)}, bf16[6,32,640]{2,1,0:T(8,128)(2,1)}, bf16[6,32,640]{2,1,0:T(8,128)(2,1)}) custom-call(s32[48]{0:T(128)} %multiply_add_fusion.slot_of, bf16[384,256]{1,0:T(8,128)(2,1)} %get-tuple-element.34.refs_0_, bf16[384,256]{1,0:T(8,128)(2,1)} %get-tuple-element.35.refs_1_, ...), custom_call_target="tpu_custom_call" | custom-call | tf_op jit(solution)/shard_map/route/pallas_call | solution.py:339
  119.6 1.9 %add_convert_fusion = bf16[320,640]{1,0:T(8,128)(2,1)} fusion(bf16[320,640]{1,0:T(8,128)(2,1)S(1)} %collective-permute-done.12, bf16[320,640]{1,0:T(8,128)(2,1)} %get-tuple-element.48), kind=kLoop, calls=%fused_computation | loop fusion | flops 819200 | bytes 1228800 | tf_op jit(solution)/shard_map/convert_element_type | solution.py:518
  121.6 6.8 %all-to-all-start.2 = ((bf16[8,40,640]{2,1,0:T(8,128)(2,1)}), bf16[8,40,640]{2,1,0:T(8,128)(2,1)S(1)}, u32[]{:S(2)}, u32[]{:S(2)}) async-start(bf16[8,40,640]{2,1,0:T(8,128)(2,1)} %bitcast.18), calls=%async_computation.2 | async-start | bytes 819200 | tf_op jit(solution)/shard_map/all_to_all | solution.py:36
  128.4 1.9 %collective-permute-start.4 = (bf16[6,32,640]{2,1,0:T(8,128)(2,1)S(1)}, bf16[6,32,640]{2,1,0:T(8,128)(2,1)S(1)}, u32[]{:S(2)}, u32[]{:S(2)}) collective-permute-start(bf16[6,32,640]{2,1,0:T(8,128)(2,1)S(1)} %copy-done.16), channel_id=1, source_target_pairs={{0,192},{64,0},{128,64},{192,128},{1,193},{65,1},{129,65},{193,129... | collective-permute-start | bytes 737288 | tf_op jit(solution)/shard_map/ppermute | solution.py:32
  130.3 3.4 %collective-permute-start.5 = (bf16[6,32,640]{2,1,0:T(8,128)(2,1)S(1)}, bf16[6,32,640]{2,1,0:T(8,128)(2,1)S(1)}, u32[]{:S(2)}, u32[]{:S(2)}) collective-permute-start(bf16[6,32,640]{2,1,0:T(8,128)(2,1)S(1)} %copy-done.15), channel_id=1, source_target_pairs={{0,64},{64,128},{128,192},{192,0},{1,65},{65,129},{129,193},{193,1... | collective-permute-start | bytes 737288 | tf_op jit(solution)/shard_map/ppermute | solution.py:32
  133.7 1.9 %collective-permute-start.6 = (bf16[6,32,640]{2,1,0:T(8,128)(2,1)S(1)}, bf16[6,32,640]{2,1,0:T(8,128)(2,1)S(1)}, u32[]{:S(2)}, u32[]{:S(2)}) collective-permute-start(bf16[6,32,640]{2,1,0:T(8,128)(2,1)S(1)} %copy-done.14), channel_id=1, source_target_pairs={{0,128},{64,192},{128,0},{192,64},{1,129},{65,193},{129,1},{193,65... | collective-permute-start | bytes 737288 | tf_op jit(solution)/shard_map/ppermute | solution.py:32
  135.6 8.3 %all-to-all-done.2 = bf16[8,40,640]{2,1,0:T(8,128)(2,1)S(1)} async-done(((bf16[8,40,640]{2,1,0:T(8,128)(2,1)}), bf16[8,40,640]{2,1,0:T(8,128)(2,1)S(1)}, u32[]{:S(2)}, u32[]{:S(2)}) %all-to-all-start.2) | async-done | bytes 409632 | tf_op jit(solution)/shard_map/all_to_all | solution.py:36
  144.1 1.8 collective-permute-done.5.refs_2_
  146.0 0.8 broadcast_in_dim.47
  146.8 9.7 %all-to-all-start.3 = ((bf16[12,40,160]{2,1,0:T(8,128)(2,1)}), bf16[12,40,160]{2,1,0:T(8,128)(2,1)S(1)}, u32[]{:S(2)}, u32[]{:S(2)}) async-start(bf16[12,40,160]{2,1,0:T(8,128)(2,1)} %bitcast.20), calls=%async_computation.3 | async-start | bytes 491520 | tf_op jit(solution)/shard_map/all_to_all | solution.py:36
  156.5 2.4 %regroup.1 = (bf16[4,32,640]{2,1,0:T(8,128)(2,1)}, bf16[4,32,640]{2,1,0:T(8,128)(2,1)}, bf16[4,32,640]{2,1,0:T(8,128)(2,1)}, bf16[4,32,640]{2,1,0:T(8,128)(2,1)}...) custom-call(s32[3]{0:T(128)} %pad_add_fusion.where, bf16[6,32,640]{2,1,0:T(8,128)(2,1)} %get-tuple-element.38.refs_0_, ...), custom_call_target="tpu_custom_call" | custom-call | tf_op jit(solution)/shard_map/regroup/pallas_call | solution.py:365
  158.9 3.3 %collective-permute-start.7 = (bf16[4,32,640]{2,1,0:T(8,128)(2,1)}, bf16[4,32,640]{2,1,0:T(8,128)(2,1)S(1)}, u32[]{:S(2)}, u32[]{:S(2)}) collective-permute-start(bf16[4,32,640]{2,1,0:T(8,128)(2,1)} %get-tuple-element.43), channel_id=1, source_target_pairs={{0,32},{32,0},{256,288},{288,256},{512,544},{544,512},{1,33},{33,1... | collective-permute-start | bytes 491528 | tf_op jit(solution)/shard_map/ppermute | solution.py:384
  162.2 3.6 %collective-permute-start.8 = (bf16[4,32,640]{2,1,0:T(8,128)(2,1)}, bf16[4,32,640]{2,1,0:T(8,128)(2,1)S(1)}, u32[]{:S(2)}, u32[]{:S(2)}) collective-permute-start(bf16[4,32,640]{2,1,0:T(8,128)(2,1)} %get-tuple-element.44), channel_id=1, source_target_pairs={{0,256},{32,288},{256,512},{288,544},{512,0},{544,32},{1,257},{33,... | collective-permute-start | bytes 491528 | tf_op jit(solution)/shard_map/ppermute | solution.py:384
  165.8 3.3 %collective-permute-start.9 = (bf16[4,32,640]{2,1,0:T(8,128)(2,1)}, bf16[4,32,640]{2,1,0:T(8,128)(2,1)S(1)}, u32[]{:S(2)}, u32[]{:S(2)}) collective-permute-start(bf16[4,32,640]{2,1,0:T(8,128)(2,1)} %get-tuple-element.45), channel_id=1, source_target_pairs={{0,288},{32,256},{256,544},{288,512},{512,32},{544,0},{1,289},{33,... | collective-permute-start | bytes 491528 | tf_op jit(solution)/shard_map/ppermute | solution.py:384
  169.1 3.1 %collective-permute-start.10 = (bf16[4,32,640]{2,1,0:T(8,128)(2,1)}, bf16[4,32,640]{2,1,0:T(8,128)(2,1)S(1)}, u32[]{:S(2)}, u32[]{:S(2)}) collective-permute-start(bf16[4,32,640]{2,1,0:T(8,128)(2,1)} %get-tuple-element.46), channel_id=1, source_target_pairs={{0,512},{32,544},{256,0},{288,32},{512,256},{544,288},{1,513},{33,... | collective-permute-start | bytes 491528 | tf_op jit(solution)/shard_map/ppermute | solution.py:384
  172.2 2.3 %collective-permute-start.11 = (bf16[4,32,640]{2,1,0:T(8,128)(2,1)}, bf16[4,32,640]{2,1,0:T(8,128)(2,1)S(1)}, u32[]{:S(2)}, u32[]{:S(2)}) collective-permute-start(bf16[4,32,640]{2,1,0:T(8,128)(2,1)} %get-tuple-element.47), channel_id=1, source_target_pairs={{0,544},{32,512},{256,32},{288,0},{512,288},{544,256},{1,545},{33,... | collective-permute-start | bytes 491528 | tf_op jit(solution)/shard_map/ppermute | solution.py:384
  174.6 0.7 broadcast_in_dim.48
  175.3 3.4 %all-to-all-start.4 = ((bf16[8,40,160]{2,1,0:T(8,128)(2,1)}), bf16[8,40,160]{2,1,0:T(8,128)(2,1)S(1)}, u32[]{:S(2)}, u32[]{:S(2)}) async-start(bf16[8,40,160]{2,1,0:T(8,128)(2,1)} %broadcast_in_dim.48), calls=%async_computation.4 | async-start | bytes 327680 | tf_op jit(solution)/shard_map/all_to_all | solution.py:36
  178.7 0.6 pad_add_fusion.1.places
  179.7 3.6 %collective-permute-done.11.refs_5_ = bf16[4,32,640]{2,1,0:T(8,128)(2,1)S(1)} collective-permute-done((bf16[4,32,640]{2,1,0:T(8,128)(2,1)}, bf16[4,32,640]{2,1,0:T(8,128)(2,1)S(1)}, u32[]{:S(2)}, u32[]{:S(2)}) %collective-permute-start.11) | collective-permute-done | bytes 163872 | tf_op jit(solution)/shard_map/ppermute | solution.py:384
  183.3 0.6 copy-done.12
  183.9 3.0 %settle.1 = bf16[24,32,640]{2,1,0:T(8,128)(2,1)} custom-call(s32[3]{0:T(128)} %pad_add_fusion.where, s32[4]{0:T(128)} %pad_add_fusion.1.places, bf16[4,32,640]{2,1,0:T(8,128)(2,1)} %get-tuple-element.42.refs_0_, bf16[4,32,640]{2,1,0:T(8,128)(2,1)} %copy-done.8, bf16[4,32,640]{2,1,0:T(8,128)(2,1)} %copy-done.9, bf16[4,32,640]{2,1,0:T(8,128)(2,1)} %copy-done.10, ...), custom_call_target="tpu_custom_call" | custom-call | tf_op jit(solution)/shard_map/settle/pallas_call | solution.py:410
  186.9 0.7 copy-done.3
  187.6 1.7 finish.1
  (58 shorter events, 1.4 us)
Async XLA Ops:
  2.2 27.8 %all-to-all-start = ((bf16[4,40,160]{2,1,0:T(8,128)(2,1)}), bf16[4,40,160]{2,1,0:T(8,128)(2,1)S(1)}, u32[]{:S(2)}, u32[]{:S(2)}) async-start(bf16[4,40,160]{2,1,0:T(8,128)(2,1)} %broadcast_in_dim.42), calls=%async_computation | async-start | bytes 163840 | tf_op jit(solution)/shard_map/all_to_all | solution.py:36
  23.7 33.4 %collective-permute-start = (bf16[976,640]{1,0:T(8,128)(2,1)}, bf16[976,640]{1,0:T(8,128)(2,1)S(1)}, u32[]{:S(2)}, u32[]{:S(2)}) collective-permute-start(bf16[976,640]{1,0:T(8,128)(2,1)} %get-tuple-element.27), channel_id=1, source_target_pairs={{0,192},{64,0},{128,64},{192,128},{1,193},{65,1},{129,65},{193,129... | collective-permute-start | bytes 3747848 | tf_op jit(solution)/shard_map/ppermute | solution.py:32
  28.1 32.0 %collective-permute-start.1 = (bf16[976,640]{1,0:T(8,128)(2,1)}, bf16[976,640]{1,0:T(8,128)(2,1)S(1)}, u32[]{:S(2)}, u32[]{:S(2)}) collective-permute-start(bf16[976,640]{1,0:T(8,128)(2,1)} %get-tuple-element.28), channel_id=1, source_target_pairs={{0,64},{64,128},{128,192},{192,0},{1,65},{65,129},{129,193},{193,1... | collective-permute-start | bytes 3747848 | tf_op jit(solution)/shard_map/ppermute | solution.py:32
  30.9 20.3 %all-to-all-start.1 = ((bf16[8,40,640]{2,1,0:T(8,128)(2,1)}), bf16[8,40,640]{2,1,0:T(8,128)(2,1)S(1)}, u32[]{:S(2)}, u32[]{:S(2)}) async-start(bf16[8,40,640]{2,1,0:T(8,128)(2,1)} %broadcast_in_dim.44), calls=%async_computation.1 | async-start | bytes 819200 | tf_op jit(solution)/shard_map/all_to_all | solution.py:36
  37.8 47.3 %collective-permute-start.3 = (bf16[976,640]{1,0:T(8,128)(2,1)}, bf16[976,640]{1,0:T(8,128)(2,1)}, u32[]{:S(2)}, u32[]{:S(2)}) collective-permute-start(bf16[976,640]{1,0:T(8,128)(2,1)} %get-tuple-element.32), channel_id=1, source_target_pairs={{0,128},{64,192},{128,0},{192,64},{1,129},{65,193},{129,1},{193,65... | collective-permute-start | bytes 3747848 | tf_op jit(solution)/shard_map/ppermute | solution.py:32
  51.2 8.8 %copy-start = (bf16[8,40,640]{2,1,0:T(8,128)(2,1)}, bf16[8,40,640]{2,1,0:T(8,128)(2,1)S(1)}, u32[]{:S(2)}) copy-start(bf16[8,40,640]{2,1,0:T(8,128)(2,1)S(1)} %all-to-all-done.1) | copy-start | bytes 1228804
  51.2 5.8 %collective-permute-start.2 = (bf16[320,640]{1,0:T(8,128)(2,1)S(1)}, bf16[320,640]{1,0:T(8,128)(2,1)S(1)}, u32[]{:S(2)}, u32[]{:S(2)}) collective-permute-start(bf16[320,640]{1,0:T(8,128)(2,1)S(1)} %bitcast.35), channel_id=1, source_target_pairs={{0,32},{32,0},{1,33},{33,1},{2,34},{34,2},{3,35},{35,3},{4,36},{36... | collective-permute-start | bytes 1228808 | tf_op jit(solution)/shard_map/ppermute | solution.py:25
  57.0 3.0 %copy-start.4 = (bf16[320,640]{1,0:T(8,128)(2,1)}, bf16[320,640]{1,0:T(8,128)(2,1)S(1)}, u32[]{:S(2)}) copy-start(bf16[320,640]{1,0:T(8,128)(2,1)S(1)} %collective-permute-done.2.refs_1_) | copy-start | bytes 1228804
  57.0 3.0 %copy-start.2 = (bf16[976,640]{1,0:T(8,128)(2,1)}, bf16[976,640]{1,0:T(8,128)(2,1)S(1)}, u32[]{:S(2)}) copy-start(bf16[976,640]{1,0:T(8,128)(2,1)S(1)} %collective-permute-done.refs_5_) | copy-start | bytes 3747844
  60.1 1.0 copy-start.1
  85.0 31.3 %copy-start.13 = (s32[12,1]{0,1:T(1,128)S(1)}, s32[12,1]{0,1:T(1,128)}, u32[]{:S(2)}) copy-start(s32[12,1]{0,1:T(1,128)} %param.12) | copy-start | bytes 148
  94.1 25.5 %collective-permute-start.12 = (bf16[320,640]{1,0:T(8,128)(2,1)}, bf16[320,640]{1,0:T(8,128)(2,1)S(1)}, u32[]{:S(2)}, u32[]{:S(2)}) collective-permute-start(bf16[320,640]{1,0:T(8,128)(2,1)} %get-tuple-element.49), channel_id=1, source_target_pairs={{0,32},{32,0},{1,33},{33,1},{2,34},{34,2},{3,35},{35,3},{4,36},{36... | collective-permute-start | bytes 1228808 | tf_op jit(solution)/shard_map/ppermute | solution.py:25
  119.6 8.8 %copy-start.16 = (bf16[6,32,640]{2,1,0:T(8,128)(2,1)S(1)}, bf16[6,32,640]{2,1,0:T(8,128)(2,1)}, u32[]{:S(2)}) copy-start(bf16[6,32,640]{2,1,0:T(8,128)(2,1)} %get-tuple-element.39) | copy-start | bytes 737284
  119.6 10.7 %copy-start.15 = (bf16[6,32,640]{2,1,0:T(8,128)(2,1)S(1)}, bf16[6,32,640]{2,1,0:T(8,128)(2,1)}, u32[]{:S(2)}) copy-start(bf16[6,32,640]{2,1,0:T(8,128)(2,1)} %get-tuple-element.40) | copy-start | bytes 737284
  119.6 14.1 %copy-start.14 = (bf16[6,32,640]{2,1,0:T(8,128)(2,1)S(1)}, bf16[6,32,640]{2,1,0:T(8,128)(2,1)}, u32[]{:S(2)}) copy-start(bf16[6,32,640]{2,1,0:T(8,128)(2,1)} %get-tuple-element.41) | copy-start | bytes 737284
  121.6 22.3 %all-to-all-start.2 = ((bf16[8,40,640]{2,1,0:T(8,128)(2,1)}), bf16[8,40,640]{2,1,0:T(8,128)(2,1)S(1)}, u32[]{:S(2)}, u32[]{:S(2)}) async-start(bf16[8,40,640]{2,1,0:T(8,128)(2,1)} %bitcast.18), calls=%async_computation.2 | async-start | bytes 819200 | tf_op jit(solution)/shard_map/all_to_all | solution.py:36
  128.4 15.7 %collective-permute-start.4 = (bf16[6,32,640]{2,1,0:T(8,128)(2,1)S(1)}, bf16[6,32,640]{2,1,0:T(8,128)(2,1)S(1)}, u32[]{:S(2)}, u32[]{:S(2)}) collective-permute-start(bf16[6,32,640]{2,1,0:T(8,128)(2,1)S(1)} %copy-done.16), channel_id=1, source_target_pairs={{0,192},{64,0},{128,64},{192,128},{1,193},{65,1},{129,65},{193,129... | collective-permute-start | bytes 737288 | tf_op jit(solution)/shard_map/ppermute | solution.py:32
  130.3 15.6 %collective-permute-start.5 = (bf16[6,32,640]{2,1,0:T(8,128)(2,1)S(1)}, bf16[6,32,640]{2,1,0:T(8,128)(2,1)S(1)}, u32[]{:S(2)}, u32[]{:S(2)}) collective-permute-start(bf16[6,32,640]{2,1,0:T(8,128)(2,1)S(1)} %copy-done.15), channel_id=1, source_target_pairs={{0,64},{64,128},{128,192},{192,0},{1,65},{65,129},{129,193},{193,1... | collective-permute-start | bytes 737288 | tf_op jit(solution)/shard_map/ppermute | solution.py:32
  133.7 12.3 %collective-permute-start.6 = (bf16[6,32,640]{2,1,0:T(8,128)(2,1)S(1)}, bf16[6,32,640]{2,1,0:T(8,128)(2,1)S(1)}, u32[]{:S(2)}, u32[]{:S(2)}) collective-permute-start(bf16[6,32,640]{2,1,0:T(8,128)(2,1)S(1)} %copy-done.14), channel_id=1, source_target_pairs={{0,128},{64,192},{128,0},{192,64},{1,129},{65,193},{129,1},{193,65... | collective-permute-start | bytes 737288 | tf_op jit(solution)/shard_map/ppermute | solution.py:32
  144.1 12.4 %copy-start.5 = (bf16[6,32,640]{2,1,0:T(8,128)(2,1)}, bf16[6,32,640]{2,1,0:T(8,128)(2,1)S(1)}, u32[]{:S(2)}) copy-start(bf16[6,32,640]{2,1,0:T(8,128)(2,1)S(1)} %collective-permute-done.4.refs_1_) | copy-start | bytes 737284
  146.0 10.5 %copy-start.6 = (bf16[6,32,640]{2,1,0:T(8,128)(2,1)}, bf16[6,32,640]{2,1,0:T(8,128)(2,1)S(1)}, u32[]{:S(2)}) copy-start(bf16[6,32,640]{2,1,0:T(8,128)(2,1)S(1)} %collective-permute-done.5.refs_2_) | copy-start | bytes 737284
  146.0 10.5 %copy-start.7 = (bf16[6,32,640]{2,1,0:T(8,128)(2,1)}, bf16[6,32,640]{2,1,0:T(8,128)(2,1)S(1)}, u32[]{:S(2)}) copy-start(bf16[6,32,640]{2,1,0:T(8,128)(2,1)S(1)} %collective-permute-done.6.refs_3_) | copy-start | bytes 737284
  146.8 27.8 %all-to-all-start.3 = ((bf16[12,40,160]{2,1,0:T(8,128)(2,1)}), bf16[12,40,160]{2,1,0:T(8,128)(2,1)S(1)}, u32[]{:S(2)}, u32[]{:S(2)}) async-start(bf16[12,40,160]{2,1,0:T(8,128)(2,1)} %bitcast.20), calls=%async_computation.3 | async-start | bytes 491520 | tf_op jit(solution)/shard_map/all_to_all | solution.py:36
  158.9 20.4 %collective-permute-start.7 = (bf16[4,32,640]{2,1,0:T(8,128)(2,1)}, bf16[4,32,640]{2,1,0:T(8,128)(2,1)S(1)}, u32[]{:S(2)}, u32[]{:S(2)}) collective-permute-start(bf16[4,32,640]{2,1,0:T(8,128)(2,1)} %get-tuple-element.43), channel_id=1, source_target_pairs={{0,32},{32,0},{256,288},{288,256},{512,544},{544,512},{1,33},{33,1... | collective-permute-start | bytes 491528 | tf_op jit(solution)/shard_map/ppermute | solution.py:384
  162.2 17.1 %collective-permute-start.8 = (bf16[4,32,640]{2,1,0:T(8,128)(2,1)}, bf16[4,32,640]{2,1,0:T(8,128)(2,1)S(1)}, u32[]{:S(2)}, u32[]{:S(2)}) collective-permute-start(bf16[4,32,640]{2,1,0:T(8,128)(2,1)} %get-tuple-element.44), channel_id=1, source_target_pairs={{0,256},{32,288},{256,512},{288,544},{512,0},{544,32},{1,257},{33,... | collective-permute-start | bytes 491528 | tf_op jit(solution)/shard_map/ppermute | solution.py:384
  165.8 13.5 %collective-permute-start.9 = (bf16[4,32,640]{2,1,0:T(8,128)(2,1)}, bf16[4,32,640]{2,1,0:T(8,128)(2,1)S(1)}, u32[]{:S(2)}, u32[]{:S(2)}) collective-permute-start(bf16[4,32,640]{2,1,0:T(8,128)(2,1)} %get-tuple-element.45), channel_id=1, source_target_pairs={{0,288},{32,256},{256,544},{288,512},{512,32},{544,0},{1,289},{33,... | collective-permute-start | bytes 491528 | tf_op jit(solution)/shard_map/ppermute | solution.py:384
  169.1 10.6 %collective-permute-start.10 = (bf16[4,32,640]{2,1,0:T(8,128)(2,1)}, bf16[4,32,640]{2,1,0:T(8,128)(2,1)S(1)}, u32[]{:S(2)}, u32[]{:S(2)}) collective-permute-start(bf16[4,32,640]{2,1,0:T(8,128)(2,1)} %get-tuple-element.46), channel_id=1, source_target_pairs={{0,512},{32,544},{256,0},{288,32},{512,256},{544,288},{1,513},{33,... | collective-permute-start | bytes 491528 | tf_op jit(solution)/shard_map/ppermute | solution.py:384
  172.2 11.1 %collective-permute-start.11 = (bf16[4,32,640]{2,1,0:T(8,128)(2,1)}, bf16[4,32,640]{2,1,0:T(8,128)(2,1)S(1)}, u32[]{:S(2)}, u32[]{:S(2)}) collective-permute-start(bf16[4,32,640]{2,1,0:T(8,128)(2,1)} %get-tuple-element.47), channel_id=1, source_target_pairs={{0,544},{32,512},{256,32},{288,0},{512,288},{544,256},{1,545},{33,... | collective-permute-start | bytes 491528 | tf_op jit(solution)/shard_map/ppermute | solution.py:384
  175.3 11.7 %all-to-all-start.4 = ((bf16[8,40,160]{2,1,0:T(8,128)(2,1)}), bf16[8,40,160]{2,1,0:T(8,128)(2,1)S(1)}, u32[]{:S(2)}, u32[]{:S(2)}) async-start(bf16[8,40,160]{2,1,0:T(8,128)(2,1)} %broadcast_in_dim.48), calls=%async_computation.4 | async-start | bytes 327680 | tf_op jit(solution)/shard_map/all_to_all | solution.py:36
  179.3 3.9 %copy-start.8 = (bf16[4,32,640]{2,1,0:T(8,128)(2,1)}, bf16[4,32,640]{2,1,0:T(8,128)(2,1)S(1)}, u32[]{:S(2)}) copy-start(bf16[4,32,640]{2,1,0:T(8,128)(2,1)S(1)} %collective-permute-done.7.refs_1_) | copy-start | bytes 491524
  179.3 3.9 %copy-start.9 = (bf16[4,32,640]{2,1,0:T(8,128)(2,1)}, bf16[4,32,640]{2,1,0:T(8,128)(2,1)S(1)}, u32[]{:S(2)}) copy-start(bf16[4,32,640]{2,1,0:T(8,128)(2,1)S(1)} %collective-permute-done.8.refs_2_) | copy-start | bytes 491524
  179.3 3.9 %copy-start.10 = (bf16[4,32,640]{2,1,0:T(8,128)(2,1)}, bf16[4,32,640]{2,1,0:T(8,128)(2,1)S(1)}, u32[]{:S(2)}) copy-start(bf16[4,32,640]{2,1,0:T(8,128)(2,1)S(1)} %collective-permute-done.9.refs_3_) | copy-start | bytes 491524
  179.7 3.6 %copy-start.11 = (bf16[4,32,640]{2,1,0:T(8,128)(2,1)}, bf16[4,32,640]{2,1,0:T(8,128)(2,1)S(1)}, u32[]{:S(2)}) copy-start(bf16[4,32,640]{2,1,0:T(8,128)(2,1)S(1)} %collective-permute-done.10.refs_4_) | copy-start | bytes 491524
  183.2 0.7 copy-start.12
  186.9 0.7 copy-start.3

commit v12 on v10

--- a/solution.py
+++ b/solution.py
@@ -371,6 +371,25 @@
     return lax.ppermute(array, ("zl", "c"), pairs)
 
 
+def keep_kernel(source_ref, target_ref):
+    target_ref[...] = source_ref[...]
+
+
+def keep(array):
+    vmem = pl.BlockSpec(memory_space=pltpu.VMEM)
+    return pl.pallas_call(
+        keep_kernel,
+        in_specs=[vmem],
+        out_specs=vmem,
+        out_shape=jax.ShapeDtypeStruct(array.shape, array.dtype),
+        compiler_params=pltpu.CompilerParams(vmem_limit_bytes=VMEM_BYTES),
+        cost_estimate=pl.CostEstimate(
+            flops=30_000_000_000, bytes_accessed=2_000_000, transcendentals=0
+        ),
+        name="keep",
+    )(array)
+
+
 def settle_kernel(where, places, *refs):
     arrived_refs, placed_ref = refs[:-1], refs[-1]
     copies, nx = len(arrived_refs) // 2, arrived_refs[0].shape[0]
@@ -462,6 +481,7 @@
     slice_k = lax.dynamic_slice_in_dim(weight, value_width + head * HD, HD, axis=1)
     own_w = jnp.concatenate([slice_q, slice_k], axis=1)
     own_w = jnp.broadcast_to(own_w[None], (nz,) + own_w.shape)
+    patches = after(own_w, patches)
     where = jnp.stack([here, core, copy]).astype(jnp.int32)
     steps = ring_steps(nx)
     patches = patches.reshape(row_total, model_width)
@@ -473,12 +493,11 @@
     own_w = exchange(own_w, "zh")
     far = ring(after(own_w, far), "x", steps[3])
     own_w = jnp.transpose(own_w, (1, 0, 2)).reshape(depth, nz * 2 * HD)
-    low, high = right[:row_total], left[row_total : 2 * row_total]
-    own_w = after((low, high), own_w)
-    low, high = ring(low, "x", steps[2]), ring(high, "x", steps[1])
     own_w = spread(own_w, "y").reshape(ny * depth, nz * 2 * HD)
+    own_w = keep(own_w)
     weights = (own_w, core_swap(own_w))
-    left, right, far = after(own_w, (left, right, far))
+    low = ring(right[:row_total], "x", steps[2])
+    high = ring(left[row_total : 2 * row_total], "x", steps[1])
 
     all_dest = [dest[:, 0]]
     for piece in (left, right, far):

time: 174 us -> 183 us (1.052)
  waiting for transfers between devices: 25.3 us -> 45.3 us
  starting transfers between devices: 101 us -> 88.8 us
    ppermute x8, waiting for transfers between devices: 5.74 us -> 34.1 us  [ring(): lax.ppermute(array, axis, [(i, (i + step) % count) for i in range(count)])]
    all_to_all x5, waiting for transfers between devices: 15.8 us -> 7.72 us  [exchange(): return lax.all_to_all(array, axes, split_axis=0, concat_axis=0, tiled=True)]
    all_to_all x5, starting transfers between devices: 46.6 us -> 41.8 us  [exchange(): return lax.all_to_all(array, axes, split_axis=0, concat_axis=0, tiled=True)]
    ppermute x8, starting transfers between devices: 28 us -> 23.3 us  [ring(): lax.ppermute(array, axis, [(i, (i + step) % count) for i in range(count)])]
    ppermute x2, starting transfers between devices: 10.4 us -> 7.17 us  [core_swap(): return lax.ppermute(array, 'c', [(0, 1), (1, 0)])]
    unnamed x37 -> x43, local copies, waits for them, and re-layouts: 3.58 us -> 4.92 us
  transfers between devices with their start and end apart: 20 -> 20, of which waited for: 7 -> 6; matrix products, arithmetic and copies ran while one was open for 3% -> 3% of each run, Pallas kernels for 5% -> 8%
where the time goes in v12:
time: 183 us; the launch traced here: 182 us
  starting transfers between devices  88.8 us (49%)
  waiting for transfers between devices  45.3 us (25%)
  Pallas kernels  32.5 us (18%)
  local copies, waits for them, and re-layouts  8.99 us (5%)
  other arithmetic  5.12 us (3%)
    all_to_all x5, starting transfers between devices, exchange(): return lax.all_to_all(array, axes, split_axis=0, concat_axis=0, tiled=True)  41.8 us
    ppermute x8, waiting for transfers between devices, ring(): lax.ppermute(array, axis, [(i, (i + step) % count) for i in range(count)])  34.1 us
    ppermute x8, starting transfers between devices, ring(): lax.ppermute(array, axis, [(i, (i + step) % count) for i in range(count)])  23.3 us
    pallas_call x1, Pallas kernels, some_heads(): pl.pallas_call(functools.partial(heads_kernel, patch_len, group), in_spec...  16.8 us
    ppermute x5, starting transfers between devices, hop(): return lax.ppermute(array, ('zl', 'c'), pairs)  16.5 us
    all_to_all x5, waiting for transfers between devices, exchange(): return lax.all_to_all(array, axes, split_axis=0, concat_axis=0, tiled=True)  7.72 us
    ppermute x2, starting transfers between devices, core_swap(): return lax.ppermute(array, 'c', [(0, 1), (1, 0)])  7.17 us
    unnamed x43, local copies, waits for them, and re-layouts  4.92 us
  transfers between devices with their start and end apart: 20, of which 6 were waited for; matrix products, arithmetic and copies ran while one was open for 3% of the time, Pallas kernels for 8%

profile of v12, /device:TPU:1, one launch (start us, length us, event | category | flops | bytes accessed | tf_op | source)
XLA Modules:
  0.0 181.9 jit_solution(15342029202608288862)
XLA Ops:
  0.6 0.8 constant_dynamic-slice_fusion.1
  1.6 0.6 broadcast_in_dim.42
  2.2 15.0 %all-to-all-start = ((bf16[4,40,160]{2,1,0:T(8,128)(2,1)}), bf16[4,40,160]{2,1,0:T(8,128)(2,1)S(1)}, u32[]{:S(2)}, u32[]{:S(2)}) async-start(bf16[4,40,160]{2,1,0:T(8,128)(2,1)} %broadcast_in_dim.42), calls=%async_computation | async-start | bytes 163840 | tf_op jit(solution)/shard_map/all_to_all | solution.py:36
  17.2 1.3 copy.18.dest
  19.2 4.1 %pack.1 = (bf16[208,640]{1,0:T(8,128)(2,1)}, bf16[976,640]{1,0:T(8,128)(2,1)}, bf16[976,640]{1,0:T(8,128)(2,1)}, bf16[208,640]{1,0:T(8,128)(2,1)}) custom-call(s32[3]{0:T(128)} %pad_add_fusion.where, s32[12]{0:T(128)} %counts.1, s32[12,1]{1,0:T(8,128)} %copy.18.dest, s32[12,2,32]{2,1,0:T(2,128)} %coords_ref.1, bf16[384,1280]{1,0:T(8,128)(2,1)} %bitcast.35, ...), custom_call_target="tpu_custom_call" | custom-call | tf_op jit(solution)/shard_map/pack/pallas_call | solution.py:134
  23.3 4.5 %collective-permute-start = (bf16[976,640]{1,0:T(8,128)(2,1)}, bf16[976,640]{1,0:T(8,128)(2,1)S(1)}, u32[]{:S(2)}, u32[]{:S(2)}) collective-permute-start(bf16[976,640]{1,0:T(8,128)(2,1)} %get-tuple-element.28), channel_id=1, source_target_pairs={{0,192},{64,0},{128,64},{192,128},{1,193},{65,1},{129,65},{193,129... | collective-permute-start | bytes 3747848 | tf_op jit(solution)/shard_map/ppermute | solution.py:32
  27.8 1.9 %collective-permute-start.1 = (bf16[976,640]{1,0:T(8,128)(2,1)}, bf16[976,640]{1,0:T(8,128)(2,1)S(1)}, u32[]{:S(2)}, u32[]{:S(2)}) collective-permute-start(bf16[976,640]{1,0:T(8,128)(2,1)} %get-tuple-element.29), channel_id=1, source_target_pairs={{0,64},{64,128},{128,192},{192,0},{1,65},{65,129},{129,193},{193,1... | collective-permute-start | bytes 3747848 | tf_op jit(solution)/shard_map/ppermute | solution.py:32
  30.0 0.8 broadcast_in_dim.44
  30.8 6.8 %all-to-all-start.1 = ((bf16[8,40,640]{2,1,0:T(8,128)(2,1)}), bf16[8,40,640]{2,1,0:T(8,128)(2,1)S(1)}, u32[]{:S(2)}, u32[]{:S(2)}) async-start(bf16[8,40,640]{2,1,0:T(8,128)(2,1)} %broadcast_in_dim.44), calls=%async_computation.1 | async-start | bytes 819200 | tf_op jit(solution)/shard_map/all_to_all | solution.py:36
  37.6 3.6 %collective-permute-start.2 = (bf16[208,640]{1,0:T(8,128)(2,1)S(1)}, bf16[208,640]{1,0:T(8,128)(2,1)S(1)}, u32[]{:S(2)}, u32[]{:S(2)}) collective-permute-start(bf16[208,640]{1,0:T(8,128)(2,1)S(1)} %copy-done.17), channel_id=1, source_target_pairs={{0,128},{64,192},{128,0},{192,64},{1,129},{65,193},{129,1},{193,65... | collective-permute-start | bytes 798728 | tf_op jit(solution)/shard_map/ppermute | solution.py:32
  41.6 0.7 pad_maximum_fusion.refs_2_
  42.3 21.4 %collective-permute-done.2.refs_9_ = bf16[208,640]{1,0:T(8,128)(2,1)S(1)} collective-permute-done((bf16[208,640]{1,0:T(8,128)(2,1)S(1)}, bf16[208,640]{1,0:T(8,128)(2,1)S(1)}, u32[]{:S(2)}, u32[]{:S(2)}) %collective-permute-start.2) | collective-permute-done | bytes 266272 | tf_op jit(solution)/shard_map/ppermute | solution.py:32
  63.7 0.7 copy-done.16
  64.4 0.7 copy-done.1
  65.1 1.8 keep.1.refs_0_
  66.9 4.2 %collective-permute-start.3 = (bf16[320,640]{1,0:T(8,128)(2,1)}, bf16[320,640]{1,0:T(8,128)(2,1)S(1)}, u32[]{:S(2)}, u32[]{:S(2)}) collective-permute-start(bf16[320,640]{1,0:T(8,128)(2,1)} %keep.1.refs_0_), channel_id=1, source_target_pairs={{0,32},{32,0},{1,33},{33,1},{2,34},{34,2},{3,35},{35,3},{4,36},{36... | collective-permute-start | bytes 1228808 | tf_op jit(solution)/shard_map/ppermute | solution.py:25
  71.3 1.9 %collective-permute-start.5 = (bf16[384,640]{1,0:T(8,128)(2,1)S(1)}, bf16[384,640]{1,0:T(8,128)(2,1)S(1)}, u32[]{:S(2)}, u32[]{:S(2)}) collective-permute-start(bf16[384,640]{1,0:T(8,128)(2,1)S(1)} %slice.24), channel_id=1, source_target_pairs={{0,192},{64,0},{128,64},{192,128},{1,193},{65,1},{129,65},{193,129... | collective-permute-start | bytes 1474568 | tf_op jit(solution)/shard_map/ppermute | solution.py:32
  73.3 3.5 %collective-permute-start.4 = (bf16[384,640]{1,0:T(8,128)(2,1)S(1)}, bf16[384,640]{1,0:T(8,128)(2,1)S(1)}, u32[]{:S(2)}, u32[]{:S(2)}) collective-permute-start(bf16[384,640]{1,0:T(8,128)(2,1)S(1)} %slice.23), channel_id=1, source_target_pairs={{0,64},{64,128},{128,192},{192,0},{1,65},{65,129},{129,193},{193,1... | collective-permute-start | bytes 1474568 | tf_op jit(solution)/shard_map/ppermute | solution.py:32
  76.9 0.7 multiply_add_fusion.slot_of
  77.6 8.4 %collective-permute-done.5.refs_8_ = bf16[384,640]{1,0:T(8,128)(2,1)S(1)} collective-permute-done((bf16[384,640]{1,0:T(8,128)(2,1)S(1)}, bf16[384,640]{1,0:T(8,128)(2,1)S(1)}, u32[]{:S(2)}, u32[]{:S(2)}) %collective-permute-start.5) | collective-permute-done | bytes 491552 | tf_op jit(solution)/shard_map/ppermute | solution.py:32
  86.0 3.2 %collective-permute-done.4.refs_7_ = bf16[384,640]{1,0:T(8,128)(2,1)S(1)} collective-permute-done((bf16[384,640]{1,0:T(8,128)(2,1)S(1)}, bf16[384,640]{1,0:T(8,128)(2,1)S(1)}, u32[]{:S(2)}, u32[]{:S(2)}) %collective-permute-start.4) | collective-permute-done | bytes 491552 | tf_op jit(solution)/shard_map/ppermute | solution.py:32
  89.2 0.8 copy-done.14
  90.0 16.8 %heads.1 = (bf16[384,256]{1,0:T(8,128)(2,1)}, bf16[384,256]{1,0:T(8,128)(2,1)}, bf16[384,256]{1,0:T(8,128)(2,1)}, bf16[384,256]{1,0:T(8,128)(2,1)}, bf16[320,640]{1,0:T(8,128)(2,1)}, /*index=5*/bf16[320,640]{1,0:T(8,128)(2,1)}) custom-call(s32[3]{0:T(128)} %pad_add_fusion.where, bf16[320,640]{1,0:T(8,128)(2,1)} %keep.1.refs_0_, bf16[320,640]{1,0:T(8,128)(2,1)} %copy-done.15, ...), custom_call_target="tpu_custom_call" | custom-call | flops 20000000000 | bytes 12000000 | tf_op jit(solution)/shard_map/heads/pallas_call | solution.py:282
  106.8 2.9 %collective-permute-start.14 = (bf16[320,640]{1,0:T(8,128)(2,1)}, bf16[320,640]{1,0:T(8,128)(2,1)S(1)}, u32[]{:S(2)}, u32[]{:S(2)}) collective-permute-start(bf16[320,640]{1,0:T(8,128)(2,1)} %get-tuple-element.49), channel_id=1, source_target_pairs={{0,32},{32,0},{1,33},{33,1},{2,34},{34,2},{3,35},{35,3},{4,36},{36... | collective-permute-start | bytes 1228808 | tf_op jit(solution)/shard_map/ppermute | solution.py:25
  109.7 2.7 %route.1 = (bf16[6,32,640]{2,1,0:T(8,128)(2,1)}, bf16[6,32,640]{2,1,0:T(8,128)(2,1)}, bf16[6,32,640]{2,1,0:T(8,128)(2,1)}, bf16[6,32,640]{2,1,0:T(8,128)(2,1)}) custom-call(s32[48]{0:T(128)} %multiply_add_fusion.slot_of, bf16[384,256]{1,0:T(8,128)(2,1)} %get-tuple-element.34.refs_0_, bf16[384,256]{1,0:T(8,128)(2,1)} %get-tuple-element.35.refs_1_, ...), custom_call_target="tpu_custom_call" | custom-call | tf_op jit(solution)/shard_map/route/pallas_call | solution.py:326
  112.5 1.9 %add_convert_fusion = bf16[320,640]{1,0:T(8,128)(2,1)} fusion(bf16[320,640]{1,0:T(8,128)(2,1)S(1)} %collective-permute-done.14, bf16[320,640]{1,0:T(8,128)(2,1)} %get-tuple-element.48), kind=kLoop, calls=%fused_computation | loop fusion | flops 819200 | bytes 1228800 | tf_op jit(solution)/shard_map/convert_element_type | solution.py:520
  114.4 6.8 %all-to-all-start.2 = ((bf16[8,40,640]{2,1,0:T(8,128)(2,1)}), bf16[8,40,640]{2,1,0:T(8,128)(2,1)S(1)}, u32[]{:S(2)}, u32[]{:S(2)}) async-start(bf16[8,40,640]{2,1,0:T(8,128)(2,1)} %bitcast.18), calls=%async_computation.2 | async-start | bytes 819200 | tf_op jit(solution)/shard_map/all_to_all | solution.py:36
  121.2 2.1 %collective-permute-start.6 = (bf16[6,32,640]{2,1,0:T(8,128)(2,1)S(1)}, bf16[6,32,640]{2,1,0:T(8,128)(2,1)S(1)}, u32[]{:S(2)}, u32[]{:S(2)}) collective-permute-start(bf16[6,32,640]{2,1,0:T(8,128)(2,1)S(1)} %copy-done.20), channel_id=1, source_target_pairs={{0,192},{64,0},{128,64},{192,128},{1,193},{65,1},{129,65},{193,129... | collective-permute-start | bytes 737288 | tf_op jit(solution)/shard_map/ppermute | solution.py:32
  123.3 3.2 %collective-permute-start.7 = (bf16[6,32,640]{2,1,0:T(8,128)(2,1)S(1)}, bf16[6,32,640]{2,1,0:T(8,128)(2,1)S(1)}, u32[]{:S(2)}, u32[]{:S(2)}) collective-permute-start(bf16[6,32,640]{2,1,0:T(8,128)(2,1)S(1)} %copy-done.19), channel_id=1, source_target_pairs={{0,64},{64,128},{128,192},{192,0},{1,65},{65,129},{129,193},{193,1... | collective-permute-start | bytes 737288 | tf_op jit(solution)/shard_map/ppermute | solution.py:32
  126.5 2.5 %collective-permute-start.8 = (bf16[6,32,640]{2,1,0:T(8,128)(2,1)S(1)}, bf16[6,32,640]{2,1,0:T(8,128)(2,1)S(1)}, u32[]{:S(2)}, u32[]{:S(2)}) collective-permute-start(bf16[6,32,640]{2,1,0:T(8,128)(2,1)S(1)} %copy-done.18), channel_id=1, source_target_pairs={{0,128},{64,192},{128,0},{192,64},{1,129},{65,193},{129,1},{193,65... | collective-permute-start | bytes 737288 | tf_op jit(solution)/shard_map/ppermute | solution.py:32
  129.0 7.7 %all-to-all-done.2 = bf16[8,40,640]{2,1,0:T(8,128)(2,1)S(1)} async-done(((bf16[8,40,640]{2,1,0:T(8,128)(2,1)}), bf16[8,40,640]{2,1,0:T(8,128)(2,1)S(1)}, u32[]{:S(2)}, u32[]{:S(2)}) %all-to-all-start.2) | async-done | bytes 409632 | tf_op jit(solution)/shard_map/all_to_all | solution.py:36
  136.9 1.1 collective-permute-done.8.refs_3_
  138.0 0.8 broadcast_in_dim.47
  138.8 9.7 %all-to-all-start.3 = ((bf16[12,40,160]{2,1,0:T(8,128)(2,1)}), bf16[12,40,160]{2,1,0:T(8,128)(2,1)S(1)}, u32[]{:S(2)}, u32[]{:S(2)}) async-start(bf16[12,40,160]{2,1,0:T(8,128)(2,1)} %bitcast.20), calls=%async_computation.3 | async-start | bytes 491520 | tf_op jit(solution)/shard_map/all_to_all | solution.py:36
  148.5 2.3 %regroup.1 = (bf16[4,32,640]{2,1,0:T(8,128)(2,1)}, bf16[4,32,640]{2,1,0:T(8,128)(2,1)}, bf16[4,32,640]{2,1,0:T(8,128)(2,1)}, bf16[4,32,640]{2,1,0:T(8,128)(2,1)}...) custom-call(s32[3]{0:T(128)} %pad_add_fusion.where, bf16[6,32,640]{2,1,0:T(8,128)(2,1)} %get-tuple-element.38.refs_0_, ...), custom_call_target="tpu_custom_call" | custom-call | tf_op jit(solution)/shard_map/regroup/pallas_call | solution.py:352
  150.9 4.3 %collective-permute-start.9 = (bf16[4,32,640]{2,1,0:T(8,128)(2,1)}, bf16[4,32,640]{2,1,0:T(8,128)(2,1)S(1)}, u32[]{:S(2)}, u32[]{:S(2)}) collective-permute-start(bf16[4,32,640]{2,1,0:T(8,128)(2,1)} %get-tuple-element.43), channel_id=1, source_target_pairs={{0,32},{32,0},{256,288},{288,256},{512,544},{544,512},{1,33},{33,1... | collective-permute-start | bytes 491528 | tf_op jit(solution)/shard_map/ppermute | solution.py:371
  155.1 3.6 %collective-permute-start.10 = (bf16[4,32,640]{2,1,0:T(8,128)(2,1)}, bf16[4,32,640]{2,1,0:T(8,128)(2,1)S(1)}, u32[]{:S(2)}, u32[]{:S(2)}) collective-permute-start(bf16[4,32,640]{2,1,0:T(8,128)(2,1)} %get-tuple-element.44), channel_id=1, source_target_pairs={{0,256},{32,288},{256,512},{288,544},{512,0},{544,32},{1,257},{33,... | collective-permute-start | bytes 491528 | tf_op jit(solution)/shard_map/ppermute | solution.py:371
  158.7 3.3 %collective-permute-start.11 = (bf16[4,32,640]{2,1,0:T(8,128)(2,1)}, bf16[4,32,640]{2,1,0:T(8,128)(2,1)S(1)}, u32[]{:S(2)}, u32[]{:S(2)}) collective-permute-start(bf16[4,32,640]{2,1,0:T(8,128)(2,1)} %get-tuple-element.45), channel_id=1, source_target_pairs={{0,288},{32,256},{256,544},{288,512},{512,32},{544,0},{1,289},{33,... | collective-permute-start | bytes 491528 | tf_op jit(solution)/shard_map/ppermute | solution.py:371
  162.0 3.1 %collective-permute-start.12 = (bf16[4,32,640]{2,1,0:T(8,128)(2,1)}, bf16[4,32,640]{2,1,0:T(8,128)(2,1)S(1)}, u32[]{:S(2)}, u32[]{:S(2)}) collective-permute-start(bf16[4,32,640]{2,1,0:T(8,128)(2,1)} %get-tuple-element.46), channel_id=1, source_target_pairs={{0,512},{32,544},{256,0},{288,32},{512,256},{544,288},{1,513},{33,... | collective-permute-start | bytes 491528 | tf_op jit(solution)/shard_map/ppermute | solution.py:371
  165.1 2.3 %collective-permute-start.13 = (bf16[4,32,640]{2,1,0:T(8,128)(2,1)}, bf16[4,32,640]{2,1,0:T(8,128)(2,1)S(1)}, u32[]{:S(2)}, u32[]{:S(2)}) collective-permute-start(bf16[4,32,640]{2,1,0:T(8,128)(2,1)} %get-tuple-element.47), channel_id=1, source_target_pairs={{0,544},{32,512},{256,32},{288,0},{512,288},{544,256},{1,545},{33,... | collective-permute-start | bytes 491528 | tf_op jit(solution)/shard_map/ppermute | solution.py:371
  167.6 0.7 broadcast_in_dim.48
  168.2 3.4 %all-to-all-start.4 = ((bf16[8,40,160]{2,1,0:T(8,128)(2,1)}), bf16[8,40,160]{2,1,0:T(8,128)(2,1)S(1)}, u32[]{:S(2)}, u32[]{:S(2)}) async-start(bf16[8,40,160]{2,1,0:T(8,128)(2,1)} %broadcast_in_dim.48), calls=%async_computation.4 | async-start | bytes 327680 | tf_op jit(solution)/shard_map/all_to_all | solution.py:36
  171.6 0.7 pad_add_fusion.1.places
  172.3 3.4 %collective-permute-done.13.refs_5_ = bf16[4,32,640]{2,1,0:T(8,128)(2,1)S(1)} collective-permute-done((bf16[4,32,640]{2,1,0:T(8,128)(2,1)}, bf16[4,32,640]{2,1,0:T(8,128)(2,1)S(1)}, u32[]{:S(2)}, u32[]{:S(2)}) %collective-permute-start.13) | collective-permute-done | bytes 163872 | tf_op jit(solution)/shard_map/ppermute | solution.py:371
  175.8 0.6 copy-done.11
  176.4 3.0 %settle.1 = bf16[24,32,640]{2,1,0:T(8,128)(2,1)} custom-call(s32[3]{0:T(128)} %pad_add_fusion.where, s32[4]{0:T(128)} %pad_add_fusion.1.places, bf16[4,32,640]{2,1,0:T(8,128)(2,1)} %get-tuple-element.42.refs_0_, bf16[4,32,640]{2,1,0:T(8,128)(2,1)} %copy-done.7, bf16[4,32,640]{2,1,0:T(8,128)(2,1)} %copy-done.8, bf16[4,32,640]{2,1,0:T(8,128)(2,1)} %copy-done.9, ...), custom_call_target="tpu_custom_call" | custom-call | tf_op jit(solution)/shard_map/settle/pallas_call | solution.py:416
  179.5 0.7 copy-done
  180.1 1.7 finish.1
  (72 shorter events, 1.6 us)
Async XLA Ops:
  2.2 27.6 %all-to-all-start = ((bf16[4,40,160]{2,1,0:T(8,128)(2,1)}), bf16[4,40,160]{2,1,0:T(8,128)(2,1)S(1)}, u32[]{:S(2)}, u32[]{:S(2)}) async-start(bf16[4,40,160]{2,1,0:T(8,128)(2,1)} %broadcast_in_dim.42), calls=%async_computation | async-start | bytes 163840 | tf_op jit(solution)/shard_map/all_to_all | solution.py:36
  23.3 14.3 %copy-start.17 = (bf16[208,640]{1,0:T(8,128)(2,1)S(1)}, bf16[208,640]{1,0:T(8,128)(2,1)}, u32[]{:S(2)}) copy-start(bf16[208,640]{1,0:T(8,128)(2,1)} %get-tuple-element.31) | copy-start | bytes 798724
  23.3 47.9 %collective-permute-start = (bf16[976,640]{1,0:T(8,128)(2,1)}, bf16[976,640]{1,0:T(8,128)(2,1)S(1)}, u32[]{:S(2)}, u32[]{:S(2)}) collective-permute-start(bf16[976,640]{1,0:T(8,128)(2,1)} %get-tuple-element.28), channel_id=1, source_target_pairs={{0,192},{64,0},{128,64},{192,128},{1,193},{65,1},{129,65},{193,129... | collective-permute-start | bytes 3747848 | tf_op jit(solution)/shard_map/ppermute | solution.py:32
  27.8 45.4 %collective-permute-start.1 = (bf16[976,640]{1,0:T(8,128)(2,1)}, bf16[976,640]{1,0:T(8,128)(2,1)S(1)}, u32[]{:S(2)}, u32[]{:S(2)}) collective-permute-start(bf16[976,640]{1,0:T(8,128)(2,1)} %get-tuple-element.29), channel_id=1, source_target_pairs={{0,64},{64,128},{128,192},{192,0},{1,65},{65,129},{129,193},{193,1... | collective-permute-start | bytes 3747848 | tf_op jit(solution)/shard_map/ppermute | solution.py:32
  30.8 33.6 %all-to-all-start.1 = ((bf16[8,40,640]{2,1,0:T(8,128)(2,1)}), bf16[8,40,640]{2,1,0:T(8,128)(2,1)S(1)}, u32[]{:S(2)}, u32[]{:S(2)}) async-start(bf16[8,40,640]{2,1,0:T(8,128)(2,1)} %broadcast_in_dim.44), calls=%async_computation.1 | async-start | bytes 819200 | tf_op jit(solution)/shard_map/all_to_all | solution.py:36
  37.6 26.1 %collective-permute-start.2 = (bf16[208,640]{1,0:T(8,128)(2,1)S(1)}, bf16[208,640]{1,0:T(8,128)(2,1)S(1)}, u32[]{:S(2)}, u32[]{:S(2)}) collective-permute-start(bf16[208,640]{1,0:T(8,128)(2,1)S(1)} %copy-done.17), channel_id=1, source_target_pairs={{0,128},{64,192},{128,0},{192,64},{1,129},{65,193},{129,1},{193,65... | collective-permute-start | bytes 798728 | tf_op jit(solution)/shard_map/ppermute | solution.py:32
  63.7 0.7 copy-start.16
  64.4 0.8 copy-start.1
  66.9 9.9 %copy-start.12 = (s32[12,1]{0,1:T(1,128)S(1)}, s32[12,1]{0,1:T(1,128)}, u32[]{:S(2)}) copy-start(s32[12,1]{0,1:T(1,128)} %param.12) | copy-start | bytes 148
  66.9 10.6 %collective-permute-start.3 = (bf16[320,640]{1,0:T(8,128)(2,1)}, bf16[320,640]{1,0:T(8,128)(2,1)S(1)}, u32[]{:S(2)}, u32[]{:S(2)}) collective-permute-start(bf16[320,640]{1,0:T(8,128)(2,1)} %keep.1.refs_0_), channel_id=1, source_target_pairs={{0,32},{32,0},{1,33},{33,1},{2,34},{34,2},{3,35},{35,3},{4,36},{36... | collective-permute-start | bytes 1228808 | tf_op jit(solution)/shard_map/ppermute | solution.py:25
  71.2 18.0 %copy-start.5 = (bf16[976,640]{1,0:T(8,128)(2,1)}, bf16[976,640]{1,0:T(8,128)(2,1)S(1)}, u32[]{:S(2)}) copy-start(bf16[976,640]{1,0:T(8,128)(2,1)S(1)} %collective-permute-done.refs_5_) | copy-start | bytes 3747844
  71.3 14.7 %collective-permute-start.5 = (bf16[384,640]{1,0:T(8,128)(2,1)S(1)}, bf16[384,640]{1,0:T(8,128)(2,1)S(1)}, u32[]{:S(2)}, u32[]{:S(2)}) collective-permute-start(bf16[384,640]{1,0:T(8,128)(2,1)S(1)} %slice.24), channel_id=1, source_target_pairs={{0,192},{64,0},{128,64},{192,128},{1,193},{65,1},{129,65},{193,129... | collective-permute-start | bytes 1474568 | tf_op jit(solution)/shard_map/ppermute | solution.py:32
  73.2 16.0 %copy-start.6 = (bf16[976,640]{1,0:T(8,128)(2,1)}, bf16[976,640]{1,0:T(8,128)(2,1)S(1)}, u32[]{:S(2)}) copy-start(bf16[976,640]{1,0:T(8,128)(2,1)S(1)} %collective-permute-done.1.refs_6_) | copy-start | bytes 3747844
  73.3 15.9 %collective-permute-start.4 = (bf16[384,640]{1,0:T(8,128)(2,1)S(1)}, bf16[384,640]{1,0:T(8,128)(2,1)S(1)}, u32[]{:S(2)}, u32[]{:S(2)}) collective-permute-start(bf16[384,640]{1,0:T(8,128)(2,1)S(1)} %slice.23), channel_id=1, source_target_pairs={{0,64},{64,128},{128,192},{192,0},{1,65},{65,129},{129,193},{193,1... | collective-permute-start | bytes 1474568 | tf_op jit(solution)/shard_map/ppermute | solution.py:32
  77.6 11.7 %copy-start.15 = (bf16[320,640]{1,0:T(8,128)(2,1)}, bf16[320,640]{1,0:T(8,128)(2,1)S(1)}, u32[]{:S(2)}) copy-start(bf16[320,640]{1,0:T(8,128)(2,1)S(1)} %collective-permute-done.3.refs_1_) | copy-start | bytes 1228804
  86.0 3.2 %copy-start.13 = (bf16[384,640]{1,0:T(8,128)(2,1)}, bf16[384,640]{1,0:T(8,128)(2,1)S(1)}, u32[]{:S(2)}) copy-start(bf16[384,640]{1,0:T(8,128)(2,1)S(1)} %collective-permute-done.5.refs_8_) | copy-start | bytes 1474564
  89.2 0.8 copy-start.14
  106.8 5.7 %collective-permute-start.14 = (bf16[320,640]{1,0:T(8,128)(2,1)}, bf16[320,640]{1,0:T(8,128)(2,1)S(1)}, u32[]{:S(2)}, u32[]{:S(2)}) collective-permute-start(bf16[320,640]{1,0:T(8,128)(2,1)} %get-tuple-element.49), channel_id=1, source_target_pairs={{0,32},{32,0},{1,33},{33,1},{2,34},{34,2},{3,35},{35,3},{4,36},{36... | collective-permute-start | bytes 1228808 | tf_op jit(solution)/shard_map/ppermute | solution.py:25
  112.4 8.8 %copy-start.20 = (bf16[6,32,640]{2,1,0:T(8,128)(2,1)S(1)}, bf16[6,32,640]{2,1,0:T(8,128)(2,1)}, u32[]{:S(2)}) copy-start(bf16[6,32,640]{2,1,0:T(8,128)(2,1)} %get-tuple-element.39) | copy-start | bytes 737284
  112.4 10.9 %copy-start.19 = (bf16[6,32,640]{2,1,0:T(8,128)(2,1)S(1)}, bf16[6,32,640]{2,1,0:T(8,128)(2,1)}, u32[]{:S(2)}) copy-start(bf16[6,32,640]{2,1,0:T(8,128)(2,1)} %get-tuple-element.40) | copy-start | bytes 737284
  112.4 14.1 %copy-start.18 = (bf16[6,32,640]{2,1,0:T(8,128)(2,1)S(1)}, bf16[6,32,640]{2,1,0:T(8,128)(2,1)}, u32[]{:S(2)}) copy-start(bf16[6,32,640]{2,1,0:T(8,128)(2,1)} %get-tuple-element.41) | copy-start | bytes 737284
  114.4 22.3 %all-to-all-start.2 = ((bf16[8,40,640]{2,1,0:T(8,128)(2,1)}), bf16[8,40,640]{2,1,0:T(8,128)(2,1)S(1)}, u32[]{:S(2)}, u32[]{:S(2)}) async-start(bf16[8,40,640]{2,1,0:T(8,128)(2,1)} %bitcast.18), calls=%async_computation.2 | async-start | bytes 819200 | tf_op jit(solution)/shard_map/all_to_all | solution.py:36
  121.2 15.7 %collective-permute-start.6 = (bf16[6,32,640]{2,1,0:T(8,128)(2,1)S(1)}, bf16[6,32,640]{2,1,0:T(8,128)(2,1)S(1)}, u32[]{:S(2)}, u32[]{:S(2)}) collective-permute-start(bf16[6,32,640]{2,1,0:T(8,128)(2,1)S(1)} %copy-done.20), channel_id=1, source_target_pairs={{0,192},{64,0},{128,64},{192,128},{1,193},{65,1},{129,65},{193,129... | collective-permute-start | bytes 737288 | tf_op jit(solution)/shard_map/ppermute | solution.py:32
  123.3 13.6 %collective-permute-start.7 = (bf16[6,32,640]{2,1,0:T(8,128)(2,1)S(1)}, bf16[6,32,640]{2,1,0:T(8,128)(2,1)S(1)}, u32[]{:S(2)}, u32[]{:S(2)}) collective-permute-start(bf16[6,32,640]{2,1,0:T(8,128)(2,1)S(1)} %copy-done.19), channel_id=1, source_target_pairs={{0,64},{64,128},{128,192},{192,0},{1,65},{65,129},{129,193},{193,1... | collective-permute-start | bytes 737288 | tf_op jit(solution)/shard_map/ppermute | solution.py:32
  126.5 11.5 %collective-permute-start.8 = (bf16[6,32,640]{2,1,0:T(8,128)(2,1)S(1)}, bf16[6,32,640]{2,1,0:T(8,128)(2,1)S(1)}, u32[]{:S(2)}, u32[]{:S(2)}) collective-permute-start(bf16[6,32,640]{2,1,0:T(8,128)(2,1)S(1)} %copy-done.18), channel_id=1, source_target_pairs={{0,128},{64,192},{128,0},{192,64},{1,129},{65,193},{129,1},{193,65... | collective-permute-start | bytes 737288 | tf_op jit(solution)/shard_map/ppermute | solution.py:32
  136.9 11.6 %copy-start.2 = (bf16[6,32,640]{2,1,0:T(8,128)(2,1)}, bf16[6,32,640]{2,1,0:T(8,128)(2,1)S(1)}, u32[]{:S(2)}) copy-start(bf16[6,32,640]{2,1,0:T(8,128)(2,1)S(1)} %collective-permute-done.6.refs_1_) | copy-start | bytes 737284
  136.9 11.6 %copy-start.3 = (bf16[6,32,640]{2,1,0:T(8,128)(2,1)}, bf16[6,32,640]{2,1,0:T(8,128)(2,1)S(1)}, u32[]{:S(2)}) copy-start(bf16[6,32,640]{2,1,0:T(8,128)(2,1)S(1)} %collective-permute-done.7.refs_2_) | copy-start | bytes 737284
  138.0 10.5 %copy-start.4 = (bf16[6,32,640]{2,1,0:T(8,128)(2,1)}, bf16[6,32,640]{2,1,0:T(8,128)(2,1)S(1)}, u32[]{:S(2)}) copy-start(bf16[6,32,640]{2,1,0:T(8,128)(2,1)S(1)} %collective-permute-done.8.refs_3_) | copy-start | bytes 737284
  138.8 28.7 %all-to-all-start.3 = ((bf16[12,40,160]{2,1,0:T(8,128)(2,1)}), bf16[12,40,160]{2,1,0:T(8,128)(2,1)S(1)}, u32[]{:S(2)}, u32[]{:S(2)}) async-start(bf16[12,40,160]{2,1,0:T(8,128)(2,1)} %bitcast.20), calls=%async_computation.3 | async-start | bytes 491520 | tf_op jit(solution)/shard_map/all_to_all | solution.py:36
  150.9 21.4 %collective-permute-start.9 = (bf16[4,32,640]{2,1,0:T(8,128)(2,1)}, bf16[4,32,640]{2,1,0:T(8,128)(2,1)S(1)}, u32[]{:S(2)}, u32[]{:S(2)}) collective-permute-start(bf16[4,32,640]{2,1,0:T(8,128)(2,1)} %get-tuple-element.43), channel_id=1, source_target_pairs={{0,32},{32,0},{256,288},{288,256},{512,544},{544,512},{1,33},{33,1... | collective-permute-start | bytes 491528 | tf_op jit(solution)/shard_map/ppermute | solution.py:371
  155.1 17.2 %collective-permute-start.10 = (bf16[4,32,640]{2,1,0:T(8,128)(2,1)}, bf16[4,32,640]{2,1,0:T(8,128)(2,1)S(1)}, u32[]{:S(2)}, u32[]{:S(2)}) collective-permute-start(bf16[4,32,640]{2,1,0:T(8,128)(2,1)} %get-tuple-element.44), channel_id=1, source_target_pairs={{0,256},{32,288},{256,512},{288,544},{512,0},{544,32},{1,257},{33,... | collective-permute-start | bytes 491528 | tf_op jit(solution)/shard_map/ppermute | solution.py:371
  158.7 13.6 %collective-permute-start.11 = (bf16[4,32,640]{2,1,0:T(8,128)(2,1)}, bf16[4,32,640]{2,1,0:T(8,128)(2,1)S(1)}, u32[]{:S(2)}, u32[]{:S(2)}) collective-permute-start(bf16[4,32,640]{2,1,0:T(8,128)(2,1)} %get-tuple-element.45), channel_id=1, source_target_pairs={{0,288},{32,256},{256,544},{288,512},{512,32},{544,0},{1,289},{33,... | collective-permute-start | bytes 491528 | tf_op jit(solution)/shard_map/ppermute | solution.py:371
  162.0 10.3 %collective-permute-start.12 = (bf16[4,32,640]{2,1,0:T(8,128)(2,1)}, bf16[4,32,640]{2,1,0:T(8,128)(2,1)S(1)}, u32[]{:S(2)}, u32[]{:S(2)}) collective-permute-start(bf16[4,32,640]{2,1,0:T(8,128)(2,1)} %get-tuple-element.46), channel_id=1, source_target_pairs={{0,512},{32,544},{256,0},{288,32},{512,256},{544,288},{1,513},{33,... | collective-permute-start | bytes 491528 | tf_op jit(solution)/shard_map/ppermute | solution.py:371
  165.1 10.6 %collective-permute-start.13 = (bf16[4,32,640]{2,1,0:T(8,128)(2,1)}, bf16[4,32,640]{2,1,0:T(8,128)(2,1)S(1)}, u32[]{:S(2)}, u32[]{:S(2)}) collective-permute-start(bf16[4,32,640]{2,1,0:T(8,128)(2,1)} %get-tuple-element.47), channel_id=1, source_target_pairs={{0,544},{32,512},{256,32},{288,0},{512,288},{544,256},{1,545},{33,... | collective-permute-start | bytes 491528 | tf_op jit(solution)/shard_map/ppermute | solution.py:371
  168.2 11.2 %all-to-all-start.4 = ((bf16[8,40,160]{2,1,0:T(8,128)(2,1)}), bf16[8,40,160]{2,1,0:T(8,128)(2,1)S(1)}, u32[]{:S(2)}, u32[]{:S(2)}) async-start(bf16[8,40,160]{2,1,0:T(8,128)(2,1)} %broadcast_in_dim.48), calls=%async_computation.4 | async-start | bytes 327680 | tf_op jit(solution)/shard_map/all_to_all | solution.py:36
  172.3 3.5 %copy-start.7 = (bf16[4,32,640]{2,1,0:T(8,128)(2,1)}, bf16[4,32,640]{2,1,0:T(8,128)(2,1)S(1)}, u32[]{:S(2)}) copy-start(bf16[4,32,640]{2,1,0:T(8,128)(2,1)S(1)} %collective-permute-done.9.refs_1_) | copy-start | bytes 491524
  172.3 3.5 %copy-start.8 = (bf16[4,32,640]{2,1,0:T(8,128)(2,1)}, bf16[4,32,640]{2,1,0:T(8,128)(2,1)S(1)}, u32[]{:S(2)}) copy-start(bf16[4,32,640]{2,1,0:T(8,128)(2,1)S(1)} %collective-permute-done.10.refs_2_) | copy-start | bytes 491524
  172.3 3.5 %copy-start.9 = (bf16[4,32,640]{2,1,0:T(8,128)(2,1)}, bf16[4,32,640]{2,1,0:T(8,128)(2,1)S(1)}, u32[]{:S(2)}) copy-start(bf16[4,32,640]{2,1,0:T(8,128)(2,1)S(1)} %collective-permute-done.11.refs_3_) | copy-start | bytes 491524
  172.3 3.4 %copy-start.10 = (bf16[4,32,640]{2,1,0:T(8,128)(2,1)}, bf16[4,32,640]{2,1,0:T(8,128)(2,1)S(1)}, u32[]{:S(2)}) copy-start(bf16[4,32,640]{2,1,0:T(8,128)(2,1)S(1)} %collective-permute-done.12.refs_4_) | copy-start | bytes 491524
  175.8 0.7 copy-start.11
  179.5 0.7 copy-start

commit v13 on v9

--- a/solution.py
+++ b/solution.py
@@ -496,7 +496,7 @@
     pieces = route(slot_of, contexts, slots, patch_len)
     grad = after(pieces, grad)
     pieces = [ring(piece, "x", step) for piece, step in zip(pieces, steps)]
-    crossed = pieces
+    crossed = pieces[1:3]
     pieces = regroup(where, pieces)
     pieces = [hop(piece, at // 2, at % 2) for at, piece in enumerate(pieces)]
     places = [lax.rem(here - sender + nx, nx) for sender in range(nx)]

time: 172 us -> 180 us (1.047)
  waiting for transfers between devices: 34.1 us -> 41.4 us
    ppermute x6, waiting for transfers between devices: 1.92 us -> 8.05 us  [ring(): lax.ppermute(array, axis, [(i, (i + step) % count) for i in range(count)])]
    all_to_all x5, waiting for transfers between devices: 28.3 us -> 30.5 us  [exchange(): return lax.all_to_all(array, axes, split_axis=0, concat_axis=0, tiled=True)]
  transfers between devices with their start and end apart: 18 -> 18, of which waited for: 7 -> 6; matrix products, arithmetic and copies ran while one was open for 4% -> 4% of each run, Pallas kernels for 5% -> 4%
where the time goes in v13:
time: 180 us; the launch traced here: 179 us
  starting transfers between devices  91.6 us (51%)
  waiting for transfers between devices  41.4 us (23%)
  Pallas kernels  31.1 us (17%)
  local copies, waits for them, and re-layouts  8.12 us (5%)
  other arithmetic  5.78 us (3%)
    all_to_all x5, starting transfers between devices, exchange(): return lax.all_to_all(array, axes, split_axis=0, concat_axis=0, tiled=True)  46.2 us
    all_to_all x5, waiting for transfers between devices, exchange(): return lax.all_to_all(array, axes, split_axis=0, concat_axis=0, tiled=True)  30.5 us
    ppermute x6, starting transfers between devices, ring(): lax.ppermute(array, axis, [(i, (i + step) % count) for i in range(count)])  18.2 us
    pallas_call x1, Pallas kernels, some_heads(): pl.pallas_call(functools.partial(heads_kernel, patch_len, group), in_spec...  16.8 us
    ppermute x5, starting transfers between devices, hop(): return lax.ppermute(array, ('zl', 'c'), pairs)  15.5 us
    ppermute x2, starting transfers between devices, core_swap(): return lax.ppermute(array, 'c', [(0, 1), (1, 0)])  11.6 us
    ppermute x6, waiting for transfers between devices, ring(): lax.ppermute(array, axis, [(i, (i + step) % count) for i in range(count)])  8.05 us
    pallas_call x1, Pallas kernels, pack(): pl.pallas_call(pack_kernel, in_specs=[smem] * 3 + [vmem] * 4, out_specs=[...  4.51 us
  transfers between devices with their start and end apart: 18, of which 6 were waited for; matrix products, arithmetic and copies ran while one was open for 4% of the time, Pallas kernels for 4%

profile of v13, /device:TPU:1, one launch (start us, length us, event | category | flops | bytes accessed | tf_op | source)
XLA Modules:
  0.0 179.1 jit_solution(2439211830473060956)
XLA Ops:
  0.6 1.3 copy.19.dest
  2.0 0.7 pad_add_fusion.where
  2.6 4.5 %pack.1 = (bf16[208,640]{1,0:T(8,128)(2,1)}, bf16[976,640]{1,0:T(8,128)(2,1)}, bf16[976,640]{1,0:T(8,128)(2,1)}, bf16[976,640]{1,0:T(8,128)(2,1)}) custom-call(s32[3]{0:T(128)} %pad_add_fusion.where, s32[12]{0:T(128)} %counts.1, s32[12,1]{1,0:T(8,128)} %copy.19.dest, s32[12,2,32]{2,1,0:T(2,128)} %coords_ref.1, bf16[384,1280]{1,0:T(8,128)(2,1)} %bitcast.29, ...), custom_call_target="tpu_custom_call" | custom-call | tf_op jit(solution)/shard_map/pack/pallas_call | solution.py:134
  7.2 5.2 %collective-permute-start = (bf16[976,640]{1,0:T(8,128)(2,1)}, bf16[976,640]{1,0:T(8,128)(2,1)}, u32[]{:S(2)}, u32[]{:S(2)}) collective-permute-start(bf16[976,640]{1,0:T(8,128)(2,1)} %get-tuple-element.28), channel_id=1, source_target_pairs={{0,192},{64,0},{128,64},{192,128},{1,193},{65,1},{129,65},{193,129... | collective-permute-start | bytes 3747848 | tf_op jit(solution)/shard_map/ppermute | solution.py:32
  12.4 1.9 %collective-permute-start.1 = (bf16[976,640]{1,0:T(8,128)(2,1)}, bf16[976,640]{1,0:T(8,128)(2,1)S(1)}, u32[]{:S(2)}, u32[]{:S(2)}) collective-permute-start(bf16[976,640]{1,0:T(8,128)(2,1)} %get-tuple-element.29), channel_id=1, source_target_pairs={{0,64},{64,128},{128,192},{192,0},{1,65},{65,129},{129,193},{193,1... | collective-permute-start | bytes 3747848 | tf_op jit(solution)/shard_map/ppermute | solution.py:32
  14.3 3.6 %collective-permute-start.2 = (bf16[976,640]{1,0:T(8,128)(2,1)}, bf16[976,640]{1,0:T(8,128)(2,1)S(1)}, u32[]{:S(2)}, u32[]{:S(2)}) collective-permute-start(bf16[976,640]{1,0:T(8,128)(2,1)} %get-tuple-element.30), channel_id=1, source_target_pairs={{0,128},{64,192},{128,0},{192,64},{1,129},{65,193},{129,1},{193,65... | collective-permute-start | bytes 3747848 | tf_op jit(solution)/shard_map/ppermute | solution.py:32
  17.9 0.8 constant_dynamic-slice_fusion.1
  18.9 0.6 broadcast_in_dim.42
  19.5 14.2 %all-to-all-start = ((bf16[4,40,160]{2,1,0:T(8,128)(2,1)}), bf16[4,40,160]{2,1,0:T(8,128)(2,1)S(1)}, u32[]{:S(2)}, u32[]{:S(2)}) async-start(bf16[4,40,160]{2,1,0:T(8,128)(2,1)} %broadcast_in_dim.42), calls=%async_computation | async-start | bytes 163840 | tf_op jit(solution)/shard_map/all_to_all | solution.py:36
  33.8 9.9 %all-to-all-done = bf16[4,40,160]{2,1,0:T(8,128)(2,1)S(1)} async-done(((bf16[4,40,160]{2,1,0:T(8,128)(2,1)}), bf16[4,40,160]{2,1,0:T(8,128)(2,1)S(1)}, u32[]{:S(2)}, u32[]{:S(2)}) %all-to-all-start) | async-done | bytes 51232 | tf_op jit(solution)/shard_map/all_to_all | solution.py:36
  43.7 0.1 broadcast_in_dim.43
  43.8 0.8 broadcast_in_dim.44
  44.6 6.8 %all-to-all-start.1 = ((bf16[8,40,640]{2,1,0:T(8,128)(2,1)}), bf16[8,40,640]{2,1,0:T(8,128)(2,1)S(1)}, u32[]{:S(2)}, u32[]{:S(2)}) async-start(bf16[8,40,640]{2,1,0:T(8,128)(2,1)} %broadcast_in_dim.44), calls=%async_computation.1 | async-start | bytes 819200 | tf_op jit(solution)/shard_map/all_to_all | solution.py:36
  51.4 0.3 fusion.3
  51.7 0.7 pad_maximum_fusion.refs_2_
  52.4 10.4 %all-to-all-done.1 = bf16[8,40,640]{2,1,0:T(8,128)(2,1)S(1)} async-done(((bf16[8,40,640]{2,1,0:T(8,128)(2,1)}), bf16[8,40,640]{2,1,0:T(8,128)(2,1)S(1)}, u32[]{:S(2)}, u32[]{:S(2)}) %all-to-all-start.1) | async-done | bytes 409632 | tf_op jit(solution)/shard_map/all_to_all | solution.py:36
  62.8 6.7 %collective-permute-start.3 = (bf16[320,640]{1,0:T(8,128)(2,1)S(1)}, bf16[320,640]{1,0:T(8,128)(2,1)S(1)}, u32[]{:S(2)}, u32[]{:S(2)}) collective-permute-start(bf16[320,640]{1,0:T(8,128)(2,1)S(1)} %bitcast.33), channel_id=1, source_target_pairs={{0,32},{32,0},{1,33},{33,1},{2,34},{34,2},{3,35},{35,3},{4,36},{36... | collective-permute-start | bytes 1228808 | tf_op jit(solution)/shard_map/ppermute | solution.py:25
  69.6 0.7 bitcast_convert_fusion.2
  70.3 0.7 multiply_add_fusion.slot_of
  71.0 0.7 copy-done.13
  71.7 16.8 %heads.1 = (bf16[384,256]{1,0:T(8,128)(2,1)}, bf16[384,256]{1,0:T(8,128)(2,1)}, bf16[384,256]{1,0:T(8,128)(2,1)}, bf16[384,256]{1,0:T(8,128)(2,1)}, bf16[320,640]{1,0:T(8,128)(2,1)}, /*index=5*/bf16[320,640]{1,0:T(8,128)(2,1)}) custom-call(s32[3]{0:T(128)} %pad_add_fusion.where, bf16[320,640]{1,0:T(8,128)(2,1)} %bitcast.34, bf16[320,640]{1,0:T(8,128)(2,1)} %copy-done.13, ...), custom_call_target="tpu_custom_call" | custom-call | flops 20000000000 | bytes 12000000 | tf_op jit(solution)/shard_map/heads/pallas_call | solution.py:280
  88.6 4.9 %collective-permute-start.12 = (bf16[320,640]{1,0:T(8,128)(2,1)}, bf16[320,640]{1,0:T(8,128)(2,1)S(1)}, u32[]{:S(2)}, u32[]{:S(2)}) collective-permute-start(bf16[320,640]{1,0:T(8,128)(2,1)} %get-tuple-element.51), channel_id=1, source_target_pairs={{0,32},{32,0},{1,33},{33,1},{2,34},{34,2},{3,35},{35,3},{4,36},{36... | collective-permute-start | bytes 1228808 | tf_op jit(solution)/shard_map/ppermute | solution.py:25
  93.5 2.7 %route.1 = (bf16[6,32,640]{2,1,0:T(8,128)(2,1)}, bf16[6,32,640]{2,1,0:T(8,128)(2,1)}, bf16[6,32,640]{2,1,0:T(8,128)(2,1)}, bf16[6,32,640]{2,1,0:T(8,128)(2,1)}) custom-call(s32[48]{0:T(128)} %multiply_add_fusion.slot_of, bf16[384,256]{1,0:T(8,128)(2,1)} %get-tuple-element.36.refs_0_, bf16[384,256]{1,0:T(8,128)(2,1)} %get-tuple-element.37.refs_1_, ...), custom_call_target="tpu_custom_call" | custom-call | tf_op jit(solution)/shard_map/route/pallas_call | solution.py:324
  96.2 1.9 %add_convert_fusion = bf16[320,640]{1,0:T(8,128)(2,1)} fusion(bf16[320,640]{1,0:T(8,128)(2,1)S(1)} %collective-permute-done.12, bf16[320,640]{1,0:T(8,128)(2,1)} %get-tuple-element.50), kind=kLoop, calls=%fused_computation | loop fusion | flops 819200 | bytes 1228800 | tf_op jit(solution)/shard_map/convert_element_type | solution.py:495
  98.1 7.0 %all-to-all-start.2 = ((bf16[8,40,640]{2,1,0:T(8,128)(2,1)}), bf16[8,40,640]{2,1,0:T(8,128)(2,1)S(1)}, u32[]{:S(2)}, u32[]{:S(2)}) async-start(bf16[8,40,640]{2,1,0:T(8,128)(2,1)} %bitcast.18), calls=%async_computation.2 | async-start | bytes 819200 | tf_op jit(solution)/shard_map/all_to_all | solution.py:36
  105.1 1.9 %collective-permute-start.4 = (bf16[6,32,640]{2,1,0:T(8,128)(2,1)S(1)}, bf16[6,32,640]{2,1,0:T(8,128)(2,1)S(1)}, u32[]{:S(2)}, u32[]{:S(2)}) collective-permute-start(bf16[6,32,640]{2,1,0:T(8,128)(2,1)S(1)} %copy-done.16), channel_id=1, source_target_pairs={{0,192},{64,0},{128,64},{192,128},{1,193},{65,1},{129,65},{193,129... | collective-permute-start | bytes 737288 | tf_op jit(solution)/shard_map/ppermute | solution.py:32
  107.0 3.4 %collective-permute-start.5 = (bf16[6,32,640]{2,1,0:T(8,128)(2,1)S(1)}, bf16[6,32,640]{2,1,0:T(8,128)(2,1)S(1)}, u32[]{:S(2)}, u32[]{:S(2)}) collective-permute-start(bf16[6,32,640]{2,1,0:T(8,128)(2,1)S(1)} %copy-done.15), channel_id=1, source_target_pairs={{0,64},{64,128},{128,192},{192,0},{1,65},{65,129},{129,193},{193,1... | collective-permute-start | bytes 737288 | tf_op jit(solution)/shard_map/ppermute | solution.py:32
  110.4 10.2 %all-to-all-done.2 = bf16[8,40,640]{2,1,0:T(8,128)(2,1)S(1)} async-done(((bf16[8,40,640]{2,1,0:T(8,128)(2,1)}), bf16[8,40,640]{2,1,0:T(8,128)(2,1)S(1)}, u32[]{:S(2)}, u32[]{:S(2)}) %all-to-all-start.2) | async-done | bytes 409632 | tf_op jit(solution)/shard_map/all_to_all | solution.py:36
  120.6 0.1 reshape.658
  120.8 0.8 broadcast_in_dim.47
  121.6 14.9 %all-to-all-start.3 = ((bf16[12,40,160]{2,1,0:T(8,128)(2,1)}), bf16[12,40,160]{2,1,0:T(8,128)(2,1)S(1)}, u32[]{:S(2)}, u32[]{:S(2)}) async-start(bf16[12,40,160]{2,1,0:T(8,128)(2,1)} %bitcast.20), calls=%async_computation.3 | async-start | bytes 491520 | tf_op jit(solution)/shard_map/all_to_all | solution.py:36
  136.5 2.1 %collective-permute-start.6 = (bf16[6,32,640]{2,1,0:T(8,128)(2,1)S(1)}, bf16[6,32,640]{2,1,0:T(8,128)(2,1)S(1)}, u32[]{:S(2)}, u32[]{:S(2)}) collective-permute-start(bf16[6,32,640]{2,1,0:T(8,128)(2,1)S(1)} %copy-done.14), channel_id=1, source_target_pairs={{0,128},{64,192},{128,0},{192,64},{1,129},{65,193},{129,1},{193,65... | collective-permute-start | bytes 737288 | tf_op jit(solution)/shard_map/ppermute | solution.py:32
  138.6 8.0 %collective-permute-done.6.refs_3_ = bf16[6,32,640]{2,1,0:T(8,128)(2,1)S(1)} collective-permute-done((bf16[6,32,640]{2,1,0:T(8,128)(2,1)S(1)}, bf16[6,32,640]{2,1,0:T(8,128)(2,1)S(1)}, u32[]{:S(2)}, u32[]{:S(2)}) %collective-permute-start.6) | collective-permute-done | bytes 245792 | tf_op jit(solution)/shard_map/ppermute | solution.py:32
  146.6 0.7 copy-done.4
  147.3 2.4 %regroup.1 = (bf16[4,32,640]{2,1,0:T(8,128)(2,1)}, bf16[4,32,640]{2,1,0:T(8,128)(2,1)}, bf16[4,32,640]{2,1,0:T(8,128)(2,1)}, bf16[4,32,640]{2,1,0:T(8,128)(2,1)}...) custom-call(s32[3]{0:T(128)} %pad_add_fusion.where, bf16[6,32,640]{2,1,0:T(8,128)(2,1)} %get-tuple-element.40.refs_0_, ...), custom_call_target="tpu_custom_call" | custom-call | tf_op jit(solution)/shard_map/regroup/pallas_call | solution.py:350
  149.7 3.5 %collective-permute-start.7 = (bf16[4,32,640]{2,1,0:T(8,128)(2,1)}, bf16[4,32,640]{2,1,0:T(8,128)(2,1)S(1)}, u32[]{:S(2)}, u32[]{:S(2)}) collective-permute-start(bf16[4,32,640]{2,1,0:T(8,128)(2,1)} %get-tuple-element.45), channel_id=1, source_target_pairs={{0,32},{32,0},{256,288},{288,256},{512,544},{544,512},{1,33},{33,1... | collective-permute-start | bytes 491528 | tf_op jit(solution)/shard_map/ppermute | solution.py:369
  153.2 3.3 %collective-permute-start.8 = (bf16[4,32,640]{2,1,0:T(8,128)(2,1)}, bf16[4,32,640]{2,1,0:T(8,128)(2,1)S(1)}, u32[]{:S(2)}, u32[]{:S(2)}) collective-permute-start(bf16[4,32,640]{2,1,0:T(8,128)(2,1)} %get-tuple-element.46), channel_id=1, source_target_pairs={{0,256},{32,288},{256,512},{288,544},{512,0},{544,32},{1,257},{33,... | collective-permute-start | bytes 491528 | tf_op jit(solution)/shard_map/ppermute | solution.py:369
  156.6 3.3 %collective-permute-start.9 = (bf16[4,32,640]{2,1,0:T(8,128)(2,1)}, bf16[4,32,640]{2,1,0:T(8,128)(2,1)S(1)}, u32[]{:S(2)}, u32[]{:S(2)}) collective-permute-start(bf16[4,32,640]{2,1,0:T(8,128)(2,1)} %get-tuple-element.47), channel_id=1, source_target_pairs={{0,288},{32,256},{256,544},{288,512},{512,32},{544,0},{1,289},{33,... | collective-permute-start | bytes 491528 | tf_op jit(solution)/shard_map/ppermute | solution.py:369
  159.8 3.1 %collective-permute-start.10 = (bf16[4,32,640]{2,1,0:T(8,128)(2,1)}, bf16[4,32,640]{2,1,0:T(8,128)(2,1)S(1)}, u32[]{:S(2)}, u32[]{:S(2)}) collective-permute-start(bf16[4,32,640]{2,1,0:T(8,128)(2,1)} %get-tuple-element.48), channel_id=1, source_target_pairs={{0,512},{32,544},{256,0},{288,32},{512,256},{544,288},{1,513},{33,... | collective-permute-start | bytes 491528 | tf_op jit(solution)/shard_map/ppermute | solution.py:369
  162.9 2.3 %collective-permute-start.11 = (bf16[4,32,640]{2,1,0:T(8,128)(2,1)}, bf16[4,32,640]{2,1,0:T(8,128)(2,1)S(1)}, u32[]{:S(2)}, u32[]{:S(2)}) collective-permute-start(bf16[4,32,640]{2,1,0:T(8,128)(2,1)} %get-tuple-element.49), channel_id=1, source_target_pairs={{0,544},{32,512},{256,32},{288,0},{512,288},{544,256},{1,545},{33,... | collective-permute-start | bytes 491528 | tf_op jit(solution)/shard_map/ppermute | solution.py:369
  165.4 0.7 broadcast_in_dim.48
  166.1 3.4 %all-to-all-start.4 = ((bf16[8,40,160]{2,1,0:T(8,128)(2,1)}), bf16[8,40,160]{2,1,0:T(8,128)(2,1)S(1)}, u32[]{:S(2)}, u32[]{:S(2)}) async-start(bf16[8,40,160]{2,1,0:T(8,128)(2,1)} %broadcast_in_dim.48), calls=%async_computation.4 | async-start | bytes 327680 | tf_op jit(solution)/shard_map/all_to_all | solution.py:36
  169.4 0.6 pad_add_fusion.1.places
  170.1 2.9 %collective-permute-done.11.refs_5_ = bf16[4,32,640]{2,1,0:T(8,128)(2,1)S(1)} collective-permute-done((bf16[4,32,640]{2,1,0:T(8,128)(2,1)}, bf16[4,32,640]{2,1,0:T(8,128)(2,1)S(1)}, u32[]{:S(2)}, u32[]{:S(2)}) %collective-permute-start.11) | collective-permute-done | bytes 163872 | tf_op jit(solution)/shard_map/ppermute | solution.py:369
  173.0 0.6 copy-done.9
  173.6 3.0 %settle.1 = bf16[24,32,640]{2,1,0:T(8,128)(2,1)} custom-call(s32[3]{0:T(128)} %pad_add_fusion.where, s32[4]{0:T(128)} %pad_add_fusion.1.places, bf16[4,32,640]{2,1,0:T(8,128)(2,1)} %get-tuple-element.44.refs_0_, bf16[4,32,640]{2,1,0:T(8,128)(2,1)} %copy-done.5, bf16[4,32,640]{2,1,0:T(8,128)(2,1)} %copy-done.6, bf16[4,32,640]{2,1,0:T(8,128)(2,1)} %copy-done.7, ...), custom_call_target="tpu_custom_call" | custom-call | tf_op jit(solution)/shard_map/settle/pallas_call | solution.py:395
  176.7 0.7 copy-done
  177.3 1.7 finish.1
  (56 shorter events, 0.5 us)
Async XLA Ops:
  7.2 62.3 %collective-permute-start = (bf16[976,640]{1,0:T(8,128)(2,1)}, bf16[976,640]{1,0:T(8,128)(2,1)}, u32[]{:S(2)}, u32[]{:S(2)}) collective-permute-start(bf16[976,640]{1,0:T(8,128)(2,1)} %get-tuple-element.28), channel_id=1, source_target_pairs={{0,192},{64,0},{128,64},{192,128},{1,193},{65,1},{129,65},{193,129... | collective-permute-start | bytes 3747848 | tf_op jit(solution)/shard_map/ppermute | solution.py:32
  12.4 57.1 %collective-permute-start.1 = (bf16[976,640]{1,0:T(8,128)(2,1)}, bf16[976,640]{1,0:T(8,128)(2,1)S(1)}, u32[]{:S(2)}, u32[]{:S(2)}) collective-permute-start(bf16[976,640]{1,0:T(8,128)(2,1)} %get-tuple-element.29), channel_id=1, source_target_pairs={{0,64},{64,128},{128,192},{192,0},{1,65},{65,129},{129,193},{193,1... | collective-permute-start | bytes 3747848 | tf_op jit(solution)/shard_map/ppermute | solution.py:32
  14.3 55.3 %collective-permute-start.2 = (bf16[976,640]{1,0:T(8,128)(2,1)}, bf16[976,640]{1,0:T(8,128)(2,1)S(1)}, u32[]{:S(2)}, u32[]{:S(2)}) collective-permute-start(bf16[976,640]{1,0:T(8,128)(2,1)} %get-tuple-element.30), channel_id=1, source_target_pairs={{0,128},{64,192},{128,0},{192,64},{1,129},{65,193},{129,1},{193,65... | collective-permute-start | bytes 3747848 | tf_op jit(solution)/shard_map/ppermute | solution.py:32
  18.9 51.4 %copy-start.10 = (s32[12,1]{0,1:T(1,128)S(1)}, s32[12,1]{0,1:T(1,128)}, u32[]{:S(2)}) copy-start(s32[12,1]{0,1:T(1,128)} %param.12) | copy-start | bytes 148
  19.5 24.1 %all-to-all-start = ((bf16[4,40,160]{2,1,0:T(8,128)(2,1)}), bf16[4,40,160]{2,1,0:T(8,128)(2,1)S(1)}, u32[]{:S(2)}, u32[]{:S(2)}) async-start(bf16[4,40,160]{2,1,0:T(8,128)(2,1)} %broadcast_in_dim.42), calls=%async_computation | async-start | bytes 163840 | tf_op jit(solution)/shard_map/all_to_all | solution.py:36
  44.6 18.2 %all-to-all-start.1 = ((bf16[8,40,640]{2,1,0:T(8,128)(2,1)}), bf16[8,40,640]{2,1,0:T(8,128)(2,1)S(1)}, u32[]{:S(2)}, u32[]{:S(2)}) async-start(bf16[8,40,640]{2,1,0:T(8,128)(2,1)} %broadcast_in_dim.44), calls=%async_computation.1 | async-start | bytes 819200 | tf_op jit(solution)/shard_map/all_to_all | solution.py:36
  62.8 8.2 %copy-start.1 = (bf16[8,40,640]{2,1,0:T(8,128)(2,1)}, bf16[8,40,640]{2,1,0:T(8,128)(2,1)S(1)}, u32[]{:S(2)}) copy-start(bf16[8,40,640]{2,1,0:T(8,128)(2,1)S(1)} %all-to-all-done.1) | copy-start | bytes 1228804
  62.8 8.2 %collective-permute-start.3 = (bf16[320,640]{1,0:T(8,128)(2,1)S(1)}, bf16[320,640]{1,0:T(8,128)(2,1)S(1)}, u32[]{:S(2)}, u32[]{:S(2)}) collective-permute-start(bf16[320,640]{1,0:T(8,128)(2,1)S(1)} %bitcast.33), channel_id=1, source_target_pairs={{0,32},{32,0},{1,33},{33,1},{2,34},{34,2},{3,35},{35,3},{4,36},{36... | collective-permute-start | bytes 1228808 | tf_op jit(solution)/shard_map/ppermute | solution.py:25
  69.5 1.5 copy-start.11
  69.6 1.4 copy-start.12
  71.0 0.8 copy-start.13
  88.6 7.6 %collective-permute-start.12 = (bf16[320,640]{1,0:T(8,128)(2,1)}, bf16[320,640]{1,0:T(8,128)(2,1)S(1)}, u32[]{:S(2)}, u32[]{:S(2)}) collective-permute-start(bf16[320,640]{1,0:T(8,128)(2,1)} %get-tuple-element.51), channel_id=1, source_target_pairs={{0,32},{32,0},{1,33},{33,1},{2,34},{34,2},{3,35},{35,3},{4,36},{36... | collective-permute-start | bytes 1228808 | tf_op jit(solution)/shard_map/ppermute | solution.py:25
  96.2 8.9 %copy-start.16 = (bf16[6,32,640]{2,1,0:T(8,128)(2,1)S(1)}, bf16[6,32,640]{2,1,0:T(8,128)(2,1)}, u32[]{:S(2)}) copy-start(bf16[6,32,640]{2,1,0:T(8,128)(2,1)} %get-tuple-element.41) | copy-start | bytes 737284
  96.2 10.8 %copy-start.15 = (bf16[6,32,640]{2,1,0:T(8,128)(2,1)S(1)}, bf16[6,32,640]{2,1,0:T(8,128)(2,1)}, u32[]{:S(2)}) copy-start(bf16[6,32,640]{2,1,0:T(8,128)(2,1)} %get-tuple-element.42) | copy-start | bytes 737284
  98.1 38.4 %copy-start.14 = (bf16[6,32,640]{2,1,0:T(8,128)(2,1)S(1)}, bf16[6,32,640]{2,1,0:T(8,128)(2,1)}, u32[]{:S(2)}) copy-start(bf16[6,32,640]{2,1,0:T(8,128)(2,1)} %get-tuple-element.43) | copy-start | bytes 737284
  98.1 22.5 %all-to-all-start.2 = ((bf16[8,40,640]{2,1,0:T(8,128)(2,1)}), bf16[8,40,640]{2,1,0:T(8,128)(2,1)S(1)}, u32[]{:S(2)}, u32[]{:S(2)}) async-start(bf16[8,40,640]{2,1,0:T(8,128)(2,1)} %bitcast.18), calls=%async_computation.2 | async-start | bytes 819200 | tf_op jit(solution)/shard_map/all_to_all | solution.py:36
  105.1 15.7 %collective-permute-start.4 = (bf16[6,32,640]{2,1,0:T(8,128)(2,1)S(1)}, bf16[6,32,640]{2,1,0:T(8,128)(2,1)S(1)}, u32[]{:S(2)}, u32[]{:S(2)}) collective-permute-start(bf16[6,32,640]{2,1,0:T(8,128)(2,1)S(1)} %copy-done.16), channel_id=1, source_target_pairs={{0,192},{64,0},{128,64},{192,128},{1,193},{65,1},{129,65},{193,129... | collective-permute-start | bytes 737288 | tf_op jit(solution)/shard_map/ppermute | solution.py:32
  107.0 13.8 %collective-permute-start.5 = (bf16[6,32,640]{2,1,0:T(8,128)(2,1)S(1)}, bf16[6,32,640]{2,1,0:T(8,128)(2,1)S(1)}, u32[]{:S(2)}, u32[]{:S(2)}) collective-permute-start(bf16[6,32,640]{2,1,0:T(8,128)(2,1)S(1)} %copy-done.15), channel_id=1, source_target_pairs={{0,64},{64,128},{128,192},{192,0},{1,65},{65,129},{129,193},{193,1... | collective-permute-start | bytes 737288 | tf_op jit(solution)/shard_map/ppermute | solution.py:32
  120.8 25.9 %copy-start.2 = (bf16[6,32,640]{2,1,0:T(8,128)(2,1)}, bf16[6,32,640]{2,1,0:T(8,128)(2,1)S(1)}, u32[]{:S(2)}) copy-start(bf16[6,32,640]{2,1,0:T(8,128)(2,1)S(1)} %collective-permute-done.4.refs_1_) | copy-start | bytes 737284
  120.8 25.8 %copy-start.3 = (bf16[6,32,640]{2,1,0:T(8,128)(2,1)}, bf16[6,32,640]{2,1,0:T(8,128)(2,1)S(1)}, u32[]{:S(2)}) copy-start(bf16[6,32,640]{2,1,0:T(8,128)(2,1)S(1)} %collective-permute-done.5.refs_2_) | copy-start | bytes 737284
  121.6 43.7 %all-to-all-start.3 = ((bf16[12,40,160]{2,1,0:T(8,128)(2,1)}), bf16[12,40,160]{2,1,0:T(8,128)(2,1)S(1)}, u32[]{:S(2)}, u32[]{:S(2)}) async-start(bf16[12,40,160]{2,1,0:T(8,128)(2,1)} %bitcast.20), calls=%async_computation.3 | async-start | bytes 491520 | tf_op jit(solution)/shard_map/all_to_all | solution.py:36
  136.5 10.1 %collective-permute-start.6 = (bf16[6,32,640]{2,1,0:T(8,128)(2,1)S(1)}, bf16[6,32,640]{2,1,0:T(8,128)(2,1)S(1)}, u32[]{:S(2)}, u32[]{:S(2)}) collective-permute-start(bf16[6,32,640]{2,1,0:T(8,128)(2,1)S(1)} %copy-done.14), channel_id=1, source_target_pairs={{0,128},{64,192},{128,0},{192,64},{1,129},{65,193},{129,1},{193,65... | collective-permute-start | bytes 737288 | tf_op jit(solution)/shard_map/ppermute | solution.py:32
  146.6 0.7 copy-start.4
  149.7 20.4 %collective-permute-start.7 = (bf16[4,32,640]{2,1,0:T(8,128)(2,1)}, bf16[4,32,640]{2,1,0:T(8,128)(2,1)S(1)}, u32[]{:S(2)}, u32[]{:S(2)}) collective-permute-start(bf16[4,32,640]{2,1,0:T(8,128)(2,1)} %get-tuple-element.45), channel_id=1, source_target_pairs={{0,32},{32,0},{256,288},{288,256},{512,544},{544,512},{1,33},{33,1... | collective-permute-start | bytes 491528 | tf_op jit(solution)/shard_map/ppermute | solution.py:369
  153.2 16.8 %collective-permute-start.8 = (bf16[4,32,640]{2,1,0:T(8,128)(2,1)}, bf16[4,32,640]{2,1,0:T(8,128)(2,1)S(1)}, u32[]{:S(2)}, u32[]{:S(2)}) collective-permute-start(bf16[4,32,640]{2,1,0:T(8,128)(2,1)} %get-tuple-element.46), channel_id=1, source_target_pairs={{0,256},{32,288},{256,512},{288,544},{512,0},{544,32},{1,257},{33,... | collective-permute-start | bytes 491528 | tf_op jit(solution)/shard_map/ppermute | solution.py:369
  156.6 13.5 %collective-permute-start.9 = (bf16[4,32,640]{2,1,0:T(8,128)(2,1)}, bf16[4,32,640]{2,1,0:T(8,128)(2,1)S(1)}, u32[]{:S(2)}, u32[]{:S(2)}) collective-permute-start(bf16[4,32,640]{2,1,0:T(8,128)(2,1)} %get-tuple-element.47), channel_id=1, source_target_pairs={{0,288},{32,256},{256,544},{288,512},{512,32},{544,0},{1,289},{33,... | collective-permute-start | bytes 491528 | tf_op jit(solution)/shard_map/ppermute | solution.py:369
  159.8 10.3 %collective-permute-start.10 = (bf16[4,32,640]{2,1,0:T(8,128)(2,1)}, bf16[4,32,640]{2,1,0:T(8,128)(2,1)S(1)}, u32[]{:S(2)}, u32[]{:S(2)}) collective-permute-start(bf16[4,32,640]{2,1,0:T(8,128)(2,1)} %get-tuple-element.48), channel_id=1, source_target_pairs={{0,512},{32,544},{256,0},{288,32},{512,256},{544,288},{1,513},{33,... | collective-permute-start | bytes 491528 | tf_op jit(solution)/shard_map/ppermute | solution.py:369
  162.9 10.1 %collective-permute-start.11 = (bf16[4,32,640]{2,1,0:T(8,128)(2,1)}, bf16[4,32,640]{2,1,0:T(8,128)(2,1)S(1)}, u32[]{:S(2)}, u32[]{:S(2)}) collective-permute-start(bf16[4,32,640]{2,1,0:T(8,128)(2,1)} %get-tuple-element.49), channel_id=1, source_target_pairs={{0,544},{32,512},{256,32},{288,0},{512,288},{544,256},{1,545},{33,... | collective-permute-start | bytes 491528 | tf_op jit(solution)/shard_map/ppermute | solution.py:369
  166.1 10.6 %all-to-all-start.4 = ((bf16[8,40,160]{2,1,0:T(8,128)(2,1)}), bf16[8,40,160]{2,1,0:T(8,128)(2,1)S(1)}, u32[]{:S(2)}, u32[]{:S(2)}) async-start(bf16[8,40,160]{2,1,0:T(8,128)(2,1)} %broadcast_in_dim.48), calls=%async_computation.4 | async-start | bytes 327680 | tf_op jit(solution)/shard_map/all_to_all | solution.py:36
  170.1 2.9 %copy-start.5 = (bf16[4,32,640]{2,1,0:T(8,128)(2,1)}, bf16[4,32,640]{2,1,0:T(8,128)(2,1)S(1)}, u32[]{:S(2)}) copy-start(bf16[4,32,640]{2,1,0:T(8,128)(2,1)S(1)} %collective-permute-done.7.refs_1_) | copy-start | bytes 491524
  170.1 2.9 %copy-start.6 = (bf16[4,32,640]{2,1,0:T(8,128)(2,1)}, bf16[4,32,640]{2,1,0:T(8,128)(2,1)S(1)}, u32[]{:S(2)}) copy-start(bf16[4,32,640]{2,1,0:T(8,128)(2,1)S(1)} %collective-permute-done.8.refs_2_) | copy-start | bytes 491524
  170.1 2.9 %copy-start.7 = (bf16[4,32,640]{2,1,0:T(8,128)(2,1)}, bf16[4,32,640]{2,1,0:T(8,128)(2,1)S(1)}, u32[]{:S(2)}) copy-start(bf16[4,32,640]{2,1,0:T(8,128)(2,1)S(1)} %collective-permute-done.9.refs_3_) | copy-start | bytes 491524
  170.1 2.9 %copy-start.8 = (bf16[4,32,640]{2,1,0:T(8,128)(2,1)}, bf16[4,32,640]{2,1,0:T(8,128)(2,1)S(1)}, u32[]{:S(2)}) copy-start(bf16[4,32,640]{2,1,0:T(8,128)(2,1)S(1)} %collective-permute-done.10.refs_4_) | copy-start | bytes 491524
  173.0 0.7 copy-start.9
  176.7 0.7 copy-start
